TPU v7x, 768 devices: a whole 4x8x12 slice. The times are simulated.
768 devices in a mesh: lat: 48 (over y_lo, z, core), lon: 4 (over y_hi), mem: 4 (over x).
Axes of the slice: x: 4, y: 8 (y_hi: 4, y_lo: 2; y = y_hi * 2 + y_lo), z: 12, core: 2. Of those that a mesh axis runs over, the one named last changes fastest.
Arguments:
- column_state: float32 [8, 64, 192, 512], P('mem', None, 'lat', 'lon'), may hold values from -6 to 6
- cotangent: float32 [8, 64, 192, 512], P('mem', None, 'lat', 'lon'), may hold values from -6 to 6
- land_mask: int32 [192, 512], P('lat', 'lon'), may hold values from 0 to 1
- orography: int32 [192, 512], P('lat', 'lon'), may hold values from 0 to 15
- member_seeds: int32 [8], P('mem'), may hold values from 0 to 31
- land_table: float32 [2, 64], replicated, may hold values from -5 to 5
- relief_table: float32 [16, 64], replicated, may hold values from -5 to 5
- seed_table: float32 [32, 64], replicated, may hold values from -5 to 5
- w_hidden: bfloat16 [384, 640], replicated, may hold values from -0.25 to 0.25
- b_hidden: float32 [384], replicated, may hold values from -4 to 4
- w_tendency: bfloat16 [64, 384], replicated, may hold values from -0.3125 to 0.3125
Outputs:
- next_state: float32 [8, 64, 192, 512], P('mem', None, 'lat', 'lon')
- state_grad: float32 [8, 64, 192, 512], P('mem', None, 'lat', 'lon')
- grad_w_hidden: float32 [384, 640], replicated
- grad_b_hidden: float32 [384], replicated
- grad_w_tendency: float32 [64, 384], replicated
All inputs are finite; a program needn't handle non-finite values.
Results may differ from a plain program's by a relative error of at most 0.0059.
Values may be sent and summed in bfloat16 or wider, within the bound.
No kernel may reach another device: no remote copies, remote signals or barrier semaphores. Data moves between devices by JAX's collectives and lax.ppermute only.
A program may use at most 64 MiB of HBM per device.

v0:
```python
import math

import jax
import jax.numpy as jnp
from jax import lax
from jax.sharding import PartitionSpec as P

MODES = 171


damp_strength = 2.0


def extended(x, sides, width, wrap):
    for axis, dim in sides:
        peers, length = (lax.axis_size(axis), x.shape[dim])
        up = [(i, (i + 1) % peers) for i in range(peers if wrap else peers - 1)]
        down = [(j, i) for i, j in up]
        last = lax.slice_in_dim(x, length - width, length, axis=dim)
        leading = lax.slice_in_dim(x, 0, width, axis=dim)
        before = lax.ppermute(last, axis, up)
        after = lax.ppermute(leading, axis, down)
        x = jnp.concatenate([before, x, after], axis=dim)
    return x


def zonal_basis(positions, lon_total):
    wavenumber = jnp.arange(MODES, dtype=jnp.int32)
    phases = wavenumber[:, None] * positions[None, :] % lon_total
    angles = phases.astype(jnp.float32) * (2.0 * math.pi / lon_total)
    analysis = jnp.concatenate([jnp.cos(angles), jnp.sin(angles)], 0)
    weights = jnp.where(wavenumber == 0, 1.0, 2.0).astype(jnp.float32) / lon_total
    weights = jnp.concatenate([weights, weights], 0)
    return (analysis, analysis * weights[:, None])


def removal_table(lat_index, lat_total):
    latitude = math.pi * ((lat_index.astype(jnp.float32) + 0.5) / lat_total - 0.5)
    fraction = jnp.arange(MODES, dtype=jnp.int32).astype(jnp.float32) / MODES
    shrink = 1.0 - jnp.exp(
        -damp_strength * fraction[None, :] ** 2 / jnp.cos(latitude)[:, None] ** 2
    )
    return jnp.concatenate([shrink, shrink], 1)


def state_rims(values):
    widened = extended(values, (("lon", 3),), 1, True)
    return extended(widened, (("lat", 2),), 1, False)


def gradient_rims(values):
    widened = extended(values, (("lon", 3),), 1, True)
    return extended(widened, (("lat", 2),), 1, False)


def zonal(values, select):
    lon_cols = values.shape[3]
    lon_total = lon_cols * lax.axis_size("lon")
    positions = lax.axis_index("lon") * lon_cols + jnp.arange(lon_cols, dtype=jnp.int32)
    matrix = zonal_basis(positions, lon_total)[select]
    partial_sum = jnp.einsum("msji,ki->msjk", values, matrix, precision=lax.Precision.HIGHEST)
    return lax.psum(partial_sum, "lon")


def on_device(
    column_state,
    cotangent,
    land_mask,
    orography,
    member_seeds,
    land_table,
    relief_table,
    seed_table,
    w_hidden,
    b_hidden,
    w_tendency,
):
    highest = lax.Precision.HIGHEST
    members, channels, lat_rows, lon_cols = column_state.shape
    columns = lat_rows * lon_cols
    lat_total = lat_rows * lax.axis_size("lat")
    lon_total = lon_cols * lax.axis_size("lon")
    padded = state_rims(column_state.astype(jnp.bfloat16))
    stencil = jnp.stack(
        [
            padded[:, :, row_off : row_off + lat_rows, col_off : col_off + lon_cols]
            for row_off in range(3)
            for col_off in range(3)
        ],
        1,
    )
    stencil = stencil.reshape(members, 9 * channels, columns)
    land_part = jnp.where(
        land_mask[None] == 1, land_table[1][:, None, None], land_table[0][:, None, None]
    )
    classes = relief_table.shape[0]
    relief_pick = (orography[None] == jnp.arange(classes, dtype=jnp.int32)[:, None, None]).astype(
        jnp.float32
    )
    relief = jnp.einsum("ce,crl->erl", relief_table, relief_pick, precision=highest)
    seed_pick = (
        member_seeds[:, None] == jnp.arange(seed_table.shape[0], dtype=jnp.int32)[None]
    ).astype(jnp.float32)
    seed_rows = jnp.einsum("mq,qe->me", seed_pick, seed_table, precision=highest)
    forcing = (land_part + relief)[None] + seed_rows[:, :, None, None]
    forcing = forcing.reshape(members, forcing.shape[1], columns).astype(jnp.bfloat16)
    features = jnp.concatenate([stencil, forcing], 1)
    preact = (
        jnp.einsum("hi,mic->mhc", w_hidden, features, preferred_element_type=jnp.float32)
        + b_hidden[None, :, None]
    )
    hidden = jax.nn.silu(preact).astype(jnp.bfloat16)
    tendency = jnp.einsum("sh,mhc->msc", w_tendency, hidden, preferred_element_type=jnp.float32)
    moist = column_state + tendency.reshape(column_state.shape)
    lat_index = lax.axis_index("lat") * lat_rows + jnp.arange(lat_rows, dtype=jnp.int32)
    removal = removal_table(lat_index, lat_total)
    positions = lax.axis_index("lon") * lon_cols + jnp.arange(lon_cols, dtype=jnp.int32)
    analysis, synthesis = zonal_basis(positions, lon_total)
    coeffs = zonal(moist, 0)
    next_state = moist - jnp.einsum(
        "msjk,ki->msji", coeffs * removal[None, None], synthesis, precision=highest
    )
    replies = zonal(cotangent, 1)
    moist_grad = cotangent - jnp.einsum(
        "msjk,ki->msji", replies * removal[None, None], analysis, precision=highest
    )
    tendency_grad = moist_grad.reshape(members, channels, columns).astype(jnp.bfloat16)
    grad_out = jnp.einsum("msc,mhc->sh", tendency_grad, hidden, preferred_element_type=jnp.float32)
    hidden_grad = jnp.einsum(
        "sh,msc->mhc", w_tendency, tendency_grad, preferred_element_type=jnp.float32
    )
    logistic = jax.nn.sigmoid(preact)
    preact_grad = (hidden_grad * logistic * (1.0 + preact * (1.0 - logistic))).astype(jnp.bfloat16)
    grad_in = jnp.einsum("mhc,mic->hi", preact_grad, features, preferred_element_type=jnp.float32)
    grad_bias = jnp.sum(preact_grad.astype(jnp.float32), (0, 2))
    stencil_grad = jnp.einsum(
        "hi,mhc->mic", w_hidden[:, : 9 * channels], preact_grad, preferred_element_type=jnp.float32
    )
    stencil_grad = stencil_grad.reshape(members, 9 * channels, lat_rows, lon_cols)
    spread = gradient_rims(stencil_grad)
    state_grad = moist_grad
    for row_off in range(3):
        for col_off in range(3):
            offset = (row_off * 3 + col_off) * channels
            state_grad = (
                state_grad
                + spread[
                    :,
                    offset : offset + channels,
                    2 - row_off : 2 - row_off + lat_rows,
                    2 - col_off : 2 - col_off + lon_cols,
                ]
            )
    summed_in, summed_bias, summed_out = lax.psum(
        (grad_in, grad_bias, grad_out), ("lat", "lon", "mem")
    )
    scaling = 1.0 / math.sqrt(members * lax.axis_size("mem") * lat_total * lon_total)
    return (
        next_state,
        state_grad,
        summed_in * scaling,
        summed_bias * scaling,
        summed_out * scaling,
    )


def solution(mesh):
    placed = (
        P("mem", None, "lat", "lon"),
        P("mem", None, "lat", "lon"),
        P("lat", "lon"),
        P("lat", "lon"),
        P("mem"),
        P(),
        P(),
        P(),
        P(),
        P(),
        P(),
    )
    return jax.shard_map(
        on_device,
        mesh=mesh,
        in_specs=placed,
        out_specs=(P("mem", None, "lat", "lon"), P("mem", None, "lat", "lon"), P(), P(), P()),
        check_vma=False,
    )
```

profile of v0, /device:TPU:1, one launch (start us, length us, event | category | flops | bytes accessed | tf_op | source)
XLA Modules:
  0.0 678.8 jit_solution(7645080347430283848)
XLA Ops:
  7.3 1.0 convert_element_type.42
  8.3 0.1 fusion.72
  8.4 5.0 collective-permute-start
  13.5 3.6 collective-permute-start.1
  17.1 0.7 broadcast_compare_fusion
  17.9 0.8 slice_bitcast_fusion.1
  18.6 0.4 fusion.55
  19.0 2.7 convolution_bitcast_fusion.1
  21.7 0.3 fusion.7
  22.0 0.2 fusion.59
  22.2 0.1 copy.88
  22.3 1.7 collective-permute-done.1
  24.1 0.4 pad_maximum_fusion.14
  24.4 0.2 fusion.71
  24.6 6.0 collective-permute-start.2
  30.7 5.5 collective-permute-start.3
  36.2 0.3 fusion.41
  36.5 0.5 fusion.40
  37.0 0.8 fusion.39
  37.7 0.2 fusion.37
  38.0 0.3 fusion.35
  38.4 0.4 fusion.33
  38.8 0.5 fusion.32
  39.3 0.8 fusion.31
  40.1 0.5 copy.50
  40.6 0.5 reshape.60
  41.2 0.7 copy.53
  41.9 3.3 fusion.5
  45.2 0.4 convolution_bitcast_fusion.2
  45.5 1.7 fusion.22
  47.2 0.2 all-reduce.5.cloned.1.call-start
  47.7 97.2 %all-reduce.7.cloned.1.call-done = (f32[2,64,4,342]{3,1,2,0:T(8,128)}, f32[2,64,4,342]{3,1,2,0:T(8,128)}) async-done(((f32[2,64,4,342]{3,1,2,0:T(8,128)}, f32[2,64,4,342]{3,1,2,0:T(8,128)}), (f32[2,64,4,342]{3,1,2,0:T(8,128)}, f32[2,64,4,342]{3,1,2,0:T(8,128)})) %all-reduce.7.cloned.1.call-update) | async-done | bytes 1400848 | tf_op jit(solution)/shard_map/psum | solution.py:62
  144.9 2.1 convolution_subtract_fusion
  147.0 0.9 convolution_bitcast_fusion.4
  147.9 0.8 convert_reduce_fusion
  148.7 0.1 copy-done.4
  148.8 1.8 convolution_bitcast_fusion
  150.6 1.8 fusion.10
  152.5 0.2 copy_bitcast_fusion
  152.7 1.2 copy-done.1
  153.9 3.5 reshape.62
  157.4 5.8 fusion.70
  163.2 2.1 copy.62
  165.3 2.1 copy.63
  167.4 4.2 collective-permute-start.5
  171.6 2.0 collective-permute-start.4
  173.6 2.7 convolution_subtract_fusion.1
  176.3 112.7 %psum.38 = f32[384]{0:T(512)S(1)} all-reduce(f32[384]{0:T(512)S(1)} %get-tuple-element.38), channel_id=1, replica_groups=mesh['lat'=48,'lon'=4,'mem'=4] {'lat','lon','mem'}, use_global_device_ids=true, to_apply=%region_4.5 | all-reduce | flops 384 | bytes 3072 | tf_op jit(solution)/shard_map/psum | solution.py:154
  289.0 2.2 copy.64
  291.2 2.2 copy.66
  293.3 4.1 pad_maximum_fusion.3
  297.4 2.5 copy.67
  299.9 2.5 copy.74
  302.3 1.9 collective-permute-start.7
  304.2 3.5 collective-permute-start.6
  307.8 0.6 broadcast_multiply_fusion.2
  308.3 0.9 copy.79
  309.2 350.6 %all-reduce.5.cloned.1.call-done = (f32[384,640]{1,0:T(8,128)}, f32[64,384]{1,0:T(8,128)}) async-done(((f32[384,640]{1,0:T(8,128)}, f32[64,384]{1,0:T(8,128)}), (f32[384,640]{1,0:T(8,128)}, f32[64,384]{1,0:T(8,128)})) %all-reduce.5.cloned.1.call-update) | async-done | bytes 1081360 | tf_op jit(solution)/shard_map/psum | solution.py:154
  659.8 1.5 broadcast_multiply_fusion.1
  661.4 2.2 broadcast_multiply_fusion
  663.6 2.4 copy.75
  666.0 2.3 copy.68
  668.3 2.8 fusion.16
  671.1 0.9 copy.80
  (43 shorter events, 0.5 us)
Async XLA Ops:
  7.2 38.0 %copy-start = (bf16[64,384]{1,0:T(8,128)(2,1)S(1)}, bf16[64,384]{1,0:T(8,128)(2,1)}, u32[]{:S(2)}) copy-start(bf16[64,384]{1,0:T(8,128)(2,1)} %param.21) | copy-start | bytes 147460
  7.2 14.5 %copy-start.8 = (f32[16,64]{1,0:T(8,128)S(1)}, f32[16,64]{1,0:T(8,128)}, u32[]{:S(2)}) copy-start(f32[16,64]{1,0:T(8,128)} %param.17) | copy-start | bytes 12292
  7.2 14.5 %copy-start.9 = (s32[4,128]{1,0:T(4,128)S(1)}, s32[4,128]{1,0:T(4,128)}, u32[]{:S(2)}) copy-start(s32[4,128]{1,0:T(4,128)} %param.14) | copy-start | bytes 6148
  7.2 14.8 %copy-start.7 = (f32[32,64]{1,0:T(8,128)S(1)}, f32[32,64]{1,0:T(8,128)}, u32[]{:S(2)}) copy-start(f32[32,64]{1,0:T(8,128)} %param.18) | copy-start | bytes 24580
  7.2 14.8 %copy-start.11 = (s32[2]{0:T(128)S(1)}, s32[2]{0:T(128)}, u32[]{:S(2)}) copy-start(s32[2]{0:T(128)} %param.15) | copy-start | bytes 28
  7.2 137.7 %all-reduce.7.cloned.1.call-start = ((), (), s32[]{:S(2)}) async-start(), calls=%async_computation.1 | async-start | bytes 3145728 | tf_op jit(solution)/shard_map/psum | solution.py:62
  8.4 13.9 %collective-permute-start = (bf16[2,64,4,1]{3,2,1,0:T(4,128)(2,1)S(1)}, bf16[2,64,4,1]{3,2,1,0:T(4,128)(2,1)S(1)}, u32[]{:S(2)}, u32[]{:S(2)}) collective-permute-start(bf16[2,64,4,1]{3,2,1,0:T(4,128)(2,1)S(1)} %get-tuple-element.30), channel_id=1, source_target_pairs={{0,4},{4,8},{8,12},{12,0},{1,5},{5,9},{9,13},{13,1},{2,6},{6,10},{... | collective-permute-start | bytes 3080 | tf_op jit(solution)/shard_map/ppermute | solution.py:21
  13.5 10.6 %collective-permute-start.1 = (bf16[2,64,4,1]{3,2,1,0:T(4,128)(2,1)S(1)}, bf16[2,64,4,1]{3,2,1,0:T(4,128)(2,1)S(1)}, u32[]{:S(2)}, u32[]{:S(2)}) collective-permute-start(bf16[2,64,4,1]{3,2,1,0:T(4,128)(2,1)S(1)} %get-tuple-element.31), channel_id=1, source_target_pairs={{4,0},{8,4},{12,8},{0,12},{5,1},{9,5},{13,9},{1,13},{6,2},{10,6},{... | collective-permute-start | bytes 3080 | tf_op jit(solution)/shard_map/ppermute | solution.py:22
  24.6 11.6 %collective-permute-start.2 = (bf16[2,64,1,130]{3,2,1,0:T(2,128)(2,1)S(1)}, bf16[2,64,1,130]{3,2,1,0:T(2,128)(2,1)S(1)}, u32[]{:S(2)}, u32[]{:S(2)}) collective-permute-start(bf16[2,64,1,130]{3,2,1,0:T(2,128)(2,1)S(1)} %get-tuple-element.29), channel_id=1, source_target_pairs={{0,16},{16,32},{32,48},{48,64},{64,80},{80,96},{96,112},{112,128},... | collective-permute-start | bytes 99848 | tf_op jit(solution)/shard_map/ppermute | solution.py:21
  30.7 11.2 %copy-start.3 = (bf16[2,64,512]{1,2,0:T(8,128)(2,1)}, bf16[2,64,512]{1,2,0:T(8,128)(2,1)S(1)}, u32[]{:S(2)}) copy-start(bf16[2,64,512]{1,2,0:T(8,128)(2,1)S(1)} %add_convert_fusion) | copy-start | bytes 393220
  30.7 7.3 %copy-start.2 = (f32[2,64,4,128]{3,2,1,0:T(4,128)S(1)}, f32[2,64,4,128]{3,2,1,0:T(4,128)}, u32[]{:S(2)}) copy-start(f32[2,64,4,128]{3,2,1,0:T(4,128)} %param.11) | copy-start | bytes 786436
  30.7 7.7 %collective-permute-start.3 = (bf16[2,64,1,130]{3,2,1,0:T(2,128)(2,1)S(1)}, bf16[2,64,1,130]{3,2,1,0:T(2,128)(2,1)S(1)}, u32[]{:S(2)}, u32[]{:S(2)}) collective-permute-start(bf16[2,64,1,130]{3,2,1,0:T(2,128)(2,1)S(1)} %get-tuple-element.28), channel_id=1, source_target_pairs={{16,0},{32,16},{48,32},{64,48},{80,64},{96,80},{112,96},{128,112},... | collective-permute-start | bytes 99848 | tf_op jit(solution)/shard_map/ppermute | solution.py:22
  41.1 0.7 copy-start.10
  45.5 99.4 %copy-start.6 = (f32[2,64,4,128]{3,2,1,0:T(4,128)S(1)}, f32[2,64,4,128]{3,2,1,0:T(4,128)}, u32[]{:S(2)}) copy-start(f32[2,64,4,128]{3,2,1,0:T(4,128)} %param.12) | copy-start | bytes 786436
  47.2 612.6 %all-reduce.5.cloned.1.call-start = ((), (), s32[]{:S(2)}) async-start(), calls=%async_computation | async-start | bytes 2162688 | tf_op jit(solution)/shard_map/psum | solution.py:154
  144.9 3.0 copy-start.12
  147.9 1.0 copy-start.4
  152.5 1.4 copy-start.1
  167.4 123.8 %collective-permute-start.5 = (f32[2,576,4,1]{1,2,3,0:T(4,128)S(1)}, f32[2,576,4,1]{1,2,3,0:T(4,128)S(1)}, u32[]{:S(2)}, u32[]{:S(2)}) collective-permute-start(f32[2,576,4,1]{1,2,3,0:T(4,128)S(1)} %copy.63), channel_id=1, source_target_pairs={{4,0},{8,4},{12,8},{0,12},{5,1},{9,5},{13,9},{1,13},{6,2},{10,6},{... | collective-permute-start | bytes 55304 | tf_op jit(solution)/shard_map/ppermute | solution.py:22
  171.6 117.4 %collective-permute-start.4 = (f32[2,576,4,1]{1,2,3,0:T(4,128)S(1)}, f32[2,576,4,1]{1,2,3,0:T(4,128)S(1)}, u32[]{:S(2)}, u32[]{:S(2)}) collective-permute-start(f32[2,576,4,1]{1,2,3,0:T(4,128)S(1)} %copy.62), channel_id=1, source_target_pairs={{0,4},{4,8},{8,12},{12,0},{1,5},{5,9},{9,13},{13,1},{2,6},{6,10},{... | collective-permute-start | bytes 55304 | tf_op jit(solution)/shard_map/ppermute | solution.py:21
  299.8 8.5 %copy-start.5 = (f32[2,64,4,128]{3,1,2,0:T(8,128)S(1)}, f32[2,64,4,128]{3,1,2,0:T(8,128)}, u32[]{:S(2)}) copy-start(f32[2,64,4,128]{3,1,2,0:T(8,128)} %convolution_subtract_fusion.1) | copy-start | bytes 786436
  302.3 361.3 %collective-permute-start.7 = (f32[2,576,1,130]{1,0,3,2:T(2,128)}, f32[2,576,1,130]{1,0,3,2:T(2,128)}, u32[]{:S(2)}, u32[]{:S(2)}) collective-permute-start(f32[2,576,1,130]{1,0,3,2:T(2,128)} %copy.74), channel_id=1, source_target_pairs={{0,16},{16,32},{32,48},{48,64},{64,80},{80,96},{96,112},{112,128},... | collective-permute-start | bytes 1797128 | tf_op jit(solution)/shard_map/ppermute | solution.py:21
  304.2 361.7 %collective-permute-start.6 = (f32[2,576,1,130]{1,0,3,2:T(2,128)}, f32[2,576,1,130]{1,0,3,2:T(2,128)}, u32[]{:S(2)}, u32[]{:S(2)}) collective-permute-start(f32[2,576,1,130]{1,0,3,2:T(2,128)} %copy.67), channel_id=1, source_target_pairs={{16,0},{32,16},{48,32},{64,48},{80,64},{96,80},{112,96},{128,112},... | collective-permute-start | bytes 1797128 | tf_op jit(solution)/shard_map/ppermute | solution.py:22
Sparse Core Ops, SparseCore 0:
  47.3 97.5 all-reduce.6
  173.7 486.0 all-reduce.4
where the time goes:
time: 681 us; the launch traced here: 679 us
  waiting for transfers between devices  450 us (66%)
  blocking collectives  113 us (17%)
  local copies, waits for them, and re-layouts  33.7 us (5%)
  starting transfers between devices  32 us (5%)
  matrix products  18.6 us (3%)
  other arithmetic  17.8 us (3%)
  between operations  14.4 us (2%)
    psum x1, waiting for transfers between devices, on_device(): lax.psum((grad_in, grad_bias, grad_out), ('lat', 'lon', 'mem'))  351 us
    psum x1, blocking collectives, on_device(): lax.psum((grad_in, grad_bias, grad_out), ('lat', 'lon', 'mem'))  113 us
    psum x1, waiting for transfers between devices, zonal(): return lax.psum(partial_sum, 'lon')  97.2 us
    ppermute x4, starting transfers between devices, extended(): after = lax.ppermute(leading, axis, down)  16.8 us
    ppermute x4, starting transfers between devices, extended(): before = lax.ppermute(last, axis, up)  14.9 us
  transfers between devices with their start and end apart: 10, of which 3 were waited for; matrix products, arithmetic and copies ran while one was open for 5% of the time, Pallas kernels for 0%

commit v1 on v0

v1 whole, which is shorter than its diff:
```python
import math

import jax
import jax.numpy as jnp
import numpy as np
from jax import lax
from jax.experimental import pallas as pl
from jax.experimental.pallas import tpu as pltpu
from jax.sharding import Mesh, PartitionSpec as P

MODES = 171
DAMP = 2.0
LANES = 128
BF = jnp.bfloat16
F32 = jnp.float32
VMEM_BYTES = 56 * 1024 * 1024
ROWS_AXES = ("ylo", "z", "core", "lon")
NEAR = ("core", "mem")
FAR = ("ylo", "lon", "z")


def filter_kernels(lat_total, lon_total):
    lat = math.pi * ((np.arange(lat_total) + 0.5) / lat_total - 0.5)
    k = np.arange(MODES)
    removal = 1.0 - np.exp(-DAMP * (k[None] / MODES) ** 2 / np.cos(lat)[:, None] ** 2)
    weights = np.where(k == 0, 1.0, 2.0) / lon_total
    phases = (k[:, None] * np.arange(lon_total)[None]) % lon_total
    return ((removal * weights) @ np.cos(phases * (2.0 * math.pi / lon_total))).astype(np.float32)


def dot(a, b, dims=((1,), (0,))):
    return lax.dot_general(a, b, (dims, ((), ())), preferred_element_type=F32)


def split_dot(x, high, low):
    x_high = x.astype(BF)
    x_low = (x - x_high.astype(F32)).astype(BF)
    return dot(x_high, high) + (dot(x_low, high) + dot(x_high, low))


def joined(ref, start, rows):
    return jnp.concatenate([ref[s, start : start + rows, :] for s in range(ref.shape[0])], axis=1)


def store_split(ref, start, value):
    for s in range(ref.shape[0]):
        ref[s, start : start + value.shape[0], :] = value[:, s * LANES : (s + 1) * LANES].astype(
            ref.dtype
        )


def adjoint_filter_kernel(row_ref, kernel_ref, moist_grad_ref, high_ref, low_ref):
    lon_total = kernel_ref.shape[1]
    rows = moist_grad_ref.shape[0]
    matrix = pltpu.roll(
        jnp.broadcast_to(kernel_ref[...], (lon_total, lon_total)), 0, 1, stride=1, stride_axis=0
    )
    high = matrix.astype(BF)
    low = (matrix - high.astype(F32)).astype(BF)
    high_ref[...] = high
    low_ref[...] = low
    cotangent = joined(row_ref, rows, rows)
    moist_grad_ref[...] = cotangent - split_dot(cotangent, high, low)


def column_kernel(
    seeds_ref,
    row_ref,
    north_ref,
    south_ref,
    moist_grad_ref,
    high_ref,
    low_ref,
    land_ref,
    relief_ref,
    seed_ref,
    w_hidden_ref,
    b_hidden_ref,
    w_tendency_ref,
    next_ref,
    grad_ref,
    to_north_ref,
    to_south_ref,
    weights_ref,
    features_ref,
):
    members = features_ref.shape[0]
    channels = w_tendency_ref.shape[0]
    hidden_units, in_channels = w_hidden_ref.shape
    rows = members * channels
    stencil_rows = 9 * channels
    lon_total = features_ref.shape[2]
    classes = relief_ref.shape[0]

    state = joined(row_ref, 0, rows)
    sources = (
        joined(north_ref, 0, rows).astype(F32),
        state.astype(BF).astype(F32),
        joined(south_ref, 0, rows).astype(F32),
    )
    for a in range(3):
        for b in range(3):
            moved = sources[a]
            if b != 1:
                moved = pltpu.roll(moved, (1 - b) % lon_total, 1)
            moved = moved.astype(BF)
            start = (3 * a + b) * channels
            for m in range(members):
                features_ref[m, start : start + channels, :] = moved[
                    m * channels : (m + 1) * channels
                ]
    code = joined(row_ref, 2 * rows, 8)[0:1]
    class_ids = lax.broadcasted_iota(jnp.int32, (2 * classes, lon_total), 0).astype(F32)
    pick = jnp.where(class_ids == code, 1.0, 0.0).astype(BF)
    surface = jnp.concatenate(
        [land_ref[0:1, :] + relief_ref[...], land_ref[1:2, :] + relief_ref[...]], axis=0
    )
    bias = jnp.transpose(jnp.broadcast_to(b_hidden_ref[...], (8, hidden_units)))[:, 0:1]
    w_hidden = w_hidden_ref[...]
    w_tendency = w_tendency_ref[...]
    high = high_ref[...]
    low = low_ref[...]
    grad_in = jnp.zeros((hidden_units, in_channels), F32)
    grad_out = jnp.zeros((channels, hidden_units), F32)
    grad_bias = jnp.zeros((16, hidden_units), F32)
    ones = jnp.ones((16, lon_total), BF)
    for m in range(members):
        table = (surface + seed_ref[pl.ds(seeds_ref[m], 1), :]).astype(BF)
        forcing = dot(table, pick, ((0,), (0,)))
        features_ref[m, stencil_rows:, :] = forcing.astype(BF)
        features = features_ref[m]
        preact = dot(w_hidden, features) + bias
        logistic = 1.0 / (1.0 + jnp.exp(-preact))
        hidden = (preact * logistic).astype(BF)
        part = slice(m * channels, (m + 1) * channels)
        moist = state[part] + dot(w_tendency, hidden)
        store_split(next_ref, m * channels, moist - split_dot(moist, high, low))
        moist_grad = moist_grad_ref[part, :]
        tendency_grad = moist_grad.astype(BF)
        hidden_grad = dot(w_tendency, tendency_grad, ((0,), (0,)))
        preact_grad = (hidden_grad * logistic * (1.0 + preact * (1.0 - logistic))).astype(BF)
        grad_out += dot(tendency_grad, hidden, ((1,), (1,)))
        grad_in += dot(preact_grad, features, ((1,), (1,)))
        grad_bias += dot(ones, preact_grad, ((1,), (1,)))
        stencil_grad = dot(w_hidden[:, :stencil_rows], preact_grad, ((0,), (0,)))
        sums = []
        for a in range(3):
            total = None
            for b in range(3):
                start = (3 * a + b) * channels
                piece = stencil_grad[start : start + channels]
                if b != 1:
                    piece = pltpu.roll(piece, (b - 1) % lon_total, 1)
                total = piece if total is None else total + piece
            sums.append(total)
        store_split(to_north_ref, m * channels, sums[0])
        store_split(grad_ref, m * channels, moist_grad + sums[1])
        store_split(to_south_ref, m * channels, sums[2])

    shares, share_rows = weights_ref.shape[:2]
    bias_high = grad_bias[0:1].astype(BF).astype(F32)
    bias_low = grad_bias[0:1] - bias_high
    row_ids = lax.broadcasted_iota(jnp.int32, (8, hidden_units), 0)
    bias_rows = jnp.where(row_ids == 0, bias_high, jnp.where(row_ids == 1, bias_low, 0.0))
    for p in range(shares):
        pieces = []
        for value in (grad_in, grad_out, bias_rows):
            count = value.shape[0] // (1 if value is bias_rows else shares)
            first = 0 if value is bias_rows else p * count
            for t in range(value.shape[1] // LANES):
                pieces.append(
                    value[first : first + count, t * LANES : (t + 1) * LANES]
                )
        filled = sum(piece.shape[0] for piece in pieces)
        if filled < share_rows:
            pieces.append(jnp.zeros((share_rows - filled, LANES), F32))
        weights_ref[p] = jnp.concatenate(pieces, axis=0).astype(BF)


def unpack_kernel(scaling, shares_ref, grad_in_ref, grad_bias_ref, grad_out_ref):
    shares = shares_ref.shape[0]
    for p in range(shares):
        share = shares_ref[p].astype(F32) * scaling
        start = 0
        for ref in (grad_in_ref, grad_out_ref):
            count = ref.shape[0] // shares
            for t in range(ref.shape[1] // LANES):
                ref[p * count : (p + 1) * count, t * LANES : (t + 1) * LANES] = share[
                    start : start + count
                ]
                start += count
        if p == 0:
            for t in range(grad_bias_ref.shape[1] // LANES):
                grad_bias_ref[0:1, t * LANES : (t + 1) * LANES] = (
                    share[start : start + 1] + share[start + 1 : start + 2]
                )
                start += 8


def call(kernel, outs, scratch=(), smem_first=False, flops=0, inputs=0):
    vmem = pl.BlockSpec(memory_space=pltpu.VMEM)
    specs = [vmem] * inputs
    if smem_first:
        specs[0] = pl.BlockSpec(memory_space=pltpu.SMEM)
    return pl.pallas_call(
        kernel,
        out_shape=outs,
        in_specs=specs,
        out_specs=jax.tree.map(lambda _: vmem, outs),
        scratch_shapes=list(scratch),
        cost_estimate=pl.CostEstimate(flops=flops, bytes_accessed=4_000_000, transcendentals=0),
        compiler_params=pltpu.CompilerParams(vmem_limit_bytes=VMEM_BYTES),
    )


def exchange(x, axes):
    return lax.all_to_all(x, axes, 0, 0, tiled=True)


def on_device(
    column_state,
    cotangent,
    land_mask,
    orography,
    member_seeds,
    land_table,
    relief_table,
    seed_table,
    w_hidden,
    b_hidden,
    w_tendency,
):
    members, channels, band, lon_cols = column_state.shape
    hidden_units, in_channels = w_hidden.shape
    classes = relief_table.shape[0]
    sectors = lax.axis_size("lon")
    lat_total = band * lax.axis_size(("ylo", "z", "core"))
    lon_total = lon_cols * sectors
    rows = members * channels
    shape = jax.ShapeDtypeStruct

    with jax.named_scope("rows_in"):
        def by_row(values):
            return jnp.transpose(values, (2, 0, 1, 3)).reshape(band, rows, lon_cols)

        code = (jnp.where(land_mask == 1, classes, 0) + orography).astype(F32)
        code = jnp.broadcast_to(code[:, None, :], (band, 8, lon_cols))
        packed = jnp.concatenate([by_row(column_state), by_row(cotangent), code], axis=1)
        row = exchange(packed, "lon")

    with jax.named_scope("row_halo"):
        peers = lax.axis_size(ROWS_AXES)
        south_going = [(i, i + 1) for i in range(peers - 1)]
        north_going = [(j, i) for i, j in south_going]
        edge = row[:, :rows, :].astype(BF)
        north = lax.ppermute(edge, ROWS_AXES, south_going)
        south = lax.ppermute(edge, ROWS_AXES, north_going)

    with jax.named_scope("adjoint_filter"):
        table = jnp.asarray(filter_kernels(lat_total, lon_total))
        kernel_row = lax.dynamic_slice_in_dim(table, lax.axis_index(ROWS_AXES), 1, 0)
        moist_grad, high, low = call(
            adjoint_filter_kernel,
            (
                shape((rows, lon_total), F32),
                shape((lon_total, lon_total), BF),
                shape((lon_total, lon_total), BF),
            ),
            inputs=2,
            flops=6 * rows * lon_total * lon_total,
        )(row, kernel_row)

    near = lax.axis_size(NEAR)
    far = lax.axis_size(FAR)
    share_rows = (
        hidden_units * (in_channels // LANES) // near
        + channels * (hidden_units // LANES) // near
        + 8 * (hidden_units // LANES)
    )
    share_rows = -(-share_rows // far) * far
    share_rows = -(-share_rows // 16) * 16 if share_rows % 16 else share_rows
    with jax.named_scope("columns"):
        block = (sectors, rows, LANES)
        next_rows, grad_rows, to_north, to_south, weights = call(
            column_kernel,
            (
                shape(block, BF),
                shape(block, F32),
                shape(block, BF),
                shape(block, BF),
                shape((near, share_rows, LANES), BF),
            ),
            scratch=[pltpu.VMEM((members, in_channels, lon_total), BF)],
            smem_first=True,
            inputs=13,
            flops=4_000_000_000,
        )(
            member_seeds,
            row,
            north,
            south,
            moist_grad,
            high,
            low,
            land_table,
            relief_table,
            seed_table,
            w_hidden,
            b_hidden.reshape(1, hidden_units),
            w_tendency,
        )

    with jax.named_scope("gradient_halo"):
        from_south = lax.ppermute(to_north, ROWS_AXES, north_going)
        from_north = lax.ppermute(to_south, ROWS_AXES, south_going)

    with jax.named_scope("weights_near"):
        parts = exchange(weights, NEAR)
        share = jnp.sum(parts.astype(F32), 0)

    with jax.named_scope("rows_out"):
        state_grad_rows = grad_rows + from_south.astype(F32) + from_north.astype(F32)
        outgoing = jnp.concatenate([next_rows, state_grad_rows.astype(BF)], axis=1)
        blocks = exchange(outgoing, "lon")

        def by_band(values):
            values = values.reshape(band, members, channels, lon_cols).astype(F32)
            return jnp.transpose(values, (1, 2, 0, 3))

        next_state = by_band(blocks[:, :rows])
        state_grad = by_band(blocks[:, rows:])

    with jax.named_scope("weights_far"):
        parts = exchange(share.reshape(far, share_rows // far, LANES), FAR)
        piece = jnp.sum(parts, 0, keepdims=True)
        gathered = exchange(jnp.broadcast_to(piece, parts.shape), FAR)

    with jax.named_scope("weights_back"):
        share = gathered.reshape(1, share_rows, LANES).astype(BF)
        shares = exchange(jnp.broadcast_to(share, (near, share_rows, LANES)), NEAR)
        columns = members * lax.axis_size("mem") * lat_total * lon_total

        def unpack(*refs):
            unpack_kernel(1.0 / math.sqrt(columns), *refs)

        grad_in, grad_bias, grad_out = call(
            unpack,
            (
                shape((hidden_units, in_channels), F32),
                shape((1, hidden_units), F32),
                shape((channels, hidden_units), F32),
            ),
            inputs=1,
        )(shares)
    return next_state, state_grad, grad_in, grad_bias.reshape(hidden_units), grad_out


def solution(mesh):
    lat, lon, mem = mesh.devices.shape
    devices = mesh.devices.reshape(2, lat // 4, 2, lon, mem)
    split = Mesh(devices, ("ylo", "z", "core", "lon", "mem"))
    lat_axes = ("ylo", "z", "core")
    field = P("mem", None, lat_axes, "lon")
    surface = P(lat_axes, "lon")
    whole = P()
    return jax.shard_map(
        on_device,
        mesh=split,
        in_specs=(field, field, surface, surface, P("mem")) + (whole,) * 6,
        out_specs=(field, field, whole, whole, whole),
        check_vma=False,
    )
```

time: 681 us -> 159 us (0.23)
  waiting for transfers between devices: 450 us -> 53 us
  blocking collectives: 113 us -> 17.4 us
  starting transfers between devices: 32 us -> 63.7 us
  local copies, waits for them, and re-layouts: 33.7 us -> 8.87 us
  matrix products: 18.6 us -> 0 us
  other arithmetic: 17.8 us -> 3.1 us
  between operations: 14.4 us -> 0.86 us
  Pallas kernels: 0 us -> 11.4 us
    psum x2 -> x0, waiting for transfers between devices: 448 us -> none  [the longest x1 351 us: on_device(): lax.psum((grad_in, grad_bias, grad_out), ('lat', 'lon', 'mem'))]
    psum x1 -> x0, blocking collectives: 113 us -> none  [on_device(): lax.psum((grad_in, grad_bias, grad_out), ('lat', 'lon', 'mem'))]
    all_to_all x0 -> x5, waiting for transfers between devices: none -> 52.5 us  [exchange(): return lax.all_to_all(x, axes, 0, 0, tiled=True)]
    all_to_all x0 -> x5, starting transfers between devices: none -> 47.8 us  [exchange(): return lax.all_to_all(x, axes, 0, 0, tiled=True)]
    dot_general x12 -> x0, matrix products: 18.6 us -> none  [the longest x2 4.4 us: zonal(): jnp.einsum('msji,ki->msjk', values, matrix, precision=lax.Precision.HIGHEST)]
    all_to_all x0 -> x1, blocking collectives: none -> 17.4 us  [exchange(): return lax.all_to_all(x, axes, 0, 0, tiled=True)]
    ppermute x8 -> x4, starting transfers between devices: 31.7 us -> 16 us  [the longest x1 5.78 us: on_device(): from_south = lax.ppermute(to_north, ROWS_AXES, north_going)]
    slice x7 -> x2, local copies, waits for them, and re-layouts: 15.2 us -> 0.04 us  [the longest x1 0.02 us: on_device(): edge = row[:, :rows, :].astype(BF)]
  transfers between devices with their start and end apart: 10 -> 9, of which waited for: 3 -> 6; matrix products, arithmetic and copies ran while one was open for 5% -> 3% of each run, Pallas kernels for 0% -> 1%
where the time goes in v1:
time: 159 us; the launch traced here: 158 us
  starting transfers between devices  63.7 us (40%)
  waiting for transfers between devices  53 us (33%)
  blocking collectives  17.4 us (11%)
  Pallas kernels  11.4 us (7%)
  local copies, waits for them, and re-layouts  8.87 us (6%)
  other arithmetic  3.1 us (2%)
    all_to_all x5, waiting for transfers between devices, exchange(): return lax.all_to_all(x, axes, 0, 0, tiled=True)  52.5 us
    all_to_all x5, starting transfers between devices, exchange(): return lax.all_to_all(x, axes, 0, 0, tiled=True)  47.8 us
    all_to_all x1, blocking collectives, exchange(): return lax.all_to_all(x, axes, 0, 0, tiled=True)  17.4 us
    pallas_call x1, Pallas kernels, on_device(): call(column_kernel, (shape(block, BF), shape(block, F32), shape(block, BF...  7.06 us
    ppermute x1, starting transfers between devices, on_device(): from_south = lax.ppermute(to_north, ROWS_AXES, north_going)  5.78 us
    ppermute x1, starting transfers between devices, on_device(): north = lax.ppermute(edge, ROWS_AXES, south_going)  5.75 us
  transfers between devices with their start and end apart: 9, of which 6 were waited for; matrix products, arithmetic and copies ran while one was open for 3% of the time, Pallas kernels for 1%

profile of v1, /device:TPU:1, one launch (start us, length us, event | category | flops | bytes accessed | tf_op | source)
XLA Modules:
  0.0 158.4 jit_solution(18421053806246098238)
XLA Ops:
  0.6 0.0 copy-start.4
  0.6 0.0 copy-start.5
  0.7 1.0 copy.21
  1.6 1.0 copy.22
  2.6 0.0 copy-done.4
  2.6 0.0 copy-done.5
  2.7 0.0 copy-start.6
  2.7 0.8 pad_maximum_fusion
  3.5 7.6 %all-to-all-start = ((f32[4,264,128]{2,1,0:T(8,128)}), f32[4,264,128]{2,1,0:T(8,128)S(1)}, u32[]{:S(2)}, u32[]{:S(2)}) async-start(f32[4,264,128]{2,1,0:T(8,128)} %pad_maximum_fusion), calls=%async_computation | async-start | bytes 1081344 | tf_op jit(solution)/shard_map/rows_in/all_to_all | solution.py:217
  11.1 0.0 copy-done.6
  11.1 0.6 reshape.44.b_hidden_ref
  11.7 13.5 %all-to-all-done.row_ref = f32[4,264,128]{2,1,0:T(8,128)S(1)} async-done(((f32[4,264,128]{2,1,0:T(8,128)}), f32[4,264,128]{2,1,0:T(8,128)S(1)}, u32[]{:S(2)}, u32[]{:S(2)}) %all-to-all-start) | async-done | bytes 540704 | tf_op jit(solution)/shard_map/rows_in/all_to_all | solution.py:217
  25.2 0.0 copy-start.1
  25.2 5.8 %collective-permute-start = (bf16[4,128,128]{2,1,0:T(8,128)(2,1)S(1)}, bf16[4,128,128]{2,1,0:T(8,128)(2,1)S(1)}, u32[]{:S(2)}, u32[]{:S(2)}) collective-permute-start(bf16[4,128,128]{2,1,0:T(8,128)(2,1)S(1)} %slice.17), channel_id=1, source_target_pairs={{0,4},{4,8},{8,12},{12,16},{16,20},{20,24},{24,28},{28,32},{32,36}... | collective-permute-start | bytes 393224 | tf_op jit(solution)/shard_map/row_halo/ppermute | solution.py:256
  31.0 2.5 %collective-permute-start.1 = (bf16[4,128,128]{2,1,0:T(8,128)(2,1)S(1)}, bf16[4,128,128]{2,1,0:T(8,128)(2,1)S(1)}, u32[]{:S(2)}, u32[]{:S(2)}) collective-permute-start(bf16[4,128,128]{2,1,0:T(8,128)(2,1)S(1)} %slice.17), channel_id=1, source_target_pairs={{4,0},{8,4},{12,8},{16,12},{20,16},{24,20},{28,24},{32,28},{36,32}... | collective-permute-start | bytes 393224 | tf_op jit(solution)/shard_map/row_halo/ppermute | solution.py:257
  33.5 1.3 constant_dynamic-slice_fusion.kernel_ref
  34.8 0.0 copy-done.1
  34.8 2.3 %adjoint_filter.1 = (f32[128,512]{1,0:T(8,128)}, bf16[512,512]{1,0:T(8,128)(2,1)}, bf16[512,512]{1,0:T(8,128)(2,1)}) custom-call(f32[4,264,128]{2,1,0:T(8,128)} %copy-done.1, f32[1,512]{1,0:T(1,128)} %constant_dynamic-slice_fusion.kernel_ref), custom_call_target="tpu_custom_call" | custom-call | flops 201326592 | bytes 4000000 | tf_op jit(solution)/shard_map/adjoint_filter/pallas_call | solution.py:262
  37.1 0.0 collective-permute-done.north_ref
  37.1 0.0 copy-start.9
  37.1 0.5 collective-permute-done.1.south_ref
  37.6 0.0 copy-start.10
  37.6 0.2 copy-done.9
  37.8 0.5 copy-done.10
  38.3 7.1 %columns.1 = (bf16[4,128,128]{2,1,0:T(8,128)(2,1)}, f32[4,128,128]{2,1,0:T(8,128)}, bf16[4,128,128]{2,1,0:T(8,128)(2,1)}, bf16[4,128,128]{2,1,0:T(8,128)(2,1)}, bf16[8,288,128]{2,1,0:T(8,128)(2,1)}) custom-call(s32[2]{0:T(128)} %seeds_ref.1, f32[4,264,128]{2,1,0:T(8,128)} %copy-done.1, bf16[4,128,128]{2,1,0:T(8,128)(2,1)} %copy-done.9, ...), custom_call_target="tpu_custom_call" | custom-call | flops 4000000000 | bytes 4000000 | tf_op jit(solution)/shard_map/columns/pallas_call | solution.py:284
  45.3 17.4 %all_to_all.30 = bf16[8,288,128]{2,1,0:T(8,128)(2,1)S(1)} all-to-all(bf16[8,288,128]{2,1,0:T(8,128)(2,1)} %get-tuple-element.23), channel_id=1, replica_groups=mesh['ylo'=2,'z'=12,'core'=2,'lon'=4,'mem'=4] {'core','mem'}, dimensions={0} | all-to-all | bytes 1179648 | tf_op jit(solution)/shard_map/weights_near/all_to_all | solution.py:217
  62.7 0.0 copy-start.8
  62.7 0.0 copy-start.7
  62.7 0.0 copy-start.2
  62.7 0.1 convert_reduce_fusion
  62.8 0.0 copy-start.3
  62.8 0.7 reshape.45
  63.6 21.5 %all-to-all-start.3 = ((f32[96,3,128]{2,1,0:T(4,128)}), f32[96,3,128]{2,1,0:T(4,128)S(1)}, u32[]{:S(2)}, u32[]{:S(2)}) async-start(f32[96,3,128]{2,1,0:T(4,128)} %reshape.45), calls=%async_computation.3 | async-start | bytes 393216 | tf_op jit(solution)/shard_map/weights_far/all_to_all | solution.py:217
  85.1 0.0 copy-done.8
  85.1 5.8 %collective-permute-start.2 = (bf16[4,128,128]{2,1,0:T(8,128)(2,1)S(1)}, bf16[4,128,128]{2,1,0:T(8,128)(2,1)S(1)}, u32[]{:S(2)}, u32[]{:S(2)}) collective-permute-start(bf16[4,128,128]{2,1,0:T(8,128)(2,1)S(1)} %copy-done.8), channel_id=1, source_target_pairs={{4,0},{8,4},{12,8},{16,12},{20,16},{24,20},{28,24},{32,28},{36,32}... | collective-permute-start | bytes 393224 | tf_op jit(solution)/shard_map/gradient_halo/ppermute | solution.py:314
  90.9 0.0 copy-done.7
  90.9 1.9 %collective-permute-start.3 = (bf16[4,128,128]{2,1,0:T(8,128)(2,1)S(1)}, bf16[4,128,128]{2,1,0:T(8,128)(2,1)S(1)}, u32[]{:S(2)}, u32[]{:S(2)}) collective-permute-start(bf16[4,128,128]{2,1,0:T(8,128)(2,1)S(1)} %copy-done.7), channel_id=1, source_target_pairs={{0,4},{4,8},{8,12},{12,16},{16,20},{20,24},{24,28},{28,32},{32,36}... | collective-permute-start | bytes 393224 | tf_op jit(solution)/shard_map/gradient_halo/ppermute | solution.py:315
  92.8 9.1 %all-to-all-done.3 = f32[96,3,128]{2,1,0:T(4,128)S(1)} async-done(((f32[96,3,128]{2,1,0:T(4,128)}), f32[96,3,128]{2,1,0:T(4,128)S(1)}, u32[]{:S(2)}, u32[]{:S(2)}) %all-to-all-start.3) | async-done | bytes 147488 | tf_op jit(solution)/shard_map/weights_far/all_to_all | solution.py:217
  101.9 0.1 reduce_sum.19
  102.0 0.7 broadcast_in_dim.28
  102.7 6.2 %all-to-all-start.4 = ((bf16[96,3,128]{2,1,0:T(4,128)(2,1)}), bf16[96,3,128]{2,1,0:T(4,128)(2,1)S(1)}, u32[]{:S(2)}, u32[]{:S(2)}) async-start(bf16[96,3,128]{2,1,0:T(4,128)(2,1)} %broadcast_in_dim.28), calls=%async_computation.4 | async-start | bytes 196608 | tf_op jit(solution)/shard_map/weights_far/all_to_all | solution.py:217
  108.9 0.0 collective-permute-done.2
  108.9 0.0 collective-permute-done.3
  108.9 0.0 copy-done.2
  109.0 0.0 copy-done.3
  109.0 0.7 pad_maximum_fusion.1
  109.7 13.1 %all-to-all-done.4 = bf16[96,3,128]{2,1,0:T(4,128)(2,1)S(1)} async-done(((bf16[96,3,128]{2,1,0:T(4,128)(2,1)}), bf16[96,3,128]{2,1,0:T(4,128)(2,1)S(1)}, u32[]{:S(2)}, u32[]{:S(2)}) %all-to-all-start.4) | async-done | bytes 73760 | tf_op jit(solution)/shard_map/weights_far/all_to_all | solution.py:217
  122.8 3.4 %all-to-all-start.1 = ((bf16[4,256,128]{2,1,0:T(8,128)(2,1)}), bf16[4,256,128]{2,1,0:T(8,128)(2,1)S(1)}, u32[]{:S(2)}, u32[]{:S(2)}) async-start(bf16[4,256,128]{2,1,0:T(8,128)(2,1)} %pad_maximum_fusion.1), calls=%async_computation.1 | async-start | bytes 524288 | tf_op jit(solution)/shard_map/rows_out/all_to_all | solution.py:217
  126.2 0.1 convert_element_type.43
  126.3 7.9 %all-to-all-done.1 = bf16[4,256,128]{2,1,0:T(8,128)(2,1)S(1)} async-done(((bf16[4,256,128]{2,1,0:T(8,128)(2,1)}), bf16[4,256,128]{2,1,0:T(8,128)(2,1)S(1)}, u32[]{:S(2)}, u32[]{:S(2)}) %all-to-all-start.1) | async-done | bytes 262176 | tf_op jit(solution)/shard_map/rows_out/all_to_all | solution.py:217
  134.2 0.9 broadcast_in_dim.29
  135.1 9.0 %all-to-all-start.5 = ((bf16[8,288,128]{2,1,0:T(8,128)(2,1)}), bf16[8,288,128]{2,1,0:T(8,128)(2,1)S(1)}, u32[]{:S(2)}, u32[]{:S(2)}) async-start(bf16[8,288,128]{2,1,0:T(8,128)(2,1)} %broadcast_in_dim.29), calls=%async_computation.5 | async-start | bytes 1179648 | tf_op jit(solution)/shard_map/weights_back/all_to_all | solution.py:217
  144.2 1.1 copy_bitcast_fusion
  145.3 8.9 %all-to-all-done.5.refs_0_ = bf16[8,288,128]{2,1,0:T(8,128)(2,1)S(1)} async-done(((bf16[8,288,128]{2,1,0:T(8,128)(2,1)}), bf16[8,288,128]{2,1,0:T(8,128)(2,1)S(1)}, u32[]{:S(2)}, u32[]{:S(2)}) %all-to-all-start.5) | async-done | bytes 589856 | tf_op jit(solution)/shard_map/weights_back/all_to_all | solution.py:217
  154.2 0.0 copy-start
  154.2 0.8 copy-done
  155.0 2.1 %weights_back.1 = (f32[384,640]{1,0:T(8,128)}, f32[1,384]{1,0:T(1,128)}, f32[64,384]{1,0:T(8,128)}) custom-call(bf16[8,288,128]{2,1,0:T(8,128)(2,1)} %copy-done), custom_call_target="tpu_custom_call" | custom-call | bytes 4000000 | tf_op jit(solution)/shard_map/weights_back/pallas_call | solution.py:346
  157.2 1.3 reduce
  (7 shorter events, 0.1 us)
Async XLA Ops:
  0.6 2.0 %copy-start.4 = (s32[4,128]{1,0:T(4,128)S(1)}, s32[4,128]{1,0:T(4,128)}, u32[]{:S(2)}) copy-start(s32[4,128]{1,0:T(4,128)} %param.15) | copy-start | bytes 6148
  0.6 2.0 %copy-start.5 = (s32[4,128]{1,0:T(4,128)S(1)}, s32[4,128]{1,0:T(4,128)}, u32[]{:S(2)}) copy-start(s32[4,128]{1,0:T(4,128)} %param.14) | copy-start | bytes 6148
  2.7 8.5 %copy-start.6 = (f32[384]{0:T(512)S(1)}, f32[384]{0:T(512)}, u32[]{:S(2)}) copy-start(f32[384]{0:T(512)} %param.21) | copy-start | bytes 4612
  3.5 21.7 %all-to-all-start = ((f32[4,264,128]{2,1,0:T(8,128)}), f32[4,264,128]{2,1,0:T(8,128)S(1)}, u32[]{:S(2)}, u32[]{:S(2)}) async-start(f32[4,264,128]{2,1,0:T(8,128)} %pad_maximum_fusion), calls=%async_computation | async-start | bytes 1081344 | tf_op jit(solution)/shard_map/rows_in/all_to_all | solution.py:217
  25.2 9.6 %copy-start.1 = (f32[4,264,128]{2,1,0:T(8,128)}, f32[4,264,128]{2,1,0:T(8,128)S(1)}, u32[]{:S(2)}) copy-start(f32[4,264,128]{2,1,0:T(8,128)S(1)} %all-to-all-done.row_ref) | copy-start | bytes 1622020
  25.2 11.9 %collective-permute-start = (bf16[4,128,128]{2,1,0:T(8,128)(2,1)S(1)}, bf16[4,128,128]{2,1,0:T(8,128)(2,1)S(1)}, u32[]{:S(2)}, u32[]{:S(2)}) collective-permute-start(bf16[4,128,128]{2,1,0:T(8,128)(2,1)S(1)} %slice.17), channel_id=1, source_target_pairs={{0,4},{4,8},{8,12},{12,16},{16,20},{20,24},{24,28},{28,32},{32,36}... | collective-permute-start | bytes 393224 | tf_op jit(solution)/shard_map/row_halo/ppermute | solution.py:256
  31.0 6.6 %collective-permute-start.1 = (bf16[4,128,128]{2,1,0:T(8,128)(2,1)S(1)}, bf16[4,128,128]{2,1,0:T(8,128)(2,1)S(1)}, u32[]{:S(2)}, u32[]{:S(2)}) collective-permute-start(bf16[4,128,128]{2,1,0:T(8,128)(2,1)S(1)} %slice.17), channel_id=1, source_target_pairs={{4,0},{8,4},{12,8},{16,12},{20,16},{24,20},{28,24},{32,28},{36,32}... | collective-permute-start | bytes 393224 | tf_op jit(solution)/shard_map/row_halo/ppermute | solution.py:257
  37.1 0.7 copy-start.9
  37.6 0.7 copy-start.10
  62.7 22.4 %copy-start.8 = (bf16[4,128,128]{2,1,0:T(8,128)(2,1)S(1)}, bf16[4,128,128]{2,1,0:T(8,128)(2,1)}, u32[]{:S(2)}) copy-start(bf16[4,128,128]{2,1,0:T(8,128)(2,1)} %get-tuple-element.21) | copy-start | bytes 393220
  62.7 28.2 %copy-start.7 = (bf16[4,128,128]{2,1,0:T(8,128)(2,1)S(1)}, bf16[4,128,128]{2,1,0:T(8,128)(2,1)}, u32[]{:S(2)}) copy-start(bf16[4,128,128]{2,1,0:T(8,128)(2,1)} %get-tuple-element.22) | copy-start | bytes 393220
  62.7 46.2 %copy-start.2 = (f32[4,128,128]{2,1,0:T(8,128)S(1)}, f32[4,128,128]{2,1,0:T(8,128)}, u32[]{:S(2)}) copy-start(f32[4,128,128]{2,1,0:T(8,128)} %get-tuple-element.20) | copy-start | bytes 786436
  62.8 46.2 %copy-start.3 = (bf16[4,128,128]{2,1,0:T(8,128)(2,1)S(1)}, bf16[4,128,128]{2,1,0:T(8,128)(2,1)}, u32[]{:S(2)}) copy-start(bf16[4,128,128]{2,1,0:T(8,128)(2,1)} %get-tuple-element.19) | copy-start | bytes 393220
  63.6 38.4 %all-to-all-start.3 = ((f32[96,3,128]{2,1,0:T(4,128)}), f32[96,3,128]{2,1,0:T(4,128)S(1)}, u32[]{:S(2)}, u32[]{:S(2)}) async-start(f32[96,3,128]{2,1,0:T(4,128)} %reshape.45), calls=%async_computation.3 | async-start | bytes 393216 | tf_op jit(solution)/shard_map/weights_far/all_to_all | solution.py:217
  85.1 23.8 %collective-permute-start.2 = (bf16[4,128,128]{2,1,0:T(8,128)(2,1)S(1)}, bf16[4,128,128]{2,1,0:T(8,128)(2,1)S(1)}, u32[]{:S(2)}, u32[]{:S(2)}) collective-permute-start(bf16[4,128,128]{2,1,0:T(8,128)(2,1)S(1)} %copy-done.8), channel_id=1, source_target_pairs={{4,0},{8,4},{12,8},{16,12},{20,16},{24,20},{28,24},{32,28},{36,32}... | collective-permute-start | bytes 393224 | tf_op jit(solution)/shard_map/gradient_halo/ppermute | solution.py:314
  90.9 18.0 %collective-permute-start.3 = (bf16[4,128,128]{2,1,0:T(8,128)(2,1)S(1)}, bf16[4,128,128]{2,1,0:T(8,128)(2,1)S(1)}, u32[]{:S(2)}, u32[]{:S(2)}) collective-permute-start(bf16[4,128,128]{2,1,0:T(8,128)(2,1)S(1)} %copy-done.7), channel_id=1, source_target_pairs={{0,4},{4,8},{8,12},{12,16},{16,20},{20,24},{24,28},{28,32},{32,36}... | collective-permute-start | bytes 393224 | tf_op jit(solution)/shard_map/gradient_halo/ppermute | solution.py:315
  102.7 20.1 %all-to-all-start.4 = ((bf16[96,3,128]{2,1,0:T(4,128)(2,1)}), bf16[96,3,128]{2,1,0:T(4,128)(2,1)S(1)}, u32[]{:S(2)}, u32[]{:S(2)}) async-start(bf16[96,3,128]{2,1,0:T(4,128)(2,1)} %broadcast_in_dim.28), calls=%async_computation.4 | async-start | bytes 196608 | tf_op jit(solution)/shard_map/weights_far/all_to_all | solution.py:217
  122.8 11.4 %all-to-all-start.1 = ((bf16[4,256,128]{2,1,0:T(8,128)(2,1)}), bf16[4,256,128]{2,1,0:T(8,128)(2,1)S(1)}, u32[]{:S(2)}, u32[]{:S(2)}) async-start(bf16[4,256,128]{2,1,0:T(8,128)(2,1)} %pad_maximum_fusion.1), calls=%async_computation.1 | async-start | bytes 524288 | tf_op jit(solution)/shard_map/rows_out/all_to_all | solution.py:217
  135.1 19.1 %all-to-all-start.5 = ((bf16[8,288,128]{2,1,0:T(8,128)(2,1)}), bf16[8,288,128]{2,1,0:T(8,128)(2,1)S(1)}, u32[]{:S(2)}, u32[]{:S(2)}) async-start(bf16[8,288,128]{2,1,0:T(8,128)(2,1)} %broadcast_in_dim.29), calls=%async_computation.5 | async-start | bytes 1179648 | tf_op jit(solution)/shard_map/weights_back/all_to_all | solution.py:217
  154.2 0.8 copy-start

commit v2 on v1

--- a/solution.py
+++ b/solution.py
@@ -16,7 +16,7 @@
 VMEM_BYTES = 56 * 1024 * 1024
 ROWS_AXES = ("ylo", "z", "core", "lon")
 NEAR = ("core", "mem")
-FAR = ("ylo", "lon", "z")
+MIDDLE = ("ylo", "lon")
 
 
 def filter_kernels(lat_total, lon_total):
@@ -49,23 +49,39 @@
         )
 
 
-def adjoint_filter_kernel(row_ref, kernel_ref, moist_grad_ref, high_ref, low_ref):
-    lon_total = kernel_ref.shape[1]
+def by_row_kernel(state_ref, cotangent_ref, land_ref, orography_ref, classes, out_ref, adjoint_ref):
+    band, rows = out_ref.shape[:2]
+    members = state_ref.shape[0]
+    channels = rows // members
+    code = jnp.where(land_ref[...] == 1, classes, 0) + orography_ref[...]
+    code = code.astype(F32)
+    for q in range(band):
+        for m in range(members):
+            picked = pl.ds(q, channels, stride=band)
+            out_ref[q, m * channels : (m + 1) * channels, :] = state_ref[m, picked, :]
+            adjoint_ref[q, m * channels : (m + 1) * channels, :] = cotangent_ref[m, picked, :]
+        adjoint_ref[q, rows:, :] = jnp.broadcast_to(code[q : q + 1], (8, LANES))
+
+
+def adjoint_filter_kernel(place_ref, row_ref, table_ref, moist_grad_ref, high_ref, low_ref):
+    lon_total = table_ref.shape[1]
     rows = moist_grad_ref.shape[0]
+    kernel = table_ref[pl.ds(place_ref[0], 1), :]
     matrix = pltpu.roll(
-        jnp.broadcast_to(kernel_ref[...], (lon_total, lon_total)), 0, 1, stride=1, stride_axis=0
+        jnp.broadcast_to(kernel, (lon_total, lon_total)), 0, 1, stride=1, stride_axis=0
     )
     high = matrix.astype(BF)
     low = (matrix - high.astype(F32)).astype(BF)
     high_ref[...] = high
     low_ref[...] = low
-    cotangent = joined(row_ref, rows, rows)
+    cotangent = joined(row_ref, 0, rows)
     moist_grad_ref[...] = cotangent - split_dot(cotangent, high, low)
 
 
 def column_kernel(
     seeds_ref,
     row_ref,
+    adjoint_ref,
     north_ref,
     south_ref,
     moist_grad_ref,
@@ -109,7 +125,7 @@
                 features_ref[m, start : start + channels, :] = moved[
                     m * channels : (m + 1) * channels
                 ]
-    code = joined(row_ref, 2 * rows, 8)[0:1]
+    code = joined(adjoint_ref, rows, 8)[0:1]
     class_ids = lax.broadcasted_iota(jnp.int32, (2 * classes, lon_total), 0).astype(F32)
     pick = jnp.where(class_ids == code, 1.0, 0.0).astype(BF)
     surface = jnp.concatenate(
@@ -160,21 +176,40 @@
     shares, share_rows = weights_ref.shape[:2]
     bias_high = grad_bias[0:1].astype(BF).astype(F32)
     bias_low = grad_bias[0:1] - bias_high
-    row_ids = lax.broadcasted_iota(jnp.int32, (8, hidden_units), 0)
-    bias_rows = jnp.where(row_ids == 0, bias_high, jnp.where(row_ids == 1, bias_low, 0.0))
+    tiles = hidden_units // LANES
+    bias_rows = [half[:, t * LANES : (t + 1) * LANES] for half in (bias_high, bias_low) for t in range(tiles)]
+    bias_rows = jnp.concatenate(bias_rows + [jnp.zeros((8 - 2 * tiles, LANES), F32)], axis=0)
     for p in range(shares):
         pieces = []
-        for value in (grad_in, grad_out, bias_rows):
-            count = value.shape[0] // (1 if value is bias_rows else shares)
-            first = 0 if value is bias_rows else p * count
+        for value in (grad_in, grad_out):
+            count = value.shape[0] // shares
             for t in range(value.shape[1] // LANES):
-                pieces.append(
-                    value[first : first + count, t * LANES : (t + 1) * LANES]
-                )
-        filled = sum(piece.shape[0] for piece in pieces)
-        if filled < share_rows:
-            pieces.append(jnp.zeros((share_rows - filled, LANES), F32))
-        weights_ref[p] = jnp.concatenate(pieces, axis=0).astype(BF)
+                pieces.append(value[p * count : (p + 1) * count, t * LANES : (t + 1) * LANES])
+        weights_ref[p] = jnp.concatenate(pieces + [bias_rows], axis=0).astype(BF)
+
+
+def near_sum_kernel(parts_ref, next_ref, grad_ref, south_ref, north_ref, share_ref, out_ref, sum_ref):
+    sectors, rows = next_ref.shape[:2]
+    for s in range(sectors):
+        out_ref[s, :rows, :] = next_ref[s]
+        total = grad_ref[s] + south_ref[s].astype(F32) + north_ref[s].astype(F32)
+        out_ref[s, rows:, :] = total.astype(BF)
+    total = parts_ref[0].astype(F32)
+    for p in range(1, parts_ref.shape[0]):
+        total = total + parts_ref[p].astype(F32)
+    sum_ref[...] = total
+    pieces, piece_rows = share_ref.shape[:2]
+    for p in range(pieces):
+        share_ref[p] = sum_ref[p * piece_rows : (p + 1) * piece_rows, :]
+
+
+def spread_kernel(pieces_ref, shares_ref, sum_ref):
+    pieces, piece_rows = pieces_ref.shape[:2]
+    for p in range(pieces):
+        sum_ref[p * piece_rows : (p + 1) * piece_rows, :] = pieces_ref[p].astype(F32)
+    share = sum_ref[...].astype(BF)
+    for p in range(shares_ref.shape[0]):
+        shares_ref[p] = share
 
 
 def unpack_kernel(scaling, shares_ref, grad_in_ref, grad_bias_ref, grad_out_ref):
@@ -190,11 +225,10 @@
                 ]
                 start += count
         if p == 0:
-            for t in range(grad_bias_ref.shape[1] // LANES):
-                grad_bias_ref[0:1, t * LANES : (t + 1) * LANES] = (
-                    share[start : start + 1] + share[start + 1 : start + 2]
-                )
-                start += 8
+            tiles = grad_bias_ref.shape[0] // LANES
+            for t in range(tiles):
+                both = share[start + t : start + t + 1] + share[start + tiles + t : start + tiles + t + 1]
+                grad_bias_ref[t * LANES : (t + 1) * LANES] = both[0]
 
 
 def call(kernel, outs, scratch=(), smem_first=False, flops=0, inputs=0):
@@ -240,25 +274,27 @@
     shape = jax.ShapeDtypeStruct
 
     with jax.named_scope("rows_in"):
-        def by_row(values):
-            return jnp.transpose(values, (2, 0, 1, 3)).reshape(band, rows, lon_cols)
-
-        code = (jnp.where(land_mask == 1, classes, 0) + orography).astype(F32)
-        code = jnp.broadcast_to(code[:, None, :], (band, 8, lon_cols))
-        packed = jnp.concatenate([by_row(column_state), by_row(cotangent), code], axis=1)
-        row = exchange(packed, "lon")
+        def by_row(*refs):
+            by_row_kernel(*refs[:4], classes, *refs[4:])
+
+        flat = (members, channels * band, lon_cols)
+        state_rows, adjoint_rows = call(
+            by_row,
+            (shape((band, rows, lon_cols), F32), shape((band, rows + 8, lon_cols), F32)),
+            inputs=4,
+        )(column_state.reshape(flat), cotangent.reshape(flat), land_mask, orography)
+        row = exchange(state_rows, "lon")
+        adjoint_row = exchange(adjoint_rows, "lon")
 
     with jax.named_scope("row_halo"):
         peers = lax.axis_size(ROWS_AXES)
         south_going = [(i, i + 1) for i in range(peers - 1)]
         north_going = [(j, i) for i, j in south_going]
-        edge = row[:, :rows, :].astype(BF)
+        edge = row.astype(BF)
         north = lax.ppermute(edge, ROWS_AXES, south_going)
         south = lax.ppermute(edge, ROWS_AXES, north_going)
 
     with jax.named_scope("adjoint_filter"):
-        table = jnp.asarray(filter_kernels(lat_total, lon_total))
-        kernel_row = lax.dynamic_slice_in_dim(table, lax.axis_index(ROWS_AXES), 1, 0)
         moist_grad, high, low = call(
             adjoint_filter_kernel,
             (
@@ -266,19 +302,20 @@
                 shape((lon_total, lon_total), BF),
                 shape((lon_total, lon_total), BF),
             ),
-            inputs=2,
+            smem_first=True,
+            inputs=3,
             flops=6 * rows * lon_total * lon_total,
-        )(row, kernel_row)
+        )(
+            lax.axis_index(ROWS_AXES).reshape(1),
+            adjoint_row,
+            jnp.asarray(filter_kernels(lat_total, lon_total)),
+        )
 
     near = lax.axis_size(NEAR)
-    far = lax.axis_size(FAR)
-    share_rows = (
-        hidden_units * (in_channels // LANES) // near
-        + channels * (hidden_units // LANES) // near
-        + 8 * (hidden_units // LANES)
-    )
-    share_rows = -(-share_rows // far) * far
-    share_rows = -(-share_rows // 16) * 16 if share_rows % 16 else share_rows
+    middle = lax.axis_size(MIDDLE)
+    length = lax.axis_size("z")
+    share_rows = (hidden_units * in_channels + channels * hidden_units) // (LANES * near) + 8
+    piece_rows = share_rows // middle
     with jax.named_scope("columns"):
         block = (sectors, rows, LANES)
         next_rows, grad_rows, to_north, to_south, weights = call(
@@ -292,11 +329,12 @@
             ),
             scratch=[pltpu.VMEM((members, in_channels, lon_total), BF)],
             smem_first=True,
-            inputs=13,
+            inputs=14,
             flops=4_000_000_000,
         )(
             member_seeds,
             row,
+            adjoint_row,
             north,
             south,
             moist_grad,
@@ -316,11 +354,18 @@
 
     with jax.named_scope("weights_near"):
         parts = exchange(weights, NEAR)
-        share = jnp.sum(parts.astype(F32), 0)
+        share, outgoing = call(
+            near_sum_kernel,
+            (shape((middle, piece_rows, LANES), F32), shape((sectors, 2 * rows, LANES), BF)),
+            scratch=[pltpu.VMEM((share_rows, LANES), F32)],
+            inputs=5,
+        )(parts, next_rows, grad_rows, from_south, from_north)
+
+    with jax.named_scope("weights_middle"):
+        parts = exchange(share, MIDDLE)
+        piece = jnp.sum(parts, 0, keepdims=True).astype(BF)
 
     with jax.named_scope("rows_out"):
-        state_grad_rows = grad_rows + from_south.astype(F32) + from_north.astype(F32)
-        outgoing = jnp.concatenate([next_rows, state_grad_rows.astype(BF)], axis=1)
         blocks = exchange(outgoing, "lon")
 
         def by_band(values):
@@ -330,14 +375,19 @@
         next_state = by_band(blocks[:, :rows])
         state_grad = by_band(blocks[:, rows:])
 
-    with jax.named_scope("weights_far"):
-        parts = exchange(share.reshape(far, share_rows // far, LANES), FAR)
-        piece = jnp.sum(parts, 0, keepdims=True)
-        gathered = exchange(jnp.broadcast_to(piece, parts.shape), FAR)
+    with jax.named_scope("weights_length"):
+        parts = exchange(jnp.broadcast_to(piece, (length, piece_rows, LANES)), "z")
+        piece = jnp.sum(parts.astype(F32), 0, keepdims=True).astype(BF)
 
     with jax.named_scope("weights_back"):
-        share = gathered.reshape(1, share_rows, LANES).astype(BF)
-        shares = exchange(jnp.broadcast_to(share, (near, share_rows, LANES)), NEAR)
+        pieces = exchange(jnp.broadcast_to(piece, (middle, piece_rows, LANES)), MIDDLE)
+        spread = call(
+            spread_kernel,
+            shape((near, share_rows, LANES), BF),
+            scratch=[pltpu.VMEM((share_rows, LANES), F32)],
+            inputs=1,
+        )(pieces)
+        shares = exchange(spread, NEAR)
         columns = members * lax.axis_size("mem") * lat_total * lon_total
 
         def unpack(*refs):
@@ -347,12 +397,12 @@
             unpack,
             (
                 shape((hidden_units, in_channels), F32),
-                shape((1, hidden_units), F32),
+                shape((hidden_units,), F32),
                 shape((channels, hidden_units), F32),
             ),
             inputs=1,
         )(shares)
-    return next_state, state_grad, grad_in, grad_bias.reshape(hidden_units), grad_out
+    return next_state, state_grad, grad_in, grad_bias, grad_out
 
 
 def solution(mesh):

time: 159 us -> 153 us (0.962)
  blocking collectives: 17.4 us -> 63.7 us
  waiting for transfers between devices: 53 us -> 22.3 us
  starting transfers between devices: 63.7 us -> 42.8 us
  Pallas kernels: 11.4 us -> 17.2 us
  local copies, waits for them, and re-layouts: 8.87 us -> 5.44 us
  other arithmetic: 3.1 us -> 0.1 us
    all_to_all x1 -> x4, blocking collectives: 17.4 us -> 63.7 us  [exchange(): return lax.all_to_all(x, axes, 0, 0, tiled=True)]
    all_to_all x5 -> x4, waiting for transfers between devices: 52.5 us -> 14.8 us  [exchange(): return lax.all_to_all(x, axes, 0, 0, tiled=True)]
    all_to_all x5 -> x4, starting transfers between devices: 47.8 us -> 22.6 us  [exchange(): return lax.all_to_all(x, axes, 0, 0, tiled=True)]
    ppermute x1, starting transfers between devices: 2.52 us -> 12.1 us  [on_device(): south = lax.ppermute(edge, ROWS_AXES, north_going)]
    pallas_call x1 -> x4, Pallas kernels: 2.11 us -> 7.79 us  [the longest x1 2.1 us: on_device(): call(unpack, (shape((hidden_units, in_channels), F32), shape((hidden_unit...]
    ppermute x1, starting transfers between devices: 5.75 us -> 1.92 us  [on_device(): north = lax.ppermute(edge, ROWS_AXES, south_going)]
    ppermute x1, waiting for transfers between devices: 0.01 us -> 3.16 us  [on_device(): from_north = lax.ppermute(to_south, ROWS_AXES, south_going)]
    ppermute x1, starting transfers between devices: 5.78 us -> 3.08 us  [on_device(): from_south = lax.ppermute(to_north, ROWS_AXES, north_going)]
  transfers between devices with their start and end apart: 9 -> 8, of which waited for: 6 -> 5; matrix products, arithmetic and copies ran while one was open for 3% -> 1% of each run, Pallas kernels for 1% -> 3%
where the time goes in v2:
time: 153 us; the launch traced here: 152 us
  blocking collectives  63.7 us (42%)
  starting transfers between devices  42.8 us (28%)
  waiting for transfers between devices  22.3 us (15%)
  Pallas kernels  17.2 us (11%)
  local copies, waits for them, and re-layouts  5.44 us (4%)
    all_to_all x4, blocking collectives, exchange(): return lax.all_to_all(x, axes, 0, 0, tiled=True)  63.7 us
    all_to_all x4, starting transfers between devices, exchange(): return lax.all_to_all(x, axes, 0, 0, tiled=True)  22.6 us
    all_to_all x4, waiting for transfers between devices, exchange(): return lax.all_to_all(x, axes, 0, 0, tiled=True)  14.8 us
    ppermute x1, starting transfers between devices, on_device(): south = lax.ppermute(edge, ROWS_AXES, north_going)  12.1 us
    pallas_call x1, Pallas kernels, on_device(): call(column_kernel, (shape(block, BF), shape(block, F32), shape(block, BF...  7.07 us
    unnamed x22, local copies, waits for them, and re-layouts  3.7 us
    ppermute x1, waiting for transfers between devices, on_device(): from_north = lax.ppermute(to_south, ROWS_AXES, south_going)  3.16 us
    ppermute x1, starting transfers between devices, on_device(): from_north = lax.ppermute(to_south, ROWS_AXES, south_going)  3.11 us
  transfers between devices with their start and end apart: 8, of which 5 were waited for; matrix products, arithmetic and copies ran while one was open for 1% of the time, Pallas kernels for 3%

profile of v2, /device:TPU:1, one launch (start us, length us, event | category | flops | bytes accessed | tf_op | source)
XLA Modules:
  0.0 152.3 jit_solution(16843631075288245610)
XLA Ops:
  0.6 1.9 %rows_in.1 = (f32[4,128,128]{2,1,0:T(8,128)}, f32[4,136,128]{2,1,0:T(8,128)}) custom-call(f32[2,256,128]{2,1,0:T(8,128)} %bitcast.13, f32[2,256,128]{2,1,0:T(8,128)} %bitcast.14, s32[4,128]{1,0:T(4,128)} %refs_2_.1, s32[4,128]{1,0:T(4,128)} %refs_3_.1), custom_call_target="tpu_custom_call" | custom-call | bytes 4000000 | tf_op jit(solution)/shard_map/rows_in/pallas_call | solution.py:281
  2.5 16.6 %all_to_all.40.row_ref = f32[4,128,128]{2,1,0:T(8,128)S(1)} all-to-all(f32[4,128,128]{2,1,0:T(8,128)} %get-tuple-element.20), channel_id=1, replica_groups=mesh['ylo'=2,'z'=12,'core'=2,'lon'=4,'mem'=4] {'lon'}, dimensions={0} | all-to-all | bytes 524288 | tf_op jit(solution)/shard_map/rows_in/all_to_all | solution.py:251
  19.1 0.0 copy-start.2
  19.1 4.0 %all-to-all-start.1 = ((f32[4,136,128]{2,1,0:T(8,128)}), f32[4,136,128]{2,1,0:T(8,128)S(1)}, u32[]{:S(2)}, u32[]{:S(2)}) async-start(f32[4,136,128]{2,1,0:T(8,128)} %get-tuple-element.21), calls=%async_computation.1 | async-start | bytes 557056 | tf_op jit(solution)/shard_map/rows_in/all_to_all | solution.py:251
  23.1 0.0 copy-done.2
  23.2 12.1 %collective-permute-start.1 = (bf16[4,128,128]{2,1,0:T(8,128)(2,1)S(1)}, bf16[4,128,128]{2,1,0:T(8,128)(2,1)S(1)}, u32[]{:S(2)}, u32[]{:S(2)}) collective-permute-start(bf16[4,128,128]{2,1,0:T(8,128)(2,1)S(1)} %convert_element_type.26), channel_id=1, source_target_pairs={{4,0},{8,4},{12,8},{16,12},{20,16},{24,20},{28,24},{32,28},{36,32}... | collective-permute-start | bytes 393224 | tf_op jit(solution)/shard_map/row_halo/ppermute | solution.py:295
  35.3 1.9 %collective-permute-start = (bf16[4,128,128]{2,1,0:T(8,128)(2,1)S(1)}, bf16[4,128,128]{2,1,0:T(8,128)(2,1)S(1)}, u32[]{:S(2)}, u32[]{:S(2)}) collective-permute-start(bf16[4,128,128]{2,1,0:T(8,128)(2,1)S(1)} %convert_element_type.26), channel_id=1, source_target_pairs={{0,4},{4,8},{8,12},{12,16},{16,20},{20,24},{24,28},{28,32},{32,36}... | collective-permute-start | bytes 393224 | tf_op jit(solution)/shard_map/row_halo/ppermute | solution.py:294
  37.2 0.0 copy-start.6
  37.2 0.7 copy-done.6
  37.9 0.6 reshape.39.b_hidden_ref
  38.5 0.0 all-to-all-done.1.row_ref.adjoint_ref
  38.5 0.0 copy-start.3
  38.5 0.7 copy-done.3
  39.2 2.3 %adjoint_filter.1 = (f32[128,512]{1,0:T(8,128)}, bf16[512,512]{1,0:T(8,128)(2,1)}, bf16[512,512]{1,0:T(8,128)(2,1)}) custom-call(s32[1]{0:T(128)} %bitcast.2.place_ref, f32[4,136,128]{2,1,0:T(8,128)} %copy-done.3, f32[192,512]{1,0:T(8,128)} %constant.31.clone.table_ref), custom_call_target="tpu_custom_call" | custom-call | flops 201326592 | bytes 4000000 | tf_op jit(solution)/shard_map/adjoint_filter/pallas_call | solution.py:298
  41.5 0.0 collective-permute-done.1.south_ref
  41.5 0.0 copy-start.7
  41.5 2.2 %collective-permute-done.north_ref = bf16[4,128,128]{2,1,0:T(8,128)(2,1)S(1)} collective-permute-done((bf16[4,128,128]{2,1,0:T(8,128)(2,1)S(1)}, bf16[4,128,128]{2,1,0:T(8,128)(2,1)S(1)}, u32[]{:S(2)}, u32[]{:S(2)}) %collective-permute-start) | collective-permute-done | bytes 131104 | tf_op jit(solution)/shard_map/row_halo/ppermute | solution.py:294
  43.7 0.0 copy-start.8
  43.7 0.0 copy-done.7
  43.7 0.7 copy-done.8
  44.3 7.1 %columns.1 = (bf16[4,128,128]{2,1,0:T(8,128)(2,1)}, f32[4,128,128]{2,1,0:T(8,128)}, bf16[4,128,128]{2,1,0:T(8,128)(2,1)}, bf16[4,128,128]{2,1,0:T(8,128)(2,1)}, bf16[8,272,128]{2,1,0:T(8,128)(2,1)}) custom-call(s32[2]{0:T(128)} %seeds_ref.1, f32[4,128,128]{2,1,0:T(8,128)} %copy-done.2, f32[4,136,128]{2,1,0:T(8,128)} %copy-done.3, ...), custom_call_target="tpu_custom_call" | custom-call | flops 4000000000 | bytes 4000000 | tf_op jit(solution)/shard_map/columns/pallas_call | solution.py:321
  51.4 0.0 copy-start.10
  51.4 0.0 copy-start.9
  51.4 4.3 %all-to-all-start.2 = ((bf16[8,272,128]{2,1,0:T(8,128)(2,1)}), bf16[8,272,128]{2,1,0:T(8,128)(2,1)S(1)}, u32[]{:S(2)}, u32[]{:S(2)}) async-start(bf16[8,272,128]{2,1,0:T(8,128)(2,1)} %get-tuple-element.25), calls=%async_computation.2 | async-start | bytes 1114112 | tf_op jit(solution)/shard_map/weights_near/all_to_all | solution.py:251
  55.7 0.0 copy-done.10
  55.8 3.1 %collective-permute-start.2 = (bf16[4,128,128]{2,1,0:T(8,128)(2,1)S(1)}, bf16[4,128,128]{2,1,0:T(8,128)(2,1)S(1)}, u32[]{:S(2)}, u32[]{:S(2)}) collective-permute-start(bf16[4,128,128]{2,1,0:T(8,128)(2,1)S(1)} %copy-done.10), channel_id=1, source_target_pairs={{4,0},{8,4},{12,8},{16,12},{20,16},{24,20},{28,24},{32,28},{36,32}... | collective-permute-start | bytes 393224 | tf_op jit(solution)/shard_map/gradient_halo/ppermute | solution.py:352
  58.8 0.0 copy-done.9
  58.8 3.1 %collective-permute-start.3 = (bf16[4,128,128]{2,1,0:T(8,128)(2,1)S(1)}, bf16[4,128,128]{2,1,0:T(8,128)(2,1)S(1)}, u32[]{:S(2)}, u32[]{:S(2)}) collective-permute-start(bf16[4,128,128]{2,1,0:T(8,128)(2,1)S(1)} %copy-done.9), channel_id=1, source_target_pairs={{0,4},{4,8},{8,12},{12,16},{16,20},{20,24},{24,28},{28,32},{32,36}... | collective-permute-start | bytes 393224 | tf_op jit(solution)/shard_map/gradient_halo/ppermute | solution.py:353
  62.0 2.1 %collective-permute-done.2.south_ref = bf16[4,128,128]{2,1,0:T(8,128)(2,1)S(1)} collective-permute-done((bf16[4,128,128]{2,1,0:T(8,128)(2,1)S(1)}, bf16[4,128,128]{2,1,0:T(8,128)(2,1)S(1)}, u32[]{:S(2)}, u32[]{:S(2)}) %collective-permute-start.2) | collective-permute-done | bytes 131104 | tf_op jit(solution)/shard_map/gradient_halo/ppermute | solution.py:352
  64.1 0.0 copy-start.4
  64.1 3.2 %collective-permute-done.3.north_ref = bf16[4,128,128]{2,1,0:T(8,128)(2,1)S(1)} collective-permute-done((bf16[4,128,128]{2,1,0:T(8,128)(2,1)S(1)}, bf16[4,128,128]{2,1,0:T(8,128)(2,1)S(1)}, u32[]{:S(2)}, u32[]{:S(2)}) %collective-permute-start.3) | collective-permute-done | bytes 131104 | tf_op jit(solution)/shard_map/gradient_halo/ppermute | solution.py:353
  67.2 0.0 copy-start.5
  67.2 0.0 all-to-all-done.2.parts_ref
  67.3 0.0 copy-start
  67.3 0.0 copy-done.4
  67.3 0.6 copy-done.5
  67.9 0.2 copy-done
  68.1 2.1 %weights_near.1 = (f32[8,34,128]{2,1,0:T(8,128)}, bf16[4,256,128]{2,1,0:T(8,128)(2,1)}) custom-call(bf16[8,272,128]{2,1,0:T(8,128)(2,1)} %copy-done, bf16[4,128,128]{2,1,0:T(8,128)(2,1)} %get-tuple-element.26.next_ref, f32[4,128,128]{2,1,0:T(8,128)} %get-tuple-element.27.grad_ref, bf16[4,128,128]{2,1,0:T(8,128)(2,1)} %copy-done.4, bf16[4,128,128]{2,1,0:T(8,128)(2,1)} %copy-done.5), custom_call_target="tpu_custom_call" | custom-call | bytes 4000000 | tf_op jit(solution)/shard_map/weights_near/pallas_call | solution.py:357
  70.2 19.6 %all_to_all.41 = f32[8,34,128]{2,1,0:T(8,128)S(1)} all-to-all(f32[8,34,128]{2,1,0:T(8,128)} %get-tuple-element.31), channel_id=1, replica_groups=mesh['ylo'=2,'z'=12,'core'=2,'lon'=4,'mem'=4] {'ylo','lon'}, dimensions={0} | all-to-all | bytes 278528 | tf_op jit(solution)/shard_map/weights_middle/all_to_all | solution.py:251
  89.8 17.6 %all_to_all.42 = bf16[12,34,128]{2,1,0:T(8,128)(2,1)S(1)} all-to-all(bf16[12,34,128]{2,1,0:T(8,128)(2,1)S(1)} %broadcast_in_dim.4), channel_id=1, replica_groups=mesh['ylo'=2,'z'=12,'core'=2,'lon'=4,'mem'=4] {'z'}, dimensions={0} | all-to-all | bytes 208896 | tf_op jit(solution)/shard_map/weights_length/all_to_all | solution.py:251
  107.4 9.9 %all_to_all.43.pieces_ref = bf16[8,34,128]{2,1,0:T(8,128)(2,1)} all-to-all(bf16[8,34,128]{2,1,0:T(8,128)(2,1)S(1)} %broadcast_in_dim.5), channel_id=1, replica_groups=mesh['ylo'=2,'z'=12,'core'=2,'lon'=4,'mem'=4] {'ylo','lon'}, dimensions={0} | all-to-all | bytes 139264 | tf_op jit(solution)/shard_map/weights_back/all_to_all | solution.py:251
  117.4 3.4 %all-to-all-start.3 = ((bf16[4,256,128]{2,1,0:T(8,128)(2,1)}), bf16[4,256,128]{2,1,0:T(8,128)(2,1)S(1)}, u32[]{:S(2)}, u32[]{:S(2)}) async-start(bf16[4,256,128]{2,1,0:T(8,128)(2,1)} %get-tuple-element.30), calls=%async_computation.3 | async-start | bytes 524288 | tf_op jit(solution)/shard_map/rows_out/all_to_all | solution.py:251
  120.8 1.7 %weights_back.2 = bf16[8,272,128]{2,1,0:T(8,128)(2,1)} custom-call(bf16[8,34,128]{2,1,0:T(8,128)(2,1)} %all_to_all.43.pieces_ref), custom_call_target="tpu_custom_call" | custom-call | bytes 4000000 | tf_op jit(solution)/shard_map/weights_back/pallas_call | solution.py:384
  122.5 6.3 %all-to-all-done.3 = bf16[4,256,128]{2,1,0:T(8,128)(2,1)S(1)} async-done(((bf16[4,256,128]{2,1,0:T(8,128)(2,1)}), bf16[4,256,128]{2,1,0:T(8,128)(2,1)S(1)}, u32[]{:S(2)}, u32[]{:S(2)}) %all-to-all-start.3) | async-done | bytes 262176 | tf_op jit(solution)/shard_map/rows_out/all_to_all | solution.py:251
  128.8 10.8 %all-to-all-start.7 = ((bf16[8,272,128]{2,1,0:T(8,128)(2,1)}), bf16[8,272,128]{2,1,0:T(8,128)(2,1)S(1)}, u32[]{:S(2)}, u32[]{:S(2)}) async-start(bf16[8,272,128]{2,1,0:T(8,128)(2,1)} %weights_back.2), calls=%async_computation.7 | async-start | bytes 1114112 | tf_op jit(solution)/shard_map/weights_back/all_to_all | solution.py:251
  139.7 1.1 copy_bitcast_fusion
  140.8 8.5 %all-to-all-done.7.refs_0_ = bf16[8,272,128]{2,1,0:T(8,128)(2,1)S(1)} async-done(((bf16[8,272,128]{2,1,0:T(8,128)(2,1)}), bf16[8,272,128]{2,1,0:T(8,128)(2,1)S(1)}, u32[]{:S(2)}, u32[]{:S(2)}) %all-to-all-start.7) | async-done | bytes 557088 | tf_op jit(solution)/shard_map/weights_back/all_to_all | solution.py:251
  149.4 0.0 copy-start.1
  149.4 0.8 copy-done.1
  150.2 2.1 %weights_back.3 = (f32[384,640]{1,0:T(8,128)}, f32[384]{0:T(512)}, f32[64,384]{1,0:T(8,128)}) custom-call(bf16[8,272,128]{2,1,0:T(8,128)(2,1)} %copy-done.1), custom_call_target="tpu_custom_call" | custom-call | bytes 4000000 | tf_op jit(solution)/shard_map/weights_back/pallas_call | solution.py:396
  (8 shorter events, 0.2 us)
Async XLA Ops:
  19.1 4.0 %copy-start.2 = (f32[4,128,128]{2,1,0:T(8,128)}, f32[4,128,128]{2,1,0:T(8,128)S(1)}, u32[]{:S(2)}) copy-start(f32[4,128,128]{2,1,0:T(8,128)S(1)} %all_to_all.40.row_ref) | copy-start | bytes 786436
  19.1 19.3 %all-to-all-start.1 = ((f32[4,136,128]{2,1,0:T(8,128)}), f32[4,136,128]{2,1,0:T(8,128)S(1)}, u32[]{:S(2)}, u32[]{:S(2)}) async-start(f32[4,136,128]{2,1,0:T(8,128)} %get-tuple-element.21), calls=%async_computation.1 | async-start | bytes 557056 | tf_op jit(solution)/shard_map/rows_in/all_to_all | solution.py:251
  23.2 18.3 %collective-permute-start.1 = (bf16[4,128,128]{2,1,0:T(8,128)(2,1)S(1)}, bf16[4,128,128]{2,1,0:T(8,128)(2,1)S(1)}, u32[]{:S(2)}, u32[]{:S(2)}) collective-permute-start(bf16[4,128,128]{2,1,0:T(8,128)(2,1)S(1)} %convert_element_type.26), channel_id=1, source_target_pairs={{4,0},{8,4},{12,8},{16,12},{20,16},{24,20},{28,24},{32,28},{36,32}... | collective-permute-start | bytes 393224 | tf_op jit(solution)/shard_map/row_halo/ppermute | solution.py:295
  35.3 8.4 %collective-permute-start = (bf16[4,128,128]{2,1,0:T(8,128)(2,1)S(1)}, bf16[4,128,128]{2,1,0:T(8,128)(2,1)S(1)}, u32[]{:S(2)}, u32[]{:S(2)}) collective-permute-start(bf16[4,128,128]{2,1,0:T(8,128)(2,1)S(1)} %convert_element_type.26), channel_id=1, source_target_pairs={{0,4},{4,8},{8,12},{12,16},{16,20},{20,24},{24,28},{28,32},{32,36}... | collective-permute-start | bytes 393224 | tf_op jit(solution)/shard_map/row_halo/ppermute | solution.py:294
  37.2 0.7 copy-start.6
  38.5 0.7 copy-start.3
  41.5 2.2 %copy-start.7 = (bf16[4,128,128]{2,1,0:T(8,128)(2,1)}, bf16[4,128,128]{2,1,0:T(8,128)(2,1)S(1)}, u32[]{:S(2)}) copy-start(bf16[4,128,128]{2,1,0:T(8,128)(2,1)S(1)} %collective-permute-done.1.south_ref) | copy-start | bytes 393220
  43.7 0.7 copy-start.8
  51.4 4.3 %copy-start.10 = (bf16[4,128,128]{2,1,0:T(8,128)(2,1)S(1)}, bf16[4,128,128]{2,1,0:T(8,128)(2,1)}, u32[]{:S(2)}) copy-start(bf16[4,128,128]{2,1,0:T(8,128)(2,1)} %get-tuple-element.28) | copy-start | bytes 393220
  51.4 7.4 %copy-start.9 = (bf16[4,128,128]{2,1,0:T(8,128)(2,1)S(1)}, bf16[4,128,128]{2,1,0:T(8,128)(2,1)}, u32[]{:S(2)}) copy-start(bf16[4,128,128]{2,1,0:T(8,128)(2,1)} %get-tuple-element.29) | copy-start | bytes 393220
  51.4 15.8 %all-to-all-start.2 = ((bf16[8,272,128]{2,1,0:T(8,128)(2,1)}), bf16[8,272,128]{2,1,0:T(8,128)(2,1)S(1)}, u32[]{:S(2)}, u32[]{:S(2)}) async-start(bf16[8,272,128]{2,1,0:T(8,128)(2,1)} %get-tuple-element.25), calls=%async_computation.2 | async-start | bytes 1114112 | tf_op jit(solution)/shard_map/weights_near/all_to_all | solution.py:251
  55.8 8.3 %collective-permute-start.2 = (bf16[4,128,128]{2,1,0:T(8,128)(2,1)S(1)}, bf16[4,128,128]{2,1,0:T(8,128)(2,1)S(1)}, u32[]{:S(2)}, u32[]{:S(2)}) collective-permute-start(bf16[4,128,128]{2,1,0:T(8,128)(2,1)S(1)} %copy-done.10), channel_id=1, source_target_pairs={{4,0},{8,4},{12,8},{16,12},{20,16},{24,20},{28,24},{32,28},{36,32}... | collective-permute-start | bytes 393224 | tf_op jit(solution)/shard_map/gradient_halo/ppermute | solution.py:352
  58.8 8.4 %collective-permute-start.3 = (bf16[4,128,128]{2,1,0:T(8,128)(2,1)S(1)}, bf16[4,128,128]{2,1,0:T(8,128)(2,1)S(1)}, u32[]{:S(2)}, u32[]{:S(2)}) collective-permute-start(bf16[4,128,128]{2,1,0:T(8,128)(2,1)S(1)} %copy-done.9), channel_id=1, source_target_pairs={{0,4},{4,8},{8,12},{12,16},{16,20},{20,24},{24,28},{28,32},{32,36}... | collective-permute-start | bytes 393224 | tf_op jit(solution)/shard_map/gradient_halo/ppermute | solution.py:353
  64.1 3.2 %copy-start.4 = (bf16[4,128,128]{2,1,0:T(8,128)(2,1)}, bf16[4,128,128]{2,1,0:T(8,128)(2,1)S(1)}, u32[]{:S(2)}) copy-start(bf16[4,128,128]{2,1,0:T(8,128)(2,1)S(1)} %collective-permute-done.2.south_ref) | copy-start | bytes 393220
  67.2 0.7 copy-start.5
  67.3 0.8 copy-start
  117.4 11.4 %all-to-all-start.3 = ((bf16[4,256,128]{2,1,0:T(8,128)(2,1)}), bf16[4,256,128]{2,1,0:T(8,128)(2,1)S(1)}, u32[]{:S(2)}, u32[]{:S(2)}) async-start(bf16[4,256,128]{2,1,0:T(8,128)(2,1)} %get-tuple-element.30), calls=%async_computation.3 | async-start | bytes 524288 | tf_op jit(solution)/shard_map/rows_out/all_to_all | solution.py:251
  128.8 20.5 %all-to-all-start.7 = ((bf16[8,272,128]{2,1,0:T(8,128)(2,1)}), bf16[8,272,128]{2,1,0:T(8,128)(2,1)S(1)}, u32[]{:S(2)}, u32[]{:S(2)}) async-start(bf16[8,272,128]{2,1,0:T(8,128)(2,1)} %weights_back.2), calls=%async_computation.7 | async-start | bytes 1114112 | tf_op jit(solution)/shard_map/weights_back/all_to_all | solution.py:251
  149.4 0.8 copy-start.1

commit v3 on v2

v3 whole, which is shorter than its diff:
```python
import math

import jax
import jax.numpy as jnp
import numpy as np
from jax import lax
from jax.experimental import pallas as pl
from jax.experimental.pallas import tpu as pltpu
from jax.sharding import Mesh, PartitionSpec as P

MODES = 171
DAMP = 2.0
LANES = 128
BF = jnp.bfloat16
F32 = jnp.float32
MIB = 1024 * 1024
PLACE = ("ylo", "z", "core", "lon")
NEAR = ("core", "mem", "ylo")
BIAS_ROWS = 8


def whole_multiple(value, unit):
    return -(-value // unit) * unit


def filter_tables(lat_total, lon_total):
    padded = whole_multiple(2 * MODES, LANES)
    k = np.arange(MODES)
    angles = (k[:, None] * np.arange(lon_total)[None]) % lon_total * (2.0 * math.pi / lon_total)
    analysis = np.zeros((padded, lon_total))
    analysis[: 2 * MODES] = np.concatenate([np.cos(angles), np.sin(angles)], 0)
    lat = math.pi * ((np.arange(lat_total) + 0.5) / lat_total - 0.5)
    removal = 1.0 - np.exp(-DAMP * (k[None] / MODES) ** 2 / np.cos(lat)[:, None] ** 2)
    removal = removal * np.where(k == 0, 1.0, 2.0) / lon_total
    scale = np.zeros((lat_total, padded), np.float32)
    scale[:, : 2 * MODES] = np.concatenate([removal, removal], 1)
    high = analysis.astype(np.float32).astype(BF)
    low = (analysis - high.astype(np.float64)).astype(np.float32).astype(BF)
    return high, low, scale


def dot(a, b, dims=((1,), (0,))):
    return lax.dot_general(a, b, (dims, ((), ())), preferred_element_type=F32)


def split_dot(x, high, low, dims=((1,), (0,))):
    x_high = x.astype(BF)
    x_low = (x - x_high.astype(F32)).astype(BF)
    return dot(x_high, high, dims) + (dot(x_low, high, dims) + dot(x_high, low, dims))


def filtered(x, scale, high, low):
    coeffs = split_dot(x, high, low, ((1,), (1,))) * scale
    return x - split_dot(coeffs, high, low)


def joined(ref, start, rows):
    return jnp.concatenate([ref[s, start : start + rows, :] for s in range(ref.shape[0])], axis=1)


def store_split(ref, start, value):
    for s in range(ref.shape[0]):
        ref[s, start : start + value.shape[0], :] = value[:, s * LANES : (s + 1) * LANES].astype(
            ref.dtype
        )


def by_row_kernel(state_ref, cotangent_ref, land_ref, orography_ref, out_ref, adjoint_ref, *, classes):
    sectors, rows = out_ref.shape[:2]
    members = state_ref.shape[0]
    band = land_ref.shape[0]
    taken = band * members // sectors
    channels = rows // taken
    code = (jnp.where(land_ref[...] == 1, classes, 0) + orography_ref[...]).astype(F32)
    for q in range(sectors):
        m, first = q * taken // band, q * taken % band
        for k in range(taken):
            picked = pl.ds(first + k, channels, stride=band)
            out_ref[q, k * channels : (k + 1) * channels, :] = state_ref[m, picked, :]
            adjoint_ref[q, k * channels : (k + 1) * channels, :] = cotangent_ref[m, picked, :]
        spare = jnp.zeros((8 - taken, LANES), F32)
        adjoint_ref[q, rows:, :] = jnp.concatenate([code[first : first + taken], spare], axis=0)


def own_scale(place, scale_ref, taken, sectors, band, rows):
    first = place // sectors * band + place % (band // taken) * taken
    channels = rows // taken
    wide = (channels, scale_ref.shape[1])
    return jnp.concatenate(
        [jnp.broadcast_to(scale_ref[pl.ds(first + k, 1), :], wide) for k in range(taken)], axis=0
    )


def adjoint_filter_kernel(
    place_ref, row_ref, scale_ref, high_ref, low_ref, moist_grad_ref, *, taken, band
):
    rows = moist_grad_ref.shape[0]
    scale = own_scale(place_ref[0], scale_ref, taken, row_ref.shape[0], band, rows)
    cotangent = joined(row_ref, 0, rows)
    moist_grad_ref[...] = filtered(cotangent, scale, high_ref[...], low_ref[...])


def column_kernel(
    place_ref,
    seeds_ref,
    row_ref,
    adjoint_ref,
    north_ref,
    south_ref,
    moist_grad_ref,
    scale_ref,
    high_ref,
    low_ref,
    land_ref,
    relief_ref,
    seed_ref,
    w_hidden_ref,
    b_hidden_ref,
    w_tendency_ref,
    next_ref,
    grad_ref,
    to_north_ref,
    to_south_ref,
    weights_ref,
    features_ref,
    stage_ref,
    *,
    band,
):
    taken = features_ref.shape[0]
    sectors = row_ref.shape[0]
    channels = w_tendency_ref.shape[0]
    hidden_units, in_channels = w_hidden_ref.shape
    rows = taken * channels
    stencil_rows = 9 * channels
    lon_total = features_ref.shape[2]
    classes = relief_ref.shape[0]
    place = place_ref[0]

    state = joined(row_ref, 0, rows)
    rounded = state.astype(BF).astype(F32)
    sources = [joined(north_ref, 0, channels).astype(F32)]
    sources += [rounded[k * channels : (k + 1) * channels] for k in range(taken)]
    sources += [joined(south_ref, 0, channels).astype(F32)]
    for j, source in enumerate(sources):
        for b in range(3):
            moved = source if b == 1 else pltpu.roll(source, (1 - b) % lon_total, 1)
            moved = moved.astype(BF)
            for a in range(3):
                if 0 <= j - a < taken:
                    start = (3 * a + b) * channels
                    features_ref[j - a, start : start + channels, :] = moved
    class_ids = lax.broadcasted_iota(jnp.int32, (2 * classes, lon_total), 0).astype(F32)
    codes = joined(adjoint_ref, rows, 8)
    surface = jnp.concatenate(
        [land_ref[0:1, :] + relief_ref[...], land_ref[1:2, :] + relief_ref[...]], axis=0
    )
    seed = seeds_ref[place % sectors * taken // band]
    table = (surface + seed_ref[pl.ds(seed, 1), :]).astype(BF)
    bias = jnp.transpose(jnp.broadcast_to(b_hidden_ref[...], (8, hidden_units)))[:, 0:1]
    w_hidden = w_hidden_ref[...]
    w_tendency = w_tendency_ref[...]
    grad_in = jnp.zeros((hidden_units, in_channels), F32)
    grad_out = jnp.zeros((channels, hidden_units), F32)
    grad_bias = jnp.zeros((16, hidden_units), F32)
    ones = jnp.ones((16, lon_total), BF)
    moist = []
    sums = []
    for k in range(taken):
        pick = jnp.where(class_ids == codes[k : k + 1], 1.0, 0.0).astype(BF)
        features_ref[k, stencil_rows:, :] = dot(table, pick, ((0,), (0,))).astype(BF)
        features = features_ref[k]
        preact = dot(w_hidden, features) + bias
        logistic = 1.0 / (1.0 + jnp.exp(-preact))
        hidden = (preact * logistic).astype(BF)
        part = slice(k * channels, (k + 1) * channels)
        moist.append(state[part] + dot(w_tendency, hidden))
        tendency_grad = moist_grad_ref[part, :].astype(BF)
        hidden_grad = dot(w_tendency, tendency_grad, ((0,), (0,)))
        preact_grad = (hidden_grad * logistic * (1.0 + preact * (1.0 - logistic))).astype(BF)
        grad_out += dot(tendency_grad, hidden, ((1,), (1,)))
        grad_in += dot(preact_grad, features, ((1,), (1,)))
        grad_bias += dot(ones, preact_grad, ((1,), (1,)))
        stencil_grad = dot(w_hidden[:, :stencil_rows], preact_grad, ((0,), (0,)))
        sums.append([])
        for a in range(3):
            total = None
            for b in range(3):
                start = (3 * a + b) * channels
                piece = stencil_grad[start : start + channels]
                if b != 1:
                    piece = pltpu.roll(piece, (b - 1) % lon_total, 1)
                total = piece if total is None else total + piece
            sums[k].append(total)
    store_split(to_north_ref, 0, sums[0][0])
    store_split(to_south_ref, 0, sums[-1][2])
    for k in range(taken):
        total = moist_grad_ref[k * channels : (k + 1) * channels, :] + sums[k][1]
        if k > 0:
            total = total + sums[k - 1][2]
        if k + 1 < taken:
            total = total + sums[k + 1][0]
        store_split(grad_ref, k * channels, total)
    scale = own_scale(place, scale_ref, taken, sectors, band, rows)
    moist = jnp.concatenate(moist, axis=0)
    store_split(next_ref, 0, filtered(moist, scale, high_ref[...], low_ref[...]))

    bias_high = grad_bias[0:1].astype(BF).astype(F32)
    bias_low = grad_bias[0:1] - bias_high
    tiles = hidden_units // LANES
    shares, share_rows = weights_ref.shape[:2]
    stage_ref[...] = jnp.zeros(stage_ref.shape, F32)
    for p in range(shares):
        start = 0
        for value in (grad_in, grad_out):
            count = value.shape[0] // shares
            for t in range(value.shape[1] // LANES):
                stage_ref[p, start : start + count, :] = value[
                    p * count : (p + 1) * count, t * LANES : (t + 1) * LANES
                ]
                start += count
        if p == 0:
            for half in (bias_high, bias_low):
                for t in range(tiles):
                    stage_ref[p, start : start + 1, :] = half[:, t * LANES : (t + 1) * LANES]
                    start += 1
        weights_ref[p] = stage_ref[p].astype(BF)


def near_sum_kernel(
    parts_ref, next_ref, grad_ref, south_ref, north_ref, out_ref, sum_ref, stage_ref
):
    sectors, rows = next_ref.shape[:2]
    channels = south_ref.shape[1]
    total = parts_ref[0].astype(F32)
    for p in range(1, parts_ref.shape[0]):
        total = total + parts_ref[p].astype(F32)
    sum_ref[...] = total
    piece_rows = sum_ref.shape[0] // sectors
    half_rows = stage_ref.shape[0] // 2
    stage_ref[...] = jnp.zeros(stage_ref.shape, F32)
    for s in range(sectors):
        out_ref[s, :rows, :] = next_ref[s]
        part = grad_ref[s]
        first = part[:channels] + north_ref[s].astype(F32)
        last = part[rows - channels :] + south_ref[s].astype(F32)
        inner = [part[channels : rows - channels]] if rows > 2 * channels else []
        part = jnp.concatenate([first] + inner + [last], axis=0)
        out_ref[s, rows : 2 * rows, :] = part.astype(BF)
        piece = sum_ref[s * piece_rows : (s + 1) * piece_rows, :]
        high = piece.astype(BF).astype(F32)
        stage_ref[:piece_rows, :] = high
        stage_ref[half_rows : half_rows + piece_rows, :] = piece - high
        out_ref[s, 2 * rows :, :] = stage_ref[...].astype(BF)


def spread_kernel(pieces_ref, shares_ref, sum_ref):
    pieces, piece_rows = pieces_ref.shape[:2]
    for p in range(pieces):
        sum_ref[p * piece_rows : (p + 1) * piece_rows, :] = pieces_ref[p].astype(F32)
    share = sum_ref[...].astype(BF)
    for p in range(shares_ref.shape[0]):
        shares_ref[p] = share


def unpack_kernel(shares_ref, grad_in_ref, grad_bias_ref, grad_out_ref, stage_ref, *, scaling):
    shares = shares_ref.shape[0]
    for p in range(shares):
        stage_ref[p] = shares_ref[p].astype(F32) * scaling
        start = 0
        for ref in (grad_in_ref, grad_out_ref):
            count = ref.shape[0] // shares
            for t in range(ref.shape[1] // LANES):
                ref[p * count : (p + 1) * count, t * LANES : (t + 1) * LANES] = stage_ref[
                    p, start : start + count, :
                ]
                start += count
        if p == 0:
            tiles = grad_bias_ref.shape[0] // LANES
            for t in range(tiles):
                both = stage_ref[p, start + t, :] + stage_ref[p, start + tiles + t, :]
                grad_bias_ref[t * LANES : (t + 1) * LANES] = both


def call(kernel, outs, inputs, smem=0, scratch=(), flops=0, vmem=8, **static):
    on_vmem = pl.BlockSpec(memory_space=pltpu.VMEM)
    on_smem = pl.BlockSpec(memory_space=pltpu.SMEM)

    def body(*refs):
        kernel(*refs, **static)

    return pl.pallas_call(
        body,
        out_shape=outs,
        in_specs=[on_smem] * smem + [on_vmem] * (inputs - smem),
        out_specs=jax.tree.map(lambda _: on_vmem, outs),
        scratch_shapes=list(scratch),
        cost_estimate=pl.CostEstimate(flops=flops, bytes_accessed=1_000_000, transcendentals=0),
        compiler_params=pltpu.CompilerParams(vmem_limit_bytes=vmem * MIB),
    )


def exchange(x, axes):
    return lax.all_to_all(x, axes, 0, 0, tiled=True)


def on_device(
    column_state,
    cotangent,
    land_mask,
    orography,
    member_seeds,
    land_table,
    relief_table,
    seed_table,
    w_hidden,
    b_hidden,
    w_tendency,
):
    members, channels, band, lon_cols = column_state.shape
    hidden_units, in_channels = w_hidden.shape
    classes = relief_table.shape[0]
    sectors = lax.axis_size("lon")
    peers = lax.axis_size(PLACE)
    lat_total = band * (peers // sectors)
    lon_total = lon_cols * sectors
    taken = band * members // sectors
    groups = band // taken
    rows = taken * channels
    shape = jax.ShapeDtypeStruct

    with jax.named_scope("rows_in"):
        flat = (members, channels * band, lon_cols)
        state_rows, adjoint_rows = call(
            by_row_kernel,
            (shape((sectors, rows, lon_cols), F32), shape((sectors, rows + 8, lon_cols), F32)),
            4,
            classes=classes,
        )(column_state.reshape(flat), cotangent.reshape(flat), land_mask, orography)
        row = exchange(state_rows, "lon")
        adjoint_row = exchange(adjoint_rows, "lon")

    with jax.named_scope("row_halo"):
        south_going = []
        for i in range(peers):
            j = i + 1 if i % groups < groups - 1 else i + sectors - (groups - 1)
            if j < peers:
                south_going.append((i, j))
        north_going = [(j, i) for i, j in south_going]
        north = lax.ppermute(row[:, rows - channels :].astype(BF), PLACE, south_going)
        south = lax.ppermute(row[:, :channels].astype(BF), PLACE, north_going)

    place = lax.axis_index(PLACE).reshape(1)
    high, low, scale = [jnp.asarray(t) for t in filter_tables(lat_total, lon_total)]
    with jax.named_scope("adjoint_filter"):
        moist_grad = call(
            adjoint_filter_kernel,
            shape((rows, lon_total), F32),
            5,
            smem=1,
            flops=12 * rows * lon_total * high.shape[0],
            vmem=12,
            taken=taken,
            band=band,
        )(place, adjoint_row, scale, high, low)

    near = lax.axis_size(NEAR)
    length = lax.axis_size("z")
    filled = (hidden_units * in_channels + channels * hidden_units) // (LANES * near)
    share_rows = whole_multiple(filled + BIAS_ROWS, 16)
    piece_rows = share_rows // sectors
    half_rows = whole_multiple(piece_rows, 16)
    with jax.named_scope("columns"):
        block = (sectors, rows, LANES)
        edge = (sectors, channels, LANES)
        next_rows, grad_rows, to_north, to_south, weights = call(
            column_kernel,
            (
                shape(block, BF),
                shape(block, F32),
                shape(edge, BF),
                shape(edge, BF),
                shape((near, share_rows, LANES), BF),
            ),
            16,
            smem=2,
            scratch=[
                pltpu.VMEM((taken, in_channels, lon_total), BF),
                pltpu.VMEM((near, share_rows, LANES), F32),
            ],
            flops=4_000_000_000,
            vmem=32,
            band=band,
        )(
            place,
            member_seeds,
            row,
            adjoint_row,
            north,
            south,
            moist_grad,
            scale,
            high,
            low,
            land_table,
            relief_table,
            seed_table,
            w_hidden,
            b_hidden.reshape(1, hidden_units),
            w_tendency,
        )

    with jax.named_scope("gradient_halo"):
        from_south = lax.ppermute(to_north, PLACE, north_going)
        from_north = lax.ppermute(to_south, PLACE, south_going)

    with jax.named_scope("weights_near"):
        parts = exchange(weights, NEAR)
        outgoing = call(
            near_sum_kernel,
            shape((sectors, 2 * rows + 2 * half_rows, LANES), BF),
            5,
            scratch=[pltpu.VMEM((share_rows, LANES), F32), pltpu.VMEM((2 * half_rows, LANES), F32)],
        )(parts, next_rows, grad_rows, from_south, from_north)

    with jax.named_scope("rows_out"):
        blocks = exchange(outgoing, "lon")

        def by_band(values):
            values = values.reshape(members, groups, taken, channels, lon_cols).astype(F32)
            values = jnp.transpose(values, (0, 3, 1, 2, 4))
            return values.reshape(members, channels, band, lon_cols)

        next_state = by_band(blocks[:, :rows])
        state_grad = by_band(blocks[:, rows : 2 * rows])

    with jax.named_scope("weights_length"):
        start = 2 * rows
        highs = blocks[:, start : start + piece_rows].astype(F32)
        start += half_rows
        lows = blocks[:, start : start + piece_rows].astype(F32)
        piece = jnp.sum(highs + lows, 0, keepdims=True).astype(BF)
        parts = exchange(jnp.broadcast_to(piece, (length, piece_rows, LANES)), "z")
        piece = jnp.sum(parts.astype(F32), 0, keepdims=True).astype(BF)

    with jax.named_scope("weights_back"):
        pieces = exchange(jnp.broadcast_to(piece, (sectors, piece_rows, LANES)), "lon")
        spread = call(
            spread_kernel,
            shape((near, share_rows, LANES), BF),
            1,
            scratch=[pltpu.VMEM((share_rows, LANES), F32)],
        )(pieces)
        shares = exchange(spread, NEAR)
        columns = members * lax.axis_size("mem") * lat_total * lon_total
        grad_in, grad_bias, grad_out = call(
            unpack_kernel,
            (
                shape((hidden_units, in_channels), F32),
                shape((hidden_units,), F32),
                shape((channels, hidden_units), F32),
            ),
            1,
            scratch=[pltpu.VMEM((near, share_rows, LANES), F32)],
            scaling=1.0 / math.sqrt(columns),
        )(shares)
    return next_state, state_grad, grad_in, grad_bias, grad_out


def solution(mesh):
    lat, lon, mem = mesh.devices.shape
    devices = mesh.devices.reshape(2, lat // 4, 2, lon, mem)
    split = Mesh(devices, ("ylo", "z", "core", "lon", "mem"))
    lat_axes = ("ylo", "z", "core")
    field = P("mem", None, lat_axes, "lon")
    surface = P(lat_axes, "lon")
    whole = P()
    return jax.shard_map(
        on_device,
        mesh=split,
        in_specs=(field, field, surface, surface, P("mem")) + (whole,) * 6,
        out_specs=(field, field, whole, whole, whole),
        check_vma=False,
    )
```

time: 153 us -> 138 us (0.902)
  Pallas kernels: 17.2 us -> 9.04 us
  waiting for transfers between devices: 22.3 us -> 14.3 us
  blocking collectives: 63.7 us -> 65.3 us
    pallas_call x6, Pallas kernels: 17.2 us -> 9.04 us  [the longest x1 5.06 us: on_device(): call(column_kernel, (shape(block, BF), shape(block, F32), shape(edge, BF)...]
    all_to_all x4 -> x3, waiting for transfers between devices: 14.8 us -> 9.3 us  [exchange(): return lax.all_to_all(x, axes, 0, 0, tiled=True)]
    ppermute x4, waiting for transfers between devices: 7.47 us -> 5.02 us  [the longest x1 3 us: on_device(): from_south = lax.ppermute(to_north, PLACE, north_going)]
    ppermute x4, starting transfers between devices: 20.2 us -> 18.1 us  [the longest x1 7.46 us: on_device(): south = lax.ppermute(row[:, :channels].astype(BF), PLACE, north_going)]
    reshape x0 -> x2, local copies, waits for them, and re-layouts: none -> 1.81 us  [by_band(): return values.reshape(members, channels, band, lon_cols)]
    all_to_all x4 -> x3, starting transfers between devices: 22.6 us -> 24.2 us  [exchange(): return lax.all_to_all(x, axes, 0, 0, tiled=True)]
    all_to_all x4, blocking collectives: 63.7 us -> 65.3 us  [exchange(): return lax.all_to_all(x, axes, 0, 0, tiled=True)]
    unnamed x22 -> x28, local copies, waits for them, and re-layouts: 3.7 us -> 3.31 us
  transfers between devices with their start and end apart: 8 -> 7, of which waited for: 5 -> 6; matrix products, arithmetic and copies ran while one was open for 1% -> 1% of each run, Pallas kernels for 3% -> 1%
where the time goes in v3:
time: 138 us; the launch traced here: 137 us
  blocking collectives  65.3 us (47%)
  starting transfers between devices  42.3 us (31%)
  waiting for transfers between devices  14.3 us (10%)
  Pallas kernels  9.04 us (7%)
  local copies, waits for them, and re-layouts  5.18 us (4%)
    all_to_all x4, blocking collectives, exchange(): return lax.all_to_all(x, axes, 0, 0, tiled=True)  65.3 us
    all_to_all x3, starting transfers between devices, exchange(): return lax.all_to_all(x, axes, 0, 0, tiled=True)  24.2 us
    all_to_all x3, waiting for transfers between devices, exchange(): return lax.all_to_all(x, axes, 0, 0, tiled=True)  9.3 us
    ppermute x1, starting transfers between devices, on_device(): south = lax.ppermute(row[:, :channels].astype(BF), PLACE, north_going)  7.46 us
    pallas_call x1, Pallas kernels, on_device(): call(column_kernel, (shape(block, BF), shape(block, F32), shape(edge, BF)...  5.06 us
    ppermute x1, starting transfers between devices, on_device(): lax.ppermute(row[:, rows - channels:].astype(BF), PLACE, south_going)  4.4 us
    ppermute x1, starting transfers between devices, on_device(): from_north = lax.ppermute(to_south, PLACE, south_going)  4.29 us
    unnamed x28, local copies, waits for them, and re-layouts  3.31 us
  transfers between devices with their start and end apart: 7, of which 6 were waited for; matrix products, arithmetic and copies ran while one was open for 1% of the time, Pallas kernels for 1%

profile of v3, /device:TPU:1, one launch (start us, length us, event | category | flops | bytes accessed | tf_op | source)
XLA Modules:
  0.0 137.1 jit_solution(15073482688159281288)
XLA Ops:
  0.6 0.0 copy-start.5
  0.6 0.7 copy-done.5
  1.3 0.0 copy-start.3
  1.3 0.9 copy-done.3
  2.3 0.0 copy-start.4
  2.3 0.9 copy-done.4
  3.2 0.0 copy-start.6
  3.2 0.7 copy-done.6
  3.9 0.7 rows_in.1
  4.6 16.4 %all_to_all.35.refs_2_ = f32[4,128,128]{2,1,0:T(8,128)S(1)} all-to-all(f32[4,128,128]{2,1,0:T(8,128)S(1)} %get-tuple-element.15), channel_id=1, replica_groups=mesh['ylo'=2,'z'=12,'core'=2,'lon'=4,'mem'=4] {'lon'}, dimensions={0} | all-to-all | bytes 524288 | tf_op jit(solution)/shard_map/rows_in/all_to_all | solution.py:304
  21.1 0.0 copy-start.13
  21.1 0.0 copy-start.1
  21.1 4.4 %all-to-all-start.1 = ((f32[4,136,128]{2,1,0:T(8,128)}), f32[4,136,128]{2,1,0:T(8,128)S(1)}, u32[]{:S(2)}, u32[]{:S(2)}) async-start(f32[4,136,128]{2,1,0:T(8,128)} %get-tuple-element.16), calls=%async_computation.1 | async-start | bytes 557056 | tf_op jit(solution)/shard_map/rows_in/all_to_all | solution.py:304
  25.5 0.0 copy-start
  25.5 0.0 copy-start.2
  25.6 4.4 %collective-permute-start = (bf16[4,64,128]{2,1,0:T(8,128)(2,1)S(1)}, bf16[4,64,128]{2,1,0:T(8,128)(2,1)S(1)}, u32[]{:S(2)}, u32[]{:S(2)}) collective-permute-start(bf16[4,64,128]{2,1,0:T(8,128)(2,1)S(1)} %get-tuple-element.28), channel_id=1, source_target_pairs={{0,4},{4,16},{8,12},{12,24},{16,20},{20,32},{24,28},{28,40},{32,36... | collective-permute-start | bytes 196616 | tf_op jit(solution)/shard_map/row_halo/ppermute | solution.py:350
  30.0 7.5 %collective-permute-start.1 = (bf16[4,64,128]{2,1,0:T(8,128)(2,1)S(1)}, bf16[4,64,128]{2,1,0:T(8,128)(2,1)S(1)}, u32[]{:S(2)}, u32[]{:S(2)}) collective-permute-start(bf16[4,64,128]{2,1,0:T(8,128)(2,1)S(1)} %get-tuple-element.27), channel_id=1, source_target_pairs={{4,0},{16,4},{12,8},{24,12},{20,16},{32,20},{28,24},{40,28},{36,32... | collective-permute-start | bytes 196616 | tf_op jit(solution)/shard_map/row_halo/ppermute | solution.py:351
  37.4 0.0 copy-done.13
  37.5 0.0 all-to-all-done.1.refs_1_.refs_3_
  37.5 0.0 copy-done.1
  37.5 0.0 copy-done
  37.5 0.0 copy-done.2
  37.5 0.0 copy-start.7
  37.5 0.0 copy-start.8
  37.5 0.0 copy-start.9
  37.6 0.0 copy-start.10
  37.6 0.0 copy-start.11
  37.6 0.0 copy-start.12
  37.6 1.2 adjoint_filter.1.refs_6_
  38.8 0.9 collective-permute-done.refs_4_
  39.7 0.4 collective-permute-done.1.refs_5_
  40.1 0.0 copy-done.7
  40.1 0.0 copy-done.8
  40.1 0.0 copy-done.9
  40.1 0.0 copy-done.10
  40.1 0.0 copy-done.11
  40.1 0.0 copy-done.12
  40.1 5.1 %columns.1 = (bf16[4,128,128]{2,1,0:T(8,128)(2,1)S(1)}, f32[4,128,128]{2,1,0:T(8,128)S(1)}, bf16[4,64,128]{2,1,0:T(8,128)(2,1)S(1)}, bf16[4,64,128]{2,1,0:T(8,128)(2,1)S(1)}, bf16[16,144,128]{2,1,0:T(8,128)(2,1)}) custom-call(s32[1]{0:T(128)} %bitcast.refs_0_, s32[2]{0:T(128)S(1)} %copy-done.12, f32[4,128,128]{2,1,0:T(8,128)S(1)} %all_to_all.35.refs_2_, ...), custom_call_target="tpu_custom_call" | custom-call | flops 4000000000 | bytes 1000000 | tf_op jit(solution)/shard_map/columns/pallas_call | solution.py:376
  45.2 10.8 %all-to-all-start.2 = ((bf16[16,144,128]{2,1,0:T(8,128)(2,1)}), bf16[16,144,128]{2,1,0:T(8,128)(2,1)S(1)}, u32[]{:S(2)}, u32[]{:S(2)}) async-start(bf16[16,144,128]{2,1,0:T(8,128)(2,1)} %get-tuple-element.17), calls=%async_computation.2 | async-start | bytes 1179648 | tf_op jit(solution)/shard_map/weights_near/all_to_all | solution.py:304
  56.0 1.9 %collective-permute-start.2 = (bf16[4,64,128]{2,1,0:T(8,128)(2,1)S(1)}, bf16[4,64,128]{2,1,0:T(8,128)(2,1)S(1)}, u32[]{:S(2)}, u32[]{:S(2)}) collective-permute-start(bf16[4,64,128]{2,1,0:T(8,128)(2,1)S(1)} %get-tuple-element.20), channel_id=1, source_target_pairs={{4,0},{16,4},{12,8},{24,12},{20,16},{32,20},{28,24},{40,28},{36,32... | collective-permute-start | bytes 196616 | tf_op jit(solution)/shard_map/gradient_halo/ppermute | solution.py:414
  57.9 4.3 %collective-permute-start.3 = (bf16[4,64,128]{2,1,0:T(8,128)(2,1)S(1)}, bf16[4,64,128]{2,1,0:T(8,128)(2,1)S(1)}, u32[]{:S(2)}, u32[]{:S(2)}) collective-permute-start(bf16[4,64,128]{2,1,0:T(8,128)(2,1)S(1)} %get-tuple-element.21), channel_id=1, source_target_pairs={{0,4},{4,16},{8,12},{12,24},{16,20},{20,32},{24,28},{28,40},{32,36... | collective-permute-start | bytes 196616 | tf_op jit(solution)/shard_map/gradient_halo/ppermute | solution.py:415
  62.2 3.0 %collective-permute-done.2.refs_3_ = bf16[4,64,128]{2,1,0:T(8,128)(2,1)S(1)} collective-permute-done((bf16[4,64,128]{2,1,0:T(8,128)(2,1)S(1)}, bf16[4,64,128]{2,1,0:T(8,128)(2,1)S(1)}, u32[]{:S(2)}, u32[]{:S(2)}) %collective-permute-start.2) | collective-permute-done | bytes 65568 | tf_op jit(solution)/shard_map/gradient_halo/ppermute | solution.py:414
  65.2 0.7 collective-permute-done.3.refs_4_
  65.9 1.0 all-to-all-done.2.refs_0_
  66.9 0.1 weights_near.1
  67.0 14.0 %all_to_all.36 = bf16[4,352,128]{2,1,0:T(8,128)(2,1)S(1)} all-to-all(bf16[4,352,128]{2,1,0:T(8,128)(2,1)S(1)} %weights_near.1), channel_id=1, replica_groups=mesh['ylo'=2,'z'=12,'core'=2,'lon'=4,'mem'=4] {'lon'}, dimensions={0} | all-to-all | bytes 720896 | tf_op jit(solution)/shard_map/rows_out/all_to_all | solution.py:304
  81.0 25.1 %all_to_all.37 = bf16[12,36,128]{2,1,0:T(8,128)(2,1)S(1)} all-to-all(bf16[12,36,128]{2,1,0:T(8,128)(2,1)S(1)} %broadcast_in_dim.4), channel_id=1, replica_groups=mesh['ylo'=2,'z'=12,'core'=2,'lon'=4,'mem'=4] {'z'}, dimensions={0} | all-to-all | bytes 221184 | tf_op jit(solution)/shard_map/weights_length/all_to_all | solution.py:304
  106.2 9.8 %all_to_all.38.refs_0_ = bf16[4,36,128]{2,1,0:T(8,128)(2,1)S(1)} all-to-all(bf16[4,36,128]{2,1,0:T(8,128)(2,1)S(1)} %broadcast_in_dim.5), channel_id=1, replica_groups=mesh['ylo'=2,'z'=12,'core'=2,'lon'=4,'mem'=4] {'lon'}, dimensions={0} | all-to-all | bytes 73728 | tf_op jit(solution)/shard_map/weights_back/all_to_all | solution.py:304
  116.0 0.9 weights_back.2
  116.8 9.0 %all-to-all-start.6 = ((bf16[16,144,128]{2,1,0:T(8,128)(2,1)}), bf16[16,144,128]{2,1,0:T(8,128)(2,1)S(1)}, u32[]{:S(2)}, u32[]{:S(2)}) async-start(bf16[16,144,128]{2,1,0:T(8,128)(2,1)} %weights_back.2), calls=%async_computation.6 | async-start | bytes 1179648 | tf_op jit(solution)/shard_map/weights_back/all_to_all | solution.py:304
  125.9 0.9 copy.21
  126.8 0.9 copy.22
  127.7 8.3 %all-to-all-done.6.refs_0_ = bf16[16,144,128]{2,1,0:T(8,128)(2,1)S(1)} async-done(((bf16[16,144,128]{2,1,0:T(8,128)(2,1)}), bf16[16,144,128]{2,1,0:T(8,128)(2,1)S(1)}, u32[]{:S(2)}, u32[]{:S(2)}) %all-to-all-start.6) | async-done | bytes 589856 | tf_op jit(solution)/shard_map/weights_back/all_to_all | solution.py:304
  136.0 1.1 weights_back.3
  (10 shorter events, 0.2 us)
Async XLA Ops:
  0.6 0.7 copy-start.5
  1.3 0.9 copy-start.3
  2.3 0.9 copy-start.4
  3.2 0.7 copy-start.6
  21.1 16.4 %copy-start.13 = (f32[384]{0:T(512)S(1)}, f32[384]{0:T(512)}, u32[]{:S(2)}) copy-start(f32[384]{0:T(512)} %param.23) | copy-start | bytes 4612
  21.1 16.4 %copy-start.1 = (bf16[384,512]{1,0:T(8,128)(2,1)S(1)}, bf16[384,512]{1,0:T(8,128)(2,1)}, u32[]{:S(2)}) copy-start(bf16[384,512]{1,0:T(8,128)(2,1)} %constant.36.clone.refs_4_.refs_9_) | copy-start | bytes 1179652
  21.1 16.4 %all-to-all-start.1 = ((f32[4,136,128]{2,1,0:T(8,128)}), f32[4,136,128]{2,1,0:T(8,128)S(1)}, u32[]{:S(2)}, u32[]{:S(2)}) async-start(f32[4,136,128]{2,1,0:T(8,128)} %get-tuple-element.16), calls=%async_computation.1 | async-start | bytes 557056 | tf_op jit(solution)/shard_map/rows_in/all_to_all | solution.py:304
  25.5 12.0 %copy-start = (bf16[384,512]{1,0:T(8,128)(2,1)S(1)}, bf16[384,512]{1,0:T(8,128)(2,1)}, u32[]{:S(2)}) copy-start(bf16[384,512]{1,0:T(8,128)(2,1)} %constant.35.clone.refs_3_.refs_8_) | copy-start | bytes 1179652
  25.5 12.0 %copy-start.2 = (f32[192,384]{1,0:T(8,128)S(1)}, f32[192,384]{1,0:T(8,128)}, u32[]{:S(2)}) copy-start(f32[192,384]{1,0:T(8,128)} %constant.37.clone.refs_2_.refs_7_) | copy-start | bytes 884740
  25.6 14.1 %collective-permute-start = (bf16[4,64,128]{2,1,0:T(8,128)(2,1)S(1)}, bf16[4,64,128]{2,1,0:T(8,128)(2,1)S(1)}, u32[]{:S(2)}, u32[]{:S(2)}) collective-permute-start(bf16[4,64,128]{2,1,0:T(8,128)(2,1)S(1)} %get-tuple-element.28), channel_id=1, source_target_pairs={{0,4},{4,16},{8,12},{12,24},{16,20},{20,32},{24,28},{28,40},{32,36... | collective-permute-start | bytes 196616 | tf_op jit(solution)/shard_map/row_halo/ppermute | solution.py:350
  30.0 10.1 %collective-permute-start.1 = (bf16[4,64,128]{2,1,0:T(8,128)(2,1)S(1)}, bf16[4,64,128]{2,1,0:T(8,128)(2,1)S(1)}, u32[]{:S(2)}, u32[]{:S(2)}) collective-permute-start(bf16[4,64,128]{2,1,0:T(8,128)(2,1)S(1)} %get-tuple-element.27), channel_id=1, source_target_pairs={{4,0},{16,4},{12,8},{24,12},{20,16},{32,20},{28,24},{40,28},{36,32... | collective-permute-start | bytes 196616 | tf_op jit(solution)/shard_map/row_halo/ppermute | solution.py:351
  37.5 2.5 %copy-start.7 = (bf16[384,640]{1,0:T(8,128)(2,1)S(1)}, bf16[384,640]{1,0:T(8,128)(2,1)}, u32[]{:S(2)}) copy-start(bf16[384,640]{1,0:T(8,128)(2,1)} %refs_13_.1) | copy-start | bytes 1474564
  37.5 2.5 %copy-start.8 = (bf16[64,384]{1,0:T(8,128)(2,1)S(1)}, bf16[64,384]{1,0:T(8,128)(2,1)}, u32[]{:S(2)}) copy-start(bf16[64,384]{1,0:T(8,128)(2,1)} %refs_15_.1) | copy-start | bytes 147460
  37.5 2.5 %copy-start.9 = (f32[32,64]{1,0:T(8,128)S(1)}, f32[32,64]{1,0:T(8,128)}, u32[]{:S(2)}) copy-start(f32[32,64]{1,0:T(8,128)} %refs_12_.1) | copy-start | bytes 24580
  37.6 2.5 %copy-start.10 = (f32[16,64]{1,0:T(8,128)S(1)}, f32[16,64]{1,0:T(8,128)}, u32[]{:S(2)}) copy-start(f32[16,64]{1,0:T(8,128)} %refs_11_.1) | copy-start | bytes 12292
  37.6 2.5 %copy-start.11 = (f32[2,64]{1,0:T(2,128)S(1)}, f32[2,64]{1,0:T(2,128)}, u32[]{:S(2)}) copy-start(f32[2,64]{1,0:T(2,128)} %refs_10_.1) | copy-start | bytes 1540
  37.6 2.5 %copy-start.12 = (s32[2]{0:T(128)S(1)}, s32[2]{0:T(128)}, u32[]{:S(2)}) copy-start(s32[2]{0:T(128)} %refs_1_.1) | copy-start | bytes 28
  45.2 21.7 %all-to-all-start.2 = ((bf16[16,144,128]{2,1,0:T(8,128)(2,1)}), bf16[16,144,128]{2,1,0:T(8,128)(2,1)S(1)}, u32[]{:S(2)}, u32[]{:S(2)}) async-start(bf16[16,144,128]{2,1,0:T(8,128)(2,1)} %get-tuple-element.17), calls=%async_computation.2 | async-start | bytes 1179648 | tf_op jit(solution)/shard_map/weights_near/all_to_all | solution.py:304
  56.0 9.2 %collective-permute-start.2 = (bf16[4,64,128]{2,1,0:T(8,128)(2,1)S(1)}, bf16[4,64,128]{2,1,0:T(8,128)(2,1)S(1)}, u32[]{:S(2)}, u32[]{:S(2)}) collective-permute-start(bf16[4,64,128]{2,1,0:T(8,128)(2,1)S(1)} %get-tuple-element.20), channel_id=1, source_target_pairs={{4,0},{16,4},{12,8},{24,12},{20,16},{32,20},{28,24},{40,28},{36,32... | collective-permute-start | bytes 196616 | tf_op jit(solution)/shard_map/gradient_halo/ppermute | solution.py:414
  57.9 8.0 %collective-permute-start.3 = (bf16[4,64,128]{2,1,0:T(8,128)(2,1)S(1)}, bf16[4,64,128]{2,1,0:T(8,128)(2,1)S(1)}, u32[]{:S(2)}, u32[]{:S(2)}) collective-permute-start(bf16[4,64,128]{2,1,0:T(8,128)(2,1)S(1)} %get-tuple-element.21), channel_id=1, source_target_pairs={{0,4},{4,16},{8,12},{12,24},{16,20},{20,32},{24,28},{28,40},{32,36... | collective-permute-start | bytes 196616 | tf_op jit(solution)/shard_map/gradient_halo/ppermute | solution.py:415
  116.8 19.2 %all-to-all-start.6 = ((bf16[16,144,128]{2,1,0:T(8,128)(2,1)}), bf16[16,144,128]{2,1,0:T(8,128)(2,1)S(1)}, u32[]{:S(2)}, u32[]{:S(2)}) async-start(bf16[16,144,128]{2,1,0:T(8,128)(2,1)} %weights_back.2), calls=%async_computation.6 | async-start | bytes 1179648 | tf_op jit(solution)/shard_map/weights_back/all_to_all | solution.py:304

commit v4 on v3

v4 whole, which is shorter than its diff:
```python
import math

import jax
import jax.numpy as jnp
import numpy as np
from jax import lax
from jax.experimental import pallas as pl
from jax.experimental.pallas import tpu as pltpu
from jax.sharding import Mesh, PartitionSpec as P

MODES = 171
DAMP = 2.0
LANES = 128
BF = jnp.bfloat16
F32 = jnp.float32
MIB = 1024 * 1024
PLACE = ("ylo", "z", "core", "lon")
NEAR = ("core", "mem", "ylo")
BIAS_ROWS = 8


def whole_multiple(value, unit):
    return -(-value // unit) * unit


def filter_tables(lat_total, lon_total):
    padded = whole_multiple(2 * MODES, LANES)
    k = np.arange(MODES)
    angles = (k[:, None] * np.arange(lon_total)[None]) % lon_total * (2.0 * math.pi / lon_total)
    analysis = np.zeros((padded, lon_total))
    analysis[: 2 * MODES] = np.concatenate([np.cos(angles), np.sin(angles)], 0)
    lat = math.pi * ((np.arange(lat_total) + 0.5) / lat_total - 0.5)
    removal = 1.0 - np.exp(-DAMP * (k[None] / MODES) ** 2 / np.cos(lat)[:, None] ** 2)
    removal = removal * np.where(k == 0, 1.0, 2.0) / lon_total
    scale = np.zeros((lat_total, padded), np.float32)
    scale[:, : 2 * MODES] = np.concatenate([removal, removal], 1)
    high = analysis.astype(np.float32).astype(BF)
    low = (analysis - high.astype(np.float64)).astype(np.float32).astype(BF)
    return high, low, scale


def dot(a, b, dims=((1,), (0,))):
    return lax.dot_general(a, b, (dims, ((), ())), preferred_element_type=F32)


def split_dot(x, high, low, dims=((1,), (0,))):
    x_high = x.astype(BF)
    x_low = (x - x_high.astype(F32)).astype(BF)
    return dot(x_high, high, dims) + (dot(x_low, high, dims) + dot(x_high, low, dims))


def filtered(x, scale, high, low):
    coeffs = split_dot(x, high, low, ((1,), (1,))) * scale
    return x - split_dot(coeffs, high, low)


def joined(ref, start, rows):
    return jnp.concatenate([ref[s, start : start + rows, :] for s in range(ref.shape[0])], axis=1)


def store_split(ref, start, value):
    for s in range(ref.shape[0]):
        ref[s, start : start + value.shape[0], :] = value[:, s * LANES : (s + 1) * LANES].astype(
            ref.dtype
        )


def by_row_kernel(
    state_hbm, cotangent_hbm, land_hbm, orography_hbm, out_ref, adjoint_ref,
    state_ref, cotangent_ref, land_ref, orography_ref, sems, *, classes
):
    moves = [
        pltpu.make_async_copy(source, target, sems.at[i])
        for i, (source, target) in enumerate(
            (
                (state_hbm, state_ref),
                (cotangent_hbm, cotangent_ref),
                (land_hbm, land_ref),
                (orography_hbm, orography_ref),
            )
        )
    ]
    for move in moves:
        move.start()
    sectors, rows = out_ref.shape[:2]
    members = state_ref.shape[0]
    band = land_ref.shape[0]
    taken = band * members // sectors
    channels = rows // taken
    for source, target, move in ((state_ref, out_ref, 0), (cotangent_ref, adjoint_ref, 1)):
        moves[move].wait()
        for q in range(sectors):
            m, first = q * taken // band, q * taken % band
            for k in range(taken):
                target[q, k * channels : (k + 1) * channels, :] = source[
                    m, pl.ds(first + k, channels, stride=band), :
                ]
    moves[2].wait()
    moves[3].wait()
    code = (jnp.where(land_ref[...] == 1, classes, 0) + orography_ref[...]).astype(F32)
    for q in range(sectors):
        first = q * taken % band
        spare = jnp.zeros((8 - taken, LANES), F32)
        adjoint_ref[q, rows:, :] = jnp.concatenate([code[first : first + taken], spare], axis=0)


def own_scale(place, scale_ref, taken, sectors, band, rows):
    first = place // sectors * band + place % (band // taken) * taken
    channels = rows // taken
    wide = (channels, scale_ref.shape[1])
    return jnp.concatenate(
        [jnp.broadcast_to(scale_ref[pl.ds(first + k, 1), :], wide) for k in range(taken)], axis=0
    )


def rolled(value, shift):
    return pltpu.roll(value, shift % value.shape[1], 1) if shift else value


def early_kernel(
    place_ref,
    seeds_ref,
    row_ref,
    adjoint_ref,
    scale_ref,
    high_ref,
    low_ref,
    land_ref,
    relief_ref,
    seed_ref,
    w_hidden_ref,
    b_hidden_ref,
    w_tendency_ref,
    moist_grad_ref,
    features_ref,
    preact_ref,
    hidden_grad_ref,
    *,
    band,
):
    taken = features_ref.shape[0]
    sectors = row_ref.shape[0]
    channels, hidden_units = w_tendency_ref.shape
    rows = taken * channels
    lon_total = features_ref.shape[2]
    classes = relief_ref.shape[0]
    place = place_ref[0]
    scale = own_scale(place, scale_ref, taken, sectors, band, rows)
    moist_grad = filtered(joined(adjoint_ref, 0, rows), scale, high_ref[...], low_ref[...])
    moist_grad_ref[...] = moist_grad
    rounded = joined(row_ref, 0, rows).astype(BF).astype(F32)
    for j in range(-1, taken + 1):
        for b in range(3):
            if 0 <= j < taken:
                moved = rolled(rounded[j * channels : (j + 1) * channels], 1 - b).astype(BF)
            else:
                moved = jnp.zeros((channels, lon_total), BF)
            for a in range(3):
                if 0 <= j + 1 - a < taken:
                    start = (3 * a + b) * channels
                    features_ref[j + 1 - a, start : start + channels, :] = moved
    class_ids = lax.broadcasted_iota(jnp.int32, (2 * classes, lon_total), 0).astype(F32)
    codes = joined(adjoint_ref, rows, 8)
    surface = jnp.concatenate(
        [land_ref[0:1, :] + relief_ref[...], land_ref[1:2, :] + relief_ref[...]], axis=0
    )
    seed = seeds_ref[place % sectors * taken // band]
    table = (surface + seed_ref[pl.ds(seed, 1), :]).astype(BF)
    bias = jnp.transpose(jnp.broadcast_to(b_hidden_ref[...], (8, hidden_units)))[:, 0:1]
    for k in range(taken):
        pick = jnp.where(class_ids == codes[k : k + 1], 1.0, 0.0).astype(BF)
        features_ref[k, 9 * channels :, :] = dot(table, pick, ((0,), (0,))).astype(BF)
        preact_ref[k] = dot(w_hidden_ref[...], features_ref[k]) + bias
        tendency_grad = moist_grad[k * channels : (k + 1) * channels].astype(BF)
        hidden_grad_ref[k] = dot(w_tendency_ref[...], tendency_grad, ((0,), (0,)))


def weights_kernel(
    north_ref,
    south_ref,
    moist_grad_ref,
    early_ref,
    preact_ref,
    hidden_grad_ref,
    w_hidden_ref,
    hidden_ref,
    preact_grad_ref,
    weights_ref,
    features_ref,
    stage_ref,
):
    taken, in_channels, lon_total = features_ref.shape
    channels = north_ref.shape[1]
    hidden_units = w_hidden_ref.shape[0]
    group = 3 * channels
    grad_in = jnp.zeros((hidden_units, in_channels), F32)
    grad_out = jnp.zeros((channels, hidden_units), F32)
    grad_bias = jnp.zeros((16, hidden_units), F32)
    ones = jnp.ones((16, lon_total), BF)
    for k in range(taken):
        features_ref[k] = early_ref[k]
        preact = preact_ref[k]
        for ref, a, row in ((north_ref, 0, 0), (south_ref, 2, taken - 1)):
            if row == k:
                edge = joined(ref, 0, channels).astype(F32)
                halo = jnp.concatenate([rolled(edge, 1 - b).astype(BF) for b in range(3)], axis=0)
                features_ref[k, a * group : (a + 1) * group, :] = halo
                preact = preact + dot(w_hidden_ref[:, a * group : (a + 1) * group], halo)
        logistic = 1.0 / (1.0 + jnp.exp(-preact))
        hidden = (preact * logistic).astype(BF)
        slope = logistic * (1.0 + preact * (1.0 - logistic))
        preact_grad = (hidden_grad_ref[k] * slope).astype(BF)
        hidden_ref[k] = hidden
        preact_grad_ref[k] = preact_grad
        tendency_grad = moist_grad_ref[k * channels : (k + 1) * channels, :].astype(BF)
        grad_out += dot(tendency_grad, hidden, ((1,), (1,)))
        grad_in += dot(preact_grad, features_ref[k], ((1,), (1,)))
        grad_bias += dot(ones, preact_grad, ((1,), (1,)))

    bias_high = grad_bias[0:1].astype(BF).astype(F32)
    bias_low = grad_bias[0:1] - bias_high
    tiles = hidden_units // LANES
    shares, share_rows = weights_ref.shape[:2]
    filled = (grad_in.size + grad_out.size) // (LANES * shares)
    for p in range(shares):
        stage_ref[p, filled // 8 * 8 :, :] = jnp.zeros((share_rows - filled // 8 * 8, LANES), F32)
        start = 0
        for value in (grad_in, grad_out):
            count = value.shape[0] // shares
            for t in range(value.shape[1] // LANES):
                stage_ref[p, start : start + count, :] = value[
                    p * count : (p + 1) * count, t * LANES : (t + 1) * LANES
                ]
                start += count
        if p == 0:
            for half in (bias_high, bias_low):
                for t in range(tiles):
                    stage_ref[p, start : start + 1, :] = half[:, t * LANES : (t + 1) * LANES]
                    start += 1
        weights_ref[p] = stage_ref[p].astype(BF)


def fields_kernel(
    place_ref,
    row_ref,
    moist_grad_ref,
    scale_ref,
    high_ref,
    low_ref,
    hidden_ref,
    preact_grad_ref,
    w_hidden_ref,
    w_tendency_ref,
    to_north_ref,
    to_south_ref,
    next_ref,
    grad_ref,
    *,
    band,
):
    taken = hidden_ref.shape[0]
    sectors, rows = row_ref.shape[:2]
    channels = rows // taken
    w_stencil = w_hidden_ref[:, : 9 * channels]
    sums = []
    for k in range(taken):
        stencil_grad = dot(w_stencil, preact_grad_ref[k], ((0,), (0,)))
        sums.append([])
        for a in range(3):
            total = None
            for b in range(3):
                start = (3 * a + b) * channels
                piece = rolled(stencil_grad[start : start + channels], b - 1)
                total = piece if total is None else total + piece
            sums[k].append(total)
    store_split(to_north_ref, 0, sums[0][0])
    store_split(to_south_ref, 0, sums[-1][2])
    for k in range(taken):
        total = moist_grad_ref[k * channels : (k + 1) * channels, :] + sums[k][1]
        if k > 0:
            total = total + sums[k - 1][2]
        if k + 1 < taken:
            total = total + sums[k + 1][0]
        store_split(grad_ref, k * channels, total)
    tendency = [dot(w_tendency_ref[...], hidden_ref[k]) for k in range(taken)]
    moist = joined(row_ref, 0, rows) + jnp.concatenate(tendency, axis=0)
    scale = own_scale(place_ref[0], scale_ref, taken, sectors, band, rows)
    store_split(next_ref, 0, filtered(moist, scale, high_ref[...], low_ref[...]))


def outgoing_kernel(place_ref, next_ref, grad_ref, south_ref, north_ref, *refs):
    sends, blocks_ref = refs[:-1], refs[-1]
    sectors, rows = next_ref.shape[:2]
    channels = south_ref.shape[1]
    for s in range(sectors):
        blocks_ref[s, :rows, :] = next_ref[s]
        part = grad_ref[s]
        first = part[:channels] + north_ref[s].astype(F32)
        last = part[rows - channels :] + south_ref[s].astype(F32)
        inner = [part[channels : rows - channels]] if rows > 2 * channels else []
        blocks_ref[s, rows:, :] = jnp.concatenate([first] + inner + [last], axis=0).astype(BF)
    for t in range(sectors):
        sends[t][...] = blocks_ref[(place_ref[0] + t) % sectors]


def by_band_kernel(place_ref, *refs, band):
    blocks_ref = refs[-1]
    outs = refs[-3:-1]
    sectors, rows = blocks_ref.shape[0], blocks_ref.shape[1] // 2
    members = outs[0].shape[0]
    taken = band * members // sectors
    channels = rows // taken
    for t in range(sectors):
        blocks_ref[t] = refs[t][...].astype(F32)
    for q in range(sectors):
        t = (place_ref[0] + sectors - q) % sectors
        m, first = q * taken // band, q * taken % band
        for i in range(2):
            for k in range(taken):
                start = i * rows + k * channels
                outs[i][m, pl.ds(first + k, channels, stride=band), :] = blocks_ref[
                    t, start : start + channels, :
                ]


def summed(ref):
    total = ref[0].astype(F32)
    for p in range(1, ref.shape[0]):
        total = total + ref[p].astype(F32)
    return total


def near_sum_kernel(parts_ref, *refs):
    pieces_ref, sum_ref = refs[-2:]
    sum_ref[...] = summed(parts_ref)
    pieces, piece_rows = pieces_ref.shape[:2]
    for p in range(pieces):
        pieces_ref[p] = sum_ref[p * piece_rows : (p + 1) * piece_rows, :]


def sum_and_copy_kernel(parts_ref, *refs):
    copies_ref = refs[-1]
    total = summed(parts_ref).astype(BF)
    for p in range(copies_ref.shape[0]):
        copies_ref[p] = total


def spread_kernel(pieces_ref, shares_ref, sum_ref):
    pieces, piece_rows = pieces_ref.shape[:2]
    for p in range(pieces):
        sum_ref[p * piece_rows : (p + 1) * piece_rows, :] = pieces_ref[p].astype(F32)
    share = sum_ref[...].astype(BF)
    for p in range(shares_ref.shape[0]):
        shares_ref[p] = share


def unpack_kernel(shares_ref, grad_in_ref, grad_bias_ref, grad_out_ref, stage_ref, *, scaling):
    shares = shares_ref.shape[0]
    for p in range(shares):
        stage_ref[p] = shares_ref[p].astype(F32) * scaling
        start = 0
        for ref in (grad_in_ref, grad_out_ref):
            count = ref.shape[0] // shares
            for t in range(ref.shape[1] // LANES):
                ref[p * count : (p + 1) * count, t * LANES : (t + 1) * LANES] = stage_ref[
                    p, start : start + count, :
                ]
                start += count
        if p == 0:
            tiles = grad_bias_ref.shape[0] // LANES
            for t in range(tiles):
                both = stage_ref[p, start + t, :] + stage_ref[p, start + tiles + t, :]
                grad_bias_ref[t * LANES : (t + 1) * LANES] = both


def call(kernel, outs, inputs, smem=0, scratch=(), flops=0, vmem=8, inputs_in=pltpu.VMEM, **static):
    on_vmem = pl.BlockSpec(memory_space=pltpu.VMEM)
    on_input = pl.BlockSpec(memory_space=inputs_in)
    on_smem = pl.BlockSpec(memory_space=pltpu.SMEM)

    def body(*refs):
        kernel(*refs, **static)

    return pl.pallas_call(
        body,
        out_shape=outs,
        in_specs=[on_smem] * smem + [on_input] * (inputs - smem),
        out_specs=jax.tree.map(lambda _: on_vmem, outs),
        scratch_shapes=list(scratch),
        cost_estimate=pl.CostEstimate(flops=flops, bytes_accessed=1_000_000, transcendentals=0),
        compiler_params=pltpu.CompilerParams(vmem_limit_bytes=vmem * MIB),
    )


def exchange(x, axes):
    return lax.all_to_all(x, axes, 0, 0, tiled=True)


def on_device(
    column_state,
    cotangent,
    land_mask,
    orography,
    member_seeds,
    land_table,
    relief_table,
    seed_table,
    w_hidden,
    b_hidden,
    w_tendency,
):
    members, channels, band, lon_cols = column_state.shape
    hidden_units, in_channels = w_hidden.shape
    classes = relief_table.shape[0]
    sectors = lax.axis_size("lon")
    peers = lax.axis_size(PLACE)
    lat_total = band * (peers // sectors)
    lon_total = lon_cols * sectors
    taken = band * members // sectors
    groups = band // taken
    rows = taken * channels
    shape = jax.ShapeDtypeStruct

    with jax.named_scope("rows_in"):
        flat = (members, channels * band, lon_cols)
        state_rows, adjoint_rows = call(
            by_row_kernel,
            (shape((sectors, rows, lon_cols), F32), shape((sectors, rows + 8, lon_cols), F32)),
            4,
            scratch=[
                pltpu.VMEM(flat, F32),
                pltpu.VMEM(flat, F32),
                pltpu.VMEM(land_mask.shape, land_mask.dtype),
                pltpu.VMEM(orography.shape, orography.dtype),
                pltpu.SemaphoreType.DMA((4,)),
            ],
            inputs_in=pltpu.HBM,
            classes=classes,
        )(column_state.reshape(flat), cotangent.reshape(flat), land_mask, orography)
        row = exchange(state_rows, "lon")
        adjoint_row = exchange(adjoint_rows, "lon")

    with jax.named_scope("row_halo"):
        south_going = []
        for i in range(peers):
            j = i + 1 if i % groups < groups - 1 else i + sectors - (groups - 1)
            if j < peers:
                south_going.append((i, j))
        north_going = [(j, i) for i, j in south_going]
        north = lax.ppermute(row[:, rows - channels :].astype(BF), PLACE, south_going)
        south = lax.ppermute(row[:, :channels].astype(BF), PLACE, north_going)

    place = lax.axis_index(PLACE).reshape(1)
    high, low, scale = [jnp.asarray(t) for t in filter_tables(lat_total, lon_total)]
    per_hidden = shape((taken, hidden_units, lon_total), F32)
    per_hidden_bf = shape((taken, hidden_units, lon_total), BF)
    features_shape = (taken, in_channels, lon_total)
    with jax.named_scope("early"):
        moist_grad, features, preact, hidden_grad = call(
            early_kernel,
            (shape((rows, lon_total), F32), shape(features_shape, BF), per_hidden, per_hidden),
            13,
            smem=2,
            flops=3_000_000_000,
            vmem=24,
            band=band,
        )(
            place,
            member_seeds,
            row,
            adjoint_row,
            scale,
            high,
            low,
            land_table,
            relief_table,
            seed_table,
            w_hidden,
            b_hidden.reshape(1, hidden_units),
            w_tendency,
        )

    near = lax.axis_size(NEAR)
    length = lax.axis_size("z")
    filled = (hidden_units * in_channels + channels * hidden_units) // (LANES * near)
    share_rows = whole_multiple(filled + BIAS_ROWS, 16)
    piece_rows = share_rows // sectors
    with jax.named_scope("weights"):
        hidden, preact_grad, weights = call(
            weights_kernel,
            (per_hidden_bf, per_hidden_bf, shape((near, share_rows, LANES), BF)),
            7,
            scratch=[
                pltpu.VMEM(features_shape, BF),
                pltpu.VMEM((near, share_rows, LANES), F32),
            ],
            flops=3_000_000_000,
            vmem=28,
        )(north, south, moist_grad, features, preact, hidden_grad, w_hidden)

    with jax.named_scope("fields"):
        block = (sectors, rows, LANES)
        edge = (sectors, channels, LANES)
        to_north, to_south, next_rows, grad_rows = call(
            fields_kernel,
            (shape(edge, BF), shape(edge, BF), shape(block, BF), shape(block, F32)),
            10,
            smem=1,
            flops=3_000_000_000,
            vmem=20,
            band=band,
        )(
            place,
            row,
            moist_grad,
            scale,
            high,
            low,
            hidden,
            preact_grad,
            w_hidden,
            w_tendency,
        )
        from_south = lax.ppermute(to_north, PLACE, north_going)
        from_north = lax.ppermute(to_south, PLACE, south_going)

    with jax.named_scope("weights_near"):
        parts = exchange(weights, NEAR)
        share = call(
            near_sum_kernel,
            shape((sectors, piece_rows, LANES), F32),
            3,
            scratch=[pltpu.VMEM((share_rows, LANES), F32)],
        )(parts, from_south, from_north)

    with jax.named_scope("rows_out"):
        sends = call(
            outgoing_kernel,
            (shape((2 * rows, LANES), BF),) * sectors,
            5,
            smem=1,
            scratch=[pltpu.VMEM((sectors, 2 * rows, LANES), BF)],
        )(place, next_rows, grad_rows, from_south, from_north)
        received = [sends[0]]
        for t in range(1, sectors):
            turn = [(i, (i + t) % sectors) for i in range(sectors)]
            received.append(lax.ppermute(sends[t], "lon", turn))
    with jax.named_scope("weights_middle"):
        copies = call(sum_and_copy_kernel, shape((length, piece_rows, LANES), BF), 2)(
            exchange(share, "lon"), received[1]
        )

    with jax.named_scope("weights_length"):
        copies = call(sum_and_copy_kernel, shape((sectors, piece_rows, LANES), BF), sectors - 1)(
            exchange(copies, "z"), *received[2:]
        )

    with jax.named_scope("bands_out"):
        next_state, state_grad = call(
            by_band_kernel,
            (shape(flat, F32), shape(flat, F32)),
            1 + sectors,
            smem=1,
            scratch=[pltpu.VMEM((sectors, 2 * rows, LANES), F32)],
            band=band,
        )(place, *received)
        next_state = next_state.reshape(column_state.shape)
        state_grad = state_grad.reshape(column_state.shape)

    with jax.named_scope("weights_back"):
        pieces = exchange(copies, "lon")
        spread = call(
            spread_kernel,
            shape((near, share_rows, LANES), BF),
            1,
            scratch=[pltpu.VMEM((share_rows, LANES), F32)],
        )(pieces)
        shares = exchange(spread, NEAR)
        columns = members * lax.axis_size("mem") * lat_total * lon_total
        grad_in, grad_bias, grad_out = call(
            unpack_kernel,
            (
                shape((hidden_units, in_channels), F32),
                shape((hidden_units,), F32),
                shape((channels, hidden_units), F32),
            ),
            1,
            scratch=[pltpu.VMEM((near, share_rows, LANES), F32)],
            scaling=1.0 / math.sqrt(columns),
        )(shares)
    return next_state, state_grad, grad_in, grad_bias, grad_out


def solution(mesh):
    lat, lon, mem = mesh.devices.shape
    devices = mesh.devices.reshape(2, lat // 4, 2, lon, mem)
    split = Mesh(devices, ("ylo", "z", "core", "lon", "mem"))
    lat_axes = ("ylo", "z", "core")
    field = P("mem", None, lat_axes, "lon")
    surface = P(lat_axes, "lon")
    whole = P()
    return jax.shard_map(
        on_device,
        mesh=split,
        in_specs=(field, field, surface, surface, P("mem")) + (whole,) * 6,
        out_specs=(field, field, whole, whole, whole),
        check_vma=False,
    )
```

time: 138 us -> 143 us (1.036)
  blocking collectives: 65.3 us -> 26.7 us
  starting transfers between devices: 42.3 us -> 72.5 us
  waiting for transfers between devices: 14.3 us -> 22 us
  Pallas kernels: 9.04 us -> 12.3 us
  local copies, waits for them, and re-layouts: 5.18 us -> 7.38 us
    all_to_all x4 -> x2, blocking collectives: 65.3 us -> 26.7 us  [exchange(): return lax.all_to_all(x, axes, 0, 0, tiled=True)]
    all_to_all x3 -> x5, starting transfers between devices: 24.2 us -> 41.5 us  [exchange(): return lax.all_to_all(x, axes, 0, 0, tiled=True)]
    ppermute x0 -> x3, starting transfers between devices: none -> 13.1 us  [on_device(): received.append(lax.ppermute(sends[t], 'lon', turn))]
    ppermute x0 -> x3, waiting for transfers between devices: none -> 8.09 us  [on_device(): received.append(lax.ppermute(sends[t], 'lon', turn))]
    unnamed x28 -> x36, local copies, waits for them, and re-layouts: 3.31 us -> 7.37 us
    pallas_call x3 -> x8, Pallas kernels: 6.34 us -> 9.49 us  [the longest x1 2.74 us: on_device(): call(weights_kernel, (per_hidden_bf, per_hidden_bf, shape((near, share_ro...]
    ppermute x1, waiting for transfers between devices: 3 us -> 0.23 us  [on_device(): from_south = lax.ppermute(to_north, PLACE, north_going)]
    ppermute x1, starting transfers between devices: 4.4 us -> 1.92 us  [on_device(): lax.ppermute(row[:, rows - channels:].astype(BF), PLACE, south_going)]
  transfers between devices with their start and end apart: 7 -> 12, of which waited for: 6 -> 7; matrix products, arithmetic and copies ran while one was open for 1% -> 0% of each run, Pallas kernels for 1% -> 4%
where the time goes in v4:
time: 143 us; the launch traced here: 142 us
  starting transfers between devices  72.5 us (51%)
  blocking collectives  26.7 us (19%)
  waiting for transfers between devices  22 us (15%)
  Pallas kernels  12.3 us (9%)
  local copies, waits for them, and re-layouts  7.38 us (5%)
    all_to_all x5, starting transfers between devices, exchange(): return lax.all_to_all(x, axes, 0, 0, tiled=True)  41.5 us
    all_to_all x2, blocking collectives, exchange(): return lax.all_to_all(x, axes, 0, 0, tiled=True)  26.7 us
    ppermute x3, starting transfers between devices, on_device(): received.append(lax.ppermute(sends[t], 'lon', turn))  13.1 us
    ppermute x1, starting transfers between devices, on_device(): south = lax.ppermute(row[:, :channels].astype(BF), PLACE, north_going)  9.81 us
    all_to_all x5, waiting for transfers between devices, exchange(): return lax.all_to_all(x, axes, 0, 0, tiled=True)  9.36 us
    ppermute x3, waiting for transfers between devices, on_device(): received.append(lax.ppermute(sends[t], 'lon', turn))  8.09 us
    unnamed x36, local copies, waits for them, and re-layouts  7.37 us
    ppermute x1, starting transfers between devices, on_device(): from_north = lax.ppermute(to_south, PLACE, south_going)  4.28 us
  transfers between devices with their start and end apart: 12, of which 7 were waited for; matrix products, arithmetic and copies ran while one was open for 0% of the time, Pallas kernels for 4%

profile of v4, /device:TPU:1, one launch (start us, length us, event | category | flops | bytes accessed | tf_op | source)
XLA Modules:
  0.0 141.8 jit_solution(12137036358547084305)
XLA Ops:
  0.6 0.0 copy-start.17
  0.6 0.0 copy-start.8
  0.7 0.0 copy-start.9
  0.7 0.0 copy-start
  0.7 1.0 copy-done
  1.6 0.0 copy-start.1
  1.6 0.9 copy-done.1
  2.6 0.0 copy-start.2
  2.6 0.7 copy-done.2
  3.3 0.0 copy-start.3
  3.3 0.7 copy-done.3
  3.9 0.0 copy-start.4
  4.0 0.0 copy-start.10
  4.0 0.0 copy-start.11
  4.0 0.0 copy-start.12
  4.0 0.8 rows_in.1
  4.8 16.4 %all_to_all.35.refs_2_.refs_1_ = f32[4,128,128]{2,1,0:T(8,128)S(1)} all-to-all(f32[4,128,128]{2,1,0:T(8,128)S(1)} %get-tuple-element.27), channel_id=1, replica_groups=mesh['ylo'=2,'z'=12,'core'=2,'lon'=4,'mem'=4] {'lon'}, dimensions={0} | all-to-all | bytes 524288 | tf_op jit(solution)/shard_map/rows_in/all_to_all | solution.py:396
  21.3 4.3 %all-to-all-start.1 = ((f32[4,136,128]{2,1,0:T(8,128)}), f32[4,136,128]{2,1,0:T(8,128)S(1)}, u32[]{:S(2)}, u32[]{:S(2)}) async-start(f32[4,136,128]{2,1,0:T(8,128)} %get-tuple-element.28), calls=%async_computation.1 | async-start | bytes 557056 | tf_op jit(solution)/shard_map/rows_in/all_to_all | solution.py:396
  25.6 0.0 copy-done.17
  25.6 9.8 %collective-permute-start.1 = (bf16[4,64,128]{2,1,0:T(8,128)(2,1)S(1)}, bf16[4,64,128]{2,1,0:T(8,128)(2,1)S(1)}, u32[]{:S(2)}, u32[]{:S(2)}) collective-permute-start(bf16[4,64,128]{2,1,0:T(8,128)(2,1)S(1)} %get-tuple-element.49), channel_id=1, source_target_pairs={{4,0},{16,4},{12,8},{24,12},{20,16},{32,20},{28,24},{40,28},{36,32... | collective-permute-start | bytes 196616 | tf_op jit(solution)/shard_map/row_halo/ppermute | solution.py:451
  35.4 1.9 %collective-permute-start = (bf16[4,64,128]{2,1,0:T(8,128)(2,1)S(1)}, bf16[4,64,128]{2,1,0:T(8,128)(2,1)S(1)}, u32[]{:S(2)}, u32[]{:S(2)}) collective-permute-start(bf16[4,64,128]{2,1,0:T(8,128)(2,1)S(1)} %get-tuple-element.50), channel_id=1, source_target_pairs={{0,4},{4,16},{8,12},{12,24},{16,20},{20,32},{24,28},{28,40},{32,36... | collective-permute-start | bytes 196616 | tf_op jit(solution)/shard_map/row_halo/ppermute | solution.py:450
  37.4 0.0 all-to-all-done.1.refs_3_
  37.4 0.0 copy-done.8
  37.4 0.0 copy-done.9
  37.4 0.0 copy-done.4
  37.4 0.0 copy-done.5
  37.4 0.0 copy-done.6
  37.4 0.0 copy-done.7
  37.4 0.0 copy-done.10
  37.4 0.0 copy-done.11
  37.5 0.0 copy-done.12
  37.5 2.5 %early.1 = (f32[128,512]{1,0:T(8,128)S(1)}, bf16[2,640,512]{2,1,0:T(8,128)(2,1)S(1)}, f32[2,384,512]{2,1,0:T(8,128)S(1)}, f32[2,384,512]{2,1,0:T(8,128)S(1)}) custom-call(s32[1]{0:T(128)} %bitcast.refs_0_, s32[2]{0:T(128)S(1)} %copy-done.9, f32[4,128,128]{2,1,0:T(8,128)S(1)} %all_to_all.35.refs_2_.refs_1_, f32[4,136,128]{2,1,0:T(8,128)S(1)} %all-to-all-done.1.refs_3_, ...), custom_call_target="tpu_custom_call" | custom-call | flops 3000000000 | bytes 1000000 | tf_op jit(solution)/shard_map/early/pallas_call | solution.py:459
  39.9 0.0 collective-permute-done.1.refs_1_
  39.9 2.0 %collective-permute-done.refs_0_ = bf16[4,64,128]{2,1,0:T(8,128)(2,1)S(1)} collective-permute-done((bf16[4,64,128]{2,1,0:T(8,128)(2,1)S(1)}, bf16[4,64,128]{2,1,0:T(8,128)(2,1)S(1)}, u32[]{:S(2)}, u32[]{:S(2)}) %collective-permute-start) | collective-permute-done | bytes 65568 | tf_op jit(solution)/shard_map/row_halo/ppermute | solution.py:450
  41.9 2.7 %weights.1 = (bf16[2,384,512]{2,1,0:T(8,128)(2,1)S(1)}, bf16[2,384,512]{2,1,0:T(8,128)(2,1)S(1)}, bf16[16,144,128]{2,1,0:T(8,128)(2,1)}) custom-call(bf16[4,64,128]{2,1,0:T(8,128)(2,1)S(1)} %collective-permute-done.refs_0_, bf16[4,64,128]{2,1,0:T(8,128)(2,1)S(1)} %collective-permute-done.1.refs_1_, f32[128,512]{1,0:T(8,128)S(1)} %get-tuple-element.29.refs_2_, ...), custom_call_target="tpu_custom_call" | custom-call | flops 3000000000 | bytes 1000000 | tf_op jit(solution)/shard_map/weights/pallas_call | solution.py:489
  44.7 0.9 copy-done.13
  45.6 0.9 copy-done.15
  46.5 12.7 %all-to-all-start.2 = ((bf16[16,144,128]{2,1,0:T(8,128)(2,1)}), bf16[16,144,128]{2,1,0:T(8,128)(2,1)S(1)}, u32[]{:S(2)}, u32[]{:S(2)}) async-start(bf16[16,144,128]{2,1,0:T(8,128)(2,1)} %get-tuple-element.45), calls=%async_computation.2 | async-start | bytes 1179648 | tf_op jit(solution)/shard_map/weights_near/all_to_all | solution.py:396
  59.2 1.1 copy-done.14
  60.3 1.1 copy-done.16
  61.5 2.0 %fields.1 = (bf16[4,64,128]{2,1,0:T(8,128)(2,1)S(1)}, bf16[4,64,128]{2,1,0:T(8,128)(2,1)S(1)}, bf16[4,128,128]{2,1,0:T(8,128)(2,1)S(1)}, f32[4,128,128]{2,1,0:T(8,128)S(1)}) custom-call(s32[1]{0:T(128)} %bitcast.refs_0_, f32[4,128,128]{2,1,0:T(8,128)S(1)} %all_to_all.35.refs_2_.refs_1_, f32[128,512]{1,0:T(8,128)S(1)} %get-tuple-element.29.refs_2_, ...), custom_call_target="tpu_custom_call" | custom-call | flops 3000000000 | bytes 1000000 | tf_op jit(solution)/shard_map/fields/pallas_call | solution.py:504
  63.4 1.9 %collective-permute-start.2 = (bf16[4,64,128]{2,1,0:T(8,128)(2,1)S(1)}, bf16[4,64,128]{2,1,0:T(8,128)(2,1)S(1)}, u32[]{:S(2)}, u32[]{:S(2)}) collective-permute-start(bf16[4,64,128]{2,1,0:T(8,128)(2,1)S(1)} %get-tuple-element.37), channel_id=1, source_target_pairs={{4,0},{16,4},{12,8},{24,12},{20,16},{32,20},{28,24},{40,28},{36,32... | collective-permute-start | bytes 196616 | tf_op jit(solution)/shard_map/fields/ppermute | solution.py:524
  65.4 4.3 %collective-permute-start.3 = (bf16[4,64,128]{2,1,0:T(8,128)(2,1)S(1)}, bf16[4,64,128]{2,1,0:T(8,128)(2,1)S(1)}, u32[]{:S(2)}, u32[]{:S(2)}) collective-permute-start(bf16[4,64,128]{2,1,0:T(8,128)(2,1)S(1)} %get-tuple-element.38), channel_id=1, source_target_pairs={{0,4},{4,16},{8,12},{12,24},{16,20},{20,32},{24,28},{28,40},{32,36... | collective-permute-start | bytes 196616 | tf_op jit(solution)/shard_map/fields/ppermute | solution.py:525
  69.7 0.2 collective-permute-done.2.refs_3_.refs_1_
  69.9 2.3 %collective-permute-done.3.refs_4_.refs_2_ = bf16[4,64,128]{2,1,0:T(8,128)(2,1)S(1)} collective-permute-done((bf16[4,64,128]{2,1,0:T(8,128)(2,1)S(1)}, bf16[4,64,128]{2,1,0:T(8,128)(2,1)S(1)}, u32[]{:S(2)}, u32[]{:S(2)}) %collective-permute-start.3) | collective-permute-done | bytes 65568 | tf_op jit(solution)/shard_map/fields/ppermute | solution.py:525
  72.2 0.0 all-to-all-done.2.refs_0_
  72.2 0.7 weights_near.1
  72.9 4.6 %all-to-all-start.3 = ((f32[4,36,128]{2,1,0:T(8,128)}), f32[4,36,128]{2,1,0:T(8,128)S(1)}, u32[]{:S(2)}, u32[]{:S(2)}) async-start(f32[4,36,128]{2,1,0:T(8,128)} %weights_near.1), calls=%async_computation.3 | async-start | bytes 163840 | tf_op jit(solution)/shard_map/weights_middle/all_to_all | solution.py:396
  77.5 4.3 %collective-permute-start.4 = (bf16[256,128]{1,0:T(8,128)(2,1)S(1)}, bf16[256,128]{1,0:T(8,128)(2,1)S(1)}, u32[]{:S(2)}, u32[]{:S(2)}) collective-permute-start(bf16[256,128]{1,0:T(8,128)(2,1)S(1)} %get-tuple-element.40), channel_id=1, source_target_pairs={{0,4},{4,8},{8,12},{12,0},{1,5},{5,9},{9,13},{13,1},{2,6},{6,10},{... | collective-permute-start | bytes 196616 | tf_op jit(solution)/shard_map/rows_out/ppermute | solution.py:547
  81.8 3.6 %collective-permute-done.4.refs_2_.refs_1_ = bf16[256,128]{1,0:T(8,128)(2,1)S(1)} collective-permute-done((bf16[256,128]{1,0:T(8,128)(2,1)S(1)}, bf16[256,128]{1,0:T(8,128)(2,1)S(1)}, u32[]{:S(2)}, u32[]{:S(2)}) %collective-permute-start.4) | collective-permute-done | bytes 65568 | tf_op jit(solution)/shard_map/rows_out/ppermute | solution.py:547
  85.4 0.0 all-to-all-done.3.refs_0_
  85.4 0.7 weights_middle.1
  86.1 10.4 %all-to-all-start.4 = ((bf16[12,36,128]{2,1,0:T(8,128)(2,1)}), bf16[12,36,128]{2,1,0:T(8,128)(2,1)S(1)}, u32[]{:S(2)}, u32[]{:S(2)}) async-start(bf16[12,36,128]{2,1,0:T(8,128)(2,1)} %weights_middle.1), calls=%async_computation.4 | async-start | bytes 245760 | tf_op jit(solution)/shard_map/weights_length/all_to_all | solution.py:396
  96.5 6.9 %collective-permute-start.5 = (bf16[256,128]{1,0:T(8,128)(2,1)S(1)}, bf16[256,128]{1,0:T(8,128)(2,1)S(1)}, u32[]{:S(2)}, u32[]{:S(2)}) collective-permute-start(bf16[256,128]{1,0:T(8,128)(2,1)S(1)} %get-tuple-element.41), channel_id=1, source_target_pairs={{0,8},{4,12},{8,0},{12,4},{1,9},{5,13},{9,1},{13,5},{2,10},{6,14},... | collective-permute-start | bytes 196616 | tf_op jit(solution)/shard_map/rows_out/ppermute | solution.py:547
  103.4 1.9 %collective-permute-start.6 = (bf16[256,128]{1,0:T(8,128)(2,1)S(1)}, bf16[256,128]{1,0:T(8,128)(2,1)S(1)}, u32[]{:S(2)}, u32[]{:S(2)}) collective-permute-start(bf16[256,128]{1,0:T(8,128)(2,1)S(1)} %get-tuple-element.42), channel_id=1, source_target_pairs={{0,12},{4,0},{8,4},{12,8},{1,13},{5,1},{9,5},{13,9},{2,14},{6,2},{... | collective-permute-start | bytes 196616 | tf_op jit(solution)/shard_map/rows_out/ppermute | solution.py:547
  105.3 0.4 collective-permute-done.5.refs_3_.refs_1_
  105.7 4.1 %collective-permute-done.6.refs_4_.refs_2_ = bf16[256,128]{1,0:T(8,128)(2,1)S(1)} collective-permute-done((bf16[256,128]{1,0:T(8,128)(2,1)S(1)}, bf16[256,128]{1,0:T(8,128)(2,1)S(1)}, u32[]{:S(2)}, u32[]{:S(2)}) %collective-permute-start.6) | collective-permute-done | bytes 65568 | tf_op jit(solution)/shard_map/rows_out/ppermute | solution.py:547
  109.8 0.0 all-to-all-done.4.refs_0_
  109.8 10.3 %all_to_all.36.refs_0_ = bf16[4,36,128]{2,1,0:T(8,128)(2,1)S(1)} all-to-all(bf16[4,36,128]{2,1,0:T(8,128)(2,1)S(1)} %weights_length.1), channel_id=1, replica_groups=mesh['ylo'=2,'z'=12,'core'=2,'lon'=4,'mem'=4] {'lon'}, dimensions={0} | all-to-all | bytes 73728 | tf_op jit(solution)/shard_map/weights_back/all_to_all | solution.py:396
  120.1 0.9 weights_back.2
  120.9 9.5 %all-to-all-start.6 = ((bf16[16,144,128]{2,1,0:T(8,128)(2,1)}), bf16[16,144,128]{2,1,0:T(8,128)(2,1)S(1)}, u32[]{:S(2)}, u32[]{:S(2)}) async-start(bf16[16,144,128]{2,1,0:T(8,128)(2,1)} %weights_back.2), calls=%async_computation.6 | async-start | bytes 1179648 | tf_op jit(solution)/shard_map/weights_back/all_to_all | solution.py:396
  130.5 0.9 bands_out.1
  131.3 9.3 %all-to-all-done.6.refs_0_ = bf16[16,144,128]{2,1,0:T(8,128)(2,1)S(1)} async-done(((bf16[16,144,128]{2,1,0:T(8,128)(2,1)}), bf16[16,144,128]{2,1,0:T(8,128)(2,1)S(1)}, u32[]{:S(2)}, u32[]{:S(2)}) %all-to-all-start.6) | async-done | bytes 589856 | tf_op jit(solution)/shard_map/weights_back/all_to_all | solution.py:396
  140.7 1.1 weights_back.3
  (12 shorter events, 0.1 us)
Async XLA Ops:
  0.6 24.9 %copy-start.17 = (f32[384]{0:T(512)S(1)}, f32[384]{0:T(512)}, u32[]{:S(2)}) copy-start(f32[384]{0:T(512)} %param.23) | copy-start | bytes 4612
  0.6 36.7 %copy-start.8 = (f32[2,64]{1,0:T(2,128)S(1)}, f32[2,64]{1,0:T(2,128)}, u32[]{:S(2)}) copy-start(f32[2,64]{1,0:T(2,128)} %refs_7_.1) | copy-start | bytes 1540
  0.7 36.7 %copy-start.9 = (s32[2]{0:T(128)S(1)}, s32[2]{0:T(128)}, u32[]{:S(2)}) copy-start(s32[2]{0:T(128)} %refs_1_.1) | copy-start | bytes 28
  0.7 1.0 copy-start
  1.6 0.9 copy-start.1
  2.6 0.7 copy-start.2
  3.3 0.7 copy-start.3
  3.9 33.4 %copy-start.4 = (bf16[384,640]{1,0:T(8,128)(2,1)S(1)}, bf16[384,640]{1,0:T(8,128)(2,1)}, u32[]{:S(2)}) copy-start(bf16[384,640]{1,0:T(8,128)(2,1)} %refs_8_.3) | copy-start | bytes 1474564
  4.0 33.5 %copy-start.5 = (bf16[64,384]{1,0:T(8,128)(2,1)S(1)}, bf16[64,384]{1,0:T(8,128)(2,1)}, u32[]{:S(2)}) copy-start(bf16[64,384]{1,0:T(8,128)(2,1)} %refs_9_.3) | copy-start | bytes 147460
  4.0 33.5 %copy-start.6 = (f32[32,64]{1,0:T(8,128)S(1)}, f32[32,64]{1,0:T(8,128)}, u32[]{:S(2)}) copy-start(f32[32,64]{1,0:T(8,128)} %refs_9_.2) | copy-start | bytes 24580
  4.0 33.5 %copy-start.7 = (f32[16,64]{1,0:T(8,128)S(1)}, f32[16,64]{1,0:T(8,128)}, u32[]{:S(2)}) copy-start(f32[16,64]{1,0:T(8,128)} %refs_8_.2) | copy-start | bytes 12292
  4.0 33.5 %copy-start.10 = (bf16[384,512]{1,0:T(8,128)(2,1)S(1)}, bf16[384,512]{1,0:T(8,128)(2,1)}, u32[]{:S(2)}) copy-start(bf16[384,512]{1,0:T(8,128)(2,1)} %constant.32.clone.refs_6_.refs_5_) | copy-start | bytes 1179652
  4.0 33.5 %copy-start.11 = (bf16[384,512]{1,0:T(8,128)(2,1)S(1)}, bf16[384,512]{1,0:T(8,128)(2,1)}, u32[]{:S(2)}) copy-start(bf16[384,512]{1,0:T(8,128)(2,1)} %constant.31.clone.refs_5_.refs_4_) | copy-start | bytes 1179652
  4.0 33.5 %copy-start.12 = (f32[192,384]{1,0:T(8,128)S(1)}, f32[192,384]{1,0:T(8,128)}, u32[]{:S(2)}) copy-start(f32[192,384]{1,0:T(8,128)} %constant.33.clone.refs_4_.refs_3_) | copy-start | bytes 884740
  21.3 16.1 %all-to-all-start.1 = ((f32[4,136,128]{2,1,0:T(8,128)}), f32[4,136,128]{2,1,0:T(8,128)S(1)}, u32[]{:S(2)}, u32[]{:S(2)}) async-start(f32[4,136,128]{2,1,0:T(8,128)} %get-tuple-element.28), calls=%async_computation.1 | async-start | bytes 557056 | tf_op jit(solution)/shard_map/rows_in/all_to_all | solution.py:396
  25.6 14.3 %collective-permute-start.1 = (bf16[4,64,128]{2,1,0:T(8,128)(2,1)S(1)}, bf16[4,64,128]{2,1,0:T(8,128)(2,1)S(1)}, u32[]{:S(2)}, u32[]{:S(2)}) collective-permute-start(bf16[4,64,128]{2,1,0:T(8,128)(2,1)S(1)} %get-tuple-element.49), channel_id=1, source_target_pairs={{4,0},{16,4},{12,8},{24,12},{20,16},{32,20},{28,24},{40,28},{36,32... | collective-permute-start | bytes 196616 | tf_op jit(solution)/shard_map/row_halo/ppermute | solution.py:451
  35.4 6.5 %collective-permute-start = (bf16[4,64,128]{2,1,0:T(8,128)(2,1)S(1)}, bf16[4,64,128]{2,1,0:T(8,128)(2,1)S(1)}, u32[]{:S(2)}, u32[]{:S(2)}) collective-permute-start(bf16[4,64,128]{2,1,0:T(8,128)(2,1)S(1)} %get-tuple-element.50), channel_id=1, source_target_pairs={{0,4},{4,16},{8,12},{12,24},{16,20},{20,32},{24,28},{28,40},{32,36... | collective-permute-start | bytes 196616 | tf_op jit(solution)/shard_map/row_halo/ppermute | solution.py:450
  44.7 0.9 copy-start.13
  45.6 0.9 copy-start.15
  46.5 25.7 %all-to-all-start.2 = ((bf16[16,144,128]{2,1,0:T(8,128)(2,1)}), bf16[16,144,128]{2,1,0:T(8,128)(2,1)S(1)}, u32[]{:S(2)}, u32[]{:S(2)}) async-start(bf16[16,144,128]{2,1,0:T(8,128)(2,1)} %get-tuple-element.45), calls=%async_computation.2 | async-start | bytes 1179648 | tf_op jit(solution)/shard_map/weights_near/all_to_all | solution.py:396
  59.2 1.1 copy-start.14
  60.3 1.1 copy-start.16
  63.4 6.4 %collective-permute-start.2 = (bf16[4,64,128]{2,1,0:T(8,128)(2,1)S(1)}, bf16[4,64,128]{2,1,0:T(8,128)(2,1)S(1)}, u32[]{:S(2)}, u32[]{:S(2)}) collective-permute-start(bf16[4,64,128]{2,1,0:T(8,128)(2,1)S(1)} %get-tuple-element.37), channel_id=1, source_target_pairs={{4,0},{16,4},{12,8},{24,12},{20,16},{32,20},{28,24},{40,28},{36,32... | collective-permute-start | bytes 196616 | tf_op jit(solution)/shard_map/fields/ppermute | solution.py:524
  65.4 6.8 %collective-permute-start.3 = (bf16[4,64,128]{2,1,0:T(8,128)(2,1)S(1)}, bf16[4,64,128]{2,1,0:T(8,128)(2,1)S(1)}, u32[]{:S(2)}, u32[]{:S(2)}) collective-permute-start(bf16[4,64,128]{2,1,0:T(8,128)(2,1)S(1)} %get-tuple-element.38), channel_id=1, source_target_pairs={{0,4},{4,16},{8,12},{12,24},{16,20},{20,32},{24,28},{28,40},{32,36... | collective-permute-start | bytes 196616 | tf_op jit(solution)/shard_map/fields/ppermute | solution.py:525
  72.9 12.5 %all-to-all-start.3 = ((f32[4,36,128]{2,1,0:T(8,128)}), f32[4,36,128]{2,1,0:T(8,128)S(1)}, u32[]{:S(2)}, u32[]{:S(2)}) async-start(f32[4,36,128]{2,1,0:T(8,128)} %weights_near.1), calls=%async_computation.3 | async-start | bytes 163840 | tf_op jit(solution)/shard_map/weights_middle/all_to_all | solution.py:396
  77.5 7.9 %collective-permute-start.4 = (bf16[256,128]{1,0:T(8,128)(2,1)S(1)}, bf16[256,128]{1,0:T(8,128)(2,1)S(1)}, u32[]{:S(2)}, u32[]{:S(2)}) collective-permute-start(bf16[256,128]{1,0:T(8,128)(2,1)S(1)} %get-tuple-element.40), channel_id=1, source_target_pairs={{0,4},{4,8},{8,12},{12,0},{1,5},{5,9},{9,13},{13,1},{2,6},{6,10},{... | collective-permute-start | bytes 196616 | tf_op jit(solution)/shard_map/rows_out/ppermute | solution.py:547
  86.1 23.7 %all-to-all-start.4 = ((bf16[12,36,128]{2,1,0:T(8,128)(2,1)}), bf16[12,36,128]{2,1,0:T(8,128)(2,1)S(1)}, u32[]{:S(2)}, u32[]{:S(2)}) async-start(bf16[12,36,128]{2,1,0:T(8,128)(2,1)} %weights_middle.1), calls=%async_computation.4 | async-start | bytes 245760 | tf_op jit(solution)/shard_map/weights_length/all_to_all | solution.py:396
  96.5 9.2 %collective-permute-start.5 = (bf16[256,128]{1,0:T(8,128)(2,1)S(1)}, bf16[256,128]{1,0:T(8,128)(2,1)S(1)}, u32[]{:S(2)}, u32[]{:S(2)}) collective-permute-start(bf16[256,128]{1,0:T(8,128)(2,1)S(1)} %get-tuple-element.41), channel_id=1, source_target_pairs={{0,8},{4,12},{8,0},{12,4},{1,9},{5,13},{9,1},{13,5},{2,10},{6,14},... | collective-permute-start | bytes 196616 | tf_op jit(solution)/shard_map/rows_out/ppermute | solution.py:547
  103.4 6.4 %collective-permute-start.6 = (bf16[256,128]{1,0:T(8,128)(2,1)S(1)}, bf16[256,128]{1,0:T(8,128)(2,1)S(1)}, u32[]{:S(2)}, u32[]{:S(2)}) collective-permute-start(bf16[256,128]{1,0:T(8,128)(2,1)S(1)} %get-tuple-element.42), channel_id=1, source_target_pairs={{0,12},{4,0},{8,4},{12,8},{1,13},{5,1},{9,5},{13,9},{2,14},{6,2},{... | collective-permute-start | bytes 196616 | tf_op jit(solution)/shard_map/rows_out/ppermute | solution.py:547
  120.9 19.7 %all-to-all-start.6 = ((bf16[16,144,128]{2,1,0:T(8,128)(2,1)}), bf16[16,144,128]{2,1,0:T(8,128)(2,1)S(1)}, u32[]{:S(2)}, u32[]{:S(2)}) async-start(bf16[16,144,128]{2,1,0:T(8,128)(2,1)} %weights_back.2), calls=%async_computation.6 | async-start | bytes 1179648 | tf_op jit(solution)/shard_map/weights_back/all_to_all | solution.py:396

commit v5 on v4

--- a/solution.py
+++ b/solution.py
@@ -66,33 +66,29 @@
 
 
 def by_row_kernel(
-    state_hbm, cotangent_hbm, land_hbm, orography_hbm, out_ref, adjoint_ref,
+    state_hbm, cotangent_hbm, land_hbm, orography_hbm, out_ref,
     state_ref, cotangent_ref, land_ref, orography_ref, sems, *, classes
 ):
+    sources = (state_hbm, cotangent_hbm, land_hbm, orography_hbm)
+    targets = (state_ref, cotangent_ref, land_ref, orography_ref)
     moves = [
         pltpu.make_async_copy(source, target, sems.at[i])
-        for i, (source, target) in enumerate(
-            (
-                (state_hbm, state_ref),
-                (cotangent_hbm, cotangent_ref),
-                (land_hbm, land_ref),
-                (orography_hbm, orography_ref),
-            )
-        )
+        for i, (source, target) in enumerate(zip(sources, targets))
     ]
     for move in moves:
         move.start()
-    sectors, rows = out_ref.shape[:2]
+    sectors, rows = out_ref.shape[0], (out_ref.shape[1] - 8) // 2
     members = state_ref.shape[0]
     band = land_ref.shape[0]
     taken = band * members // sectors
     channels = rows // taken
-    for source, target, move in ((state_ref, out_ref, 0), (cotangent_ref, adjoint_ref, 1)):
-        moves[move].wait()
+    for i in range(2):
+        moves[i].wait()
         for q in range(sectors):
             m, first = q * taken // band, q * taken % band
             for k in range(taken):
-                target[q, k * channels : (k + 1) * channels, :] = source[
+                start = i * rows + k * channels
+                out_ref[q, start : start + channels, :] = targets[i][
                     m, pl.ds(first + k, channels, stride=band), :
                 ]
     moves[2].wait()
@@ -101,7 +97,7 @@
     for q in range(sectors):
         first = q * taken % band
         spare = jnp.zeros((8 - taken, LANES), F32)
-        adjoint_ref[q, rows:, :] = jnp.concatenate([code[first : first + taken], spare], axis=0)
+        out_ref[q, 2 * rows :, :] = jnp.concatenate([code[first : first + taken], spare], axis=0)
 
 
 def own_scale(place, scale_ref, taken, sectors, band, rows):
@@ -121,7 +117,6 @@
     place_ref,
     seeds_ref,
     row_ref,
-    adjoint_ref,
     scale_ref,
     high_ref,
     low_ref,
@@ -146,7 +141,7 @@
     classes = relief_ref.shape[0]
     place = place_ref[0]
     scale = own_scale(place, scale_ref, taken, sectors, band, rows)
-    moist_grad = filtered(joined(adjoint_ref, 0, rows), scale, high_ref[...], low_ref[...])
+    moist_grad = filtered(joined(row_ref, rows, rows), scale, high_ref[...], low_ref[...])
     moist_grad_ref[...] = moist_grad
     rounded = joined(row_ref, 0, rows).astype(BF).astype(F32)
     for j in range(-1, taken + 1):
@@ -160,7 +155,7 @@
                     start = (3 * a + b) * channels
                     features_ref[j + 1 - a, start : start + channels, :] = moved
     class_ids = lax.broadcasted_iota(jnp.int32, (2 * classes, lon_total), 0).astype(F32)
-    codes = joined(adjoint_ref, rows, 8)
+    codes = joined(row_ref, 2 * rows, 8)
     surface = jnp.concatenate(
         [land_ref[0:1, :] + relief_ref[...], land_ref[1:2, :] + relief_ref[...]], axis=0
     )
@@ -178,26 +173,33 @@
 def weights_kernel(
     north_ref,
     south_ref,
+    row_ref,
     moist_grad_ref,
     early_ref,
     preact_ref,
     hidden_grad_ref,
     w_hidden_ref,
-    hidden_ref,
-    preact_grad_ref,
+    w_tendency_ref,
+    to_north_ref,
+    to_south_ref,
+    moist_ref,
+    grad_ref,
     weights_ref,
     features_ref,
     stage_ref,
 ):
     taken, in_channels, lon_total = features_ref.shape
-    channels = north_ref.shape[1]
-    hidden_units = w_hidden_ref.shape[0]
+    channels, hidden_units = w_tendency_ref.shape
     group = 3 * channels
+    w_stencil = w_hidden_ref[:, : 3 * group]
+    state = joined(row_ref, 0, taken * channels)
     grad_in = jnp.zeros((hidden_units, in_channels), F32)
     grad_out = jnp.zeros((channels, hidden_units), F32)
     grad_bias = jnp.zeros((16, hidden_units), F32)
     ones = jnp.ones((16, lon_total), BF)
+    sums = []
     for k in range(taken):
+        part = slice(k * channels, (k + 1) * channels)
         features_ref[k] = early_ref[k]
         preact = preact_ref[k]
         for ref, a, row in ((north_ref, 0, 0), (south_ref, 2, taken - 1)):
@@ -206,16 +208,33 @@
                 halo = jnp.concatenate([rolled(edge, 1 - b).astype(BF) for b in range(3)], axis=0)
                 features_ref[k, a * group : (a + 1) * group, :] = halo
                 preact = preact + dot(w_hidden_ref[:, a * group : (a + 1) * group], halo)
-        logistic = 1.0 / (1.0 + jnp.exp(-preact))
+        logistic = 0.5 + 0.5 * jnp.tanh(0.5 * preact)
         hidden = (preact * logistic).astype(BF)
         slope = logistic * (1.0 + preact * (1.0 - logistic))
         preact_grad = (hidden_grad_ref[k] * slope).astype(BF)
-        hidden_ref[k] = hidden
-        preact_grad_ref[k] = preact_grad
-        tendency_grad = moist_grad_ref[k * channels : (k + 1) * channels, :].astype(BF)
+        tendency_grad = moist_grad_ref[part, :].astype(BF)
         grad_out += dot(tendency_grad, hidden, ((1,), (1,)))
         grad_in += dot(preact_grad, features_ref[k], ((1,), (1,)))
         grad_bias += dot(ones, preact_grad, ((1,), (1,)))
+        moist_ref[part, :] = state[part] + dot(w_tendency_ref[...], hidden)
+        stencil_grad = dot(w_stencil, preact_grad, ((0,), (0,)))
+        sums.append([])
+        for a in range(3):
+            total = None
+            for b in range(3):
+                start = (3 * a + b) * channels
+                piece = rolled(stencil_grad[start : start + channels], b - 1)
+                total = piece if total is None else total + piece
+            sums[k].append(total)
+    store_split(to_north_ref, 0, sums[0][0])
+    store_split(to_south_ref, 0, sums[-1][2])
+    for k in range(taken):
+        total = moist_grad_ref[k * channels : (k + 1) * channels, :] + sums[k][1]
+        if k > 0:
+            total = total + sums[k - 1][2]
+        if k + 1 < taken:
+            total = total + sums[k + 1][0]
+        store_split(grad_ref, k * channels, total)
 
     bias_high = grad_bias[0:1].astype(BF).astype(F32)
     bias_low = grad_bias[0:1] - bias_high
@@ -241,86 +260,19 @@
 
 
 def fields_kernel(
-    place_ref,
-    row_ref,
-    moist_grad_ref,
-    scale_ref,
-    high_ref,
-    low_ref,
-    hidden_ref,
-    preact_grad_ref,
-    w_hidden_ref,
-    w_tendency_ref,
-    to_north_ref,
-    to_south_ref,
-    next_ref,
-    grad_ref,
-    *,
-    band,
+    place_ref, moist_ref, scale_ref, high_ref, low_ref, grad_ref, south_ref, north_ref, out_ref,
+    *, band
 ):
-    taken = hidden_ref.shape[0]
-    sectors, rows = row_ref.shape[:2]
-    channels = rows // taken
-    w_stencil = w_hidden_ref[:, : 9 * channels]
-    sums = []
-    for k in range(taken):
-        stencil_grad = dot(w_stencil, preact_grad_ref[k], ((0,), (0,)))
-        sums.append([])
-        for a in range(3):
-            total = None
-            for b in range(3):
-                start = (3 * a + b) * channels
-                piece = rolled(stencil_grad[start : start + channels], b - 1)
-                total = piece if total is None else total + piece
-            sums[k].append(total)
-    store_split(to_north_ref, 0, sums[0][0])
-    store_split(to_south_ref, 0, sums[-1][2])
-    for k in range(taken):
-        total = moist_grad_ref[k * channels : (k + 1) * channels, :] + sums[k][1]
-        if k > 0:
-            total = total + sums[k - 1][2]
-        if k + 1 < taken:
-            total = total + sums[k + 1][0]
-        store_split(grad_ref, k * channels, total)
-    tendency = [dot(w_tendency_ref[...], hidden_ref[k]) for k in range(taken)]
-    moist = joined(row_ref, 0, rows) + jnp.concatenate(tendency, axis=0)
-    scale = own_scale(place_ref[0], scale_ref, taken, sectors, band, rows)
-    store_split(next_ref, 0, filtered(moist, scale, high_ref[...], low_ref[...]))
-
-
-def outgoing_kernel(place_ref, next_ref, grad_ref, south_ref, north_ref, *refs):
-    sends, blocks_ref = refs[:-1], refs[-1]
-    sectors, rows = next_ref.shape[:2]
+    sectors, rows = grad_ref.shape[:2]
     channels = south_ref.shape[1]
+    scale = own_scale(place_ref[0], scale_ref, rows // channels, sectors, band, rows)
+    store_split(out_ref, 0, filtered(moist_ref[...], scale, high_ref[...], low_ref[...]))
     for s in range(sectors):
-        blocks_ref[s, :rows, :] = next_ref[s]
         part = grad_ref[s]
         first = part[:channels] + north_ref[s].astype(F32)
         last = part[rows - channels :] + south_ref[s].astype(F32)
         inner = [part[channels : rows - channels]] if rows > 2 * channels else []
-        blocks_ref[s, rows:, :] = jnp.concatenate([first] + inner + [last], axis=0).astype(BF)
-    for t in range(sectors):
-        sends[t][...] = blocks_ref[(place_ref[0] + t) % sectors]
-
-
-def by_band_kernel(place_ref, *refs, band):
-    blocks_ref = refs[-1]
-    outs = refs[-3:-1]
-    sectors, rows = blocks_ref.shape[0], blocks_ref.shape[1] // 2
-    members = outs[0].shape[0]
-    taken = band * members // sectors
-    channels = rows // taken
-    for t in range(sectors):
-        blocks_ref[t] = refs[t][...].astype(F32)
-    for q in range(sectors):
-        t = (place_ref[0] + sectors - q) % sectors
-        m, first = q * taken // band, q * taken % band
-        for i in range(2):
-            for k in range(taken):
-                start = i * rows + k * channels
-                outs[i][m, pl.ds(first + k, channels, stride=band), :] = blocks_ref[
-                    t, start : start + channels, :
-                ]
+        out_ref[s, rows:, :] = jnp.concatenate([first] + inner + [last], axis=0).astype(BF)
 
 
 def summed(ref):
@@ -345,10 +297,21 @@
         copies_ref[p] = total
 
 
-def spread_kernel(pieces_ref, shares_ref, sum_ref):
-    pieces, piece_rows = pieces_ref.shape[:2]
+def join_kernel(parts_ref, fields_ref, out_ref, stage_ref):
+    rows, piece_rows = fields_ref.shape[1], parts_ref.shape[1]
+    stage_ref[...] = jnp.zeros(stage_ref.shape, F32)
+    stage_ref[:piece_rows, :] = summed(parts_ref)
+    for s in range(out_ref.shape[0]):
+        out_ref[s, :rows, :] = fields_ref[s]
+        out_ref[s, rows:, :] = stage_ref[...].astype(BF)
+
+
+def spread_kernel(blocks_ref, shares_ref, sum_ref, *, start):
+    pieces = blocks_ref.shape[0]
+    piece_rows = shares_ref.shape[1] // pieces
     for p in range(pieces):
-        sum_ref[p * piece_rows : (p + 1) * piece_rows, :] = pieces_ref[p].astype(F32)
+        piece = blocks_ref[p, start:, :].astype(F32)
+        sum_ref[p * piece_rows : (p + 1) * piece_rows, :] = piece[:piece_rows]
     share = sum_ref[...].astype(BF)
     for p in range(shares_ref.shape[0]):
         shares_ref[p] = share
@@ -423,9 +386,9 @@
 
     with jax.named_scope("rows_in"):
         flat = (members, channels * band, lon_cols)
-        state_rows, adjoint_rows = call(
+        packed = call(
             by_row_kernel,
-            (shape((sectors, rows, lon_cols), F32), shape((sectors, rows + 8, lon_cols), F32)),
+            shape((sectors, 2 * rows + 8, lon_cols), F32),
             4,
             scratch=[
                 pltpu.VMEM(flat, F32),
@@ -434,11 +397,11 @@
                 pltpu.VMEM(orography.shape, orography.dtype),
                 pltpu.SemaphoreType.DMA((4,)),
             ],
+            vmem=56,
             inputs_in=pltpu.HBM,
             classes=classes,
         )(column_state.reshape(flat), cotangent.reshape(flat), land_mask, orography)
-        row = exchange(state_rows, "lon")
-        adjoint_row = exchange(adjoint_rows, "lon")
+        row = exchange(packed, "lon")
 
     with jax.named_scope("row_halo"):
         south_going = []
@@ -447,19 +410,18 @@
             if j < peers:
                 south_going.append((i, j))
         north_going = [(j, i) for i, j in south_going]
-        north = lax.ppermute(row[:, rows - channels :].astype(BF), PLACE, south_going)
+        north = lax.ppermute(row[:, rows - channels : rows].astype(BF), PLACE, south_going)
         south = lax.ppermute(row[:, :channels].astype(BF), PLACE, north_going)
 
     place = lax.axis_index(PLACE).reshape(1)
     high, low, scale = [jnp.asarray(t) for t in filter_tables(lat_total, lon_total)]
     per_hidden = shape((taken, hidden_units, lon_total), F32)
-    per_hidden_bf = shape((taken, hidden_units, lon_total), BF)
     features_shape = (taken, in_channels, lon_total)
     with jax.named_scope("early"):
         moist_grad, features, preact, hidden_grad = call(
             early_kernel,
             (shape((rows, lon_total), F32), shape(features_shape, BF), per_hidden, per_hidden),
-            13,
+            12,
             smem=2,
             flops=3_000_000_000,
             vmem=24,
@@ -468,7 +430,6 @@
             place,
             member_seeds,
             row,
-            adjoint_row,
             scale,
             high,
             low,
@@ -486,41 +447,25 @@
     share_rows = whole_multiple(filled + BIAS_ROWS, 16)
     piece_rows = share_rows // sectors
     with jax.named_scope("weights"):
-        hidden, preact_grad, weights = call(
+        block = (sectors, rows, LANES)
+        edge = (sectors, channels, LANES)
+        to_north, to_south, moist, grad_rows, weights = call(
             weights_kernel,
-            (per_hidden_bf, per_hidden_bf, shape((near, share_rows, LANES), BF)),
-            7,
+            (
+                shape(edge, BF),
+                shape(edge, BF),
+                shape((rows, lon_total), F32),
+                shape(block, F32),
+                shape((near, share_rows, LANES), BF),
+            ),
+            9,
             scratch=[
                 pltpu.VMEM(features_shape, BF),
                 pltpu.VMEM((near, share_rows, LANES), F32),
             ],
             flops=3_000_000_000,
             vmem=28,
-        )(north, south, moist_grad, features, preact, hidden_grad, w_hidden)
-
-    with jax.named_scope("fields"):
-        block = (sectors, rows, LANES)
-        edge = (sectors, channels, LANES)
-        to_north, to_south, next_rows, grad_rows = call(
-            fields_kernel,
-            (shape(edge, BF), shape(edge, BF), shape(block, BF), shape(block, F32)),
-            10,
-            smem=1,
-            flops=3_000_000_000,
-            vmem=20,
-            band=band,
-        )(
-            place,
-            row,
-            moist_grad,
-            scale,
-            high,
-            low,
-            hidden,
-            preact_grad,
-            w_hidden,
-            w_tendency,
-        )
+        )(north, south, row, moist_grad, features, preact, hidden_grad, w_hidden, w_tendency)
         from_south = lax.ppermute(to_north, PLACE, north_going)
         from_north = lax.ppermute(to_south, PLACE, south_going)
 
@@ -529,52 +474,53 @@
         share = call(
             near_sum_kernel,
             shape((sectors, piece_rows, LANES), F32),
-            3,
+            2,
             scratch=[pltpu.VMEM((share_rows, LANES), F32)],
-        )(parts, from_south, from_north)
-
-    with jax.named_scope("rows_out"):
-        sends = call(
-            outgoing_kernel,
-            (shape((2 * rows, LANES), BF),) * sectors,
-            5,
-            smem=1,
-            scratch=[pltpu.VMEM((sectors, 2 * rows, LANES), BF)],
-        )(place, next_rows, grad_rows, from_south, from_north)
-        received = [sends[0]]
-        for t in range(1, sectors):
-            turn = [(i, (i + t) % sectors) for i in range(sectors)]
-            received.append(lax.ppermute(sends[t], "lon", turn))
+        )(parts, from_south)
+
     with jax.named_scope("weights_middle"):
         copies = call(sum_and_copy_kernel, shape((length, piece_rows, LANES), BF), 2)(
-            exchange(share, "lon"), received[1]
+            exchange(share, "lon"), from_north
         )
 
+    with jax.named_scope("fields"):
+        fields = call(
+            fields_kernel,
+            shape((sectors, 2 * rows, LANES), BF),
+            8,
+            smem=1,
+            flops=1_000_000_000,
+            band=band,
+        )(place, moist, scale, high, low, grad_rows, from_south, from_north)
+
     with jax.named_scope("weights_length"):
-        copies = call(sum_and_copy_kernel, shape((sectors, piece_rows, LANES), BF), sectors - 1)(
-            exchange(copies, "z"), *received[2:]
-        )
-
-    with jax.named_scope("bands_out"):
-        next_state, state_grad = call(
-            by_band_kernel,
-            (shape(flat, F32), shape(flat, F32)),
-            1 + sectors,
-            smem=1,
-            scratch=[pltpu.VMEM((sectors, 2 * rows, LANES), F32)],
-            band=band,
-        )(place, *received)
-        next_state = next_state.reshape(column_state.shape)
-        state_grad = state_grad.reshape(column_state.shape)
+        half_rows = whole_multiple(piece_rows, 16)
+        outgoing = call(
+            join_kernel,
+            shape((sectors, 2 * rows + half_rows, LANES), BF),
+            2,
+            scratch=[pltpu.VMEM((half_rows, LANES), F32)],
+        )(exchange(copies, "z"), fields)
+
+    with jax.named_scope("rows_out"):
+        blocks = exchange(outgoing, "lon")
+
+        def by_band(values):
+            values = values.reshape(members, groups, taken, channels, lon_cols).astype(F32)
+            values = jnp.transpose(values, (0, 3, 1, 2, 4))
+            return values.reshape(members, channels, band, lon_cols)
+
+        next_state = by_band(blocks[:, :rows])
+        state_grad = by_band(blocks[:, rows : 2 * rows])
 
     with jax.named_scope("weights_back"):
-        pieces = exchange(copies, "lon")
         spread = call(
             spread_kernel,
             shape((near, share_rows, LANES), BF),
             1,
             scratch=[pltpu.VMEM((share_rows, LANES), F32)],
-        )(pieces)
+            start=2 * rows,
+        )(blocks)
         shares = exchange(spread, NEAR)
         columns = members * lax.axis_size("mem") * lat_total * lon_total
         grad_in, grad_bias, grad_out = call(

time: 143 us -> 134 us (0.937)
  waiting for transfers between devices: 22 us -> 49.1 us
  starting transfers between devices: 72.5 us -> 55.8 us
  blocking collectives: 26.7 us -> 13.3 us
  local copies, waits for them, and re-layouts: 7.38 us -> 1.89 us
    all_to_all x5, waiting for transfers between devices: 9.36 us -> 34.1 us  [exchange(): return lax.all_to_all(x, axes, 0, 0, tiled=True)]
    all_to_all x2 -> x1, blocking collectives: 26.7 us -> 13.3 us  [exchange(): return lax.all_to_all(x, axes, 0, 0, tiled=True)]
    ppermute x4 -> x1, starting transfers between devices: 15 us -> 1.92 us  [on_device(): lax.ppermute(row[:, rows - channels:rows].astype(BF), PLACE, south_going)]
    ppermute x4 -> x1, waiting for transfers between devices: 10.1 us -> 2.7 us  [on_device(): lax.ppermute(row[:, rows - channels:rows].astype(BF), PLACE, south_going)]
    unnamed x36 -> x20, local copies, waits for them, and re-layouts: 7.37 us -> 0.05 us
    ppermute x1, waiting for transfers between devices: 0.23 us -> 6.61 us  [on_device(): from_south = lax.ppermute(to_north, PLACE, north_going)]
    ppermute x1, waiting for transfers between devices: 2.29 us -> 5.66 us  [on_device(): from_north = lax.ppermute(to_south, PLACE, south_going)]
    ppermute x1, starting transfers between devices: 9.81 us -> 6.59 us  [on_device(): south = lax.ppermute(row[:, :channels].astype(BF), PLACE, north_going)]
  transfers between devices with their start and end apart: 12 -> 9, of which waited for: 7 -> 7; matrix products, arithmetic and copies ran while one was open for 0% -> 1% of each run, Pallas kernels for 4% -> 3%
where the time goes in v5:
time: 134 us
  starting transfers between devices  55.8 us (42%)
  waiting for transfers between devices  49.1 us (37%)
  blocking collectives  13.3 us (10%)
  Pallas kernels  12.7 us (9%)
  local copies, waits for them, and re-layouts  1.89 us (1%)
    all_to_all x5, starting transfers between devices, exchange(): return lax.all_to_all(x, axes, 0, 0, tiled=True)  41.1 us
    all_to_all x5, waiting for transfers between devices, exchange(): return lax.all_to_all(x, axes, 0, 0, tiled=True)  34.1 us
    all_to_all x1, blocking collectives, exchange(): return lax.all_to_all(x, axes, 0, 0, tiled=True)  13.3 us
    ppermute x1, waiting for transfers between devices, on_device(): from_south = lax.ppermute(to_north, PLACE, north_going)  6.61 us
    ppermute x1, starting transfers between devices, on_device(): south = lax.ppermute(row[:, :channels].astype(BF), PLACE, north_going)  6.59 us
    ppermute x1, waiting for transfers between devices, on_device(): from_north = lax.ppermute(to_south, PLACE, south_going)  5.66 us
    ppermute x1, starting transfers between devices, on_device(): from_north = lax.ppermute(to_south, PLACE, south_going)  4.22 us
    pallas_call x1, Pallas kernels, on_device(): call(weights_kernel, (shape(edge, BF), shape(edge, BF), shape((rows, lon_...  3.68 us
  transfers between devices with their start and end apart: 9, of which 7 were waited for; matrix products, arithmetic and copies ran while one was open for 1% of the time, Pallas kernels for 3%

profile of v5, /device:TPU:1, one launch (start us, length us, event | category | flops | bytes accessed | tf_op | source)
XLA Modules:
  0.0 133.7 jit_solution(7152805631990927533)
XLA Ops:
  0.6 0.0 copy-start.9
  0.6 0.0 copy-start
  0.7 0.0 copy-start.1
  0.7 0.0 copy-start.2
  0.7 0.0 copy-start.3
  0.7 0.0 copy-start.4
  0.7 0.0 copy-start.5
  0.7 0.0 copy-start.6
  0.7 0.0 copy-start.7
  0.7 0.0 copy-start.8
  0.7 2.0 %rows_in.1 = f32[4,264,128]{2,1,0:T(8,128)} custom-call(f32[2,256,128]{2,1,0:T(8,128)} %bitcast.17, f32[2,256,128]{2,1,0:T(8,128)} %bitcast.18, s32[4,128]{1,0:T(4,128)} %refs_2_.2, s32[4,128]{1,0:T(4,128)} %refs_3_.3), custom_call_target="tpu_custom_call" | custom-call | bytes 1000000 | tf_op jit(solution)/shard_map/rows_in/pallas_call | solution.py:389
  2.7 7.7 %all-to-all-start = ((f32[4,264,128]{2,1,0:T(8,128)}), f32[4,264,128]{2,1,0:T(8,128)S(1)}, u32[]{:S(2)}, u32[]{:S(2)}) async-start(f32[4,264,128]{2,1,0:T(8,128)} %rows_in.1), calls=%async_computation | async-start | bytes 1081344 | tf_op jit(solution)/shard_map/rows_in/all_to_all | solution.py:359
  10.4 0.0 copy-done.9
  10.4 14.1 %all-to-all-done.refs_2_ = f32[4,264,128]{2,1,0:T(8,128)S(1)} async-done(((f32[4,264,128]{2,1,0:T(8,128)}), f32[4,264,128]{2,1,0:T(8,128)S(1)}, u32[]{:S(2)}, u32[]{:S(2)}) %all-to-all-start) | async-done | bytes 540704 | tf_op jit(solution)/shard_map/rows_in/all_to_all | solution.py:359
  24.5 6.6 %collective-permute-start.1 = (bf16[4,64,128]{2,1,0:T(8,128)(2,1)S(1)}, bf16[4,64,128]{2,1,0:T(8,128)(2,1)S(1)}, u32[]{:S(2)}, u32[]{:S(2)}) collective-permute-start(bf16[4,64,128]{2,1,0:T(8,128)(2,1)S(1)} %get-tuple-element.31), channel_id=1, source_target_pairs={{4,0},{16,4},{12,8},{24,12},{20,16},{32,20},{28,24},{40,28},{36,32... | collective-permute-start | bytes 196616 | tf_op jit(solution)/shard_map/row_halo/ppermute | solution.py:414
  31.1 1.9 %collective-permute-start = (bf16[4,64,128]{2,1,0:T(8,128)(2,1)S(1)}, bf16[4,64,128]{2,1,0:T(8,128)(2,1)S(1)}, u32[]{:S(2)}, u32[]{:S(2)}) collective-permute-start(bf16[4,64,128]{2,1,0:T(8,128)(2,1)S(1)} %get-tuple-element.32), channel_id=1, source_target_pairs={{0,4},{4,16},{8,12},{12,24},{16,20},{20,32},{24,28},{28,40},{32,36... | collective-permute-start | bytes 196616 | tf_op jit(solution)/shard_map/row_halo/ppermute | solution.py:413
  33.1 0.0 copy-done
  33.1 0.0 copy-done.1
  33.1 0.0 copy-done.2
  33.1 0.0 copy-done.3
  33.1 0.0 copy-done.4
  33.1 0.0 copy-done.5
  33.1 0.0 copy-done.6
  33.1 0.0 copy-done.7
  33.1 0.0 copy-done.8
  33.1 2.5 %early.1 = (f32[128,512]{1,0:T(8,128)S(1)}, bf16[2,640,512]{2,1,0:T(8,128)(2,1)S(1)}, f32[2,384,512]{2,1,0:T(8,128)S(1)}, f32[2,384,512]{2,1,0:T(8,128)S(1)}) custom-call(s32[1]{0:T(128)} %bitcast.2.refs_0_, s32[2]{0:T(128)S(1)} %copy-done.5, f32[4,264,128]{2,1,0:T(8,128)S(1)} %all-to-all-done.refs_2_, f32[192,384]{1,0:T(8,128)S(1)} %copy-done.8, ...), custom_call_target="tpu_custom_call" | custom-call | flops 3000000000 | bytes 1000000 | tf_op jit(solution)/shard_map/early/pallas_call | solution.py:421
  35.6 0.0 collective-permute-done.1.refs_1_
  35.6 2.7 %collective-permute-done.refs_0_ = bf16[4,64,128]{2,1,0:T(8,128)(2,1)S(1)} collective-permute-done((bf16[4,64,128]{2,1,0:T(8,128)(2,1)S(1)}, bf16[4,64,128]{2,1,0:T(8,128)(2,1)S(1)}, u32[]{:S(2)}, u32[]{:S(2)}) %collective-permute-start) | collective-permute-done | bytes 65568 | tf_op jit(solution)/shard_map/row_halo/ppermute | solution.py:413
  38.3 3.7 %weights.1 = (bf16[4,64,128]{2,1,0:T(8,128)(2,1)S(1)}, bf16[4,64,128]{2,1,0:T(8,128)(2,1)S(1)}, f32[128,512]{1,0:T(8,128)S(1)}, f32[4,128,128]{2,1,0:T(8,128)S(1)}, bf16[16,144,128]{2,1,0:T(8,128)(2,1)}) custom-call(bf16[4,64,128]{2,1,0:T(8,128)(2,1)S(1)} %collective-permute-done.refs_0_, bf16[4,64,128]{2,1,0:T(8,128)(2,1)S(1)} %collective-permute-done.1.refs_1_, ...), custom_call_target="tpu_custom_call" | custom-call | flops 3000000000 | bytes 1000000 | tf_op jit(solution)/shard_map/weights/pallas_call | solution.py:452
  42.0 16.8 %all-to-all-start.1 = ((bf16[16,144,128]{2,1,0:T(8,128)(2,1)}), bf16[16,144,128]{2,1,0:T(8,128)(2,1)S(1)}, u32[]{:S(2)}, u32[]{:S(2)}) async-start(bf16[16,144,128]{2,1,0:T(8,128)(2,1)} %get-tuple-element.21), calls=%async_computation.1 | async-start | bytes 1179648 | tf_op jit(solution)/shard_map/weights_near/all_to_all | solution.py:359
  58.8 1.9 %collective-permute-start.2 = (bf16[4,64,128]{2,1,0:T(8,128)(2,1)S(1)}, bf16[4,64,128]{2,1,0:T(8,128)(2,1)S(1)}, u32[]{:S(2)}, u32[]{:S(2)}) collective-permute-start(bf16[4,64,128]{2,1,0:T(8,128)(2,1)S(1)} %get-tuple-element.22), channel_id=1, source_target_pairs={{4,0},{16,4},{12,8},{24,12},{20,16},{32,20},{28,24},{40,28},{36,32... | collective-permute-start | bytes 196616 | tf_op jit(solution)/shard_map/weights/ppermute | solution.py:469
  60.7 6.6 %collective-permute-done.2.refs_1_.refs_6_ = bf16[4,64,128]{2,1,0:T(8,128)(2,1)S(1)} collective-permute-done((bf16[4,64,128]{2,1,0:T(8,128)(2,1)S(1)}, bf16[4,64,128]{2,1,0:T(8,128)(2,1)S(1)}, u32[]{:S(2)}, u32[]{:S(2)}) %collective-permute-start.2) | collective-permute-done | bytes 65568 | tf_op jit(solution)/shard_map/weights/ppermute | solution.py:469
  67.4 2.1 %all-to-all-done.1.refs_0_ = bf16[16,144,128]{2,1,0:T(8,128)(2,1)S(1)} async-done(((bf16[16,144,128]{2,1,0:T(8,128)(2,1)}), bf16[16,144,128]{2,1,0:T(8,128)(2,1)S(1)}, u32[]{:S(2)}, u32[]{:S(2)}) %all-to-all-start.1) | async-done | bytes 589856 | tf_op jit(solution)/shard_map/weights_near/all_to_all | solution.py:359
  69.5 0.7 weights_near.1
  70.2 3.3 %all-to-all-start.2 = ((f32[4,36,128]{2,1,0:T(8,128)}), f32[4,36,128]{2,1,0:T(8,128)S(1)}, u32[]{:S(2)}, u32[]{:S(2)}) async-start(f32[4,36,128]{2,1,0:T(8,128)} %weights_near.1), calls=%async_computation.2 | async-start | bytes 163840 | tf_op jit(solution)/shard_map/weights_middle/all_to_all | solution.py:359
  73.5 4.2 %collective-permute-start.3 = (bf16[4,64,128]{2,1,0:T(8,128)(2,1)S(1)}, bf16[4,64,128]{2,1,0:T(8,128)(2,1)S(1)}, u32[]{:S(2)}, u32[]{:S(2)}) collective-permute-start(bf16[4,64,128]{2,1,0:T(8,128)(2,1)S(1)} %get-tuple-element.23), channel_id=1, source_target_pairs={{0,4},{4,16},{8,12},{12,24},{16,20},{20,32},{24,28},{28,40},{32,36... | collective-permute-start | bytes 196616 | tf_op jit(solution)/shard_map/weights/ppermute | solution.py:470
  77.7 5.7 %collective-permute-done.3.refs_1_.refs_7_ = bf16[4,64,128]{2,1,0:T(8,128)(2,1)S(1)} collective-permute-done((bf16[4,64,128]{2,1,0:T(8,128)(2,1)S(1)}, bf16[4,64,128]{2,1,0:T(8,128)(2,1)S(1)}, u32[]{:S(2)}, u32[]{:S(2)}) %collective-permute-start.3) | collective-permute-done | bytes 65568 | tf_op jit(solution)/shard_map/weights/ppermute | solution.py:470
  83.4 0.0 all-to-all-done.2.refs_0_
  83.4 0.7 weights_middle.1
  84.1 3.5 %all-to-all-start.3 = ((bf16[12,36,128]{2,1,0:T(8,128)(2,1)}), bf16[12,36,128]{2,1,0:T(8,128)(2,1)S(1)}, u32[]{:S(2)}, u32[]{:S(2)}) async-start(bf16[12,36,128]{2,1,0:T(8,128)(2,1)} %weights_middle.1), calls=%async_computation.3 | async-start | bytes 245760 | tf_op jit(solution)/shard_map/weights_length/all_to_all | solution.py:359
  87.6 1.2 fields.1.refs_1_
  88.7 9.6 %all-to-all-done.3.refs_0_ = bf16[12,36,128]{2,1,0:T(8,128)(2,1)S(1)} async-done(((bf16[12,36,128]{2,1,0:T(8,128)(2,1)}), bf16[12,36,128]{2,1,0:T(8,128)(2,1)S(1)}, u32[]{:S(2)}, u32[]{:S(2)}) %all-to-all-start.3) | async-done | bytes 110624 | tf_op jit(solution)/shard_map/weights_length/all_to_all | solution.py:359
  98.4 13.3 %all_to_all.30.refs_0_ = bf16[4,304,128]{2,1,0:T(8,128)(2,1)S(1)} all-to-all(bf16[4,304,128]{2,1,0:T(8,128)(2,1)S(1)} %weights_length.1), channel_id=1, replica_groups=mesh['ylo'=2,'z'=12,'core'=2,'lon'=4,'mem'=4] {'lon'}, dimensions={0} | all-to-all | bytes 622592 | tf_op jit(solution)/shard_map/rows_out/all_to_all | solution.py:359
  111.7 0.9 weights_back.2
  112.6 9.9 %all-to-all-start.5 = ((bf16[16,144,128]{2,1,0:T(8,128)(2,1)}), bf16[16,144,128]{2,1,0:T(8,128)(2,1)S(1)}, u32[]{:S(2)}, u32[]{:S(2)}) async-start(bf16[16,144,128]{2,1,0:T(8,128)(2,1)} %weights_back.2), calls=%async_computation.5 | async-start | bytes 1179648 | tf_op jit(solution)/shard_map/weights_back/all_to_all | solution.py:359
  122.5 0.9 copy.19
  123.4 0.9 copy.20
  124.3 8.3 %all-to-all-done.5.refs_0_ = bf16[16,144,128]{2,1,0:T(8,128)(2,1)S(1)} async-done(((bf16[16,144,128]{2,1,0:T(8,128)(2,1)}), bf16[16,144,128]{2,1,0:T(8,128)(2,1)S(1)}, u32[]{:S(2)}, u32[]{:S(2)}) %all-to-all-start.5) | async-done | bytes 589856 | tf_op jit(solution)/shard_map/weights_back/all_to_all | solution.py:359
  132.6 1.1 weights_back.3
  (7 shorter events, 0.1 us)
Async XLA Ops:
  0.6 9.8 %copy-start.9 = (f32[384]{0:T(512)S(1)}, f32[384]{0:T(512)}, u32[]{:S(2)}) copy-start(f32[384]{0:T(512)} %param.23) | copy-start | bytes 4612
  0.6 32.4 %copy-start = (bf16[384,640]{1,0:T(8,128)(2,1)S(1)}, bf16[384,640]{1,0:T(8,128)(2,1)}, u32[]{:S(2)}) copy-start(bf16[384,640]{1,0:T(8,128)(2,1)} %refs_7_.3) | copy-start | bytes 1474564
  0.7 32.4 %copy-start.1 = (bf16[64,384]{1,0:T(8,128)(2,1)S(1)}, bf16[64,384]{1,0:T(8,128)(2,1)}, u32[]{:S(2)}) copy-start(bf16[64,384]{1,0:T(8,128)(2,1)} %refs_8_.3) | copy-start | bytes 147460
  0.7 32.4 %copy-start.2 = (f32[32,64]{1,0:T(8,128)S(1)}, f32[32,64]{1,0:T(8,128)}, u32[]{:S(2)}) copy-start(f32[32,64]{1,0:T(8,128)} %refs_8_.2) | copy-start | bytes 24580
  0.7 32.4 %copy-start.3 = (f32[16,64]{1,0:T(8,128)S(1)}, f32[16,64]{1,0:T(8,128)}, u32[]{:S(2)}) copy-start(f32[16,64]{1,0:T(8,128)} %refs_7_.2) | copy-start | bytes 12292
  0.7 32.4 %copy-start.4 = (f32[2,64]{1,0:T(2,128)S(1)}, f32[2,64]{1,0:T(2,128)}, u32[]{:S(2)}) copy-start(f32[2,64]{1,0:T(2,128)} %refs_6_.1) | copy-start | bytes 1540
  0.7 32.4 %copy-start.5 = (s32[2]{0:T(128)S(1)}, s32[2]{0:T(128)}, u32[]{:S(2)}) copy-start(s32[2]{0:T(128)} %refs_1_.1) | copy-start | bytes 28
  0.7 32.4 %copy-start.6 = (bf16[384,512]{1,0:T(8,128)(2,1)S(1)}, bf16[384,512]{1,0:T(8,128)(2,1)}, u32[]{:S(2)}) copy-start(bf16[384,512]{1,0:T(8,128)(2,1)} %constant.32.clone.refs_5_.refs_4_) | copy-start | bytes 1179652
  0.7 32.4 %copy-start.7 = (bf16[384,512]{1,0:T(8,128)(2,1)S(1)}, bf16[384,512]{1,0:T(8,128)(2,1)}, u32[]{:S(2)}) copy-start(bf16[384,512]{1,0:T(8,128)(2,1)} %constant.31.clone.refs_4_.refs_3_) | copy-start | bytes 1179652
  0.7 32.4 %copy-start.8 = (f32[192,384]{1,0:T(8,128)S(1)}, f32[192,384]{1,0:T(8,128)}, u32[]{:S(2)}) copy-start(f32[192,384]{1,0:T(8,128)} %constant.33.clone.refs_3_.refs_2_) | copy-start | bytes 884740
  2.7 21.7 %all-to-all-start = ((f32[4,264,128]{2,1,0:T(8,128)}), f32[4,264,128]{2,1,0:T(8,128)S(1)}, u32[]{:S(2)}, u32[]{:S(2)}) async-start(f32[4,264,128]{2,1,0:T(8,128)} %rows_in.1), calls=%async_computation | async-start | bytes 1081344 | tf_op jit(solution)/shard_map/rows_in/all_to_all | solution.py:359
  24.5 11.1 %collective-permute-start.1 = (bf16[4,64,128]{2,1,0:T(8,128)(2,1)S(1)}, bf16[4,64,128]{2,1,0:T(8,128)(2,1)S(1)}, u32[]{:S(2)}, u32[]{:S(2)}) collective-permute-start(bf16[4,64,128]{2,1,0:T(8,128)(2,1)S(1)} %get-tuple-element.31), channel_id=1, source_target_pairs={{4,0},{16,4},{12,8},{24,12},{20,16},{32,20},{28,24},{40,28},{36,32... | collective-permute-start | bytes 196616 | tf_op jit(solution)/shard_map/row_halo/ppermute | solution.py:414
  31.1 7.2 %collective-permute-start = (bf16[4,64,128]{2,1,0:T(8,128)(2,1)S(1)}, bf16[4,64,128]{2,1,0:T(8,128)(2,1)S(1)}, u32[]{:S(2)}, u32[]{:S(2)}) collective-permute-start(bf16[4,64,128]{2,1,0:T(8,128)(2,1)S(1)} %get-tuple-element.32), channel_id=1, source_target_pairs={{0,4},{4,16},{8,12},{12,24},{16,20},{20,32},{24,28},{28,40},{32,36... | collective-permute-start | bytes 196616 | tf_op jit(solution)/shard_map/row_halo/ppermute | solution.py:413
  42.0 27.5 %all-to-all-start.1 = ((bf16[16,144,128]{2,1,0:T(8,128)(2,1)}), bf16[16,144,128]{2,1,0:T(8,128)(2,1)S(1)}, u32[]{:S(2)}, u32[]{:S(2)}) async-start(bf16[16,144,128]{2,1,0:T(8,128)(2,1)} %get-tuple-element.21), calls=%async_computation.1 | async-start | bytes 1179648 | tf_op jit(solution)/shard_map/weights_near/all_to_all | solution.py:359
  58.8 8.5 %collective-permute-start.2 = (bf16[4,64,128]{2,1,0:T(8,128)(2,1)S(1)}, bf16[4,64,128]{2,1,0:T(8,128)(2,1)S(1)}, u32[]{:S(2)}, u32[]{:S(2)}) collective-permute-start(bf16[4,64,128]{2,1,0:T(8,128)(2,1)S(1)} %get-tuple-element.22), channel_id=1, source_target_pairs={{4,0},{16,4},{12,8},{24,12},{20,16},{32,20},{28,24},{40,28},{36,32... | collective-permute-start | bytes 196616 | tf_op jit(solution)/shard_map/weights/ppermute | solution.py:469
  70.2 13.2 %all-to-all-start.2 = ((f32[4,36,128]{2,1,0:T(8,128)}), f32[4,36,128]{2,1,0:T(8,128)S(1)}, u32[]{:S(2)}, u32[]{:S(2)}) async-start(f32[4,36,128]{2,1,0:T(8,128)} %weights_near.1), calls=%async_computation.2 | async-start | bytes 163840 | tf_op jit(solution)/shard_map/weights_middle/all_to_all | solution.py:359
  73.5 9.9 %collective-permute-start.3 = (bf16[4,64,128]{2,1,0:T(8,128)(2,1)S(1)}, bf16[4,64,128]{2,1,0:T(8,128)(2,1)S(1)}, u32[]{:S(2)}, u32[]{:S(2)}) collective-permute-start(bf16[4,64,128]{2,1,0:T(8,128)(2,1)S(1)} %get-tuple-element.23), channel_id=1, source_target_pairs={{0,4},{4,16},{8,12},{12,24},{16,20},{20,32},{24,28},{28,40},{32,36... | collective-permute-start | bytes 196616 | tf_op jit(solution)/shard_map/weights/ppermute | solution.py:470
  84.1 14.3 %all-to-all-start.3 = ((bf16[12,36,128]{2,1,0:T(8,128)(2,1)}), bf16[12,36,128]{2,1,0:T(8,128)(2,1)S(1)}, u32[]{:S(2)}, u32[]{:S(2)}) async-start(bf16[12,36,128]{2,1,0:T(8,128)(2,1)} %weights_middle.1), calls=%async_computation.3 | async-start | bytes 245760 | tf_op jit(solution)/shard_map/weights_length/all_to_all | solution.py:359
  112.6 20.1 %all-to-all-start.5 = ((bf16[16,144,128]{2,1,0:T(8,128)(2,1)}), bf16[16,144,128]{2,1,0:T(8,128)(2,1)S(1)}, u32[]{:S(2)}, u32[]{:S(2)}) async-start(bf16[16,144,128]{2,1,0:T(8,128)(2,1)} %weights_back.2), calls=%async_computation.5 | async-start | bytes 1179648 | tf_op jit(solution)/shard_map/weights_back/all_to_all | solution.py:359

commit v6 on v5

--- a/solution.py
+++ b/solution.py
@@ -65,9 +65,14 @@
         )
 
 
+def position(place, sectors):
+    band, q = place // sectors, place % sectors
+    return band, q, (q + band) % 2
+
+
 def by_row_kernel(
-    state_hbm, cotangent_hbm, land_hbm, orography_hbm, out_ref,
-    state_ref, cotangent_ref, land_ref, orography_ref, sems, *, classes
+    place_ref, state_hbm, cotangent_hbm, land_hbm, orography_hbm, out_hbm,
+    state_ref, cotangent_ref, land_ref, orography_ref, out_ref, sems, *, classes
 ):
     sources = (state_hbm, cotangent_hbm, land_hbm, orography_hbm)
     targets = (state_ref, cotangent_ref, land_ref, orography_ref)
@@ -77,31 +82,46 @@
     ]
     for move in moves:
         move.start()
-    sectors, rows = out_ref.shape[0], (out_ref.shape[1] - 8) // 2
+    sectors, packed_rows = out_ref.shape[:2]
+    rows = (packed_rows - 8) // 2
     members = state_ref.shape[0]
     band = land_ref.shape[0]
     taken = band * members // sectors
     channels = rows // taken
+    odd = place_ref[0] // sectors % 2
+    leaving = []
     for i in range(2):
         moves[i].wait()
-        for q in range(sectors):
-            m, first = q * taken // band, q * taken % band
-            for k in range(taken):
-                start = i * rows + k * channels
-                out_ref[q, start : start + channels, :] = targets[i][
-                    m, pl.ds(first + k, channels, stride=band), :
-                ]
-    moves[2].wait()
-    moves[3].wait()
-    code = (jnp.where(land_ref[...] == 1, classes, 0) + orography_ref[...]).astype(F32)
-    for q in range(sectors):
-        first = q * taken % band
-        spare = jnp.zeros((8 - taken, LANES), F32)
-        out_ref[q, 2 * rows :, :] = jnp.concatenate([code[first : first + taken], spare], axis=0)
-
-
-def own_scale(place, scale_ref, taken, sectors, band, rows):
-    first = place // sectors * band + place % (band // taken) * taken
+        if i == 1:
+            moves[2].wait()
+            moves[3].wait()
+            code = (jnp.where(land_ref[...] == 1, classes, 0) + orography_ref[...]).astype(F32)
+        for m in range(members):
+            for pair in range(2):
+                q = 2 * m + (pair + odd) % 2
+                first = pair * taken
+                for k in range(taken):
+                    start = i * rows + k * channels
+                    out_ref[q, start : start + channels, :] = targets[i][
+                        m, pl.ds(first + k, channels, stride=band), :
+                    ]
+                if i == 1:
+                    spare = jnp.zeros((8 - taken, LANES), F32)
+                    out_ref[q, 2 * rows :, :] = jnp.concatenate(
+                        [code[first : first + taken], spare], axis=0
+                    )
+        part = pl.ds(i * rows, rows if i == 0 else rows + 8)
+        leaving.append(
+            pltpu.make_async_copy(out_ref.at[:, part], out_hbm.at[:, part], sems.at[4 + i])
+        )
+        leaving[i].start()
+    for move in leaving:
+        move.wait()
+
+
+def own_scale(place, scale_ref, taken, sectors, rows):
+    band, _, pair = position(place, sectors)
+    first = (2 * band + pair) * taken
     channels = rows // taken
     wide = (channels, scale_ref.shape[1])
     return jnp.concatenate(
@@ -130,8 +150,6 @@
     features_ref,
     preact_ref,
     hidden_grad_ref,
-    *,
-    band,
 ):
     taken = features_ref.shape[0]
     sectors = row_ref.shape[0]
@@ -140,7 +158,7 @@
     lon_total = features_ref.shape[2]
     classes = relief_ref.shape[0]
     place = place_ref[0]
-    scale = own_scale(place, scale_ref, taken, sectors, band, rows)
+    scale = own_scale(place, scale_ref, taken, sectors, rows)
     moist_grad = filtered(joined(row_ref, rows, rows), scale, high_ref[...], low_ref[...])
     moist_grad_ref[...] = moist_grad
     rounded = joined(row_ref, 0, rows).astype(BF).astype(F32)
@@ -159,7 +177,7 @@
     surface = jnp.concatenate(
         [land_ref[0:1, :] + relief_ref[...], land_ref[1:2, :] + relief_ref[...]], axis=0
     )
-    seed = seeds_ref[place % sectors * taken // band]
+    seed = seeds_ref[place % sectors // 2]
     table = (surface + seed_ref[pl.ds(seed, 1), :]).astype(BF)
     bias = jnp.transpose(jnp.broadcast_to(b_hidden_ref[...], (8, hidden_units)))[:, 0:1]
     for k in range(taken):
@@ -171,8 +189,9 @@
 
 
 def weights_kernel(
-    north_ref,
-    south_ref,
+    place_ref,
+    across_ref,
+    inside_ref,
     row_ref,
     moist_grad_ref,
     early_ref,
@@ -180,8 +199,8 @@
     hidden_grad_ref,
     w_hidden_ref,
     w_tendency_ref,
-    to_north_ref,
-    to_south_ref,
+    to_across_ref,
+    to_inside_ref,
     moist_ref,
     grad_ref,
     weights_ref,
@@ -197,14 +216,20 @@
     grad_out = jnp.zeros((channels, hidden_units), F32)
     grad_bias = jnp.zeros((16, hidden_units), F32)
     ones = jnp.ones((16, lon_total), BF)
+    northern = position(place_ref[0], row_ref.shape[0])[2] == 0
+    across = joined(across_ref, 0, channels).astype(F32)
+    inside = joined(inside_ref, 0, channels).astype(F32)
+    edges = (
+        (jnp.where(northern, across, inside), 0, 0),
+        (jnp.where(northern, inside, across), 2, taken - 1),
+    )
     sums = []
     for k in range(taken):
         part = slice(k * channels, (k + 1) * channels)
         features_ref[k] = early_ref[k]
         preact = preact_ref[k]
-        for ref, a, row in ((north_ref, 0, 0), (south_ref, 2, taken - 1)):
+        for edge, a, row in edges:
             if row == k:
-                edge = joined(ref, 0, channels).astype(F32)
                 halo = jnp.concatenate([rolled(edge, 1 - b).astype(BF) for b in range(3)], axis=0)
                 features_ref[k, a * group : (a + 1) * group, :] = halo
                 preact = preact + dot(w_hidden_ref[:, a * group : (a + 1) * group], halo)
@@ -226,8 +251,9 @@
                 piece = rolled(stencil_grad[start : start + channels], b - 1)
                 total = piece if total is None else total + piece
             sums[k].append(total)
-    store_split(to_north_ref, 0, sums[0][0])
-    store_split(to_south_ref, 0, sums[-1][2])
+    to_north, to_south = sums[0][0], sums[-1][2]
+    store_split(to_across_ref, 0, jnp.where(northern, to_north, to_south))
+    store_split(to_inside_ref, 0, jnp.where(northern, to_south, to_north))
     for k in range(taken):
         total = moist_grad_ref[k * channels : (k + 1) * channels, :] + sums[k][1]
         if k > 0:
@@ -260,17 +286,19 @@
 
 
 def fields_kernel(
-    place_ref, moist_ref, scale_ref, high_ref, low_ref, grad_ref, south_ref, north_ref, out_ref,
-    *, band
+    place_ref, moist_ref, scale_ref, high_ref, low_ref, grad_ref, across_ref, inside_ref, out_ref
 ):
     sectors, rows = grad_ref.shape[:2]
-    channels = south_ref.shape[1]
-    scale = own_scale(place_ref[0], scale_ref, rows // channels, sectors, band, rows)
+    channels = across_ref.shape[1]
+    place = place_ref[0]
+    northern = position(place, sectors)[2] == 0
+    scale = own_scale(place, scale_ref, rows // channels, sectors, rows)
     store_split(out_ref, 0, filtered(moist_ref[...], scale, high_ref[...], low_ref[...]))
     for s in range(sectors):
         part = grad_ref[s]
-        first = part[:channels] + north_ref[s].astype(F32)
-        last = part[rows - channels :] + south_ref[s].astype(F32)
+        across, inside = across_ref[s].astype(F32), inside_ref[s].astype(F32)
+        first = part[:channels] + jnp.where(northern, across, inside)
+        last = part[rows - channels :] + jnp.where(northern, inside, across)
         inner = [part[channels : rows - channels]] if rows > 2 * channels else []
         out_ref[s, rows:, :] = jnp.concatenate([first] + inner + [last], axis=0).astype(BF)
 
@@ -288,13 +316,6 @@
     pieces, piece_rows = pieces_ref.shape[:2]
     for p in range(pieces):
         pieces_ref[p] = sum_ref[p * piece_rows : (p + 1) * piece_rows, :]
-
-
-def sum_and_copy_kernel(parts_ref, *refs):
-    copies_ref = refs[-1]
-    total = summed(parts_ref).astype(BF)
-    for p in range(copies_ref.shape[0]):
-        copies_ref[p] = total
 
 
 def join_kernel(parts_ref, fields_ref, out_ref, stage_ref):
@@ -336,8 +357,8 @@
                 grad_bias_ref[t * LANES : (t + 1) * LANES] = both
 
 
-def call(kernel, outs, inputs, smem=0, scratch=(), flops=0, vmem=8, inputs_in=pltpu.VMEM, **static):
-    on_vmem = pl.BlockSpec(memory_space=pltpu.VMEM)
+def call(kernel, outs, inputs, smem=0, scratch=(), flops=0, vmem=8, inputs_in=pltpu.VMEM, outs_in=pltpu.VMEM, **static):
+    on_output = pl.BlockSpec(memory_space=outs_in)
     on_input = pl.BlockSpec(memory_space=inputs_in)
     on_smem = pl.BlockSpec(memory_space=pltpu.SMEM)
 
@@ -348,7 +369,7 @@
         body,
         out_shape=outs,
         in_specs=[on_smem] * smem + [on_input] * (inputs - smem),
-        out_specs=jax.tree.map(lambda _: on_vmem, outs),
+        out_specs=jax.tree.map(lambda _: on_output, outs),
         scratch_shapes=list(scratch),
         cost_estimate=pl.CostEstimate(flops=flops, bytes_accessed=1_000_000, transcendentals=0),
         compiler_params=pltpu.CompilerParams(vmem_limit_bytes=vmem * MIB),
@@ -380,40 +401,52 @@
     lat_total = band * (peers // sectors)
     lon_total = lon_cols * sectors
     taken = band * members // sectors
-    groups = band // taken
     rows = taken * channels
+    assert 2 * taken == band and 2 * members == sectors
     shape = jax.ShapeDtypeStruct
+    place = lax.axis_index(PLACE)
+    band_index, _, pair = position(place, sectors)
+    place = place.reshape(1)
 
     with jax.named_scope("rows_in"):
         flat = (members, channels * band, lon_cols)
+        packed_shape = (sectors, 2 * rows + 8, lon_cols)
         packed = call(
             by_row_kernel,
-            shape((sectors, 2 * rows + 8, lon_cols), F32),
-            4,
+            shape(packed_shape, F32),
+            5,
+            smem=1,
             scratch=[
                 pltpu.VMEM(flat, F32),
                 pltpu.VMEM(flat, F32),
                 pltpu.VMEM(land_mask.shape, land_mask.dtype),
                 pltpu.VMEM(orography.shape, orography.dtype),
-                pltpu.SemaphoreType.DMA((4,)),
+                pltpu.VMEM(packed_shape, F32),
+                pltpu.SemaphoreType.DMA((6,)),
             ],
             vmem=56,
             inputs_in=pltpu.HBM,
+            outs_in=pltpu.HBM,
             classes=classes,
-        )(column_state.reshape(flat), cotangent.reshape(flat), land_mask, orography)
+        )(place, column_state.reshape(flat), cotangent.reshape(flat), land_mask, orography)
         row = exchange(packed, "lon")
 
     with jax.named_scope("row_halo"):
-        south_going = []
+        inside_swaps, across_swaps = [], []
         for i in range(peers):
-            j = i + 1 if i % groups < groups - 1 else i + sectors - (groups - 1)
-            if j < peers:
-                south_going.append((i, j))
-        north_going = [(j, i) for i, j in south_going]
-        north = lax.ppermute(row[:, rows - channels : rows].astype(BF), PLACE, south_going)
-        south = lax.ppermute(row[:, :channels].astype(BF), PLACE, north_going)
-
-    place = lax.axis_index(PLACE).reshape(1)
+            _, q, southern = position(i, sectors)
+            inside_swaps.append((i, i - q + (q ^ 1)))
+            j = i + sectors if southern else i - sectors
+            if 0 <= j < peers:
+                across_swaps.append((i, j))
+
+        def edge_row(southern):
+            start = southern * (rows - channels)
+            return lax.dynamic_slice_in_dim(row, start, channels, 1).astype(BF)
+
+        inside = lax.ppermute(edge_row(1 - pair), PLACE, inside_swaps)
+        across = lax.ppermute(edge_row(pair), PLACE, across_swaps)
+
     high, low, scale = [jnp.asarray(t) for t in filter_tables(lat_total, lon_total)]
     per_hidden = shape((taken, hidden_units, lon_total), F32)
     features_shape = (taken, in_channels, lon_total)
@@ -425,7 +458,6 @@
             smem=2,
             flops=3_000_000_000,
             vmem=24,
-            band=band,
         )(
             place,
             member_seeds,
@@ -449,7 +481,7 @@
     with jax.named_scope("weights"):
         block = (sectors, rows, LANES)
         edge = (sectors, channels, LANES)
-        to_north, to_south, moist, grad_rows, weights = call(
+        to_across, to_inside, moist, grad_rows, weights = call(
             weights_kernel,
             (
                 shape(edge, BF),
@@ -458,16 +490,37 @@
                 shape(block, F32),
                 shape((near, share_rows, LANES), BF),
             ),
-            9,
+            10,
+            smem=1,
             scratch=[
                 pltpu.VMEM(features_shape, BF),
                 pltpu.VMEM((near, share_rows, LANES), F32),
             ],
             flops=3_000_000_000,
             vmem=28,
-        )(north, south, row, moist_grad, features, preact, hidden_grad, w_hidden, w_tendency)
-        from_south = lax.ppermute(to_north, PLACE, north_going)
-        from_north = lax.ppermute(to_south, PLACE, south_going)
+        )(
+            place,
+            across,
+            inside,
+            row,
+            moist_grad,
+            features,
+            preact,
+            hidden_grad,
+            w_hidden,
+            w_tendency,
+        )
+
+    with jax.named_scope("fields"):
+        from_across = lax.ppermute(to_across, PLACE, across_swaps)
+        from_inside = lax.ppermute(to_inside, PLACE, inside_swaps)
+        fields = call(
+            fields_kernel,
+            shape((sectors, 2 * rows, LANES), BF),
+            8,
+            smem=1,
+            flops=1_000_000_000,
+        )(place, moist, scale, high, low, grad_rows, from_across, from_inside)
 
     with jax.named_scope("weights_near"):
         parts = exchange(weights, NEAR)
@@ -476,22 +529,11 @@
             shape((sectors, piece_rows, LANES), F32),
             2,
             scratch=[pltpu.VMEM((share_rows, LANES), F32)],
-        )(parts, from_south)
+        )(parts, fields)
 
     with jax.named_scope("weights_middle"):
-        copies = call(sum_and_copy_kernel, shape((length, piece_rows, LANES), BF), 2)(
-            exchange(share, "lon"), from_north
-        )
-
-    with jax.named_scope("fields"):
-        fields = call(
-            fields_kernel,
-            shape((sectors, 2 * rows, LANES), BF),
-            8,
-            smem=1,
-            flops=1_000_000_000,
-            band=band,
-        )(place, moist, scale, high, low, grad_rows, from_south, from_north)
+        piece = jnp.sum(exchange(share, "lon"), 0, keepdims=True).astype(BF)
+        copies = jnp.broadcast_to(piece, (length, piece_rows, LANES))
 
     with jax.named_scope("weights_length"):
         half_rows = whole_multiple(piece_rows, 16)
@@ -506,7 +548,8 @@
         blocks = exchange(outgoing, "lon")
 
         def by_band(values):
-            values = values.reshape(members, groups, taken, channels, lon_cols).astype(F32)
+            values = values.reshape(members, 2, taken, channels, lon_cols).astype(F32)
+            values = jnp.where(band_index % 2 == 1, values[:, ::-1], values)
             values = jnp.transpose(values, (0, 3, 1, 2, 4))
             return values.reshape(members, channels, band, lon_cols)
 

time: 134 us -> 127 us (0.948)
  blocking collectives: 13.3 us -> 38.6 us
  waiting for transfers between devices: 49.1 us -> 27.5 us
  starting transfers between devices: 55.8 us -> 46.4 us
  Pallas kernels: 12.7 us -> 10.9 us
    all_to_all x1 -> x3, blocking collectives: 13.3 us -> 38.6 us  [exchange(): return lax.all_to_all(x, axes, 0, 0, tiled=True)]
    all_to_all x5 -> x3, waiting for transfers between devices: 34.1 us -> 22.4 us  [exchange(): return lax.all_to_all(x, axes, 0, 0, tiled=True)]
    ppermute x4, waiting for transfers between devices: 15 us -> 5.18 us  [the longest x1 3.15 us: on_device(): from_inside = lax.ppermute(to_inside, PLACE, inside_swaps)]
    all_to_all x5 -> x3, starting transfers between devices: 41.1 us -> 31.5 us  [exchange(): return lax.all_to_all(x, axes, 0, 0, tiled=True)]
    reshape x2 -> x0, local copies, waits for them, and re-layouts: 1.81 us -> none  [by_band(): return values.reshape(members, channels, band, lon_cols)]
    transpose x0 -> x2, local copies, waits for them, and re-layouts: none -> 1.81 us  [by_band(): values = jnp.transpose(values, (0, 3, 1, 2, 4))]
  transfers between devices with their start and end apart: 9 -> 7, of which waited for: 7 -> 4; matrix products, arithmetic and copies ran while one was open for 1% -> 2% of each run, Pallas kernels for 3% -> 3%
where the time goes in v6:
time: 127 us; the launch traced here: 126 us
  starting transfers between devices  46.4 us (37%)
  blocking collectives  38.6 us (30%)
  waiting for transfers between devices  27.5 us (22%)
  Pallas kernels  10.9 us (9%)
  local copies, waits for them, and re-layouts  1.92 us (2%)
    all_to_all x3, blocking collectives, exchange(): return lax.all_to_all(x, axes, 0, 0, tiled=True)  38.6 us
    all_to_all x3, starting transfers between devices, exchange(): return lax.all_to_all(x, axes, 0, 0, tiled=True)  31.5 us
    all_to_all x3, waiting for transfers between devices, exchange(): return lax.all_to_all(x, axes, 0, 0, tiled=True)  22.4 us
    ppermute x1, starting transfers between devices, on_device(): inside = lax.ppermute(edge_row(1 - pair), PLACE, inside_swaps)  5.75 us
    ppermute x1, starting transfers between devices, on_device(): across = lax.ppermute(edge_row(pair), PLACE, across_swaps)  5.34 us
    pallas_call x1, Pallas kernels, on_device(): call(weights_kernel, (shape(edge, BF), shape(edge, BF), shape((rows, lon_...  3.31 us
    ppermute x1, waiting for transfers between devices, on_device(): from_inside = lax.ppermute(to_inside, PLACE, inside_swaps)  3.15 us
  transfers between devices with their start and end apart: 7, of which 4 were waited for; matrix products, arithmetic and copies ran while one was open for 2% of the time, Pallas kernels for 3%

profile of v6, /device:TPU:1, one launch (start us, length us, event | category | flops | bytes accessed | tf_op | source)
XLA Modules:
  0.0 126.5 jit_solution(6446795402071334651)
XLA Ops:
  0.6 0.0 copy-start.8
  0.6 0.0 copy-start.6
  0.7 0.0 copy-start.7
  0.7 0.0 copy-start.9
  0.7 0.0 copy-start.1
  0.7 0.0 copy-start
  0.7 0.0 copy-start.2
  0.7 0.0 copy-start.3
  0.7 0.0 copy-start.4
  0.7 0.0 copy-start.5
  0.8 1.9 %rows_in.1 = f32[4,264,128]{2,1,0:T(8,128)} custom-call(s32[1]{0:T(128)} %bitcast.refs_0_, f32[2,256,128]{2,1,0:T(8,128)} %bitcast.17, f32[2,256,128]{2,1,0:T(8,128)} %bitcast.18, s32[4,128]{1,0:T(4,128)} %refs_3_.3, s32[4,128]{1,0:T(4,128)} %refs_4_.3), custom_call_target="tpu_custom_call" | custom-call | bytes 1000000 | tf_op jit(solution)/shard_map/rows_in/pallas_call | solution.py:414
  2.7 7.7 %all-to-all-start = ((f32[4,264,128]{2,1,0:T(8,128)}), f32[4,264,128]{2,1,0:T(8,128)S(1)}, u32[]{:S(2)}, u32[]{:S(2)}) async-start(f32[4,264,128]{2,1,0:T(8,128)} %rows_in.1), calls=%async_computation | async-start | bytes 1081344 | tf_op jit(solution)/shard_map/rows_in/all_to_all | solution.py:380
  10.3 0.0 copy-done.9
  10.3 14.1 %all-to-all-done.refs_2_.refs_3_ = f32[4,264,128]{2,1,0:T(8,128)S(1)} async-done(((f32[4,264,128]{2,1,0:T(8,128)}), f32[4,264,128]{2,1,0:T(8,128)S(1)}, u32[]{:S(2)}, u32[]{:S(2)}) %all-to-all-start) | async-done | bytes 540704 | tf_op jit(solution)/shard_map/rows_in/all_to_all | solution.py:380
  24.4 5.8 %collective-permute-start.1 = (bf16[4,64,128]{2,1,0:T(8,128)(2,1)S(1)}, bf16[4,64,128]{2,1,0:T(8,128)(2,1)S(1)}, u32[]{:S(2)}, u32[]{:S(2)}) collective-permute-start(bf16[4,64,128]{2,1,0:T(8,128)(2,1)S(1)} %get-tuple-element.29), channel_id=1, source_target_pairs={{0,4},{4,0},{8,12},{12,8},{16,20},{20,16},{24,28},{28,24},{32,36},... | collective-permute-start | bytes 196616 | tf_op jit(solution)/shard_map/row_halo/ppermute | solution.py:447
  30.2 5.3 %collective-permute-start = (bf16[4,64,128]{2,1,0:T(8,128)(2,1)S(1)}, bf16[4,64,128]{2,1,0:T(8,128)(2,1)S(1)}, u32[]{:S(2)}, u32[]{:S(2)}) collective-permute-start(bf16[4,64,128]{2,1,0:T(8,128)(2,1)S(1)} %get-tuple-element.30), channel_id=1, source_target_pairs={{4,20},{12,28},{16,32},{20,4},{24,40},{28,12},{32,16},{36,52},{40,... | collective-permute-start | bytes 196616 | tf_op jit(solution)/shard_map/row_halo/ppermute | solution.py:448
  35.5 0.0 copy-done.8
  35.5 0.0 copy-done.6
  35.6 0.0 copy-done.7
  35.6 0.0 copy-done.1
  35.6 0.0 copy-done
  35.6 0.0 copy-done.2
  35.6 0.0 copy-done.3
  35.6 0.0 copy-done.4
  35.6 0.0 copy-done.5
  35.6 2.5 %early.1 = (f32[128,512]{1,0:T(8,128)S(1)}, bf16[2,640,512]{2,1,0:T(8,128)(2,1)S(1)}, f32[2,384,512]{2,1,0:T(8,128)S(1)}, f32[2,384,512]{2,1,0:T(8,128)S(1)}) custom-call(s32[1]{0:T(128)} %bitcast.refs_0_, s32[2]{0:T(128)S(1)} %copy-done.5, f32[4,264,128]{2,1,0:T(8,128)S(1)} %all-to-all-done.refs_2_.refs_3_, f32[192,384]{1,0:T(8,128)S(1)} %copy-done.8, ...), custom_call_target="tpu_custom_call" | custom-call | flops 3000000000 | bytes 1000000 | tf_op jit(solution)/shard_map/early/pallas_call | solution.py:454
  38.1 0.0 collective-permute-done.1.refs_2_
  38.1 0.0 collective-permute-done.refs_1_
  38.1 3.3 %weights.1 = (bf16[4,64,128]{2,1,0:T(8,128)(2,1)S(1)}, bf16[4,64,128]{2,1,0:T(8,128)(2,1)S(1)}, f32[128,512]{1,0:T(8,128)S(1)}, f32[4,128,128]{2,1,0:T(8,128)S(1)}, bf16[16,144,128]{2,1,0:T(8,128)(2,1)}) custom-call(s32[1]{0:T(128)} %bitcast.refs_0_, bf16[4,64,128]{2,1,0:T(8,128)(2,1)S(1)} %collective-permute-done.refs_1_, ...), custom_call_target="tpu_custom_call" | custom-call | flops 3000000000 | bytes 1000000 | tf_op jit(solution)/shard_map/weights/pallas_call | solution.py:484
  41.4 14.9 %all-to-all-start.1 = ((bf16[16,144,128]{2,1,0:T(8,128)(2,1)}), bf16[16,144,128]{2,1,0:T(8,128)(2,1)S(1)}, u32[]{:S(2)}, u32[]{:S(2)}) async-start(bf16[16,144,128]{2,1,0:T(8,128)(2,1)} %get-tuple-element.21), calls=%async_computation.1 | async-start | bytes 1179648 | tf_op jit(solution)/shard_map/weights_near/all_to_all | solution.py:380
  56.3 1.9 %collective-permute-start.2 = (bf16[4,64,128]{2,1,0:T(8,128)(2,1)S(1)}, bf16[4,64,128]{2,1,0:T(8,128)(2,1)S(1)}, u32[]{:S(2)}, u32[]{:S(2)}) collective-permute-start(bf16[4,64,128]{2,1,0:T(8,128)(2,1)S(1)} %get-tuple-element.24), channel_id=1, source_target_pairs={{4,20},{12,28},{16,32},{20,4},{24,40},{28,12},{32,16},{36,52},{40,... | collective-permute-start | bytes 196616 | tf_op jit(solution)/shard_map/fields/ppermute | solution.py:515
  58.2 1.9 %collective-permute-start.3 = (bf16[4,64,128]{2,1,0:T(8,128)(2,1)S(1)}, bf16[4,64,128]{2,1,0:T(8,128)(2,1)S(1)}, u32[]{:S(2)}, u32[]{:S(2)}) collective-permute-start(bf16[4,64,128]{2,1,0:T(8,128)(2,1)S(1)} %get-tuple-element.25), channel_id=1, source_target_pairs={{0,4},{4,0},{8,12},{12,8},{16,20},{20,16},{24,28},{28,24},{32,36},... | collective-permute-start | bytes 196616 | tf_op jit(solution)/shard_map/fields/ppermute | solution.py:516
  60.2 2.0 %collective-permute-done.2.refs_6_ = bf16[4,64,128]{2,1,0:T(8,128)(2,1)S(1)} collective-permute-done((bf16[4,64,128]{2,1,0:T(8,128)(2,1)S(1)}, bf16[4,64,128]{2,1,0:T(8,128)(2,1)S(1)}, u32[]{:S(2)}, u32[]{:S(2)}) %collective-permute-start.2) | collective-permute-done | bytes 65568 | tf_op jit(solution)/shard_map/fields/ppermute | solution.py:515
  62.2 3.1 %collective-permute-done.3.refs_7_ = bf16[4,64,128]{2,1,0:T(8,128)(2,1)S(1)} collective-permute-done((bf16[4,64,128]{2,1,0:T(8,128)(2,1)S(1)}, bf16[4,64,128]{2,1,0:T(8,128)(2,1)S(1)}, u32[]{:S(2)}, u32[]{:S(2)}) %collective-permute-start.3) | collective-permute-done | bytes 65568 | tf_op jit(solution)/shard_map/fields/ppermute | solution.py:516
  65.4 1.2 fields.1.refs_1_
  66.5 0.0 all-to-all-done.1.refs_0_
  66.5 0.1 weights_near.1
  66.6 11.1 %all_to_all.30 = f32[4,36,128]{2,1,0:T(8,128)S(1)} all-to-all(f32[4,36,128]{2,1,0:T(8,128)S(1)} %weights_near.1), channel_id=1, replica_groups=mesh['ylo'=2,'z'=12,'core'=2,'lon'=4,'mem'=4] {'lon'}, dimensions={0} | all-to-all | bytes 147456 | tf_op jit(solution)/shard_map/weights_middle/all_to_all | solution.py:380
  77.8 16.5 %all_to_all.31.refs_0_ = bf16[12,36,128]{2,1,0:T(8,128)(2,1)S(1)} all-to-all(bf16[12,36,128]{2,1,0:T(8,128)(2,1)S(1)} %broadcast_in_dim.2), channel_id=1, replica_groups=mesh['ylo'=2,'z'=12,'core'=2,'lon'=4,'mem'=4] {'z'}, dimensions={0} | all-to-all | bytes 221184 | tf_op jit(solution)/shard_map/weights_length/all_to_all | solution.py:380
  94.3 11.0 %all_to_all.32.refs_0_ = bf16[4,304,128]{2,1,0:T(8,128)(2,1)S(1)} all-to-all(bf16[4,304,128]{2,1,0:T(8,128)(2,1)S(1)} %weights_length.1), channel_id=1, replica_groups=mesh['ylo'=2,'z'=12,'core'=2,'lon'=4,'mem'=4] {'lon'}, dimensions={0} | all-to-all | bytes 622592 | tf_op jit(solution)/shard_map/rows_out/all_to_all | solution.py:380
  105.3 0.9 weights_back.2
  106.2 9.0 %all-to-all-start.5 = ((bf16[16,144,128]{2,1,0:T(8,128)(2,1)}), bf16[16,144,128]{2,1,0:T(8,128)(2,1)S(1)}, u32[]{:S(2)}, u32[]{:S(2)}) async-start(bf16[16,144,128]{2,1,0:T(8,128)(2,1)} %weights_back.2), calls=%async_computation.5 | async-start | bytes 1179648 | tf_op jit(solution)/shard_map/weights_back/all_to_all | solution.py:380
  115.3 0.9 copy.19
  116.2 0.9 copy.20
  117.1 8.3 %all-to-all-done.5.refs_0_ = bf16[16,144,128]{2,1,0:T(8,128)(2,1)S(1)} async-done(((bf16[16,144,128]{2,1,0:T(8,128)(2,1)}), bf16[16,144,128]{2,1,0:T(8,128)(2,1)S(1)}, u32[]{:S(2)}, u32[]{:S(2)}) %all-to-all-start.5) | async-done | bytes 589856 | tf_op jit(solution)/shard_map/weights_back/all_to_all | solution.py:380
  125.4 1.1 weights_back.3
  (9 shorter events, 0.2 us)
Async XLA Ops:
  0.6 34.9 %copy-start.8 = (f32[192,384]{1,0:T(8,128)S(1)}, f32[192,384]{1,0:T(8,128)}, u32[]{:S(2)}) copy-start(f32[192,384]{1,0:T(8,128)} %constant.79.clone.refs_3_.refs_2_) | copy-start | bytes 884740
  0.6 34.9 %copy-start.6 = (bf16[384,512]{1,0:T(8,128)(2,1)S(1)}, bf16[384,512]{1,0:T(8,128)(2,1)}, u32[]{:S(2)}) copy-start(bf16[384,512]{1,0:T(8,128)(2,1)} %constant.78.clone.refs_5_.refs_4_) | copy-start | bytes 1179652
  0.7 34.9 %copy-start.7 = (bf16[384,512]{1,0:T(8,128)(2,1)S(1)}, bf16[384,512]{1,0:T(8,128)(2,1)}, u32[]{:S(2)}) copy-start(bf16[384,512]{1,0:T(8,128)(2,1)} %constant.77.clone.refs_4_.refs_3_) | copy-start | bytes 1179652
  0.7 9.7 %copy-start.9 = (f32[384]{0:T(512)S(1)}, f32[384]{0:T(512)}, u32[]{:S(2)}) copy-start(f32[384]{0:T(512)} %param.23) | copy-start | bytes 4612
  0.7 34.9 %copy-start.1 = (bf16[64,384]{1,0:T(8,128)(2,1)S(1)}, bf16[64,384]{1,0:T(8,128)(2,1)}, u32[]{:S(2)}) copy-start(bf16[64,384]{1,0:T(8,128)(2,1)} %refs_9_.3) | copy-start | bytes 147460
  0.7 34.9 %copy-start = (bf16[384,640]{1,0:T(8,128)(2,1)S(1)}, bf16[384,640]{1,0:T(8,128)(2,1)}, u32[]{:S(2)}) copy-start(bf16[384,640]{1,0:T(8,128)(2,1)} %refs_8_.3) | copy-start | bytes 1474564
  0.7 34.9 %copy-start.2 = (f32[32,64]{1,0:T(8,128)S(1)}, f32[32,64]{1,0:T(8,128)}, u32[]{:S(2)}) copy-start(f32[32,64]{1,0:T(8,128)} %refs_8_.2) | copy-start | bytes 24580
  0.7 34.9 %copy-start.3 = (f32[16,64]{1,0:T(8,128)S(1)}, f32[16,64]{1,0:T(8,128)}, u32[]{:S(2)}) copy-start(f32[16,64]{1,0:T(8,128)} %refs_7_.1) | copy-start | bytes 12292
  0.7 34.9 %copy-start.4 = (f32[2,64]{1,0:T(2,128)S(1)}, f32[2,64]{1,0:T(2,128)}, u32[]{:S(2)}) copy-start(f32[2,64]{1,0:T(2,128)} %refs_6_.1) | copy-start | bytes 1540
  0.7 34.9 %copy-start.5 = (s32[2]{0:T(128)S(1)}, s32[2]{0:T(128)}, u32[]{:S(2)}) copy-start(s32[2]{0:T(128)} %refs_1_.1) | copy-start | bytes 28
  2.7 21.7 %all-to-all-start = ((f32[4,264,128]{2,1,0:T(8,128)}), f32[4,264,128]{2,1,0:T(8,128)S(1)}, u32[]{:S(2)}, u32[]{:S(2)}) async-start(f32[4,264,128]{2,1,0:T(8,128)} %rows_in.1), calls=%async_computation | async-start | bytes 1081344 | tf_op jit(solution)/shard_map/rows_in/all_to_all | solution.py:380
  24.4 13.7 %collective-permute-start.1 = (bf16[4,64,128]{2,1,0:T(8,128)(2,1)S(1)}, bf16[4,64,128]{2,1,0:T(8,128)(2,1)S(1)}, u32[]{:S(2)}, u32[]{:S(2)}) collective-permute-start(bf16[4,64,128]{2,1,0:T(8,128)(2,1)S(1)} %get-tuple-element.29), channel_id=1, source_target_pairs={{0,4},{4,0},{8,12},{12,8},{16,20},{20,16},{24,28},{28,24},{32,36},... | collective-permute-start | bytes 196616 | tf_op jit(solution)/shard_map/row_halo/ppermute | solution.py:447
  30.2 7.9 %collective-permute-start = (bf16[4,64,128]{2,1,0:T(8,128)(2,1)S(1)}, bf16[4,64,128]{2,1,0:T(8,128)(2,1)S(1)}, u32[]{:S(2)}, u32[]{:S(2)}) collective-permute-start(bf16[4,64,128]{2,1,0:T(8,128)(2,1)S(1)} %get-tuple-element.30), channel_id=1, source_target_pairs={{4,20},{12,28},{16,32},{20,4},{24,40},{28,12},{32,16},{36,52},{40,... | collective-permute-start | bytes 196616 | tf_op jit(solution)/shard_map/row_halo/ppermute | solution.py:448
  41.4 25.1 %all-to-all-start.1 = ((bf16[16,144,128]{2,1,0:T(8,128)(2,1)}), bf16[16,144,128]{2,1,0:T(8,128)(2,1)S(1)}, u32[]{:S(2)}, u32[]{:S(2)}) async-start(bf16[16,144,128]{2,1,0:T(8,128)(2,1)} %get-tuple-element.21), calls=%async_computation.1 | async-start | bytes 1179648 | tf_op jit(solution)/shard_map/weights_near/all_to_all | solution.py:380
  56.3 5.9 %collective-permute-start.2 = (bf16[4,64,128]{2,1,0:T(8,128)(2,1)S(1)}, bf16[4,64,128]{2,1,0:T(8,128)(2,1)S(1)}, u32[]{:S(2)}, u32[]{:S(2)}) collective-permute-start(bf16[4,64,128]{2,1,0:T(8,128)(2,1)S(1)} %get-tuple-element.24), channel_id=1, source_target_pairs={{4,20},{12,28},{16,32},{20,4},{24,40},{28,12},{32,16},{36,52},{40,... | collective-permute-start | bytes 196616 | tf_op jit(solution)/shard_map/fields/ppermute | solution.py:515
  58.2 7.1 %collective-permute-start.3 = (bf16[4,64,128]{2,1,0:T(8,128)(2,1)S(1)}, bf16[4,64,128]{2,1,0:T(8,128)(2,1)S(1)}, u32[]{:S(2)}, u32[]{:S(2)}) collective-permute-start(bf16[4,64,128]{2,1,0:T(8,128)(2,1)S(1)} %get-tuple-element.25), channel_id=1, source_target_pairs={{0,4},{4,0},{8,12},{12,8},{16,20},{20,16},{24,28},{28,24},{32,36},... | collective-permute-start | bytes 196616 | tf_op jit(solution)/shard_map/fields/ppermute | solution.py:516
  106.2 19.2 %all-to-all-start.5 = ((bf16[16,144,128]{2,1,0:T(8,128)(2,1)}), bf16[16,144,128]{2,1,0:T(8,128)(2,1)S(1)}, u32[]{:S(2)}, u32[]{:S(2)}) async-start(bf16[16,144,128]{2,1,0:T(8,128)(2,1)} %weights_back.2), calls=%async_computation.5 | async-start | bytes 1179648 | tf_op jit(solution)/shard_map/weights_back/all_to_all | solution.py:380

commit v7 on v6

--- a/solution.py
+++ b/solution.py
@@ -15,8 +15,7 @@
 F32 = jnp.float32
 MIB = 1024 * 1024
 PLACE = ("ylo", "z", "core", "lon")
-NEAR = ("core", "mem", "ylo")
-BIAS_ROWS = 8
+PLANE = ("mem", "ylo", "lon")
 
 
 def whole_multiple(value, unit):
@@ -37,6 +36,11 @@
     high = analysis.astype(np.float32).astype(BF)
     low = (analysis - high.astype(np.float64)).astype(np.float32).astype(BF)
     return high, low, scale
+
+
+def split_rows(total, pieces):
+    each = total // pieces
+    return each // 8 * 8, each % 8
 
 
 def dot(a, b, dims=((1,), (0,))):
@@ -203,8 +207,10 @@
     to_inside_ref,
     moist_ref,
     grad_ref,
-    weights_ref,
+    own_ref,
+    other_ref,
     features_ref,
+    flat_ref,
     stage_ref,
 ):
     taken, in_channels, lon_total = features_ref.shape
@@ -265,96 +271,111 @@
     bias_high = grad_bias[0:1].astype(BF).astype(F32)
     bias_low = grad_bias[0:1] - bias_high
     tiles = hidden_units // LANES
-    shares, share_rows = weights_ref.shape[:2]
-    filled = (grad_in.size + grad_out.size) // (LANES * shares)
-    for p in range(shares):
-        stage_ref[p, filled // 8 * 8 :, :] = jnp.zeros((share_rows - filled // 8 * 8, LANES), F32)
+    pieces = own_ref.shape[0]
+    base, rest = split_rows(flat_ref.shape[1], pieces)
+    stage_ref[:, :, base + rest :, :] = jnp.zeros((2, pieces, tiles, LANES), F32)
+    for h in range(2):
         start = 0
         for value in (grad_in, grad_out):
-            count = value.shape[0] // shares
+            count = value.shape[0] // 2
             for t in range(value.shape[1] // LANES):
-                stage_ref[p, start : start + count, :] = value[
-                    p * count : (p + 1) * count, t * LANES : (t + 1) * LANES
+                flat_ref[h, start : start + count, :] = value[
+                    h * count : (h + 1) * count, t * LANES : (t + 1) * LANES
                 ]
                 start += count
-        if p == 0:
-            for half in (bias_high, bias_low):
-                for t in range(tiles):
-                    stage_ref[p, start : start + 1, :] = half[:, t * LANES : (t + 1) * LANES]
-                    start += 1
-        weights_ref[p] = stage_ref[p].astype(BF)
+        for p in range(pieces):
+            stage_ref[h, p, :base, :] = flat_ref[h, p * base : (p + 1) * base, :]
+            start = pieces * base + p * rest
+            stage_ref[h, p, base : base + rest, :] = flat_ref[h, start : start + rest, :]
+        for p, half in enumerate((bias_high, bias_low)):
+            for t in range(tiles):
+                row = base + rest + t
+                stage_ref[h, p, row : row + 1, :] = half[:, t * LANES : (t + 1) * LANES]
+    core = position(place_ref[0], row_ref.shape[0])[0] % 2
+    own_ref[...] = stage_ref[core]
+    other_ref[...] = stage_ref[1 - core].astype(BF)
 
 
 def fields_kernel(
-    place_ref, moist_ref, scale_ref, high_ref, low_ref, grad_ref, across_ref, inside_ref, out_ref
+    place_ref, moist_ref, scale_ref, high_ref, low_ref, grad_ref, across_ref, inside_ref, *refs
 ):
+    sends, blocks_ref = refs[:-1], refs[-1]
     sectors, rows = grad_ref.shape[:2]
     channels = across_ref.shape[1]
     place = place_ref[0]
-    northern = position(place, sectors)[2] == 0
+    _, q, pair = position(place, sectors)
     scale = own_scale(place, scale_ref, rows // channels, sectors, rows)
-    store_split(out_ref, 0, filtered(moist_ref[...], scale, high_ref[...], low_ref[...]))
+    store_split(blocks_ref, 0, filtered(moist_ref[...], scale, high_ref[...], low_ref[...]))
     for s in range(sectors):
         part = grad_ref[s]
         across, inside = across_ref[s].astype(F32), inside_ref[s].astype(F32)
-        first = part[:channels] + jnp.where(northern, across, inside)
-        last = part[rows - channels :] + jnp.where(northern, inside, across)
+        first = part[:channels] + jnp.where(pair == 0, across, inside)
+        last = part[rows - channels :] + jnp.where(pair == 0, inside, across)
         inner = [part[channels : rows - channels]] if rows > 2 * channels else []
-        out_ref[s, rows:, :] = jnp.concatenate([first] + inner + [last], axis=0).astype(BF)
-
-
-def summed(ref):
-    total = ref[0].astype(F32)
-    for p in range(1, ref.shape[0]):
-        total = total + ref[p].astype(F32)
-    return total
-
-
-def near_sum_kernel(parts_ref, *refs):
-    pieces_ref, sum_ref = refs[-2:]
-    sum_ref[...] = summed(parts_ref)
-    pieces, piece_rows = pieces_ref.shape[:2]
-    for p in range(pieces):
-        pieces_ref[p] = sum_ref[p * piece_rows : (p + 1) * piece_rows, :]
-
-
-def join_kernel(parts_ref, fields_ref, out_ref, stage_ref):
-    rows, piece_rows = fields_ref.shape[1], parts_ref.shape[1]
-    stage_ref[...] = jnp.zeros(stage_ref.shape, F32)
-    stage_ref[:piece_rows, :] = summed(parts_ref)
-    for s in range(out_ref.shape[0]):
-        out_ref[s, :rows, :] = fields_ref[s]
-        out_ref[s, rows:, :] = stage_ref[...].astype(BF)
-
-
-def spread_kernel(blocks_ref, shares_ref, sum_ref, *, start):
-    pieces = blocks_ref.shape[0]
-    piece_rows = shares_ref.shape[1] // pieces
-    for p in range(pieces):
-        piece = blocks_ref[p, start:, :].astype(F32)
-        sum_ref[p * piece_rows : (p + 1) * piece_rows, :] = piece[:piece_rows]
-    share = sum_ref[...].astype(BF)
-    for p in range(shares_ref.shape[0]):
-        shares_ref[p] = share
-
-
-def unpack_kernel(shares_ref, grad_in_ref, grad_bias_ref, grad_out_ref, stage_ref, *, scaling):
-    shares = shares_ref.shape[0]
-    for p in range(shares):
-        stage_ref[p] = shares_ref[p].astype(F32) * scaling
+        blocks_ref[s, rows:, :] = jnp.concatenate([first] + inner + [last], axis=0).astype(BF)
+    for t in range(sectors):
+        sends[t][...] = blocks_ref[q ^ t]
+
+
+def by_band_kernel(place_ref, *refs, band):
+    blocks_ref = refs[-1]
+    outs = refs[-3:-1]
+    sectors, rows = blocks_ref.shape[0], blocks_ref.shape[1] // 2
+    members = outs[0].shape[0]
+    taken = band * members // sectors
+    channels = rows // taken
+    band_index, q, _ = position(place_ref[0], sectors)
+    for t in range(sectors):
+        blocks_ref[t] = refs[t][...].astype(F32)
+    for m in range(members):
+        for pair in range(2):
+            t = q ^ (2 * m + (pair + band_index) % 2)
+            for i in range(2):
+                for k in range(taken):
+                    start = i * rows + k * channels
+                    outs[i][m, pl.ds(pair * taken + k, channels, stride=band), :] = blocks_ref[
+                        t, start : start + channels, :
+                    ]
+
+
+def sum_and_copy_kernel(parts_ref, *refs):
+    copies_ref = refs[-1]
+    total = parts_ref[0].astype(F32)
+    for p in range(1, parts_ref.shape[0]):
+        total = total + parts_ref[p].astype(F32)
+    total = total.astype(BF)
+    for p in range(copies_ref.shape[0]):
+        copies_ref[p] = total
+
+
+def unpack_kernel(
+    place_ref, own_ref, other_ref, grad_in_ref, grad_bias_ref, grad_out_ref, flat_ref,
+    *, scaling, sectors
+):
+    pieces = own_ref.shape[0]
+    base, rest = split_rows(flat_ref.shape[1], pieces)
+    core = position(place_ref[0], sectors)[0] % 2
+    bias = None
+    for ref, h in ((own_ref, core), (other_ref, 1 - core)):
+        for p in range(pieces):
+            piece = ref[p].astype(F32) * scaling
+            flat_ref[h, p * base : (p + 1) * base, :] = piece[:base]
+            start = pieces * base + p * rest
+            flat_ref[h, start : start + rest, :] = piece[base : base + rest]
+            if ref is own_ref and p < 2:
+                half = piece[base + rest :]
+                bias = half if bias is None else bias + half
+    for t in range(grad_bias_ref.shape[0] // LANES):
+        grad_bias_ref[t * LANES : (t + 1) * LANES] = bias[t]
+    for h in range(2):
         start = 0
         for ref in (grad_in_ref, grad_out_ref):
-            count = ref.shape[0] // shares
+            count = ref.shape[0] // 2
             for t in range(ref.shape[1] // LANES):
-                ref[p * count : (p + 1) * count, t * LANES : (t + 1) * LANES] = stage_ref[
-                    p, start : start + count, :
+                ref[h * count : (h + 1) * count, t * LANES : (t + 1) * LANES] = flat_ref[
+                    h, start : start + count, :
                 ]
                 start += count
-        if p == 0:
-            tiles = grad_bias_ref.shape[0] // LANES
-            for t in range(tiles):
-                both = stage_ref[p, start + t, :] + stage_ref[p, start + tiles + t, :]
-                grad_bias_ref[t * LANES : (t + 1) * LANES] = both
 
 
 def call(kernel, outs, inputs, smem=0, scratch=(), flops=0, vmem=8, inputs_in=pltpu.VMEM, outs_in=pltpu.VMEM, **static):
@@ -473,28 +494,31 @@
             w_tendency,
         )
 
-    near = lax.axis_size(NEAR)
+    pieces = lax.axis_size(PLANE)
     length = lax.axis_size("z")
-    filled = (hidden_units * in_channels + channels * hidden_units) // (LANES * near)
-    share_rows = whole_multiple(filled + BIAS_ROWS, 16)
-    piece_rows = share_rows // sectors
+    half_rows = (hidden_units * in_channels + channels * hidden_units) // (2 * LANES)
+    piece_rows = half_rows // pieces + hidden_units // LANES
+    share = (pieces, piece_rows, LANES)
+    flat_rows = pltpu.VMEM((2, half_rows, LANES), F32)
     with jax.named_scope("weights"):
         block = (sectors, rows, LANES)
         edge = (sectors, channels, LANES)
-        to_across, to_inside, moist, grad_rows, weights = call(
+        to_across, to_inside, moist, grad_rows, own, other = call(
             weights_kernel,
             (
                 shape(edge, BF),
                 shape(edge, BF),
                 shape((rows, lon_total), F32),
                 shape(block, F32),
-                shape((near, share_rows, LANES), BF),
+                shape(share, F32),
+                shape(share, BF),
             ),
             10,
             smem=1,
             scratch=[
                 pltpu.VMEM(features_shape, BF),
-                pltpu.VMEM((near, share_rows, LANES), F32),
+                flat_rows,
+                pltpu.VMEM((2,) + share, F32),
             ],
             flops=3_000_000_000,
             vmem=28,
@@ -511,60 +535,52 @@
             w_tendency,
         )
 
+    with jax.named_scope("weights_core"):
+        swap = [(0, 1), (1, 0)]
+        halves = (own + lax.ppermute(other, "core", swap).astype(F32)).astype(BF)
+
     with jax.named_scope("fields"):
         from_across = lax.ppermute(to_across, PLACE, across_swaps)
         from_inside = lax.ppermute(to_inside, PLACE, inside_swaps)
         fields = call(
             fields_kernel,
-            shape((sectors, 2 * rows, LANES), BF),
+            (shape((2 * rows, LANES), BF),) * sectors,
             8,
             smem=1,
+            scratch=[pltpu.VMEM((sectors, 2 * rows, LANES), BF)],
             flops=1_000_000_000,
         )(place, moist, scale, high, low, grad_rows, from_across, from_inside)
 
-    with jax.named_scope("weights_near"):
-        parts = exchange(weights, NEAR)
-        share = call(
-            near_sum_kernel,
-            shape((sectors, piece_rows, LANES), F32),
-            2,
-            scratch=[pltpu.VMEM((share_rows, LANES), F32)],
-        )(parts, fields)
-
-    with jax.named_scope("weights_middle"):
-        piece = jnp.sum(exchange(share, "lon"), 0, keepdims=True).astype(BF)
-        copies = jnp.broadcast_to(piece, (length, piece_rows, LANES))
+    with jax.named_scope("weights_plane"):
+        copies = call(sum_and_copy_kernel, shape((length, piece_rows, LANES), BF), 2)(
+            exchange(halves, PLANE), fields[0]
+        )
+
+    with jax.named_scope("rows_out"):
+        received = [fields[0]]
+        for t in range(1, sectors):
+            received.append(lax.ppermute(fields[t], "lon", [(i, i ^ t) for i in range(sectors)]))
 
     with jax.named_scope("weights_length"):
-        half_rows = whole_multiple(piece_rows, 16)
-        outgoing = call(
-            join_kernel,
-            shape((sectors, 2 * rows + half_rows, LANES), BF),
-            2,
-            scratch=[pltpu.VMEM((half_rows, LANES), F32)],
-        )(exchange(copies, "z"), fields)
-
-    with jax.named_scope("rows_out"):
-        blocks = exchange(outgoing, "lon")
-
-        def by_band(values):
-            values = values.reshape(members, 2, taken, channels, lon_cols).astype(F32)
-            values = jnp.where(band_index % 2 == 1, values[:, ::-1], values)
-            values = jnp.transpose(values, (0, 3, 1, 2, 4))
-            return values.reshape(members, channels, band, lon_cols)
-
-        next_state = by_band(blocks[:, :rows])
-        state_grad = by_band(blocks[:, rows : 2 * rows])
+        copies = call(sum_and_copy_kernel, shape(share, BF), sectors)(
+            exchange(copies, "z"), *received[1:]
+        )
+
+    with jax.named_scope("bands_out"):
+        next_state, state_grad = call(
+            by_band_kernel,
+            (shape(flat, F32), shape(flat, F32)),
+            1 + sectors,
+            smem=1,
+            scratch=[pltpu.VMEM((sectors, 2 * rows, LANES), F32)],
+            band=band,
+        )(place, *received)
+        next_state = next_state.reshape(column_state.shape)
+        state_grad = state_grad.reshape(column_state.shape)
 
     with jax.named_scope("weights_back"):
-        spread = call(
-            spread_kernel,
-            shape((near, share_rows, LANES), BF),
-            1,
-            scratch=[pltpu.VMEM((share_rows, LANES), F32)],
-            start=2 * rows,
-        )(blocks)
-        shares = exchange(spread, NEAR)
+        own = exchange(copies, PLANE)
+        other = lax.ppermute(own, "core", swap)
         columns = members * lax.axis_size("mem") * lat_total * lon_total
         grad_in, grad_bias, grad_out = call(
             unpack_kernel,
@@ -573,10 +589,12 @@
                 shape((hidden_units,), F32),
                 shape((channels, hidden_units), F32),
             ),
-            1,
-            scratch=[pltpu.VMEM((near, share_rows, LANES), F32)],
+            3,
+            smem=1,
+            scratch=[flat_rows],
             scaling=1.0 / math.sqrt(columns),
-        )(shares)
+            sectors=sectors,
+        )(place, own, other)
     return next_state, state_grad, grad_in, grad_bias, grad_out
 
 

time: 127 us -> 123 us (0.969)
  blocking collectives: 38.6 us -> 19.5 us
  starting transfers between devices: 46.4 us -> 63.5 us
  waiting for transfers between devices: 27.5 us -> 25.6 us
  local copies, waits for them, and re-layouts: 1.92 us -> 0.07 us
    all_to_all x3 -> x1, blocking collectives: 38.6 us -> 19.5 us  [exchange(): return lax.all_to_all(x, axes, 0, 0, tiled=True)]
    ppermute x0 -> x5, starting transfers between devices: none -> 18.2 us  [the longest x3 11.4 us: on_device(): lax.ppermute(fields[t], 'lon', [(i, i ^ t) for i in range(sectors)])]
    all_to_all x3, waiting for transfers between devices: 22.4 us -> 14.1 us  [exchange(): return lax.all_to_all(x, axes, 0, 0, tiled=True)]
    ppermute x0 -> x5, waiting for transfers between devices: none -> 5.59 us  [the longest x3 3.64 us: on_device(): lax.ppermute(fields[t], 'lon', [(i, i ^ t) for i in range(sectors)])]
    all_to_all x3, starting transfers between devices: 31.5 us -> 27.4 us  [exchange(): return lax.all_to_all(x, axes, 0, 0, tiled=True)]
    ppermute x1, starting transfers between devices: 1.92 us -> 4.96 us  [on_device(): from_inside = lax.ppermute(to_inside, PLACE, inside_swaps)]
    ppermute x1, waiting for transfers between devices: 3.15 us -> 5.92 us  [on_device(): from_inside = lax.ppermute(to_inside, PLACE, inside_swaps)]
    ppermute x1, waiting for transfers between devices: 2.02 us -> 0.01 us  [on_device(): from_across = lax.ppermute(to_across, PLACE, across_swaps)]
  transfers between devices with their start and end apart: 7 -> 12, of which waited for: 4 -> 5; matrix products, arithmetic and copies ran while one was open for 2% -> 0% of each run, Pallas kernels for 3% -> 4%
where the time goes in v7:
time: 123 us; the launch traced here: 122 us
  starting transfers between devices  63.5 us (52%)
  waiting for transfers between devices  25.6 us (21%)
  blocking collectives  19.5 us (16%)
  Pallas kernels  11.5 us (9%)
    all_to_all x3, starting transfers between devices, exchange(): return lax.all_to_all(x, axes, 0, 0, tiled=True)  27.4 us
    all_to_all x1, blocking collectives, exchange(): return lax.all_to_all(x, axes, 0, 0, tiled=True)  19.5 us
    all_to_all x3, waiting for transfers between devices, exchange(): return lax.all_to_all(x, axes, 0, 0, tiled=True)  14.1 us
    ppermute x3, starting transfers between devices, on_device(): lax.ppermute(fields[t], 'lon', [(i, i ^ t) for i in range(sectors)])  11.4 us
    ppermute x1, waiting for transfers between devices, on_device(): from_inside = lax.ppermute(to_inside, PLACE, inside_swaps)  5.92 us
    ppermute x1, starting transfers between devices, on_device(): inside = lax.ppermute(edge_row(1 - pair), PLACE, inside_swaps)  5.75 us
    ppermute x1, starting transfers between devices, on_device(): across = lax.ppermute(edge_row(pair), PLACE, across_swaps)  5.34 us
    ppermute x1, starting transfers between devices, on_device(): from_inside = lax.ppermute(to_inside, PLACE, inside_swaps)  4.96 us
  transfers between devices with their start and end apart: 12, of which 5 were waited for; matrix products, arithmetic and copies ran while one was open for 0% of the time, Pallas kernels for 4%

profile of v7, /device:TPU:1, one launch (start us, length us, event | category | flops | bytes accessed | tf_op | source)
XLA Modules:
  0.0 122.0 jit_solution(6761779192928458601)
XLA Ops:
  0.6 0.0 copy-start.8
  0.6 0.0 copy-start.6
  0.7 0.0 copy-start.7
  0.7 0.0 copy-start.9
  0.7 0.0 copy-start.1
  0.7 0.0 copy-start
  0.7 0.0 copy-start.2
  0.7 0.0 copy-start.3
  0.7 0.0 copy-start.4
  0.7 0.0 copy-start.5
  0.8 1.9 %rows_in.1 = f32[4,264,128]{2,1,0:T(8,128)} custom-call(s32[1]{0:T(128)} %bitcast.refs_0_, f32[2,256,128]{2,1,0:T(8,128)} %bitcast.5, f32[2,256,128]{2,1,0:T(8,128)} %bitcast.6, s32[4,128]{1,0:T(4,128)} %refs_3_.3, s32[4,128]{1,0:T(4,128)} %refs_4_.3), custom_call_target="tpu_custom_call" | custom-call | bytes 1000000 | tf_op jit(solution)/shard_map/rows_in/pallas_call | solution.py:435
  2.7 7.7 %all-to-all-start = ((f32[4,264,128]{2,1,0:T(8,128)}), f32[4,264,128]{2,1,0:T(8,128)S(1)}, u32[]{:S(2)}, u32[]{:S(2)}) async-start(f32[4,264,128]{2,1,0:T(8,128)} %rows_in.1), calls=%async_computation | async-start | bytes 1081344 | tf_op jit(solution)/shard_map/rows_in/all_to_all | solution.py:401
  10.3 0.0 copy-done.9
  10.3 14.1 %all-to-all-done.refs_2_.refs_3_ = f32[4,264,128]{2,1,0:T(8,128)S(1)} async-done(((f32[4,264,128]{2,1,0:T(8,128)}), f32[4,264,128]{2,1,0:T(8,128)S(1)}, u32[]{:S(2)}, u32[]{:S(2)}) %all-to-all-start) | async-done | bytes 540704 | tf_op jit(solution)/shard_map/rows_in/all_to_all | solution.py:401
  24.4 5.8 %collective-permute-start.1 = (bf16[4,64,128]{2,1,0:T(8,128)(2,1)S(1)}, bf16[4,64,128]{2,1,0:T(8,128)(2,1)S(1)}, u32[]{:S(2)}, u32[]{:S(2)}) collective-permute-start(bf16[4,64,128]{2,1,0:T(8,128)(2,1)S(1)} %get-tuple-element.43), channel_id=1, source_target_pairs={{0,4},{4,0},{8,12},{12,8},{16,20},{20,16},{24,28},{28,24},{32,36},... | collective-permute-start | bytes 196616 | tf_op jit(solution)/shard_map/row_halo/ppermute | solution.py:468
  30.2 5.3 %collective-permute-start = (bf16[4,64,128]{2,1,0:T(8,128)(2,1)S(1)}, bf16[4,64,128]{2,1,0:T(8,128)(2,1)S(1)}, u32[]{:S(2)}, u32[]{:S(2)}) collective-permute-start(bf16[4,64,128]{2,1,0:T(8,128)(2,1)S(1)} %get-tuple-element.44), channel_id=1, source_target_pairs={{4,20},{12,28},{16,32},{20,4},{24,40},{28,12},{32,16},{36,52},{40,... | collective-permute-start | bytes 196616 | tf_op jit(solution)/shard_map/row_halo/ppermute | solution.py:469
  35.5 0.0 copy-done.8
  35.5 0.0 copy-done.6
  35.6 0.0 copy-done.7
  35.6 0.0 copy-done.1
  35.6 0.0 copy-done
  35.6 0.0 copy-done.2
  35.6 0.0 copy-done.3
  35.6 0.0 copy-done.4
  35.6 0.0 copy-done.5
  35.6 2.5 %early.1 = (f32[128,512]{1,0:T(8,128)S(1)}, bf16[2,640,512]{2,1,0:T(8,128)(2,1)S(1)}, f32[2,384,512]{2,1,0:T(8,128)S(1)}, f32[2,384,512]{2,1,0:T(8,128)S(1)}) custom-call(s32[1]{0:T(128)} %bitcast.refs_0_, s32[2]{0:T(128)S(1)} %copy-done.5, f32[4,264,128]{2,1,0:T(8,128)S(1)} %all-to-all-done.refs_2_.refs_3_, f32[192,384]{1,0:T(8,128)S(1)} %copy-done.8, ...), custom_call_target="tpu_custom_call" | custom-call | flops 3000000000 | bytes 1000000 | tf_op jit(solution)/shard_map/early/pallas_call | solution.py:475
  38.1 0.0 collective-permute-done.1.refs_2_
  38.1 0.0 collective-permute-done.refs_1_
  38.1 3.2 %weights.1 = (bf16[4,64,128]{2,1,0:T(8,128)(2,1)S(1)}, bf16[4,64,128]{2,1,0:T(8,128)(2,1)S(1)}, f32[128,512]{1,0:T(8,128)S(1)}, f32[4,128,128]{2,1,0:T(8,128)S(1...) custom-call(s32[1]{0:T(128)} %bitcast.refs_0_, bf16[4,64,128]{2,1,0:T(8,128)(2,1)S(1)} %collective-permute-done.refs_1_, ...), custom_call_target="tpu_custom_call" | custom-call | flops 3000000000 | bytes 1000000 | tf_op jit(solution)/shard_map/weights/pallas_call | solution.py:506
  41.3 1.9 %collective-permute-start.7 = (bf16[32,36,128]{2,1,0:T(8,128)(2,1)S(1)}, bf16[32,36,128]{2,1,0:T(8,128)(2,1)S(1)}, u32[]{:S(2)}, u32[]{:S(2)}) collective-permute-start(bf16[32,36,128]{2,1,0:T(8,128)(2,1)S(1)} %get-tuple-element.39), channel_id=1, source_target_pairs={{0,16},{16,0},{1,17},{17,1},{2,18},{18,2},{3,19},{19,3},{4,20},{20... | collective-permute-start | bytes 884744 | tf_op jit(solution)/shard_map/weights_core/ppermute | solution.py:540
  43.2 1.6 %collective-permute-done.7 = bf16[32,36,128]{2,1,0:T(8,128)(2,1)S(1)} collective-permute-done((bf16[32,36,128]{2,1,0:T(8,128)(2,1)S(1)}, bf16[32,36,128]{2,1,0:T(8,128)(2,1)S(1)}, u32[]{:S(2)}, u32[]{:S(2)}) %collective-permute-start.7) | collective-permute-done | bytes 294944 | tf_op jit(solution)/shard_map/weights_core/ppermute | solution.py:540
  44.8 0.8 add_convert_fusion
  45.6 14.6 %all-to-all-start.1 = ((bf16[32,36,128]{2,1,0:T(8,128)(2,1)}), bf16[32,36,128]{2,1,0:T(8,128)(2,1)S(1)}, u32[]{:S(2)}, u32[]{:S(2)}) async-start(bf16[32,36,128]{2,1,0:T(8,128)(2,1)} %add_convert_fusion), calls=%async_computation.1 | async-start | bytes 655360 | tf_op jit(solution)/shard_map/weights_plane/all_to_all | solution.py:401
  60.3 1.9 %collective-permute-start.2 = (bf16[4,64,128]{2,1,0:T(8,128)(2,1)S(1)}, bf16[4,64,128]{2,1,0:T(8,128)(2,1)S(1)}, u32[]{:S(2)}, u32[]{:S(2)}) collective-permute-start(bf16[4,64,128]{2,1,0:T(8,128)(2,1)S(1)} %get-tuple-element.30), channel_id=1, source_target_pairs={{4,20},{12,28},{16,32},{20,4},{24,40},{28,12},{32,16},{36,52},{40,... | collective-permute-start | bytes 196616 | tf_op jit(solution)/shard_map/fields/ppermute | solution.py:543
  62.2 5.0 %collective-permute-start.3 = (bf16[4,64,128]{2,1,0:T(8,128)(2,1)S(1)}, bf16[4,64,128]{2,1,0:T(8,128)(2,1)S(1)}, u32[]{:S(2)}, u32[]{:S(2)}) collective-permute-start(bf16[4,64,128]{2,1,0:T(8,128)(2,1)S(1)} %get-tuple-element.31), channel_id=1, source_target_pairs={{0,4},{4,0},{8,12},{12,8},{16,20},{20,16},{24,28},{28,24},{32,36},... | collective-permute-start | bytes 196616 | tf_op jit(solution)/shard_map/fields/ppermute | solution.py:544
  67.2 0.0 collective-permute-done.2.refs_6_
  67.2 5.9 %collective-permute-done.3.refs_7_ = bf16[4,64,128]{2,1,0:T(8,128)(2,1)S(1)} collective-permute-done((bf16[4,64,128]{2,1,0:T(8,128)(2,1)S(1)}, bf16[4,64,128]{2,1,0:T(8,128)(2,1)S(1)}, u32[]{:S(2)}, u32[]{:S(2)}) %collective-permute-start.3) | collective-permute-done | bytes 65568 | tf_op jit(solution)/shard_map/fields/ppermute | solution.py:544
  73.1 1.2 fields.1
  74.3 0.0 all-to-all-done.1.refs_0_
  74.3 0.7 weights_plane.1
  75.0 5.1 %all-to-all-start.2 = ((bf16[12,36,128]{2,1,0:T(8,128)(2,1)}), bf16[12,36,128]{2,1,0:T(8,128)(2,1)S(1)}, u32[]{:S(2)}, u32[]{:S(2)}) async-start(bf16[12,36,128]{2,1,0:T(8,128)(2,1)} %weights_plane.1), calls=%async_computation.2 | async-start | bytes 245760 | tf_op jit(solution)/shard_map/weights_length/all_to_all | solution.py:401
  80.1 2.1 %collective-permute-start.4 = (bf16[256,128]{1,0:T(8,128)(2,1)S(1)}, bf16[256,128]{1,0:T(8,128)(2,1)S(1)}, u32[]{:S(2)}, u32[]{:S(2)}) collective-permute-start(bf16[256,128]{1,0:T(8,128)(2,1)S(1)} %get-tuple-element.33), channel_id=1, source_target_pairs={{0,4},{4,0},{8,12},{12,8},{1,5},{5,1},{9,13},{13,9},{2,6},{6,2},{1... | collective-permute-start | bytes 196616 | tf_op jit(solution)/shard_map/rows_out/ppermute | solution.py:562
  82.2 5.8 %collective-permute-start.5 = (bf16[256,128]{1,0:T(8,128)(2,1)S(1)}, bf16[256,128]{1,0:T(8,128)(2,1)S(1)}, u32[]{:S(2)}, u32[]{:S(2)}) collective-permute-start(bf16[256,128]{1,0:T(8,128)(2,1)S(1)} %get-tuple-element.34), channel_id=1, source_target_pairs={{0,8},{4,12},{8,0},{12,4},{1,9},{5,13},{9,1},{13,5},{2,10},{6,14},... | collective-permute-start | bytes 196616 | tf_op jit(solution)/shard_map/rows_out/ppermute | solution.py:562
  88.0 3.5 %collective-permute-start.6 = (bf16[256,128]{1,0:T(8,128)(2,1)S(1)}, bf16[256,128]{1,0:T(8,128)(2,1)S(1)}, u32[]{:S(2)}, u32[]{:S(2)}) collective-permute-start(bf16[256,128]{1,0:T(8,128)(2,1)S(1)} %get-tuple-element.35), channel_id=1, source_target_pairs={{0,12},{4,8},{8,4},{12,0},{1,13},{5,9},{9,5},{13,1},{2,14},{6,10},... | collective-permute-start | bytes 196616 | tf_op jit(solution)/shard_map/rows_out/ppermute | solution.py:562
  91.5 0.0 collective-permute-done.4.refs_2_.refs_1_
  91.5 0.0 collective-permute-done.5.refs_3_.refs_2_
  91.5 3.6 %collective-permute-done.6.refs_4_.refs_3_ = bf16[256,128]{1,0:T(8,128)(2,1)S(1)} collective-permute-done((bf16[256,128]{1,0:T(8,128)(2,1)S(1)}, bf16[256,128]{1,0:T(8,128)(2,1)S(1)}, u32[]{:S(2)}, u32[]{:S(2)}) %collective-permute-start.6) | collective-permute-done | bytes 65568 | tf_op jit(solution)/shard_map/rows_out/ppermute | solution.py:562
  95.2 0.0 all-to-all-done.2.refs_0_
  95.2 19.5 %all_to_all.20.refs_1_ = bf16[32,36,128]{2,1,0:T(8,128)(2,1)S(1)} all-to-all(bf16[32,36,128]{2,1,0:T(8,128)(2,1)S(1)} %weights_length.1), channel_id=1, replica_groups=mesh['ylo'=2,'z'=12,'core'=2,'lon'=4,'mem'=4] {'mem','ylo','lon'}, dimensions={0} | all-to-all | bytes 589824 | tf_op jit(solution)/shard_map/weights_back/all_to_all | solution.py:401
  114.7 4.8 %collective-permute-start.8 = (bf16[32,36,128]{2,1,0:T(8,128)(2,1)S(1)}, bf16[32,36,128]{2,1,0:T(8,128)(2,1)S(1)}, u32[]{:S(2)}, u32[]{:S(2)}) collective-permute-start(bf16[32,36,128]{2,1,0:T(8,128)(2,1)S(1)} %all_to_all.20.refs_1_), channel_id=1, source_target_pairs={{0,16},{16,0},{1,17},{17,1},{2,18},{18,2},{3,19},{19,3},{4,20},{20... | collective-permute-start | bytes 884744 | tf_op jit(solution)/shard_map/weights_back/ppermute | solution.py:583
  119.6 0.9 bands_out.1
  120.5 0.4 collective-permute-done.8.refs_2_
  120.8 1.2 weights_back.1
  (3 shorter events, 0.1 us)
Async XLA Ops:
  0.6 34.9 %copy-start.8 = (f32[192,384]{1,0:T(8,128)S(1)}, f32[192,384]{1,0:T(8,128)}, u32[]{:S(2)}) copy-start(f32[192,384]{1,0:T(8,128)} %constant.71.clone.refs_3_.refs_2_) | copy-start | bytes 884740
  0.6 34.9 %copy-start.6 = (bf16[384,512]{1,0:T(8,128)(2,1)S(1)}, bf16[384,512]{1,0:T(8,128)(2,1)}, u32[]{:S(2)}) copy-start(bf16[384,512]{1,0:T(8,128)(2,1)} %constant.70.clone.refs_5_.refs_4_) | copy-start | bytes 1179652
  0.7 34.9 %copy-start.7 = (bf16[384,512]{1,0:T(8,128)(2,1)S(1)}, bf16[384,512]{1,0:T(8,128)(2,1)}, u32[]{:S(2)}) copy-start(bf16[384,512]{1,0:T(8,128)(2,1)} %constant.69.clone.refs_4_.refs_3_) | copy-start | bytes 1179652
  0.7 9.7 %copy-start.9 = (f32[384]{0:T(512)S(1)}, f32[384]{0:T(512)}, u32[]{:S(2)}) copy-start(f32[384]{0:T(512)} %param.23) | copy-start | bytes 4612
  0.7 34.9 %copy-start.1 = (bf16[64,384]{1,0:T(8,128)(2,1)S(1)}, bf16[64,384]{1,0:T(8,128)(2,1)}, u32[]{:S(2)}) copy-start(bf16[64,384]{1,0:T(8,128)(2,1)} %refs_9_.3) | copy-start | bytes 147460
  0.7 34.9 %copy-start = (bf16[384,640]{1,0:T(8,128)(2,1)S(1)}, bf16[384,640]{1,0:T(8,128)(2,1)}, u32[]{:S(2)}) copy-start(bf16[384,640]{1,0:T(8,128)(2,1)} %refs_8_.3) | copy-start | bytes 1474564
  0.7 34.9 %copy-start.2 = (f32[32,64]{1,0:T(8,128)S(1)}, f32[32,64]{1,0:T(8,128)}, u32[]{:S(2)}) copy-start(f32[32,64]{1,0:T(8,128)} %refs_8_.2) | copy-start | bytes 24580
  0.7 34.9 %copy-start.3 = (f32[16,64]{1,0:T(8,128)S(1)}, f32[16,64]{1,0:T(8,128)}, u32[]{:S(2)}) copy-start(f32[16,64]{1,0:T(8,128)} %refs_7_.1) | copy-start | bytes 12292
  0.7 34.9 %copy-start.4 = (f32[2,64]{1,0:T(2,128)S(1)}, f32[2,64]{1,0:T(2,128)}, u32[]{:S(2)}) copy-start(f32[2,64]{1,0:T(2,128)} %refs_6_.1) | copy-start | bytes 1540
  0.7 34.9 %copy-start.5 = (s32[2]{0:T(128)S(1)}, s32[2]{0:T(128)}, u32[]{:S(2)}) copy-start(s32[2]{0:T(128)} %refs_1_.1) | copy-start | bytes 28
  2.7 21.7 %all-to-all-start = ((f32[4,264,128]{2,1,0:T(8,128)}), f32[4,264,128]{2,1,0:T(8,128)S(1)}, u32[]{:S(2)}, u32[]{:S(2)}) async-start(f32[4,264,128]{2,1,0:T(8,128)} %rows_in.1), calls=%async_computation | async-start | bytes 1081344 | tf_op jit(solution)/shard_map/rows_in/all_to_all | solution.py:401
  24.4 13.7 %collective-permute-start.1 = (bf16[4,64,128]{2,1,0:T(8,128)(2,1)S(1)}, bf16[4,64,128]{2,1,0:T(8,128)(2,1)S(1)}, u32[]{:S(2)}, u32[]{:S(2)}) collective-permute-start(bf16[4,64,128]{2,1,0:T(8,128)(2,1)S(1)} %get-tuple-element.43), channel_id=1, source_target_pairs={{0,4},{4,0},{8,12},{12,8},{16,20},{20,16},{24,28},{28,24},{32,36},... | collective-permute-start | bytes 196616 | tf_op jit(solution)/shard_map/row_halo/ppermute | solution.py:468
  30.2 7.9 %collective-permute-start = (bf16[4,64,128]{2,1,0:T(8,128)(2,1)S(1)}, bf16[4,64,128]{2,1,0:T(8,128)(2,1)S(1)}, u32[]{:S(2)}, u32[]{:S(2)}) collective-permute-start(bf16[4,64,128]{2,1,0:T(8,128)(2,1)S(1)} %get-tuple-element.44), channel_id=1, source_target_pairs={{4,20},{12,28},{16,32},{20,4},{24,40},{28,12},{32,16},{36,52},{40,... | collective-permute-start | bytes 196616 | tf_op jit(solution)/shard_map/row_halo/ppermute | solution.py:469
  41.3 3.5 %collective-permute-start.7 = (bf16[32,36,128]{2,1,0:T(8,128)(2,1)S(1)}, bf16[32,36,128]{2,1,0:T(8,128)(2,1)S(1)}, u32[]{:S(2)}, u32[]{:S(2)}) collective-permute-start(bf16[32,36,128]{2,1,0:T(8,128)(2,1)S(1)} %get-tuple-element.39), channel_id=1, source_target_pairs={{0,16},{16,0},{1,17},{17,1},{2,18},{18,2},{3,19},{19,3},{4,20},{20... | collective-permute-start | bytes 884744 | tf_op jit(solution)/shard_map/weights_core/ppermute | solution.py:540
  45.6 28.7 %all-to-all-start.1 = ((bf16[32,36,128]{2,1,0:T(8,128)(2,1)}), bf16[32,36,128]{2,1,0:T(8,128)(2,1)S(1)}, u32[]{:S(2)}, u32[]{:S(2)}) async-start(bf16[32,36,128]{2,1,0:T(8,128)(2,1)} %add_convert_fusion), calls=%async_computation.1 | async-start | bytes 655360 | tf_op jit(solution)/shard_map/weights_plane/all_to_all | solution.py:401
  60.3 6.9 %collective-permute-start.2 = (bf16[4,64,128]{2,1,0:T(8,128)(2,1)S(1)}, bf16[4,64,128]{2,1,0:T(8,128)(2,1)S(1)}, u32[]{:S(2)}, u32[]{:S(2)}) collective-permute-start(bf16[4,64,128]{2,1,0:T(8,128)(2,1)S(1)} %get-tuple-element.30), channel_id=1, source_target_pairs={{4,20},{12,28},{16,32},{20,4},{24,40},{28,12},{32,16},{36,52},{40,... | collective-permute-start | bytes 196616 | tf_op jit(solution)/shard_map/fields/ppermute | solution.py:543
  62.2 10.9 %collective-permute-start.3 = (bf16[4,64,128]{2,1,0:T(8,128)(2,1)S(1)}, bf16[4,64,128]{2,1,0:T(8,128)(2,1)S(1)}, u32[]{:S(2)}, u32[]{:S(2)}) collective-permute-start(bf16[4,64,128]{2,1,0:T(8,128)(2,1)S(1)} %get-tuple-element.31), channel_id=1, source_target_pairs={{0,4},{4,0},{8,12},{12,8},{16,20},{20,16},{24,28},{28,24},{32,36},... | collective-permute-start | bytes 196616 | tf_op jit(solution)/shard_map/fields/ppermute | solution.py:544
  75.0 20.2 %all-to-all-start.2 = ((bf16[12,36,128]{2,1,0:T(8,128)(2,1)}), bf16[12,36,128]{2,1,0:T(8,128)(2,1)S(1)}, u32[]{:S(2)}, u32[]{:S(2)}) async-start(bf16[12,36,128]{2,1,0:T(8,128)(2,1)} %weights_plane.1), calls=%async_computation.2 | async-start | bytes 245760 | tf_op jit(solution)/shard_map/weights_length/all_to_all | solution.py:401
  80.1 11.4 %collective-permute-start.4 = (bf16[256,128]{1,0:T(8,128)(2,1)S(1)}, bf16[256,128]{1,0:T(8,128)(2,1)S(1)}, u32[]{:S(2)}, u32[]{:S(2)}) collective-permute-start(bf16[256,128]{1,0:T(8,128)(2,1)S(1)} %get-tuple-element.33), channel_id=1, source_target_pairs={{0,4},{4,0},{8,12},{12,8},{1,5},{5,1},{9,13},{13,9},{2,6},{6,2},{1... | collective-permute-start | bytes 196616 | tf_op jit(solution)/shard_map/rows_out/ppermute | solution.py:562
  82.2 9.3 %collective-permute-start.5 = (bf16[256,128]{1,0:T(8,128)(2,1)S(1)}, bf16[256,128]{1,0:T(8,128)(2,1)S(1)}, u32[]{:S(2)}, u32[]{:S(2)}) collective-permute-start(bf16[256,128]{1,0:T(8,128)(2,1)S(1)} %get-tuple-element.34), channel_id=1, source_target_pairs={{0,8},{4,12},{8,0},{12,4},{1,9},{5,13},{9,1},{13,5},{2,10},{6,14},... | collective-permute-start | bytes 196616 | tf_op jit(solution)/shard_map/rows_out/ppermute | solution.py:562
  88.0 7.2 %collective-permute-start.6 = (bf16[256,128]{1,0:T(8,128)(2,1)S(1)}, bf16[256,128]{1,0:T(8,128)(2,1)S(1)}, u32[]{:S(2)}, u32[]{:S(2)}) collective-permute-start(bf16[256,128]{1,0:T(8,128)(2,1)S(1)} %get-tuple-element.35), channel_id=1, source_target_pairs={{0,12},{4,8},{8,4},{12,0},{1,13},{5,9},{9,5},{13,1},{2,14},{6,10},... | collective-permute-start | bytes 196616 | tf_op jit(solution)/shard_map/rows_out/ppermute | solution.py:562
  114.7 6.1 %collective-permute-start.8 = (bf16[32,36,128]{2,1,0:T(8,128)(2,1)S(1)}, bf16[32,36,128]{2,1,0:T(8,128)(2,1)S(1)}, u32[]{:S(2)}, u32[]{:S(2)}) collective-permute-start(bf16[32,36,128]{2,1,0:T(8,128)(2,1)S(1)} %all_to_all.20.refs_1_), channel_id=1, source_target_pairs={{0,16},{16,0},{1,17},{17,1},{2,18},{18,2},{3,19},{19,3},{4,20},{20... | collective-permute-start | bytes 884744 | tf_op jit(solution)/shard_map/weights_back/ppermute | solution.py:583

commit v8 on v7

--- a/solution.py
+++ b/solution.py
@@ -397,6 +397,10 @@
     )
 
 
+def copy_kernel(x_ref, *refs):
+    refs[-1][...] = x_ref[...]
+
+
 def exchange(x, axes):
     return lax.all_to_all(x, axes, 0, 0, tiled=True)
 
@@ -553,7 +557,7 @@
 
     with jax.named_scope("weights_plane"):
         copies = call(sum_and_copy_kernel, shape((length, piece_rows, LANES), BF), 2)(
-            exchange(halves, PLANE), fields[0]
+            exchange(halves, PLANE), from_across
         )
 
     with jax.named_scope("rows_out"):
@@ -562,8 +566,8 @@
             received.append(lax.ppermute(fields[t], "lon", [(i, i ^ t) for i in range(sectors)]))
 
     with jax.named_scope("weights_length"):
-        copies = call(sum_and_copy_kernel, shape(share, BF), sectors)(
-            exchange(copies, "z"), *received[1:]
+        copies = call(sum_and_copy_kernel, shape(share, BF), 2)(
+            exchange(copies, "z"), fields[0]
         )
 
     with jax.named_scope("bands_out"):
@@ -579,7 +583,7 @@
         state_grad = state_grad.reshape(column_state.shape)
 
     with jax.named_scope("weights_back"):
-        own = exchange(copies, PLANE)
+        own = call(copy_kernel, shape(share, BF), sectors)(exchange(copies, PLANE), *received[1:])
         other = lax.ppermute(own, "core", swap)
         columns = members * lax.axis_size("mem") * lat_total * lon_total
         grad_in, grad_bias, grad_out = call(

time: 123 us -> 122 us (level)
  blocking collectives: 19.5 us -> 0 us
  waiting for transfers between devices: 25.6 us -> 34.9 us
  starting transfers between devices: 63.5 us -> 71.9 us
    all_to_all x1 -> x0, blocking collectives: 19.5 us -> none  [exchange(): return lax.all_to_all(x, axes, 0, 0, tiled=True)]
    all_to_all x3 -> x4, waiting for transfers between devices: 14.1 us -> 21.7 us  [exchange(): return lax.all_to_all(x, axes, 0, 0, tiled=True)]
    all_to_all x3 -> x4, starting transfers between devices: 27.4 us -> 33.7 us  [exchange(): return lax.all_to_all(x, axes, 0, 0, tiled=True)]
    ppermute x1, waiting for transfers between devices: 5.92 us -> 1.64 us  [on_device(): from_inside = lax.ppermute(to_inside, PLACE, inside_swaps)]
    ppermute x1, waiting for transfers between devices: 0.01 us -> 3.95 us  [on_device(): from_across = lax.ppermute(to_across, PLACE, across_swaps)]
    ppermute x3, waiting for transfers between devices: 3.64 us -> 5.64 us  [on_device(): lax.ppermute(fields[t], 'lon', [(i, i ^ t) for i in range(sectors)])]
    ppermute x1, starting transfers between devices: 4.85 us -> 6.71 us  [on_device(): other = lax.ppermute(own, 'core', swap)]
  transfers between devices with their start and end apart: 12 -> 13, of which waited for: 5 -> 9; matrix products, arithmetic and copies ran while one was open for 0% -> 0% of each run, Pallas kernels for 4% -> 4%
where the time goes in v8:
time: 122 us; the launch traced here: 121 us
  starting transfers between devices  71.9 us (59%)
  waiting for transfers between devices  34.9 us (29%)
  Pallas kernels  12.3 us (10%)
    all_to_all x4, starting transfers between devices, exchange(): return lax.all_to_all(x, axes, 0, 0, tiled=True)  33.7 us
    all_to_all x4, waiting for transfers between devices, exchange(): return lax.all_to_all(x, axes, 0, 0, tiled=True)  21.7 us
    ppermute x3, starting transfers between devices, on_device(): lax.ppermute(fields[t], 'lon', [(i, i ^ t) for i in range(sectors)])  11.4 us
    ppermute x1, starting transfers between devices, on_device(): other = lax.ppermute(own, 'core', swap)  6.71 us
    ppermute x1, starting transfers between devices, on_device(): inside = lax.ppermute(edge_row(1 - pair), PLACE, inside_swaps)  5.75 us
    ppermute x3, waiting for transfers between devices, on_device(): lax.ppermute(fields[t], 'lon', [(i, i ^ t) for i in range(sectors)])  5.64 us
    ppermute x1, starting transfers between devices, on_device(): across = lax.ppermute(edge_row(pair), PLACE, across_swaps)  5.34 us
    ppermute x1, starting transfers between devices, on_device(): from_inside = lax.ppermute(to_inside, PLACE, inside_swaps)  5.15 us
  transfers between devices with their start and end apart: 13, of which 9 were waited for; matrix products, arithmetic and copies ran while one was open for 0% of the time, Pallas kernels for 4%

profile of v8, /device:TPU:1, one launch (start us, length us, event | category | flops | bytes accessed | tf_op | source)
XLA Modules:
  0.0 121.0 jit_solution(11139646093435132656)
XLA Ops:
  0.6 0.0 copy-start.8
  0.6 0.0 copy-start.6
  0.7 0.0 copy-start.7
  0.7 0.0 copy-start.9
  0.7 0.0 copy-start.1
  0.7 0.0 copy-start
  0.7 0.0 copy-start.2
  0.7 0.0 copy-start.3
  0.7 0.0 copy-start.4
  0.7 0.0 copy-start.5
  0.8 1.9 %rows_in.1 = f32[4,264,128]{2,1,0:T(8,128)} custom-call(s32[1]{0:T(128)} %bitcast.refs_0_, f32[2,256,128]{2,1,0:T(8,128)} %bitcast.5, f32[2,256,128]{2,1,0:T(8,128)} %bitcast.6, s32[4,128]{1,0:T(4,128)} %refs_3_.3, s32[4,128]{1,0:T(4,128)} %refs_4_.3), custom_call_target="tpu_custom_call" | custom-call | bytes 1000000 | tf_op jit(solution)/shard_map/rows_in/pallas_call | solution.py:439
  2.7 7.7 %all-to-all-start = ((f32[4,264,128]{2,1,0:T(8,128)}), f32[4,264,128]{2,1,0:T(8,128)S(1)}, u32[]{:S(2)}, u32[]{:S(2)}) async-start(f32[4,264,128]{2,1,0:T(8,128)} %rows_in.1), calls=%async_computation | async-start | bytes 1081344 | tf_op jit(solution)/shard_map/rows_in/all_to_all | solution.py:405
  10.3 0.0 copy-done.9
  10.3 14.1 %all-to-all-done.refs_2_.refs_3_ = f32[4,264,128]{2,1,0:T(8,128)S(1)} async-done(((f32[4,264,128]{2,1,0:T(8,128)}), f32[4,264,128]{2,1,0:T(8,128)S(1)}, u32[]{:S(2)}, u32[]{:S(2)}) %all-to-all-start) | async-done | bytes 540704 | tf_op jit(solution)/shard_map/rows_in/all_to_all | solution.py:405
  24.4 5.8 %collective-permute-start.1 = (bf16[4,64,128]{2,1,0:T(8,128)(2,1)S(1)}, bf16[4,64,128]{2,1,0:T(8,128)(2,1)S(1)}, u32[]{:S(2)}, u32[]{:S(2)}) collective-permute-start(bf16[4,64,128]{2,1,0:T(8,128)(2,1)S(1)} %get-tuple-element.43), channel_id=1, source_target_pairs={{0,4},{4,0},{8,12},{12,8},{16,20},{20,16},{24,28},{28,24},{32,36},... | collective-permute-start | bytes 196616 | tf_op jit(solution)/shard_map/row_halo/ppermute | solution.py:472
  30.2 5.3 %collective-permute-start = (bf16[4,64,128]{2,1,0:T(8,128)(2,1)S(1)}, bf16[4,64,128]{2,1,0:T(8,128)(2,1)S(1)}, u32[]{:S(2)}, u32[]{:S(2)}) collective-permute-start(bf16[4,64,128]{2,1,0:T(8,128)(2,1)S(1)} %get-tuple-element.44), channel_id=1, source_target_pairs={{4,20},{12,28},{16,32},{20,4},{24,40},{28,12},{32,16},{36,52},{40,... | collective-permute-start | bytes 196616 | tf_op jit(solution)/shard_map/row_halo/ppermute | solution.py:473
  35.5 0.0 copy-done.8
  35.5 0.0 copy-done.6
  35.6 0.0 copy-done.7
  35.6 0.0 copy-done.1
  35.6 0.0 copy-done
  35.6 0.0 copy-done.2
  35.6 0.0 copy-done.3
  35.6 0.0 copy-done.4
  35.6 0.0 copy-done.5
  35.6 2.5 %early.1 = (f32[128,512]{1,0:T(8,128)S(1)}, bf16[2,640,512]{2,1,0:T(8,128)(2,1)S(1)}, f32[2,384,512]{2,1,0:T(8,128)S(1)}, f32[2,384,512]{2,1,0:T(8,128)S(1)}) custom-call(s32[1]{0:T(128)} %bitcast.refs_0_, s32[2]{0:T(128)S(1)} %copy-done.5, f32[4,264,128]{2,1,0:T(8,128)S(1)} %all-to-all-done.refs_2_.refs_3_, f32[192,384]{1,0:T(8,128)S(1)} %copy-done.8, ...), custom_call_target="tpu_custom_call" | custom-call | flops 3000000000 | bytes 1000000 | tf_op jit(solution)/shard_map/early/pallas_call | solution.py:479
  38.1 0.0 collective-permute-done.1.refs_2_
  38.1 0.0 collective-permute-done.refs_1_
  38.1 3.2 %weights.1 = (bf16[4,64,128]{2,1,0:T(8,128)(2,1)S(1)}, bf16[4,64,128]{2,1,0:T(8,128)(2,1)S(1)}, f32[128,512]{1,0:T(8,128)S(1)}, f32[4,128,128]{2,1,0:T(8,128)S(1...) custom-call(s32[1]{0:T(128)} %bitcast.refs_0_, bf16[4,64,128]{2,1,0:T(8,128)(2,1)S(1)} %collective-permute-done.refs_1_, ...), custom_call_target="tpu_custom_call" | custom-call | flops 3000000000 | bytes 1000000 | tf_op jit(solution)/shard_map/weights/pallas_call | solution.py:510
  41.4 1.9 %collective-permute-start.7 = (bf16[32,36,128]{2,1,0:T(8,128)(2,1)S(1)}, bf16[32,36,128]{2,1,0:T(8,128)(2,1)S(1)}, u32[]{:S(2)}, u32[]{:S(2)}) collective-permute-start(bf16[32,36,128]{2,1,0:T(8,128)(2,1)S(1)} %get-tuple-element.39), channel_id=1, source_target_pairs={{0,16},{16,0},{1,17},{17,1},{2,18},{18,2},{3,19},{19,3},{4,20},{20... | collective-permute-start | bytes 884744 | tf_op jit(solution)/shard_map/weights_core/ppermute | solution.py:544
  43.3 1.6 %collective-permute-done.7 = bf16[32,36,128]{2,1,0:T(8,128)(2,1)S(1)} collective-permute-done((bf16[32,36,128]{2,1,0:T(8,128)(2,1)S(1)}, bf16[32,36,128]{2,1,0:T(8,128)(2,1)S(1)}, u32[]{:S(2)}, u32[]{:S(2)}) %collective-permute-start.7) | collective-permute-done | bytes 294944 | tf_op jit(solution)/shard_map/weights_core/ppermute | solution.py:544
  44.9 0.8 add_convert_fusion
  45.7 14.6 %all-to-all-start.1 = ((bf16[32,36,128]{2,1,0:T(8,128)(2,1)}), bf16[32,36,128]{2,1,0:T(8,128)(2,1)S(1)}, u32[]{:S(2)}, u32[]{:S(2)}) async-start(bf16[32,36,128]{2,1,0:T(8,128)(2,1)} %add_convert_fusion), calls=%async_computation.1 | async-start | bytes 655360 | tf_op jit(solution)/shard_map/weights_plane/all_to_all | solution.py:405
  60.4 1.9 %collective-permute-start.2 = (bf16[4,64,128]{2,1,0:T(8,128)(2,1)S(1)}, bf16[4,64,128]{2,1,0:T(8,128)(2,1)S(1)}, u32[]{:S(2)}, u32[]{:S(2)}) collective-permute-start(bf16[4,64,128]{2,1,0:T(8,128)(2,1)S(1)} %get-tuple-element.30), channel_id=1, source_target_pairs={{4,20},{12,28},{16,32},{20,4},{24,40},{28,12},{32,16},{36,52},{40,... | collective-permute-start | bytes 196616 | tf_op jit(solution)/shard_map/fields/ppermute | solution.py:547
  62.3 4.0 %collective-permute-done.2.refs_6_.refs_1_ = bf16[4,64,128]{2,1,0:T(8,128)(2,1)S(1)} collective-permute-done((bf16[4,64,128]{2,1,0:T(8,128)(2,1)S(1)}, bf16[4,64,128]{2,1,0:T(8,128)(2,1)S(1)}, u32[]{:S(2)}, u32[]{:S(2)}) %collective-permute-start.2) | collective-permute-done | bytes 65568 | tf_op jit(solution)/shard_map/fields/ppermute | solution.py:547
  66.2 5.2 %all-to-all-done.1.refs_0_ = bf16[32,36,128]{2,1,0:T(8,128)(2,1)S(1)} async-done(((bf16[32,36,128]{2,1,0:T(8,128)(2,1)}), bf16[32,36,128]{2,1,0:T(8,128)(2,1)S(1)}, u32[]{:S(2)}, u32[]{:S(2)}) %all-to-all-start.1) | async-done | bytes 294944 | tf_op jit(solution)/shard_map/weights_plane/all_to_all | solution.py:405
  71.4 0.7 weights_plane.1
  72.2 4.9 %all-to-all-start.2 = ((bf16[12,36,128]{2,1,0:T(8,128)(2,1)}), bf16[12,36,128]{2,1,0:T(8,128)(2,1)S(1)}, u32[]{:S(2)}, u32[]{:S(2)}) async-start(bf16[12,36,128]{2,1,0:T(8,128)(2,1)} %weights_plane.1), calls=%async_computation.2 | async-start | bytes 245760 | tf_op jit(solution)/shard_map/weights_length/all_to_all | solution.py:405
  77.1 5.2 %collective-permute-start.3 = (bf16[4,64,128]{2,1,0:T(8,128)(2,1)S(1)}, bf16[4,64,128]{2,1,0:T(8,128)(2,1)S(1)}, u32[]{:S(2)}, u32[]{:S(2)}) collective-permute-start(bf16[4,64,128]{2,1,0:T(8,128)(2,1)S(1)} %get-tuple-element.31), channel_id=1, source_target_pairs={{0,4},{4,0},{8,12},{12,8},{16,20},{20,16},{24,28},{28,24},{32,36},... | collective-permute-start | bytes 196616 | tf_op jit(solution)/shard_map/fields/ppermute | solution.py:548
  82.2 1.6 %collective-permute-done.3.refs_7_ = bf16[4,64,128]{2,1,0:T(8,128)(2,1)S(1)} collective-permute-done((bf16[4,64,128]{2,1,0:T(8,128)(2,1)S(1)}, bf16[4,64,128]{2,1,0:T(8,128)(2,1)S(1)}, u32[]{:S(2)}, u32[]{:S(2)}) %collective-permute-start.3) | collective-permute-done | bytes 65568 | tf_op jit(solution)/shard_map/fields/ppermute | solution.py:548
  83.9 1.2 fields.1
  85.1 2.5 %all-to-all-done.2.refs_0_ = bf16[12,36,128]{2,1,0:T(8,128)(2,1)S(1)} async-done(((bf16[12,36,128]{2,1,0:T(8,128)(2,1)}), bf16[12,36,128]{2,1,0:T(8,128)(2,1)S(1)}, u32[]{:S(2)}, u32[]{:S(2)}) %all-to-all-start.2) | async-done | bytes 110624 | tf_op jit(solution)/shard_map/weights_length/all_to_all | solution.py:405
  87.5 0.8 weights_length.1
  88.3 6.5 %all-to-all-start.3 = ((bf16[32,36,128]{2,1,0:T(8,128)(2,1)}), bf16[32,36,128]{2,1,0:T(8,128)(2,1)S(1)}, u32[]{:S(2)}, u32[]{:S(2)}) async-start(bf16[32,36,128]{2,1,0:T(8,128)(2,1)} %weights_length.1), calls=%async_computation.3 | async-start | bytes 655360 | tf_op jit(solution)/shard_map/weights_back/all_to_all | solution.py:405
  94.8 4.0 %collective-permute-start.4 = (bf16[256,128]{1,0:T(8,128)(2,1)S(1)}, bf16[256,128]{1,0:T(8,128)(2,1)S(1)}, u32[]{:S(2)}, u32[]{:S(2)}) collective-permute-start(bf16[256,128]{1,0:T(8,128)(2,1)S(1)} %get-tuple-element.33), channel_id=1, source_target_pairs={{0,4},{4,0},{8,12},{12,8},{1,5},{5,1},{9,13},{13,9},{2,6},{6,2},{1... | collective-permute-start | bytes 196616 | tf_op jit(solution)/shard_map/rows_out/ppermute | solution.py:566
  98.8 5.2 %collective-permute-start.5 = (bf16[256,128]{1,0:T(8,128)(2,1)S(1)}, bf16[256,128]{1,0:T(8,128)(2,1)S(1)}, u32[]{:S(2)}, u32[]{:S(2)}) collective-permute-start(bf16[256,128]{1,0:T(8,128)(2,1)S(1)} %get-tuple-element.34), channel_id=1, source_target_pairs={{0,8},{4,12},{8,0},{12,4},{1,9},{5,13},{9,1},{13,5},{2,10},{6,14},... | collective-permute-start | bytes 196616 | tf_op jit(solution)/shard_map/rows_out/ppermute | solution.py:566
  104.0 2.1 %collective-permute-start.6 = (bf16[256,128]{1,0:T(8,128)(2,1)S(1)}, bf16[256,128]{1,0:T(8,128)(2,1)S(1)}, u32[]{:S(2)}, u32[]{:S(2)}) collective-permute-start(bf16[256,128]{1,0:T(8,128)(2,1)S(1)} %get-tuple-element.35), channel_id=1, source_target_pairs={{0,12},{4,8},{8,4},{12,0},{1,13},{5,9},{9,5},{13,1},{2,14},{6,10},... | collective-permute-start | bytes 196616 | tf_op jit(solution)/shard_map/rows_out/ppermute | solution.py:566
  106.2 0.0 collective-permute-done.4.refs_2_.refs_1_
  106.2 3.0 %collective-permute-done.5.refs_3_.refs_2_ = bf16[256,128]{1,0:T(8,128)(2,1)S(1)} collective-permute-done((bf16[256,128]{1,0:T(8,128)(2,1)S(1)}, bf16[256,128]{1,0:T(8,128)(2,1)S(1)}, u32[]{:S(2)}, u32[]{:S(2)}) %collective-permute-start.5) | collective-permute-done | bytes 65568 | tf_op jit(solution)/shard_map/rows_out/ppermute | solution.py:566
  109.2 2.7 %collective-permute-done.6.refs_4_.refs_3_ = bf16[256,128]{1,0:T(8,128)(2,1)S(1)} collective-permute-done((bf16[256,128]{1,0:T(8,128)(2,1)S(1)}, bf16[256,128]{1,0:T(8,128)(2,1)S(1)}, u32[]{:S(2)}, u32[]{:S(2)}) %collective-permute-start.6) | collective-permute-done | bytes 65568 | tf_op jit(solution)/shard_map/rows_out/ppermute | solution.py:566
  111.8 0.0 all-to-all-done.3.refs_0_
  111.9 6.7 %collective-permute-start.8 = (bf16[32,36,128]{2,1,0:T(8,128)(2,1)S(1)}, bf16[32,36,128]{2,1,0:T(8,128)(2,1)S(1)}, u32[]{:S(2)}, u32[]{:S(2)}) collective-permute-start(bf16[32,36,128]{2,1,0:T(8,128)(2,1)S(1)} %weights_back.2.refs_1_), channel_id=1, source_target_pairs={{0,16},{16,0},{1,17},{17,1},{2,18},{18,2},{3,19},{19,3},{4,20},{20... | collective-permute-start | bytes 884744 | tf_op jit(solution)/shard_map/weights_back/ppermute | solution.py:587
  118.6 0.9 bands_out.1
  119.5 0.4 collective-permute-done.8.refs_2_
  119.8 1.2 weights_back.3
  (3 shorter events, 0.0 us)
Async XLA Ops:
  0.6 34.9 %copy-start.8 = (f32[192,384]{1,0:T(8,128)S(1)}, f32[192,384]{1,0:T(8,128)}, u32[]{:S(2)}) copy-start(f32[192,384]{1,0:T(8,128)} %constant.71.clone.refs_3_.refs_2_) | copy-start | bytes 884740
  0.6 34.9 %copy-start.6 = (bf16[384,512]{1,0:T(8,128)(2,1)S(1)}, bf16[384,512]{1,0:T(8,128)(2,1)}, u32[]{:S(2)}) copy-start(bf16[384,512]{1,0:T(8,128)(2,1)} %constant.70.clone.refs_5_.refs_4_) | copy-start | bytes 1179652
  0.7 34.9 %copy-start.7 = (bf16[384,512]{1,0:T(8,128)(2,1)S(1)}, bf16[384,512]{1,0:T(8,128)(2,1)}, u32[]{:S(2)}) copy-start(bf16[384,512]{1,0:T(8,128)(2,1)} %constant.69.clone.refs_4_.refs_3_) | copy-start | bytes 1179652
  0.7 9.7 %copy-start.9 = (f32[384]{0:T(512)S(1)}, f32[384]{0:T(512)}, u32[]{:S(2)}) copy-start(f32[384]{0:T(512)} %param.23) | copy-start | bytes 4612
  0.7 34.9 %copy-start.1 = (bf16[64,384]{1,0:T(8,128)(2,1)S(1)}, bf16[64,384]{1,0:T(8,128)(2,1)}, u32[]{:S(2)}) copy-start(bf16[64,384]{1,0:T(8,128)(2,1)} %refs_9_.3) | copy-start | bytes 147460
  0.7 34.9 %copy-start = (bf16[384,640]{1,0:T(8,128)(2,1)S(1)}, bf16[384,640]{1,0:T(8,128)(2,1)}, u32[]{:S(2)}) copy-start(bf16[384,640]{1,0:T(8,128)(2,1)} %refs_8_.3) | copy-start | bytes 1474564
  0.7 34.9 %copy-start.2 = (f32[32,64]{1,0:T(8,128)S(1)}, f32[32,64]{1,0:T(8,128)}, u32[]{:S(2)}) copy-start(f32[32,64]{1,0:T(8,128)} %refs_8_.2) | copy-start | bytes 24580
  0.7 34.9 %copy-start.3 = (f32[16,64]{1,0:T(8,128)S(1)}, f32[16,64]{1,0:T(8,128)}, u32[]{:S(2)}) copy-start(f32[16,64]{1,0:T(8,128)} %refs_7_.1) | copy-start | bytes 12292
  0.7 34.9 %copy-start.4 = (f32[2,64]{1,0:T(2,128)S(1)}, f32[2,64]{1,0:T(2,128)}, u32[]{:S(2)}) copy-start(f32[2,64]{1,0:T(2,128)} %refs_6_.1) | copy-start | bytes 1540
  0.7 34.9 %copy-start.5 = (s32[2]{0:T(128)S(1)}, s32[2]{0:T(128)}, u32[]{:S(2)}) copy-start(s32[2]{0:T(128)} %refs_1_.1) | copy-start | bytes 28
  2.7 21.7 %all-to-all-start = ((f32[4,264,128]{2,1,0:T(8,128)}), f32[4,264,128]{2,1,0:T(8,128)S(1)}, u32[]{:S(2)}, u32[]{:S(2)}) async-start(f32[4,264,128]{2,1,0:T(8,128)} %rows_in.1), calls=%async_computation | async-start | bytes 1081344 | tf_op jit(solution)/shard_map/rows_in/all_to_all | solution.py:405
  24.4 13.7 %collective-permute-start.1 = (bf16[4,64,128]{2,1,0:T(8,128)(2,1)S(1)}, bf16[4,64,128]{2,1,0:T(8,128)(2,1)S(1)}, u32[]{:S(2)}, u32[]{:S(2)}) collective-permute-start(bf16[4,64,128]{2,1,0:T(8,128)(2,1)S(1)} %get-tuple-element.43), channel_id=1, source_target_pairs={{0,4},{4,0},{8,12},{12,8},{16,20},{20,16},{24,28},{28,24},{32,36},... | collective-permute-start | bytes 196616 | tf_op jit(solution)/shard_map/row_halo/ppermute | solution.py:472
  30.2 7.9 %collective-permute-start = (bf16[4,64,128]{2,1,0:T(8,128)(2,1)S(1)}, bf16[4,64,128]{2,1,0:T(8,128)(2,1)S(1)}, u32[]{:S(2)}, u32[]{:S(2)}) collective-permute-start(bf16[4,64,128]{2,1,0:T(8,128)(2,1)S(1)} %get-tuple-element.44), channel_id=1, source_target_pairs={{4,20},{12,28},{16,32},{20,4},{24,40},{28,12},{32,16},{36,52},{40,... | collective-permute-start | bytes 196616 | tf_op jit(solution)/shard_map/row_halo/ppermute | solution.py:473
  41.4 3.5 %collective-permute-start.7 = (bf16[32,36,128]{2,1,0:T(8,128)(2,1)S(1)}, bf16[32,36,128]{2,1,0:T(8,128)(2,1)S(1)}, u32[]{:S(2)}, u32[]{:S(2)}) collective-permute-start(bf16[32,36,128]{2,1,0:T(8,128)(2,1)S(1)} %get-tuple-element.39), channel_id=1, source_target_pairs={{0,16},{16,0},{1,17},{17,1},{2,18},{18,2},{3,19},{19,3},{4,20},{20... | collective-permute-start | bytes 884744 | tf_op jit(solution)/shard_map/weights_core/ppermute | solution.py:544
  45.7 25.7 %all-to-all-start.1 = ((bf16[32,36,128]{2,1,0:T(8,128)(2,1)}), bf16[32,36,128]{2,1,0:T(8,128)(2,1)S(1)}, u32[]{:S(2)}, u32[]{:S(2)}) async-start(bf16[32,36,128]{2,1,0:T(8,128)(2,1)} %add_convert_fusion), calls=%async_computation.1 | async-start | bytes 655360 | tf_op jit(solution)/shard_map/weights_plane/all_to_all | solution.py:405
  60.4 5.9 %collective-permute-start.2 = (bf16[4,64,128]{2,1,0:T(8,128)(2,1)S(1)}, bf16[4,64,128]{2,1,0:T(8,128)(2,1)S(1)}, u32[]{:S(2)}, u32[]{:S(2)}) collective-permute-start(bf16[4,64,128]{2,1,0:T(8,128)(2,1)S(1)} %get-tuple-element.30), channel_id=1, source_target_pairs={{4,20},{12,28},{16,32},{20,4},{24,40},{28,12},{32,16},{36,52},{40,... | collective-permute-start | bytes 196616 | tf_op jit(solution)/shard_map/fields/ppermute | solution.py:547
  72.2 15.4 %all-to-all-start.2 = ((bf16[12,36,128]{2,1,0:T(8,128)(2,1)}), bf16[12,36,128]{2,1,0:T(8,128)(2,1)S(1)}, u32[]{:S(2)}, u32[]{:S(2)}) async-start(bf16[12,36,128]{2,1,0:T(8,128)(2,1)} %weights_plane.1), calls=%async_computation.2 | async-start | bytes 245760 | tf_op jit(solution)/shard_map/weights_length/all_to_all | solution.py:405
  77.1 6.8 %collective-permute-start.3 = (bf16[4,64,128]{2,1,0:T(8,128)(2,1)S(1)}, bf16[4,64,128]{2,1,0:T(8,128)(2,1)S(1)}, u32[]{:S(2)}, u32[]{:S(2)}) collective-permute-start(bf16[4,64,128]{2,1,0:T(8,128)(2,1)S(1)} %get-tuple-element.31), channel_id=1, source_target_pairs={{0,4},{4,0},{8,12},{12,8},{16,20},{20,16},{24,28},{28,24},{32,36},... | collective-permute-start | bytes 196616 | tf_op jit(solution)/shard_map/fields/ppermute | solution.py:548
  88.3 23.5 %all-to-all-start.3 = ((bf16[32,36,128]{2,1,0:T(8,128)(2,1)}), bf16[32,36,128]{2,1,0:T(8,128)(2,1)S(1)}, u32[]{:S(2)}, u32[]{:S(2)}) async-start(bf16[32,36,128]{2,1,0:T(8,128)(2,1)} %weights_length.1), calls=%async_computation.3 | async-start | bytes 655360 | tf_op jit(solution)/shard_map/weights_back/all_to_all | solution.py:405
  94.8 11.4 %collective-permute-start.4 = (bf16[256,128]{1,0:T(8,128)(2,1)S(1)}, bf16[256,128]{1,0:T(8,128)(2,1)S(1)}, u32[]{:S(2)}, u32[]{:S(2)}) collective-permute-start(bf16[256,128]{1,0:T(8,128)(2,1)S(1)} %get-tuple-element.33), channel_id=1, source_target_pairs={{0,4},{4,0},{8,12},{12,8},{1,5},{5,1},{9,13},{13,9},{2,6},{6,2},{1... | collective-permute-start | bytes 196616 | tf_op jit(solution)/shard_map/rows_out/ppermute | solution.py:566
  98.8 10.4 %collective-permute-start.5 = (bf16[256,128]{1,0:T(8,128)(2,1)S(1)}, bf16[256,128]{1,0:T(8,128)(2,1)S(1)}, u32[]{:S(2)}, u32[]{:S(2)}) collective-permute-start(bf16[256,128]{1,0:T(8,128)(2,1)S(1)} %get-tuple-element.34), channel_id=1, source_target_pairs={{0,8},{4,12},{8,0},{12,4},{1,9},{5,13},{9,1},{13,5},{2,10},{6,14},... | collective-permute-start | bytes 196616 | tf_op jit(solution)/shard_map/rows_out/ppermute | solution.py:566
  104.0 7.8 %collective-permute-start.6 = (bf16[256,128]{1,0:T(8,128)(2,1)S(1)}, bf16[256,128]{1,0:T(8,128)(2,1)S(1)}, u32[]{:S(2)}, u32[]{:S(2)}) collective-permute-start(bf16[256,128]{1,0:T(8,128)(2,1)S(1)} %get-tuple-element.35), channel_id=1, source_target_pairs={{0,12},{4,8},{8,4},{12,0},{1,13},{5,9},{9,5},{13,1},{2,14},{6,10},... | collective-permute-start | bytes 196616 | tf_op jit(solution)/shard_map/rows_out/ppermute | solution.py:566
  111.9 8.0 %collective-permute-start.8 = (bf16[32,36,128]{2,1,0:T(8,128)(2,1)S(1)}, bf16[32,36,128]{2,1,0:T(8,128)(2,1)S(1)}, u32[]{:S(2)}, u32[]{:S(2)}) collective-permute-start(bf16[32,36,128]{2,1,0:T(8,128)(2,1)S(1)} %weights_back.2.refs_1_), channel_id=1, source_target_pairs={{0,16},{16,0},{1,17},{17,1},{2,18},{18,2},{3,19},{19,3},{4,20},{20... | collective-permute-start | bytes 884744 | tf_op jit(solution)/shard_map/weights_back/ppermute | solution.py:587

commit v9 on v8

--- a/solution.py
+++ b/solution.py
@@ -78,14 +78,6 @@
     place_ref, state_hbm, cotangent_hbm, land_hbm, orography_hbm, out_hbm,
     state_ref, cotangent_ref, land_ref, orography_ref, out_ref, sems, *, classes
 ):
-    sources = (state_hbm, cotangent_hbm, land_hbm, orography_hbm)
-    targets = (state_ref, cotangent_ref, land_ref, orography_ref)
-    moves = [
-        pltpu.make_async_copy(source, target, sems.at[i])
-        for i, (source, target) in enumerate(zip(sources, targets))
-    ]
-    for move in moves:
-        move.start()
     sectors, packed_rows = out_ref.shape[:2]
     rows = (packed_rows - 8) // 2
     members = state_ref.shape[0]
@@ -93,32 +85,41 @@
     taken = band * members // sectors
     channels = rows // taken
     odd = place_ref[0] // sectors % 2
+    fields = ((state_hbm, state_ref), (cotangent_hbm, cotangent_ref))
+    parts = [(source.at[m], target.at[m]) for source, target in fields for m in range(members)]
+    parts += [(land_hbm, land_ref), (orography_hbm, orography_ref)]
+    moves = [
+        pltpu.make_async_copy(source, target, sems.at[i])
+        for i, (source, target) in enumerate(parts)
+    ]
+    for move in moves:
+        move.start()
     leaving = []
-    for i in range(2):
-        moves[i].wait()
-        if i == 1:
-            moves[2].wait()
-            moves[3].wait()
+    for n in range(2 * members):
+        i, m = n // members, n % members
+        moves[n].wait()
+        if n == members:
+            moves[-2].wait()
+            moves[-1].wait()
             code = (jnp.where(land_ref[...] == 1, classes, 0) + orography_ref[...]).astype(F32)
-        for m in range(members):
-            for pair in range(2):
-                q = 2 * m + (pair + odd) % 2
-                first = pair * taken
-                for k in range(taken):
-                    start = i * rows + k * channels
-                    out_ref[q, start : start + channels, :] = targets[i][
-                        m, pl.ds(first + k, channels, stride=band), :
-                    ]
-                if i == 1:
-                    spare = jnp.zeros((8 - taken, LANES), F32)
-                    out_ref[q, 2 * rows :, :] = jnp.concatenate(
-                        [code[first : first + taken], spare], axis=0
-                    )
-        part = pl.ds(i * rows, rows if i == 0 else rows + 8)
+        for pair in range(2):
+            q = 2 * m + (pair + odd) % 2
+            first = pair * taken
+            for k in range(taken):
+                start = i * rows + k * channels
+                out_ref[q, start : start + channels, :] = fields[i][1][
+                    m, pl.ds(first + k, channels, stride=band), :
+                ]
+            if i == 1:
+                spare = jnp.zeros((8 - taken, LANES), F32)
+                out_ref[q, 2 * rows :, :] = jnp.concatenate(
+                    [code[first : first + taken], spare], axis=0
+                )
+        part = (pl.ds(2 * m, 2), pl.ds(i * rows, rows if i == 0 else rows + 8))
         leaving.append(
-            pltpu.make_async_copy(out_ref.at[:, part], out_hbm.at[:, part], sems.at[4 + i])
+            pltpu.make_async_copy(out_ref.at[part], out_hbm.at[part], sems.at[len(parts) + n])
         )
-        leaving[i].start()
+        leaving[n].start()
     for move in leaving:
         move.wait()
 
@@ -447,7 +448,7 @@
                 pltpu.VMEM(land_mask.shape, land_mask.dtype),
                 pltpu.VMEM(orography.shape, orography.dtype),
                 pltpu.VMEM(packed_shape, F32),
-                pltpu.SemaphoreType.DMA((6,)),
+                pltpu.SemaphoreType.DMA((4 * members + 2,)),
             ],
             vmem=56,
             inputs_in=pltpu.HBM,
@@ -556,8 +557,8 @@
         )(place, moist, scale, high, low, grad_rows, from_across, from_inside)
 
     with jax.named_scope("weights_plane"):
-        copies = call(sum_and_copy_kernel, shape((length, piece_rows, LANES), BF), 2)(
-            exchange(halves, PLANE), from_across
+        copies = call(sum_and_copy_kernel, shape((length, piece_rows, LANES), BF), 3)(
+            exchange(halves, PLANE), from_across, from_inside
         )
 
     with jax.named_scope("rows_out"):
@@ -567,7 +568,7 @@
 
     with jax.named_scope("weights_length"):
         copies = call(sum_and_copy_kernel, shape(share, BF), 2)(
-            exchange(copies, "z"), fields[0]
+            exchange(copies, "z"), received[1]
         )
 
     with jax.named_scope("bands_out"):
@@ -583,7 +584,7 @@
         state_grad = state_grad.reshape(column_state.shape)
 
     with jax.named_scope("weights_back"):
-        own = call(copy_kernel, shape(share, BF), sectors)(exchange(copies, PLANE), *received[1:])
+        own = call(copy_kernel, shape(share, BF), sectors - 1)(exchange(copies, PLANE), *received[2:])
         other = lax.ppermute(own, "core", swap)
         columns = members * lax.axis_size("mem") * lat_total * lon_total
         grad_in, grad_bias, grad_out = call(

time: 122 us -> 122 us (level)
  waiting for transfers between devices: 34.9 us -> 33.6 us
    all_to_all x4, waiting for transfers between devices: 21.7 us -> 16.9 us  [exchange(): return lax.all_to_all(x, axes, 0, 0, tiled=True)]
    ppermute x1, waiting for transfers between devices: 1.64 us -> 5.93 us  [on_device(): from_inside = lax.ppermute(to_inside, PLACE, inside_swaps)]
    ppermute x1, waiting for transfers between devices: 3.95 us -> 0.01 us  [on_device(): from_across = lax.ppermute(to_across, PLACE, across_swaps)]
    ppermute x3, waiting for transfers between devices: 5.64 us -> 8.87 us  [on_device(): lax.ppermute(fields[t], 'lon', [(i, i ^ t) for i in range(sectors)])]
    all_to_all x4, starting transfers between devices: 33.7 us -> 35 us  [exchange(): return lax.all_to_all(x, axes, 0, 0, tiled=True)]
  transfers between devices with their start and end apart: 13 -> 13, of which waited for: 9 -> 8; matrix products, arithmetic and copies ran while one was open for 0% -> 0% of each run, Pallas kernels for 4% -> 4%
where the time goes in v9:
time: 122 us; the launch traced here: 121 us
  starting transfers between devices  73 us (60%)
  waiting for transfers between devices  33.6 us (28%)
  Pallas kernels  12.4 us (10%)
    all_to_all x4, starting transfers between devices, exchange(): return lax.all_to_all(x, axes, 0, 0, tiled=True)  35 us
    all_to_all x4, waiting for transfers between devices, exchange(): return lax.all_to_all(x, axes, 0, 0, tiled=True)  16.9 us
    ppermute x3, starting transfers between devices, on_device(): lax.ppermute(fields[t], 'lon', [(i, i ^ t) for i in range(sectors)])  12.5 us
    ppermute x3, waiting for transfers between devices, on_device(): lax.ppermute(fields[t], 'lon', [(i, i ^ t) for i in range(sectors)])  8.87 us
    ppermute x1, waiting for transfers between devices, on_device(): from_inside = lax.ppermute(to_inside, PLACE, inside_swaps)  5.93 us
    ppermute x1, starting transfers between devices, on_device(): inside = lax.ppermute(edge_row(1 - pair), PLACE, inside_swaps)  5.75 us
    ppermute x1, starting transfers between devices, on_device(): other = lax.ppermute(own, 'core', swap)  5.68 us
    ppermute x1, starting transfers between devices, on_device(): across = lax.ppermute(edge_row(pair), PLACE, across_swaps)  5.34 us
  transfers between devices with their start and end apart: 13, of which 8 were waited for; matrix products, arithmetic and copies ran while one was open for 0% of the time, Pallas kernels for 4%

profile of v9, /device:TPU:1, one launch (start us, length us, event | category | flops | bytes accessed | tf_op | source)
XLA Modules:
  0.0 120.9 jit_solution(13074935445620316967)
XLA Ops:
  0.6 0.0 copy-start.8
  0.6 0.0 copy-start.6
  0.7 0.0 copy-start.7
  0.7 0.0 copy-start.9
  0.7 0.0 copy-start.1
  0.7 0.0 copy-start
  0.7 0.0 copy-start.2
  0.7 0.0 copy-start.3
  0.7 0.0 copy-start.4
  0.7 0.0 copy-start.5
  0.8 1.9 %rows_in.1 = f32[4,264,128]{2,1,0:T(8,128)} custom-call(s32[1]{0:T(128)} %bitcast.refs_0_, f32[2,256,128]{2,1,0:T(8,128)} %bitcast.5, f32[2,256,128]{2,1,0:T(8,128)} %bitcast.6, s32[4,128]{1,0:T(4,128)} %refs_3_.3, s32[4,128]{1,0:T(4,128)} %refs_4_.3), custom_call_target="tpu_custom_call" | custom-call | bytes 1000000 | tf_op jit(solution)/shard_map/rows_in/pallas_call | solution.py:440
  2.7 7.7 %all-to-all-start = ((f32[4,264,128]{2,1,0:T(8,128)}), f32[4,264,128]{2,1,0:T(8,128)S(1)}, u32[]{:S(2)}, u32[]{:S(2)}) async-start(f32[4,264,128]{2,1,0:T(8,128)} %rows_in.1), calls=%async_computation | async-start | bytes 1081344 | tf_op jit(solution)/shard_map/rows_in/all_to_all | solution.py:406
  10.4 0.0 copy-done.9
  10.4 14.1 %all-to-all-done.refs_2_.refs_3_ = f32[4,264,128]{2,1,0:T(8,128)S(1)} async-done(((f32[4,264,128]{2,1,0:T(8,128)}), f32[4,264,128]{2,1,0:T(8,128)S(1)}, u32[]{:S(2)}, u32[]{:S(2)}) %all-to-all-start) | async-done | bytes 540704 | tf_op jit(solution)/shard_map/rows_in/all_to_all | solution.py:406
  24.5 5.8 %collective-permute-start.1 = (bf16[4,64,128]{2,1,0:T(8,128)(2,1)S(1)}, bf16[4,64,128]{2,1,0:T(8,128)(2,1)S(1)}, u32[]{:S(2)}, u32[]{:S(2)}) collective-permute-start(bf16[4,64,128]{2,1,0:T(8,128)(2,1)S(1)} %get-tuple-element.43), channel_id=1, source_target_pairs={{0,4},{4,0},{8,12},{12,8},{16,20},{20,16},{24,28},{28,24},{32,36},... | collective-permute-start | bytes 196616 | tf_op jit(solution)/shard_map/row_halo/ppermute | solution.py:473
  30.2 5.3 %collective-permute-start = (bf16[4,64,128]{2,1,0:T(8,128)(2,1)S(1)}, bf16[4,64,128]{2,1,0:T(8,128)(2,1)S(1)}, u32[]{:S(2)}, u32[]{:S(2)}) collective-permute-start(bf16[4,64,128]{2,1,0:T(8,128)(2,1)S(1)} %get-tuple-element.44), channel_id=1, source_target_pairs={{4,20},{12,28},{16,32},{20,4},{24,40},{28,12},{32,16},{36,52},{40,... | collective-permute-start | bytes 196616 | tf_op jit(solution)/shard_map/row_halo/ppermute | solution.py:474
  35.6 0.0 copy-done.8
  35.6 0.0 copy-done.6
  35.6 0.0 copy-done.7
  35.6 0.0 copy-done.1
  35.6 0.0 copy-done
  35.6 0.0 copy-done.2
  35.6 0.0 copy-done.3
  35.6 0.0 copy-done.4
  35.7 0.0 copy-done.5
  35.7 2.5 %early.1 = (f32[128,512]{1,0:T(8,128)S(1)}, bf16[2,640,512]{2,1,0:T(8,128)(2,1)S(1)}, f32[2,384,512]{2,1,0:T(8,128)S(1)}, f32[2,384,512]{2,1,0:T(8,128)S(1)}) custom-call(s32[1]{0:T(128)} %bitcast.refs_0_, s32[2]{0:T(128)S(1)} %copy-done.5, f32[4,264,128]{2,1,0:T(8,128)S(1)} %all-to-all-done.refs_2_.refs_3_, f32[192,384]{1,0:T(8,128)S(1)} %copy-done.8, ...), custom_call_target="tpu_custom_call" | custom-call | flops 3000000000 | bytes 1000000 | tf_op jit(solution)/shard_map/early/pallas_call | solution.py:480
  38.1 0.0 collective-permute-done.1.refs_2_
  38.1 0.0 collective-permute-done.refs_1_
  38.2 3.2 %weights.1 = (bf16[4,64,128]{2,1,0:T(8,128)(2,1)S(1)}, bf16[4,64,128]{2,1,0:T(8,128)(2,1)S(1)}, f32[128,512]{1,0:T(8,128)S(1)}, f32[4,128,128]{2,1,0:T(8,128)S(1...) custom-call(s32[1]{0:T(128)} %bitcast.refs_0_, bf16[4,64,128]{2,1,0:T(8,128)(2,1)S(1)} %collective-permute-done.refs_1_, ...), custom_call_target="tpu_custom_call" | custom-call | flops 3000000000 | bytes 1000000 | tf_op jit(solution)/shard_map/weights/pallas_call | solution.py:511
  41.4 1.9 %collective-permute-start.7 = (bf16[32,36,128]{2,1,0:T(8,128)(2,1)S(1)}, bf16[32,36,128]{2,1,0:T(8,128)(2,1)S(1)}, u32[]{:S(2)}, u32[]{:S(2)}) collective-permute-start(bf16[32,36,128]{2,1,0:T(8,128)(2,1)S(1)} %get-tuple-element.39), channel_id=1, source_target_pairs={{0,16},{16,0},{1,17},{17,1},{2,18},{18,2},{3,19},{19,3},{4,20},{20... | collective-permute-start | bytes 884744 | tf_op jit(solution)/shard_map/weights_core/ppermute | solution.py:545
  43.3 1.6 %collective-permute-done.7 = bf16[32,36,128]{2,1,0:T(8,128)(2,1)S(1)} collective-permute-done((bf16[32,36,128]{2,1,0:T(8,128)(2,1)S(1)}, bf16[32,36,128]{2,1,0:T(8,128)(2,1)S(1)}, u32[]{:S(2)}, u32[]{:S(2)}) %collective-permute-start.7) | collective-permute-done | bytes 294944 | tf_op jit(solution)/shard_map/weights_core/ppermute | solution.py:545
  44.9 0.8 add_convert_fusion
  45.7 14.6 %all-to-all-start.1 = ((bf16[32,36,128]{2,1,0:T(8,128)(2,1)}), bf16[32,36,128]{2,1,0:T(8,128)(2,1)S(1)}, u32[]{:S(2)}, u32[]{:S(2)}) async-start(bf16[32,36,128]{2,1,0:T(8,128)(2,1)} %add_convert_fusion), calls=%async_computation.1 | async-start | bytes 655360 | tf_op jit(solution)/shard_map/weights_plane/all_to_all | solution.py:406
  60.4 1.9 %collective-permute-start.2 = (bf16[4,64,128]{2,1,0:T(8,128)(2,1)S(1)}, bf16[4,64,128]{2,1,0:T(8,128)(2,1)S(1)}, u32[]{:S(2)}, u32[]{:S(2)}) collective-permute-start(bf16[4,64,128]{2,1,0:T(8,128)(2,1)S(1)} %get-tuple-element.30), channel_id=1, source_target_pairs={{4,20},{12,28},{16,32},{20,4},{24,40},{28,12},{32,16},{36,52},{40,... | collective-permute-start | bytes 196616 | tf_op jit(solution)/shard_map/fields/ppermute | solution.py:548
  62.3 5.0 %collective-permute-start.3 = (bf16[4,64,128]{2,1,0:T(8,128)(2,1)S(1)}, bf16[4,64,128]{2,1,0:T(8,128)(2,1)S(1)}, u32[]{:S(2)}, u32[]{:S(2)}) collective-permute-start(bf16[4,64,128]{2,1,0:T(8,128)(2,1)S(1)} %get-tuple-element.31), channel_id=1, source_target_pairs={{0,4},{4,0},{8,12},{12,8},{16,20},{20,16},{24,28},{28,24},{32,36},... | collective-permute-start | bytes 196616 | tf_op jit(solution)/shard_map/fields/ppermute | solution.py:549
  67.3 0.0 collective-permute-done.2.refs_6_.refs_1_
  67.3 5.9 %collective-permute-done.3.refs_7_.refs_2_ = bf16[4,64,128]{2,1,0:T(8,128)(2,1)S(1)} collective-permute-done((bf16[4,64,128]{2,1,0:T(8,128)(2,1)S(1)}, bf16[4,64,128]{2,1,0:T(8,128)(2,1)S(1)}, u32[]{:S(2)}, u32[]{:S(2)}) %collective-permute-start.3) | collective-permute-done | bytes 65568 | tf_op jit(solution)/shard_map/fields/ppermute | solution.py:549
  73.2 0.0 all-to-all-done.1.refs_0_
  73.2 0.7 weights_plane.1
  73.9 5.1 %all-to-all-start.2 = ((bf16[12,36,128]{2,1,0:T(8,128)(2,1)}), bf16[12,36,128]{2,1,0:T(8,128)(2,1)S(1)}, u32[]{:S(2)}, u32[]{:S(2)}) async-start(bf16[12,36,128]{2,1,0:T(8,128)(2,1)} %weights_plane.1), calls=%async_computation.2 | async-start | bytes 245760 | tf_op jit(solution)/shard_map/weights_length/all_to_all | solution.py:406
  79.0 1.2 fields.1
  80.2 3.3 %collective-permute-start.4 = (bf16[256,128]{1,0:T(8,128)(2,1)S(1)}, bf16[256,128]{1,0:T(8,128)(2,1)S(1)}, u32[]{:S(2)}, u32[]{:S(2)}) collective-permute-start(bf16[256,128]{1,0:T(8,128)(2,1)S(1)} %get-tuple-element.33), channel_id=1, source_target_pairs={{0,4},{4,0},{8,12},{12,8},{1,5},{5,1},{9,13},{13,9},{2,6},{6,2},{1... | collective-permute-start | bytes 196616 | tf_op jit(solution)/shard_map/rows_out/ppermute | solution.py:567
  83.5 3.6 %collective-permute-done.4.refs_2_.refs_1_ = bf16[256,128]{1,0:T(8,128)(2,1)S(1)} collective-permute-done((bf16[256,128]{1,0:T(8,128)(2,1)S(1)}, bf16[256,128]{1,0:T(8,128)(2,1)S(1)}, u32[]{:S(2)}, u32[]{:S(2)}) %collective-permute-start.4) | collective-permute-done | bytes 65568 | tf_op jit(solution)/shard_map/rows_out/ppermute | solution.py:567
  87.1 2.8 %all-to-all-done.2.refs_0_ = bf16[12,36,128]{2,1,0:T(8,128)(2,1)S(1)} async-done(((bf16[12,36,128]{2,1,0:T(8,128)(2,1)}), bf16[12,36,128]{2,1,0:T(8,128)(2,1)S(1)}, u32[]{:S(2)}, u32[]{:S(2)}) %all-to-all-start.2) | async-done | bytes 110624 | tf_op jit(solution)/shard_map/weights_length/all_to_all | solution.py:406
  89.9 0.8 weights_length.1
  90.7 7.6 %all-to-all-start.3 = ((bf16[32,36,128]{2,1,0:T(8,128)(2,1)}), bf16[32,36,128]{2,1,0:T(8,128)(2,1)S(1)}, u32[]{:S(2)}, u32[]{:S(2)}) async-start(bf16[32,36,128]{2,1,0:T(8,128)(2,1)} %weights_length.1), calls=%async_computation.3 | async-start | bytes 655360 | tf_op jit(solution)/shard_map/weights_back/all_to_all | solution.py:406
  98.3 7.0 %collective-permute-start.5 = (bf16[256,128]{1,0:T(8,128)(2,1)S(1)}, bf16[256,128]{1,0:T(8,128)(2,1)S(1)}, u32[]{:S(2)}, u32[]{:S(2)}) collective-permute-start(bf16[256,128]{1,0:T(8,128)(2,1)S(1)} %get-tuple-element.34), channel_id=1, source_target_pairs={{0,8},{4,12},{8,0},{12,4},{1,9},{5,13},{9,1},{13,5},{2,10},{6,14},... | collective-permute-start | bytes 196616 | tf_op jit(solution)/shard_map/rows_out/ppermute | solution.py:567
  105.3 2.2 %collective-permute-start.6 = (bf16[256,128]{1,0:T(8,128)(2,1)S(1)}, bf16[256,128]{1,0:T(8,128)(2,1)S(1)}, u32[]{:S(2)}, u32[]{:S(2)}) collective-permute-start(bf16[256,128]{1,0:T(8,128)(2,1)S(1)} %get-tuple-element.35), channel_id=1, source_target_pairs={{0,12},{4,8},{8,4},{12,0},{1,13},{5,9},{9,5},{13,1},{2,14},{6,10},... | collective-permute-start | bytes 196616 | tf_op jit(solution)/shard_map/rows_out/ppermute | solution.py:567
  107.5 3.2 %collective-permute-done.5.refs_3_.refs_1_ = bf16[256,128]{1,0:T(8,128)(2,1)S(1)} collective-permute-done((bf16[256,128]{1,0:T(8,128)(2,1)S(1)}, bf16[256,128]{1,0:T(8,128)(2,1)S(1)}, u32[]{:S(2)}, u32[]{:S(2)}) %collective-permute-start.5) | collective-permute-done | bytes 65568 | tf_op jit(solution)/shard_map/rows_out/ppermute | solution.py:567
  110.7 2.1 %collective-permute-done.6.refs_4_.refs_2_ = bf16[256,128]{1,0:T(8,128)(2,1)S(1)} collective-permute-done((bf16[256,128]{1,0:T(8,128)(2,1)S(1)}, bf16[256,128]{1,0:T(8,128)(2,1)S(1)}, u32[]{:S(2)}, u32[]{:S(2)}) %collective-permute-start.6) | collective-permute-done | bytes 65568 | tf_op jit(solution)/shard_map/rows_out/ppermute | solution.py:567
  112.8 0.0 all-to-all-done.3.refs_0_
  112.8 5.7 %collective-permute-start.8 = (bf16[32,36,128]{2,1,0:T(8,128)(2,1)S(1)}, bf16[32,36,128]{2,1,0:T(8,128)(2,1)S(1)}, u32[]{:S(2)}, u32[]{:S(2)}) collective-permute-start(bf16[32,36,128]{2,1,0:T(8,128)(2,1)S(1)} %weights_back.2.refs_1_), channel_id=1, source_target_pairs={{0,16},{16,0},{1,17},{17,1},{2,18},{18,2},{3,19},{19,3},{4,20},{20... | collective-permute-start | bytes 884744 | tf_op jit(solution)/shard_map/weights_back/ppermute | solution.py:588
  118.5 0.9 bands_out.1
  119.4 0.4 collective-permute-done.8.refs_2_
  119.7 1.2 weights_back.3
  (3 shorter events, 0.0 us)
Async XLA Ops:
  0.6 34.9 %copy-start.8 = (f32[192,384]{1,0:T(8,128)S(1)}, f32[192,384]{1,0:T(8,128)}, u32[]{:S(2)}) copy-start(f32[192,384]{1,0:T(8,128)} %constant.71.clone.refs_3_.refs_2_) | copy-start | bytes 884740
  0.6 34.9 %copy-start.6 = (bf16[384,512]{1,0:T(8,128)(2,1)S(1)}, bf16[384,512]{1,0:T(8,128)(2,1)}, u32[]{:S(2)}) copy-start(bf16[384,512]{1,0:T(8,128)(2,1)} %constant.70.clone.refs_5_.refs_4_) | copy-start | bytes 1179652
  0.7 34.9 %copy-start.7 = (bf16[384,512]{1,0:T(8,128)(2,1)S(1)}, bf16[384,512]{1,0:T(8,128)(2,1)}, u32[]{:S(2)}) copy-start(bf16[384,512]{1,0:T(8,128)(2,1)} %constant.69.clone.refs_4_.refs_3_) | copy-start | bytes 1179652
  0.7 9.7 %copy-start.9 = (f32[384]{0:T(512)S(1)}, f32[384]{0:T(512)}, u32[]{:S(2)}) copy-start(f32[384]{0:T(512)} %param.23) | copy-start | bytes 4612
  0.7 34.9 %copy-start.1 = (bf16[64,384]{1,0:T(8,128)(2,1)S(1)}, bf16[64,384]{1,0:T(8,128)(2,1)}, u32[]{:S(2)}) copy-start(bf16[64,384]{1,0:T(8,128)(2,1)} %refs_9_.3) | copy-start | bytes 147460
  0.7 34.9 %copy-start = (bf16[384,640]{1,0:T(8,128)(2,1)S(1)}, bf16[384,640]{1,0:T(8,128)(2,1)}, u32[]{:S(2)}) copy-start(bf16[384,640]{1,0:T(8,128)(2,1)} %refs_8_.3) | copy-start | bytes 1474564
  0.7 34.9 %copy-start.2 = (f32[32,64]{1,0:T(8,128)S(1)}, f32[32,64]{1,0:T(8,128)}, u32[]{:S(2)}) copy-start(f32[32,64]{1,0:T(8,128)} %refs_8_.2) | copy-start | bytes 24580
  0.7 34.9 %copy-start.3 = (f32[16,64]{1,0:T(8,128)S(1)}, f32[16,64]{1,0:T(8,128)}, u32[]{:S(2)}) copy-start(f32[16,64]{1,0:T(8,128)} %refs_7_.1) | copy-start | bytes 12292
  0.7 34.9 %copy-start.4 = (f32[2,64]{1,0:T(2,128)S(1)}, f32[2,64]{1,0:T(2,128)}, u32[]{:S(2)}) copy-start(f32[2,64]{1,0:T(2,128)} %refs_6_.1) | copy-start | bytes 1540
  0.7 34.9 %copy-start.5 = (s32[2]{0:T(128)S(1)}, s32[2]{0:T(128)}, u32[]{:S(2)}) copy-start(s32[2]{0:T(128)} %refs_1_.1) | copy-start | bytes 28
  2.7 21.7 %all-to-all-start = ((f32[4,264,128]{2,1,0:T(8,128)}), f32[4,264,128]{2,1,0:T(8,128)S(1)}, u32[]{:S(2)}, u32[]{:S(2)}) async-start(f32[4,264,128]{2,1,0:T(8,128)} %rows_in.1), calls=%async_computation | async-start | bytes 1081344 | tf_op jit(solution)/shard_map/rows_in/all_to_all | solution.py:406
  24.5 13.7 %collective-permute-start.1 = (bf16[4,64,128]{2,1,0:T(8,128)(2,1)S(1)}, bf16[4,64,128]{2,1,0:T(8,128)(2,1)S(1)}, u32[]{:S(2)}, u32[]{:S(2)}) collective-permute-start(bf16[4,64,128]{2,1,0:T(8,128)(2,1)S(1)} %get-tuple-element.43), channel_id=1, source_target_pairs={{0,4},{4,0},{8,12},{12,8},{16,20},{20,16},{24,28},{28,24},{32,36},... | collective-permute-start | bytes 196616 | tf_op jit(solution)/shard_map/row_halo/ppermute | solution.py:473
  30.2 7.9 %collective-permute-start = (bf16[4,64,128]{2,1,0:T(8,128)(2,1)S(1)}, bf16[4,64,128]{2,1,0:T(8,128)(2,1)S(1)}, u32[]{:S(2)}, u32[]{:S(2)}) collective-permute-start(bf16[4,64,128]{2,1,0:T(8,128)(2,1)S(1)} %get-tuple-element.44), channel_id=1, source_target_pairs={{4,20},{12,28},{16,32},{20,4},{24,40},{28,12},{32,16},{36,52},{40,... | collective-permute-start | bytes 196616 | tf_op jit(solution)/shard_map/row_halo/ppermute | solution.py:474
  41.4 3.5 %collective-permute-start.7 = (bf16[32,36,128]{2,1,0:T(8,128)(2,1)S(1)}, bf16[32,36,128]{2,1,0:T(8,128)(2,1)S(1)}, u32[]{:S(2)}, u32[]{:S(2)}) collective-permute-start(bf16[32,36,128]{2,1,0:T(8,128)(2,1)S(1)} %get-tuple-element.39), channel_id=1, source_target_pairs={{0,16},{16,0},{1,17},{17,1},{2,18},{18,2},{3,19},{19,3},{4,20},{20... | collective-permute-start | bytes 884744 | tf_op jit(solution)/shard_map/weights_core/ppermute | solution.py:545
  45.7 27.5 %all-to-all-start.1 = ((bf16[32,36,128]{2,1,0:T(8,128)(2,1)}), bf16[32,36,128]{2,1,0:T(8,128)(2,1)S(1)}, u32[]{:S(2)}, u32[]{:S(2)}) async-start(bf16[32,36,128]{2,1,0:T(8,128)(2,1)} %add_convert_fusion), calls=%async_computation.1 | async-start | bytes 655360 | tf_op jit(solution)/shard_map/weights_plane/all_to_all | solution.py:406
  60.4 6.9 %collective-permute-start.2 = (bf16[4,64,128]{2,1,0:T(8,128)(2,1)S(1)}, bf16[4,64,128]{2,1,0:T(8,128)(2,1)S(1)}, u32[]{:S(2)}, u32[]{:S(2)}) collective-permute-start(bf16[4,64,128]{2,1,0:T(8,128)(2,1)S(1)} %get-tuple-element.30), channel_id=1, source_target_pairs={{4,20},{12,28},{16,32},{20,4},{24,40},{28,12},{32,16},{36,52},{40,... | collective-permute-start | bytes 196616 | tf_op jit(solution)/shard_map/fields/ppermute | solution.py:548
  62.3 10.9 %collective-permute-start.3 = (bf16[4,64,128]{2,1,0:T(8,128)(2,1)S(1)}, bf16[4,64,128]{2,1,0:T(8,128)(2,1)S(1)}, u32[]{:S(2)}, u32[]{:S(2)}) collective-permute-start(bf16[4,64,128]{2,1,0:T(8,128)(2,1)S(1)} %get-tuple-element.31), channel_id=1, source_target_pairs={{0,4},{4,0},{8,12},{12,8},{16,20},{20,16},{24,28},{28,24},{32,36},... | collective-permute-start | bytes 196616 | tf_op jit(solution)/shard_map/fields/ppermute | solution.py:549
  73.9 16.0 %all-to-all-start.2 = ((bf16[12,36,128]{2,1,0:T(8,128)(2,1)}), bf16[12,36,128]{2,1,0:T(8,128)(2,1)S(1)}, u32[]{:S(2)}, u32[]{:S(2)}) async-start(bf16[12,36,128]{2,1,0:T(8,128)(2,1)} %weights_plane.1), calls=%async_computation.2 | async-start | bytes 245760 | tf_op jit(solution)/shard_map/weights_length/all_to_all | solution.py:406
  80.2 6.9 %collective-permute-start.4 = (bf16[256,128]{1,0:T(8,128)(2,1)S(1)}, bf16[256,128]{1,0:T(8,128)(2,1)S(1)}, u32[]{:S(2)}, u32[]{:S(2)}) collective-permute-start(bf16[256,128]{1,0:T(8,128)(2,1)S(1)} %get-tuple-element.33), channel_id=1, source_target_pairs={{0,4},{4,0},{8,12},{12,8},{1,5},{5,1},{9,13},{13,9},{2,6},{6,2},{1... | collective-permute-start | bytes 196616 | tf_op jit(solution)/shard_map/rows_out/ppermute | solution.py:567
  90.7 22.1 %all-to-all-start.3 = ((bf16[32,36,128]{2,1,0:T(8,128)(2,1)}), bf16[32,36,128]{2,1,0:T(8,128)(2,1)S(1)}, u32[]{:S(2)}, u32[]{:S(2)}) async-start(bf16[32,36,128]{2,1,0:T(8,128)(2,1)} %weights_length.1), calls=%async_computation.3 | async-start | bytes 655360 | tf_op jit(solution)/shard_map/weights_back/all_to_all | solution.py:406
  98.3 12.4 %collective-permute-start.5 = (bf16[256,128]{1,0:T(8,128)(2,1)S(1)}, bf16[256,128]{1,0:T(8,128)(2,1)S(1)}, u32[]{:S(2)}, u32[]{:S(2)}) collective-permute-start(bf16[256,128]{1,0:T(8,128)(2,1)S(1)} %get-tuple-element.34), channel_id=1, source_target_pairs={{0,8},{4,12},{8,0},{12,4},{1,9},{5,13},{9,1},{13,5},{2,10},{6,14},... | collective-permute-start | bytes 196616 | tf_op jit(solution)/shard_map/rows_out/ppermute | solution.py:567
  105.3 7.4 %collective-permute-start.6 = (bf16[256,128]{1,0:T(8,128)(2,1)S(1)}, bf16[256,128]{1,0:T(8,128)(2,1)S(1)}, u32[]{:S(2)}, u32[]{:S(2)}) collective-permute-start(bf16[256,128]{1,0:T(8,128)(2,1)S(1)} %get-tuple-element.35), channel_id=1, source_target_pairs={{0,12},{4,8},{8,4},{12,0},{1,13},{5,9},{9,5},{13,1},{2,14},{6,10},... | collective-permute-start | bytes 196616 | tf_op jit(solution)/shard_map/rows_out/ppermute | solution.py:567
  112.8 6.9 %collective-permute-start.8 = (bf16[32,36,128]{2,1,0:T(8,128)(2,1)S(1)}, bf16[32,36,128]{2,1,0:T(8,128)(2,1)S(1)}, u32[]{:S(2)}, u32[]{:S(2)}) collective-permute-start(bf16[32,36,128]{2,1,0:T(8,128)(2,1)S(1)} %weights_back.2.refs_1_), channel_id=1, source_target_pairs={{0,16},{16,0},{1,17},{17,1},{2,18},{18,2},{3,19},{19,3},{4,20},{20... | collective-permute-start | bytes 884744 | tf_op jit(solution)/shard_map/weights_back/ppermute | solution.py:588

commit v10 on v9

--- a/solution.py
+++ b/solution.py
@@ -557,9 +557,9 @@
         )(place, moist, scale, high, low, grad_rows, from_across, from_inside)
 
     with jax.named_scope("weights_plane"):
-        copies = call(sum_and_copy_kernel, shape((length, piece_rows, LANES), BF), 3)(
-            exchange(halves, PLANE), from_across, from_inside
-        )
+        parts = exchange(halves, PLANE)
+        piece = jnp.sum(parts.astype(F32), 0, keepdims=True).astype(BF)
+        copies = jnp.broadcast_to(piece, (length, piece_rows, LANES))
 
     with jax.named_scope("rows_out"):
         received = [fields[0]]
@@ -568,7 +568,7 @@
 
     with jax.named_scope("weights_length"):
         copies = call(sum_and_copy_kernel, shape(share, BF), 2)(
-            exchange(copies, "z"), received[1]
+            exchange(copies, "z"), fields[0]
         )
 
     with jax.named_scope("bands_out"):
@@ -584,7 +584,7 @@
         state_grad = state_grad.reshape(column_state.shape)
 
     with jax.named_scope("weights_back"):
-        own = call(copy_kernel, shape(share, BF), sectors - 1)(exchange(copies, PLANE), *received[2:])
+        own = call(copy_kernel, shape(share, BF), sectors)(exchange(copies, PLANE), *received[1:])
         other = lax.ppermute(own, "core", swap)
         columns = members * lax.axis_size("mem") * lat_total * lon_total
         grad_in, grad_bias, grad_out = call(

time: 122 us -> 121 us (level)
  blocking collectives: 0 us -> 25.5 us
  starting transfers between devices: 73 us -> 56.2 us
  waiting for transfers between devices: 33.6 us -> 24.9 us
    all_to_all x0 -> x1, blocking collectives: none -> 25.5 us  [exchange(): return lax.all_to_all(x, axes, 0, 0, tiled=True)]
    all_to_all x4 -> x3, starting transfers between devices: 35 us -> 18.7 us  [exchange(): return lax.all_to_all(x, axes, 0, 0, tiled=True)]
    ppermute x1, starting transfers between devices: 1.92 us -> 6.06 us  [on_device(): from_across = lax.ppermute(to_across, PLACE, across_swaps)]
    ppermute x3, waiting for transfers between devices: 8.87 us -> 5.81 us  [on_device(): lax.ppermute(fields[t], 'lon', [(i, i ^ t) for i in range(sectors)])]
    ppermute x1, waiting for transfers between devices: 5.93 us -> 3.04 us  [on_device(): from_inside = lax.ppermute(to_inside, PLACE, inside_swaps)]
    all_to_all x4 -> x3, waiting for transfers between devices: 16.9 us -> 14.1 us  [exchange(): return lax.all_to_all(x, axes, 0, 0, tiled=True)]
    ppermute x1, starting transfers between devices: 4.96 us -> 3.16 us  [on_device(): from_inside = lax.ppermute(to_inside, PLACE, inside_swaps)]
    ppermute x1, starting transfers between devices: 5.68 us -> 3.9 us  [on_device(): other = lax.ppermute(own, 'core', swap)]
  transfers between devices with their start and end apart: 13 -> 12, of which waited for: 8 -> 6; matrix products, arithmetic and copies ran while one was open for 0% -> 0% of each run, Pallas kernels for 4% -> 4%
where the time goes in v10:
time: 121 us; the launch traced here: 120 us
  starting transfers between devices  56.2 us (46%)
  blocking collectives  25.5 us (21%)
  waiting for transfers between devices  24.9 us (21%)
  Pallas kernels  11.6 us (10%)
    all_to_all x1, blocking collectives, exchange(): return lax.all_to_all(x, axes, 0, 0, tiled=True)  25.5 us
    all_to_all x3, starting transfers between devices, exchange(): return lax.all_to_all(x, axes, 0, 0, tiled=True)  18.7 us
    all_to_all x3, waiting for transfers between devices, exchange(): return lax.all_to_all(x, axes, 0, 0, tiled=True)  14.1 us
    ppermute x3, starting transfers between devices, on_device(): lax.ppermute(fields[t], 'lon', [(i, i ^ t) for i in range(sectors)])  11.4 us
    ppermute x1, starting transfers between devices, on_device(): from_across = lax.ppermute(to_across, PLACE, across_swaps)  6.06 us
    ppermute x3, waiting for transfers between devices, on_device(): lax.ppermute(fields[t], 'lon', [(i, i ^ t) for i in range(sectors)])  5.81 us
    ppermute x1, starting transfers between devices, on_device(): inside = lax.ppermute(edge_row(1 - pair), PLACE, inside_swaps)  5.75 us
    ppermute x1, starting transfers between devices, on_device(): across = lax.ppermute(edge_row(pair), PLACE, across_swaps)  5.34 us
  transfers between devices with their start and end apart: 12, of which 6 were waited for; matrix products, arithmetic and copies ran while one was open for 0% of the time, Pallas kernels for 4%

profile of v10, /device:TPU:1, one launch (start us, length us, event | category | flops | bytes accessed | tf_op | source)
XLA Modules:
  0.0 120.1 jit_solution(14891002288609132944)
XLA Ops:
  0.6 0.0 copy-start.8
  0.6 0.0 copy-start.6
  0.7 0.0 copy-start.7
  0.7 0.0 copy-start.9
  0.7 0.0 copy-start.1
  0.7 0.0 copy-start
  0.7 0.0 copy-start.2
  0.7 0.0 copy-start.3
  0.7 0.0 copy-start.4
  0.7 0.0 copy-start.5
  0.8 1.9 %rows_in.1 = f32[4,264,128]{2,1,0:T(8,128)} custom-call(s32[1]{0:T(128)} %bitcast.refs_0_, f32[2,256,128]{2,1,0:T(8,128)} %bitcast.5, f32[2,256,128]{2,1,0:T(8,128)} %bitcast.6, s32[4,128]{1,0:T(4,128)} %refs_3_.3, s32[4,128]{1,0:T(4,128)} %refs_4_.3), custom_call_target="tpu_custom_call" | custom-call | bytes 1000000 | tf_op jit(solution)/shard_map/rows_in/pallas_call | solution.py:440
  2.7 7.7 %all-to-all-start = ((f32[4,264,128]{2,1,0:T(8,128)}), f32[4,264,128]{2,1,0:T(8,128)S(1)}, u32[]{:S(2)}, u32[]{:S(2)}) async-start(f32[4,264,128]{2,1,0:T(8,128)} %rows_in.1), calls=%async_computation | async-start | bytes 1081344 | tf_op jit(solution)/shard_map/rows_in/all_to_all | solution.py:406
  10.4 0.0 copy-done.9
  10.4 14.1 %all-to-all-done.refs_2_.refs_3_ = f32[4,264,128]{2,1,0:T(8,128)S(1)} async-done(((f32[4,264,128]{2,1,0:T(8,128)}), f32[4,264,128]{2,1,0:T(8,128)S(1)}, u32[]{:S(2)}, u32[]{:S(2)}) %all-to-all-start) | async-done | bytes 540704 | tf_op jit(solution)/shard_map/rows_in/all_to_all | solution.py:406
  24.5 5.8 %collective-permute-start.1 = (bf16[4,64,128]{2,1,0:T(8,128)(2,1)S(1)}, bf16[4,64,128]{2,1,0:T(8,128)(2,1)S(1)}, u32[]{:S(2)}, u32[]{:S(2)}) collective-permute-start(bf16[4,64,128]{2,1,0:T(8,128)(2,1)S(1)} %get-tuple-element.43), channel_id=1, source_target_pairs={{0,4},{4,0},{8,12},{12,8},{16,20},{20,16},{24,28},{28,24},{32,36},... | collective-permute-start | bytes 196616 | tf_op jit(solution)/shard_map/row_halo/ppermute | solution.py:473
  30.2 5.3 %collective-permute-start = (bf16[4,64,128]{2,1,0:T(8,128)(2,1)S(1)}, bf16[4,64,128]{2,1,0:T(8,128)(2,1)S(1)}, u32[]{:S(2)}, u32[]{:S(2)}) collective-permute-start(bf16[4,64,128]{2,1,0:T(8,128)(2,1)S(1)} %get-tuple-element.44), channel_id=1, source_target_pairs={{4,20},{12,28},{16,32},{20,4},{24,40},{28,12},{32,16},{36,52},{40,... | collective-permute-start | bytes 196616 | tf_op jit(solution)/shard_map/row_halo/ppermute | solution.py:474
  35.6 0.0 copy-done.8
  35.6 0.0 copy-done.6
  35.6 0.0 copy-done.7
  35.6 0.0 copy-done.1
  35.6 0.0 copy-done
  35.6 0.0 copy-done.2
  35.6 0.0 copy-done.3
  35.6 0.0 copy-done.4
  35.7 0.0 copy-done.5
  35.7 2.5 %early.1 = (f32[128,512]{1,0:T(8,128)S(1)}, bf16[2,640,512]{2,1,0:T(8,128)(2,1)S(1)}, f32[2,384,512]{2,1,0:T(8,128)S(1)}, f32[2,384,512]{2,1,0:T(8,128)S(1)}) custom-call(s32[1]{0:T(128)} %bitcast.refs_0_, s32[2]{0:T(128)S(1)} %copy-done.5, f32[4,264,128]{2,1,0:T(8,128)S(1)} %all-to-all-done.refs_2_.refs_3_, f32[192,384]{1,0:T(8,128)S(1)} %copy-done.8, ...), custom_call_target="tpu_custom_call" | custom-call | flops 3000000000 | bytes 1000000 | tf_op jit(solution)/shard_map/early/pallas_call | solution.py:480
  38.1 0.0 collective-permute-done.1.refs_2_
  38.1 0.0 collective-permute-done.refs_1_
  38.1 3.2 %weights.1 = (bf16[4,64,128]{2,1,0:T(8,128)(2,1)S(1)}, bf16[4,64,128]{2,1,0:T(8,128)(2,1)S(1)}, f32[128,512]{1,0:T(8,128)S(1)}, f32[4,128,128]{2,1,0:T(8,128)S(1...) custom-call(s32[1]{0:T(128)} %bitcast.refs_0_, bf16[4,64,128]{2,1,0:T(8,128)(2,1)S(1)} %collective-permute-done.refs_1_, ...), custom_call_target="tpu_custom_call" | custom-call | flops 3000000000 | bytes 1000000 | tf_op jit(solution)/shard_map/weights/pallas_call | solution.py:511
  41.3 1.9 %collective-permute-start.7 = (bf16[32,36,128]{2,1,0:T(8,128)(2,1)S(1)}, bf16[32,36,128]{2,1,0:T(8,128)(2,1)S(1)}, u32[]{:S(2)}, u32[]{:S(2)}) collective-permute-start(bf16[32,36,128]{2,1,0:T(8,128)(2,1)S(1)} %get-tuple-element.39), channel_id=1, source_target_pairs={{0,16},{16,0},{1,17},{17,1},{2,18},{18,2},{3,19},{19,3},{4,20},{20... | collective-permute-start | bytes 884744 | tf_op jit(solution)/shard_map/weights_core/ppermute | solution.py:545
  43.3 1.6 %collective-permute-done.7 = bf16[32,36,128]{2,1,0:T(8,128)(2,1)S(1)} collective-permute-done((bf16[32,36,128]{2,1,0:T(8,128)(2,1)S(1)}, bf16[32,36,128]{2,1,0:T(8,128)(2,1)S(1)}, u32[]{:S(2)}, u32[]{:S(2)}) %collective-permute-start.7) | collective-permute-done | bytes 294944 | tf_op jit(solution)/shard_map/weights_core/ppermute | solution.py:545
  44.9 0.1 add_convert_fusion
  44.9 25.5 %all_to_all.20 = bf16[32,36,128]{2,1,0:T(8,128)(2,1)S(1)} all-to-all(bf16[32,36,128]{2,1,0:T(8,128)(2,1)S(1)} %add_convert_fusion), channel_id=1, replica_groups=mesh['ylo'=2,'z'=12,'core'=2,'lon'=4,'mem'=4] {'mem','ylo','lon'}, dimensions={0} | all-to-all | bytes 589824 | tf_op jit(solution)/shard_map/weights_plane/all_to_all | solution.py:406
  70.4 0.1 reduce_sum.12
  70.5 0.7 broadcast_in_dim.2
  71.2 4.9 %all-to-all-start.2 = ((bf16[12,36,128]{2,1,0:T(8,128)(2,1)}), bf16[12,36,128]{2,1,0:T(8,128)(2,1)S(1)}, u32[]{:S(2)}, u32[]{:S(2)}) async-start(bf16[12,36,128]{2,1,0:T(8,128)(2,1)} %broadcast_in_dim.2), calls=%async_computation.2 | async-start | bytes 245760 | tf_op jit(solution)/shard_map/weights_length/all_to_all | solution.py:406
  76.1 6.1 %collective-permute-start.2 = (bf16[4,64,128]{2,1,0:T(8,128)(2,1)S(1)}, bf16[4,64,128]{2,1,0:T(8,128)(2,1)S(1)}, u32[]{:S(2)}, u32[]{:S(2)}) collective-permute-start(bf16[4,64,128]{2,1,0:T(8,128)(2,1)S(1)} %get-tuple-element.30), channel_id=1, source_target_pairs={{4,20},{12,28},{16,32},{20,4},{24,40},{28,12},{32,16},{36,52},{40,... | collective-permute-start | bytes 196616 | tf_op jit(solution)/shard_map/fields/ppermute | solution.py:548
  82.2 3.2 %collective-permute-start.3 = (bf16[4,64,128]{2,1,0:T(8,128)(2,1)S(1)}, bf16[4,64,128]{2,1,0:T(8,128)(2,1)S(1)}, u32[]{:S(2)}, u32[]{:S(2)}) collective-permute-start(bf16[4,64,128]{2,1,0:T(8,128)(2,1)S(1)} %get-tuple-element.31), channel_id=1, source_target_pairs={{0,4},{4,0},{8,12},{12,8},{16,20},{20,16},{24,28},{28,24},{32,36},... | collective-permute-start | bytes 196616 | tf_op jit(solution)/shard_map/fields/ppermute | solution.py:549
  85.4 0.0 collective-permute-done.2.refs_6_
  85.4 3.0 %collective-permute-done.3.refs_7_ = bf16[4,64,128]{2,1,0:T(8,128)(2,1)S(1)} collective-permute-done((bf16[4,64,128]{2,1,0:T(8,128)(2,1)S(1)}, bf16[4,64,128]{2,1,0:T(8,128)(2,1)S(1)}, u32[]{:S(2)}, u32[]{:S(2)}) %collective-permute-start.3) | collective-permute-done | bytes 65568 | tf_op jit(solution)/shard_map/fields/ppermute | solution.py:549
  88.4 1.2 fields.1
  89.6 0.0 all-to-all-done.2.refs_0_
  89.6 0.8 weights_length.1
  90.4 6.1 %all-to-all-start.3 = ((bf16[32,36,128]{2,1,0:T(8,128)(2,1)}), bf16[32,36,128]{2,1,0:T(8,128)(2,1)S(1)}, u32[]{:S(2)}, u32[]{:S(2)}) async-start(bf16[32,36,128]{2,1,0:T(8,128)(2,1)} %weights_length.1), calls=%async_computation.3 | async-start | bytes 655360 | tf_op jit(solution)/shard_map/weights_back/all_to_all | solution.py:406
  96.5 4.0 %collective-permute-start.4 = (bf16[256,128]{1,0:T(8,128)(2,1)S(1)}, bf16[256,128]{1,0:T(8,128)(2,1)S(1)}, u32[]{:S(2)}, u32[]{:S(2)}) collective-permute-start(bf16[256,128]{1,0:T(8,128)(2,1)S(1)} %get-tuple-element.33), channel_id=1, source_target_pairs={{0,4},{4,0},{8,12},{12,8},{1,5},{5,1},{9,13},{13,9},{2,6},{6,2},{1... | collective-permute-start | bytes 196616 | tf_op jit(solution)/shard_map/rows_out/ppermute | solution.py:567
  100.6 5.2 %collective-permute-start.5 = (bf16[256,128]{1,0:T(8,128)(2,1)S(1)}, bf16[256,128]{1,0:T(8,128)(2,1)S(1)}, u32[]{:S(2)}, u32[]{:S(2)}) collective-permute-start(bf16[256,128]{1,0:T(8,128)(2,1)S(1)} %get-tuple-element.34), channel_id=1, source_target_pairs={{0,8},{4,12},{8,0},{12,4},{1,9},{5,13},{9,1},{13,5},{2,10},{6,14},... | collective-permute-start | bytes 196616 | tf_op jit(solution)/shard_map/rows_out/ppermute | solution.py:567
  105.8 2.1 %collective-permute-start.6 = (bf16[256,128]{1,0:T(8,128)(2,1)S(1)}, bf16[256,128]{1,0:T(8,128)(2,1)S(1)}, u32[]{:S(2)}, u32[]{:S(2)}) collective-permute-start(bf16[256,128]{1,0:T(8,128)(2,1)S(1)} %get-tuple-element.35), channel_id=1, source_target_pairs={{0,12},{4,8},{8,4},{12,0},{1,13},{5,9},{9,5},{13,1},{2,14},{6,10},... | collective-permute-start | bytes 196616 | tf_op jit(solution)/shard_map/rows_out/ppermute | solution.py:567
  107.9 0.0 collective-permute-done.4.refs_2_.refs_1_
  107.9 3.7 %collective-permute-done.5.refs_3_.refs_2_ = bf16[256,128]{1,0:T(8,128)(2,1)S(1)} collective-permute-done((bf16[256,128]{1,0:T(8,128)(2,1)S(1)}, bf16[256,128]{1,0:T(8,128)(2,1)S(1)}, u32[]{:S(2)}, u32[]{:S(2)}) %collective-permute-start.5) | collective-permute-done | bytes 65568 | tf_op jit(solution)/shard_map/rows_out/ppermute | solution.py:567
  111.6 2.1 %collective-permute-done.6.refs_4_.refs_3_ = bf16[256,128]{1,0:T(8,128)(2,1)S(1)} collective-permute-done((bf16[256,128]{1,0:T(8,128)(2,1)S(1)}, bf16[256,128]{1,0:T(8,128)(2,1)S(1)}, u32[]{:S(2)}, u32[]{:S(2)}) %collective-permute-start.6) | collective-permute-done | bytes 65568 | tf_op jit(solution)/shard_map/rows_out/ppermute | solution.py:567
  113.7 0.0 all-to-all-done.3.refs_0_
  113.8 3.9 %collective-permute-start.8 = (bf16[32,36,128]{2,1,0:T(8,128)(2,1)S(1)}, bf16[32,36,128]{2,1,0:T(8,128)(2,1)S(1)}, u32[]{:S(2)}, u32[]{:S(2)}) collective-permute-start(bf16[32,36,128]{2,1,0:T(8,128)(2,1)S(1)} %weights_back.2.refs_1_), channel_id=1, source_target_pairs={{0,16},{16,0},{1,17},{17,1},{2,18},{18,2},{3,19},{19,3},{4,20},{20... | collective-permute-start | bytes 884744 | tf_op jit(solution)/shard_map/weights_back/ppermute | solution.py:588
  117.7 0.9 bands_out.1
  118.6 0.4 collective-permute-done.8.refs_2_
  118.9 1.2 weights_back.3
  (3 shorter events, 0.0 us)
Async XLA Ops:
  0.6 34.9 %copy-start.8 = (f32[192,384]{1,0:T(8,128)S(1)}, f32[192,384]{1,0:T(8,128)}, u32[]{:S(2)}) copy-start(f32[192,384]{1,0:T(8,128)} %constant.74.clone.refs_3_.refs_2_) | copy-start | bytes 884740
  0.6 34.9 %copy-start.6 = (bf16[384,512]{1,0:T(8,128)(2,1)S(1)}, bf16[384,512]{1,0:T(8,128)(2,1)}, u32[]{:S(2)}) copy-start(bf16[384,512]{1,0:T(8,128)(2,1)} %constant.73.clone.refs_5_.refs_4_) | copy-start | bytes 1179652
  0.7 34.9 %copy-start.7 = (bf16[384,512]{1,0:T(8,128)(2,1)S(1)}, bf16[384,512]{1,0:T(8,128)(2,1)}, u32[]{:S(2)}) copy-start(bf16[384,512]{1,0:T(8,128)(2,1)} %constant.72.clone.refs_4_.refs_3_) | copy-start | bytes 1179652
  0.7 9.7 %copy-start.9 = (f32[384]{0:T(512)S(1)}, f32[384]{0:T(512)}, u32[]{:S(2)}) copy-start(f32[384]{0:T(512)} %param.23) | copy-start | bytes 4612
  0.7 34.9 %copy-start.1 = (bf16[64,384]{1,0:T(8,128)(2,1)S(1)}, bf16[64,384]{1,0:T(8,128)(2,1)}, u32[]{:S(2)}) copy-start(bf16[64,384]{1,0:T(8,128)(2,1)} %refs_9_.3) | copy-start | bytes 147460
  0.7 34.9 %copy-start = (bf16[384,640]{1,0:T(8,128)(2,1)S(1)}, bf16[384,640]{1,0:T(8,128)(2,1)}, u32[]{:S(2)}) copy-start(bf16[384,640]{1,0:T(8,128)(2,1)} %refs_8_.3) | copy-start | bytes 1474564
  0.7 34.9 %copy-start.2 = (f32[32,64]{1,0:T(8,128)S(1)}, f32[32,64]{1,0:T(8,128)}, u32[]{:S(2)}) copy-start(f32[32,64]{1,0:T(8,128)} %refs_8_.2) | copy-start | bytes 24580
  0.7 34.9 %copy-start.3 = (f32[16,64]{1,0:T(8,128)S(1)}, f32[16,64]{1,0:T(8,128)}, u32[]{:S(2)}) copy-start(f32[16,64]{1,0:T(8,128)} %refs_7_.1) | copy-start | bytes 12292
  0.7 34.9 %copy-start.4 = (f32[2,64]{1,0:T(2,128)S(1)}, f32[2,64]{1,0:T(2,128)}, u32[]{:S(2)}) copy-start(f32[2,64]{1,0:T(2,128)} %refs_6_.1) | copy-start | bytes 1540
  0.7 34.9 %copy-start.5 = (s32[2]{0:T(128)S(1)}, s32[2]{0:T(128)}, u32[]{:S(2)}) copy-start(s32[2]{0:T(128)} %refs_1_.1) | copy-start | bytes 28
  2.7 21.7 %all-to-all-start = ((f32[4,264,128]{2,1,0:T(8,128)}), f32[4,264,128]{2,1,0:T(8,128)S(1)}, u32[]{:S(2)}, u32[]{:S(2)}) async-start(f32[4,264,128]{2,1,0:T(8,128)} %rows_in.1), calls=%async_computation | async-start | bytes 1081344 | tf_op jit(solution)/shard_map/rows_in/all_to_all | solution.py:406
  24.5 13.7 %collective-permute-start.1 = (bf16[4,64,128]{2,1,0:T(8,128)(2,1)S(1)}, bf16[4,64,128]{2,1,0:T(8,128)(2,1)S(1)}, u32[]{:S(2)}, u32[]{:S(2)}) collective-permute-start(bf16[4,64,128]{2,1,0:T(8,128)(2,1)S(1)} %get-tuple-element.43), channel_id=1, source_target_pairs={{0,4},{4,0},{8,12},{12,8},{16,20},{20,16},{24,28},{28,24},{32,36},... | collective-permute-start | bytes 196616 | tf_op jit(solution)/shard_map/row_halo/ppermute | solution.py:473
  30.2 7.9 %collective-permute-start = (bf16[4,64,128]{2,1,0:T(8,128)(2,1)S(1)}, bf16[4,64,128]{2,1,0:T(8,128)(2,1)S(1)}, u32[]{:S(2)}, u32[]{:S(2)}) collective-permute-start(bf16[4,64,128]{2,1,0:T(8,128)(2,1)S(1)} %get-tuple-element.44), channel_id=1, source_target_pairs={{4,20},{12,28},{16,32},{20,4},{24,40},{28,12},{32,16},{36,52},{40,... | collective-permute-start | bytes 196616 | tf_op jit(solution)/shard_map/row_halo/ppermute | solution.py:474
  41.3 3.5 %collective-permute-start.7 = (bf16[32,36,128]{2,1,0:T(8,128)(2,1)S(1)}, bf16[32,36,128]{2,1,0:T(8,128)(2,1)S(1)}, u32[]{:S(2)}, u32[]{:S(2)}) collective-permute-start(bf16[32,36,128]{2,1,0:T(8,128)(2,1)S(1)} %get-tuple-element.39), channel_id=1, source_target_pairs={{0,16},{16,0},{1,17},{17,1},{2,18},{18,2},{3,19},{19,3},{4,20},{20... | collective-permute-start | bytes 884744 | tf_op jit(solution)/shard_map/weights_core/ppermute | solution.py:545
  71.2 18.4 %all-to-all-start.2 = ((bf16[12,36,128]{2,1,0:T(8,128)(2,1)}), bf16[12,36,128]{2,1,0:T(8,128)(2,1)S(1)}, u32[]{:S(2)}, u32[]{:S(2)}) async-start(bf16[12,36,128]{2,1,0:T(8,128)(2,1)} %broadcast_in_dim.2), calls=%async_computation.2 | async-start | bytes 245760 | tf_op jit(solution)/shard_map/weights_length/all_to_all | solution.py:406
  76.1 9.2 %collective-permute-start.2 = (bf16[4,64,128]{2,1,0:T(8,128)(2,1)S(1)}, bf16[4,64,128]{2,1,0:T(8,128)(2,1)S(1)}, u32[]{:S(2)}, u32[]{:S(2)}) collective-permute-start(bf16[4,64,128]{2,1,0:T(8,128)(2,1)S(1)} %get-tuple-element.30), channel_id=1, source_target_pairs={{4,20},{12,28},{16,32},{20,4},{24,40},{28,12},{32,16},{36,52},{40,... | collective-permute-start | bytes 196616 | tf_op jit(solution)/shard_map/fields/ppermute | solution.py:548
  82.2 6.2 %collective-permute-start.3 = (bf16[4,64,128]{2,1,0:T(8,128)(2,1)S(1)}, bf16[4,64,128]{2,1,0:T(8,128)(2,1)S(1)}, u32[]{:S(2)}, u32[]{:S(2)}) collective-permute-start(bf16[4,64,128]{2,1,0:T(8,128)(2,1)S(1)} %get-tuple-element.31), channel_id=1, source_target_pairs={{0,4},{4,0},{8,12},{12,8},{16,20},{20,16},{24,28},{28,24},{32,36},... | collective-permute-start | bytes 196616 | tf_op jit(solution)/shard_map/fields/ppermute | solution.py:549
  90.4 23.4 %all-to-all-start.3 = ((bf16[32,36,128]{2,1,0:T(8,128)(2,1)}), bf16[32,36,128]{2,1,0:T(8,128)(2,1)S(1)}, u32[]{:S(2)}, u32[]{:S(2)}) async-start(bf16[32,36,128]{2,1,0:T(8,128)(2,1)} %weights_length.1), calls=%async_computation.3 | async-start | bytes 655360 | tf_op jit(solution)/shard_map/weights_back/all_to_all | solution.py:406
  96.5 11.4 %collective-permute-start.4 = (bf16[256,128]{1,0:T(8,128)(2,1)S(1)}, bf16[256,128]{1,0:T(8,128)(2,1)S(1)}, u32[]{:S(2)}, u32[]{:S(2)}) collective-permute-start(bf16[256,128]{1,0:T(8,128)(2,1)S(1)} %get-tuple-element.33), channel_id=1, source_target_pairs={{0,4},{4,0},{8,12},{12,8},{1,5},{5,1},{9,13},{13,9},{2,6},{6,2},{1... | collective-permute-start | bytes 196616 | tf_op jit(solution)/shard_map/rows_out/ppermute | solution.py:567
  100.6 11.0 %collective-permute-start.5 = (bf16[256,128]{1,0:T(8,128)(2,1)S(1)}, bf16[256,128]{1,0:T(8,128)(2,1)S(1)}, u32[]{:S(2)}, u32[]{:S(2)}) collective-permute-start(bf16[256,128]{1,0:T(8,128)(2,1)S(1)} %get-tuple-element.34), channel_id=1, source_target_pairs={{0,8},{4,12},{8,0},{12,4},{1,9},{5,13},{9,1},{13,5},{2,10},{6,14},... | collective-permute-start | bytes 196616 | tf_op jit(solution)/shard_map/rows_out/ppermute | solution.py:567
  105.8 8.0 %collective-permute-start.6 = (bf16[256,128]{1,0:T(8,128)(2,1)S(1)}, bf16[256,128]{1,0:T(8,128)(2,1)S(1)}, u32[]{:S(2)}, u32[]{:S(2)}) collective-permute-start(bf16[256,128]{1,0:T(8,128)(2,1)S(1)} %get-tuple-element.35), channel_id=1, source_target_pairs={{0,12},{4,8},{8,4},{12,0},{1,13},{5,9},{9,5},{13,1},{2,14},{6,10},... | collective-permute-start | bytes 196616 | tf_op jit(solution)/shard_map/rows_out/ppermute | solution.py:567
  113.8 5.1 %collective-permute-start.8 = (bf16[32,36,128]{2,1,0:T(8,128)(2,1)S(1)}, bf16[32,36,128]{2,1,0:T(8,128)(2,1)S(1)}, u32[]{:S(2)}, u32[]{:S(2)}) collective-permute-start(bf16[32,36,128]{2,1,0:T(8,128)(2,1)S(1)} %weights_back.2.refs_1_), channel_id=1, source_target_pairs={{0,16},{16,0},{1,17},{17,1},{2,18},{18,2},{3,19},{19,3},{4,20},{20... | collective-permute-start | bytes 884744 | tf_op jit(solution)/shard_map/weights_back/ppermute | solution.py:588

commit v11 on v10

--- a/solution.py
+++ b/solution.py
@@ -50,7 +50,9 @@
 def split_dot(x, high, low, dims=((1,), (0,))):
     x_high = x.astype(BF)
     x_low = (x - x_high.astype(F32)).astype(BF)
-    return dot(x_high, high, dims) + (dot(x_low, high, dims) + dot(x_high, low, dims))
+    both = dot(jnp.concatenate([x_high, x_low], axis=0), high, dims)
+    count = x.shape[0]
+    return both[:count] + (both[count:] + dot(x_high, low, dims))
 
 
 def filtered(x, scale, high, low):
@@ -158,7 +160,7 @@
 ):
     taken = features_ref.shape[0]
     sectors = row_ref.shape[0]
-    channels, hidden_units = w_tendency_ref.shape
+    hidden_units, channels = w_tendency_ref.shape
     rows = taken * channels
     lon_total = features_ref.shape[2]
     classes = relief_ref.shape[0]
@@ -190,7 +192,7 @@
         features_ref[k, 9 * channels :, :] = dot(table, pick, ((0,), (0,))).astype(BF)
         preact_ref[k] = dot(w_hidden_ref[...], features_ref[k]) + bias
         tendency_grad = moist_grad[k * channels : (k + 1) * channels].astype(BF)
-        hidden_grad_ref[k] = dot(w_tendency_ref[...], tendency_grad, ((0,), (0,)))
+        hidden_grad_ref[k] = dot(w_tendency_ref[...], tendency_grad)
 
 
 def weights_kernel(
@@ -203,6 +205,7 @@
     preact_ref,
     hidden_grad_ref,
     w_hidden_ref,
+    w_stencil_ref,
     w_tendency_ref,
     to_across_ref,
     to_inside_ref,
@@ -217,7 +220,6 @@
     taken, in_channels, lon_total = features_ref.shape
     channels, hidden_units = w_tendency_ref.shape
     group = 3 * channels
-    w_stencil = w_hidden_ref[:, : 3 * group]
     state = joined(row_ref, 0, taken * channels)
     grad_in = jnp.zeros((hidden_units, in_channels), F32)
     grad_out = jnp.zeros((channels, hidden_units), F32)
@@ -249,7 +251,7 @@
         grad_in += dot(preact_grad, features_ref[k], ((1,), (1,)))
         grad_bias += dot(ones, preact_grad, ((1,), (1,)))
         moist_ref[part, :] = state[part] + dot(w_tendency_ref[...], hidden)
-        stencil_grad = dot(w_stencil, preact_grad, ((0,), (0,)))
+        stencil_grad = dot(w_stencil_ref[...], preact_grad)
         sums.append([])
         for a in range(3):
             total = None
@@ -496,7 +498,7 @@
             seed_table,
             w_hidden,
             b_hidden.reshape(1, hidden_units),
-            w_tendency,
+            w_tendency.T,
         )
 
     pieces = lax.axis_size(PLANE)
@@ -518,7 +520,7 @@
                 shape(share, F32),
                 shape(share, BF),
             ),
-            10,
+            11,
             smem=1,
             scratch=[
                 pltpu.VMEM(features_shape, BF),
@@ -537,6 +539,7 @@
             preact,
             hidden_grad,
             w_hidden,
+            w_hidden[:, : 9 * channels].T,
             w_tendency,
         )
 
@@ -557,9 +560,9 @@
         )(place, moist, scale, high, low, grad_rows, from_across, from_inside)
 
     with jax.named_scope("weights_plane"):
-        parts = exchange(halves, PLANE)
-        piece = jnp.sum(parts.astype(F32), 0, keepdims=True).astype(BF)
-        copies = jnp.broadcast_to(piece, (length, piece_rows, LANES))
+        copies = call(sum_and_copy_kernel, shape((length, piece_rows, LANES), BF), 2)(
+            exchange(halves, PLANE), from_across
+        )
 
     with jax.named_scope("rows_out"):
         received = [fields[0]]

time: 121 us -> 121 us (level)
  blocking collectives: 25.5 us -> 0 us
  starting transfers between devices: 56.2 us -> 71.2 us
  waiting for transfers between devices: 24.9 us -> 35.4 us
    all_to_all x1 -> x0, blocking collectives: 25.5 us -> none  [exchange(): return lax.all_to_all(x, axes, 0, 0, tiled=True)]
    all_to_all x3 -> x4, starting transfers between devices: 18.7 us -> 33.8 us  [exchange(): return lax.all_to_all(x, axes, 0, 0, tiled=True)]
    all_to_all x3 -> x4, waiting for transfers between devices: 14.1 us -> 21.6 us  [exchange(): return lax.all_to_all(x, axes, 0, 0, tiled=True)]
    ppermute x1, starting transfers between devices: 6.06 us -> 1.92 us  [on_device(): from_across = lax.ppermute(to_across, PLACE, across_swaps)]
    ppermute x1, waiting for transfers between devices: 0.01 us -> 3.95 us  [on_device(): from_across = lax.ppermute(to_across, PLACE, across_swaps)]
    ppermute x1, starting transfers between devices: 3.16 us -> 5.32 us  [on_device(): from_inside = lax.ppermute(to_inside, PLACE, inside_swaps)]
    ppermute x1, starting transfers between devices: 3.9 us -> 5.8 us  [on_device(): other = lax.ppermute(own, 'core', swap)]
    ppermute x1, waiting for transfers between devices: 3.04 us -> 1.64 us  [on_device(): from_inside = lax.ppermute(to_inside, PLACE, inside_swaps)]
  transfers between devices with their start and end apart: 12 -> 13, of which waited for: 6 -> 9; matrix products, arithmetic and copies ran while one was open for 0% -> 0% of each run, Pallas kernels for 4% -> 3%
where the time goes in v11:
time: 121 us; the launch traced here: 120 us
  starting transfers between devices  71.2 us (59%)
  waiting for transfers between devices  35.4 us (29%)
  Pallas kernels  11.7 us (10%)
    all_to_all x4, starting transfers between devices, exchange(): return lax.all_to_all(x, axes, 0, 0, tiled=True)  33.8 us
    all_to_all x4, waiting for transfers between devices, exchange(): return lax.all_to_all(x, axes, 0, 0, tiled=True)  21.6 us
    ppermute x3, starting transfers between devices, on_device(): lax.ppermute(fields[t], 'lon', [(i, i ^ t) for i in range(sectors)])  11.4 us
    ppermute x3, waiting for transfers between devices, on_device(): lax.ppermute(fields[t], 'lon', [(i, i ^ t) for i in range(sectors)])  6.17 us
    ppermute x1, starting transfers between devices, on_device(): other = lax.ppermute(own, 'core', swap)  5.8 us
    ppermute x1, starting transfers between devices, on_device(): inside = lax.ppermute(edge_row(1 - pair), PLACE, inside_swaps)  5.75 us
    ppermute x1, starting transfers between devices, on_device(): across = lax.ppermute(edge_row(pair), PLACE, across_swaps)  5.34 us
    ppermute x1, starting transfers between devices, on_device(): from_inside = lax.ppermute(to_inside, PLACE, inside_swaps)  5.32 us
  transfers between devices with their start and end apart: 13, of which 9 were waited for; matrix products, arithmetic and copies ran while one was open for 0% of the time, Pallas kernels for 3%

profile of v11, /device:TPU:1, one launch (start us, length us, event | category | flops | bytes accessed | tf_op | source)
XLA Modules:
  0.0 120.5 jit_solution(13946702974577418310)
XLA Ops:
  0.6 0.0 copy-start.9
  0.6 0.0 copy-start.1
  0.7 0.0 copy-start
  0.7 0.0 copy-start.2
  0.7 0.0 copy-start.3
  0.7 0.0 copy-start.4
  0.7 0.0 copy-start.5
  0.7 0.0 copy-start.6
  0.7 0.0 copy-start.7
  0.7 0.0 copy-start.8
  0.8 2.0 %rows_in.1 = f32[4,264,128]{2,1,0:T(8,128)} custom-call(s32[1]{0:T(128)} %bitcast.refs_0_, f32[2,256,128]{2,1,0:T(8,128)} %bitcast.11, f32[2,256,128]{2,1,0:T(8,128)} %bitcast.12, s32[4,128]{1,0:T(4,128)} %refs_3_.3, s32[4,128]{1,0:T(4,128)} %refs_4_.3), custom_call_target="tpu_custom_call" | custom-call | bytes 1000000 | tf_op jit(solution)/shard_map/rows_in/pallas_call | solution.py:442
  2.7 7.7 %all-to-all-start = ((f32[4,264,128]{2,1,0:T(8,128)}), f32[4,264,128]{2,1,0:T(8,128)S(1)}, u32[]{:S(2)}, u32[]{:S(2)}) async-start(f32[4,264,128]{2,1,0:T(8,128)} %rows_in.1), calls=%async_computation | async-start | bytes 1081344 | tf_op jit(solution)/shard_map/rows_in/all_to_all | solution.py:408
  10.4 0.0 copy-done.9
  10.4 0.0 copy-done.1
  10.4 0.1 copy.19
  10.5 0.0 copy-done
  10.6 0.2 copy.21
  10.8 13.7 %all-to-all-done.refs_2_.refs_3_ = f32[4,264,128]{2,1,0:T(8,128)S(1)} async-done(((f32[4,264,128]{2,1,0:T(8,128)}), f32[4,264,128]{2,1,0:T(8,128)S(1)}, u32[]{:S(2)}, u32[]{:S(2)}) %all-to-all-start) | async-done | bytes 540704 | tf_op jit(solution)/shard_map/rows_in/all_to_all | solution.py:408
  24.5 5.8 %collective-permute-start.1 = (bf16[4,64,128]{2,1,0:T(8,128)(2,1)S(1)}, bf16[4,64,128]{2,1,0:T(8,128)(2,1)S(1)}, u32[]{:S(2)}, u32[]{:S(2)}) collective-permute-start(bf16[4,64,128]{2,1,0:T(8,128)(2,1)S(1)} %get-tuple-element.43), channel_id=1, source_target_pairs={{0,4},{4,0},{8,12},{12,8},{16,20},{20,16},{24,28},{28,24},{32,36},... | collective-permute-start | bytes 196616 | tf_op jit(solution)/shard_map/row_halo/ppermute | solution.py:475
  30.3 5.3 %collective-permute-start = (bf16[4,64,128]{2,1,0:T(8,128)(2,1)S(1)}, bf16[4,64,128]{2,1,0:T(8,128)(2,1)S(1)}, u32[]{:S(2)}, u32[]{:S(2)}) collective-permute-start(bf16[4,64,128]{2,1,0:T(8,128)(2,1)S(1)} %get-tuple-element.44), channel_id=1, source_target_pairs={{4,20},{12,28},{16,32},{20,4},{24,40},{28,12},{32,16},{36,52},{40,... | collective-permute-start | bytes 196616 | tf_op jit(solution)/shard_map/row_halo/ppermute | solution.py:476
  35.6 0.0 copy-done.2
  35.6 0.0 copy-done.3
  35.6 0.0 copy-done.4
  35.6 0.0 copy-done.5
  35.6 0.0 copy-done.6
  35.7 0.0 copy-done.7
  35.7 0.0 copy-done.8
  35.7 2.3 %early.1 = (f32[128,512]{1,0:T(8,128)S(1)}, bf16[2,640,512]{2,1,0:T(8,128)(2,1)S(1)}, f32[2,384,512]{2,1,0:T(8,128)S(1)}, f32[2,384,512]{2,1,0:T(8,128)S(1)}) custom-call(s32[1]{0:T(128)} %bitcast.refs_0_, s32[2]{0:T(128)S(1)} %copy-done.5, f32[4,264,128]{2,1,0:T(8,128)S(1)} %all-to-all-done.refs_2_.refs_3_, f32[192,384]{1,0:T(8,128)S(1)} %copy-done.8, ...), custom_call_target="tpu_custom_call" | custom-call | flops 3000000000 | bytes 1000000 | tf_op jit(solution)/shard_map/early/pallas_call | solution.py:482
  37.9 0.0 collective-permute-done.1.refs_2_
  38.0 0.0 collective-permute-done.refs_1_
  38.0 3.2 %weights.1 = (bf16[4,64,128]{2,1,0:T(8,128)(2,1)S(1)}, bf16[4,64,128]{2,1,0:T(8,128)(2,1)S(1)}, f32[128,512]{1,0:T(8,128)S(1)}, f32[4,128,128]{2,1,0:T(8,128)S(1...) custom-call(s32[1]{0:T(128)} %bitcast.refs_0_, bf16[4,64,128]{2,1,0:T(8,128)(2,1)S(1)} %collective-permute-done.refs_1_, ...), custom_call_target="tpu_custom_call" | custom-call | flops 3000000000 | bytes 1000000 | tf_op jit(solution)/shard_map/weights/pallas_call | solution.py:513
  41.1 1.9 %collective-permute-start.7 = (bf16[32,36,128]{2,1,0:T(8,128)(2,1)S(1)}, bf16[32,36,128]{2,1,0:T(8,128)(2,1)S(1)}, u32[]{:S(2)}, u32[]{:S(2)}) collective-permute-start(bf16[32,36,128]{2,1,0:T(8,128)(2,1)S(1)} %get-tuple-element.39), channel_id=1, source_target_pairs={{0,16},{16,0},{1,17},{17,1},{2,18},{18,2},{3,19},{19,3},{4,20},{20... | collective-permute-start | bytes 884744 | tf_op jit(solution)/shard_map/weights_core/ppermute | solution.py:548
  43.1 1.6 %collective-permute-done.7 = bf16[32,36,128]{2,1,0:T(8,128)(2,1)S(1)} collective-permute-done((bf16[32,36,128]{2,1,0:T(8,128)(2,1)S(1)}, bf16[32,36,128]{2,1,0:T(8,128)(2,1)S(1)}, u32[]{:S(2)}, u32[]{:S(2)}) %collective-permute-start.7) | collective-permute-done | bytes 294944 | tf_op jit(solution)/shard_map/weights_core/ppermute | solution.py:548
  44.7 0.8 add_convert_fusion
  45.5 14.6 %all-to-all-start.1 = ((bf16[32,36,128]{2,1,0:T(8,128)(2,1)}), bf16[32,36,128]{2,1,0:T(8,128)(2,1)S(1)}, u32[]{:S(2)}, u32[]{:S(2)}) async-start(bf16[32,36,128]{2,1,0:T(8,128)(2,1)} %add_convert_fusion), calls=%async_computation.1 | async-start | bytes 655360 | tf_op jit(solution)/shard_map/weights_plane/all_to_all | solution.py:408
  60.1 1.9 %collective-permute-start.2 = (bf16[4,64,128]{2,1,0:T(8,128)(2,1)S(1)}, bf16[4,64,128]{2,1,0:T(8,128)(2,1)S(1)}, u32[]{:S(2)}, u32[]{:S(2)}) collective-permute-start(bf16[4,64,128]{2,1,0:T(8,128)(2,1)S(1)} %get-tuple-element.30), channel_id=1, source_target_pairs={{4,20},{12,28},{16,32},{20,4},{24,40},{28,12},{32,16},{36,52},{40,... | collective-permute-start | bytes 196616 | tf_op jit(solution)/shard_map/fields/ppermute | solution.py:551
  62.0 4.0 %collective-permute-done.2.refs_6_.refs_1_ = bf16[4,64,128]{2,1,0:T(8,128)(2,1)S(1)} collective-permute-done((bf16[4,64,128]{2,1,0:T(8,128)(2,1)S(1)}, bf16[4,64,128]{2,1,0:T(8,128)(2,1)S(1)}, u32[]{:S(2)}, u32[]{:S(2)}) %collective-permute-start.2) | collective-permute-done | bytes 65568 | tf_op jit(solution)/shard_map/fields/ppermute | solution.py:551
  66.0 5.2 %all-to-all-done.1.refs_0_ = bf16[32,36,128]{2,1,0:T(8,128)(2,1)S(1)} async-done(((bf16[32,36,128]{2,1,0:T(8,128)(2,1)}), bf16[32,36,128]{2,1,0:T(8,128)(2,1)S(1)}, u32[]{:S(2)}, u32[]{:S(2)}) %all-to-all-start.1) | async-done | bytes 294944 | tf_op jit(solution)/shard_map/weights_plane/all_to_all | solution.py:408
  71.2 0.7 weights_plane.1
  71.9 4.9 %all-to-all-start.2 = ((bf16[12,36,128]{2,1,0:T(8,128)(2,1)}), bf16[12,36,128]{2,1,0:T(8,128)(2,1)S(1)}, u32[]{:S(2)}, u32[]{:S(2)}) async-start(bf16[12,36,128]{2,1,0:T(8,128)(2,1)} %weights_plane.1), calls=%async_computation.2 | async-start | bytes 245760 | tf_op jit(solution)/shard_map/weights_length/all_to_all | solution.py:408
  76.8 5.3 %collective-permute-start.3 = (bf16[4,64,128]{2,1,0:T(8,128)(2,1)S(1)}, bf16[4,64,128]{2,1,0:T(8,128)(2,1)S(1)}, u32[]{:S(2)}, u32[]{:S(2)}) collective-permute-start(bf16[4,64,128]{2,1,0:T(8,128)(2,1)S(1)} %get-tuple-element.31), channel_id=1, source_target_pairs={{0,4},{4,0},{8,12},{12,8},{16,20},{20,16},{24,28},{28,24},{32,36},... | collective-permute-start | bytes 196616 | tf_op jit(solution)/shard_map/fields/ppermute | solution.py:552
  82.2 1.6 %collective-permute-done.3.refs_7_ = bf16[4,64,128]{2,1,0:T(8,128)(2,1)S(1)} collective-permute-done((bf16[4,64,128]{2,1,0:T(8,128)(2,1)S(1)}, bf16[4,64,128]{2,1,0:T(8,128)(2,1)S(1)}, u32[]{:S(2)}, u32[]{:S(2)}) %collective-permute-start.3) | collective-permute-done | bytes 65568 | tf_op jit(solution)/shard_map/fields/ppermute | solution.py:552
  83.8 0.7 fields.1
  84.5 2.8 %all-to-all-done.2.refs_0_ = bf16[12,36,128]{2,1,0:T(8,128)(2,1)S(1)} async-done(((bf16[12,36,128]{2,1,0:T(8,128)(2,1)}), bf16[12,36,128]{2,1,0:T(8,128)(2,1)S(1)}, u32[]{:S(2)}, u32[]{:S(2)}) %all-to-all-start.2) | async-done | bytes 110624 | tf_op jit(solution)/shard_map/weights_length/all_to_all | solution.py:408
  87.3 0.8 weights_length.1
  88.0 6.6 %all-to-all-start.3 = ((bf16[32,36,128]{2,1,0:T(8,128)(2,1)}), bf16[32,36,128]{2,1,0:T(8,128)(2,1)S(1)}, u32[]{:S(2)}, u32[]{:S(2)}) async-start(bf16[32,36,128]{2,1,0:T(8,128)(2,1)} %weights_length.1), calls=%async_computation.3 | async-start | bytes 655360 | tf_op jit(solution)/shard_map/weights_back/all_to_all | solution.py:408
  94.6 4.0 %collective-permute-start.4 = (bf16[256,128]{1,0:T(8,128)(2,1)S(1)}, bf16[256,128]{1,0:T(8,128)(2,1)S(1)}, u32[]{:S(2)}, u32[]{:S(2)}) collective-permute-start(bf16[256,128]{1,0:T(8,128)(2,1)S(1)} %get-tuple-element.33), channel_id=1, source_target_pairs={{0,4},{4,0},{8,12},{12,8},{1,5},{5,1},{9,13},{13,9},{2,6},{6,2},{1... | collective-permute-start | bytes 196616 | tf_op jit(solution)/shard_map/rows_out/ppermute | solution.py:570
  98.7 5.2 %collective-permute-start.5 = (bf16[256,128]{1,0:T(8,128)(2,1)S(1)}, bf16[256,128]{1,0:T(8,128)(2,1)S(1)}, u32[]{:S(2)}, u32[]{:S(2)}) collective-permute-start(bf16[256,128]{1,0:T(8,128)(2,1)S(1)} %get-tuple-element.34), channel_id=1, source_target_pairs={{0,8},{4,12},{8,0},{12,4},{1,9},{5,13},{9,1},{13,5},{2,10},{6,14},... | collective-permute-start | bytes 196616 | tf_op jit(solution)/shard_map/rows_out/ppermute | solution.py:570
  103.9 2.1 %collective-permute-start.6 = (bf16[256,128]{1,0:T(8,128)(2,1)S(1)}, bf16[256,128]{1,0:T(8,128)(2,1)S(1)}, u32[]{:S(2)}, u32[]{:S(2)}) collective-permute-start(bf16[256,128]{1,0:T(8,128)(2,1)S(1)} %get-tuple-element.35), channel_id=1, source_target_pairs={{0,12},{4,8},{8,4},{12,0},{1,13},{5,9},{9,5},{13,1},{2,14},{6,10},... | collective-permute-start | bytes 196616 | tf_op jit(solution)/shard_map/rows_out/ppermute | solution.py:570
  106.0 0.0 collective-permute-done.4.refs_2_.refs_1_
  106.1 3.0 %collective-permute-done.5.refs_3_.refs_2_ = bf16[256,128]{1,0:T(8,128)(2,1)S(1)} collective-permute-done((bf16[256,128]{1,0:T(8,128)(2,1)S(1)}, bf16[256,128]{1,0:T(8,128)(2,1)S(1)}, u32[]{:S(2)}, u32[]{:S(2)}) %collective-permute-start.5) | collective-permute-done | bytes 65568 | tf_op jit(solution)/shard_map/rows_out/ppermute | solution.py:570
  109.1 3.2 %collective-permute-done.6.refs_4_.refs_3_ = bf16[256,128]{1,0:T(8,128)(2,1)S(1)} collective-permute-done((bf16[256,128]{1,0:T(8,128)(2,1)S(1)}, bf16[256,128]{1,0:T(8,128)(2,1)S(1)}, u32[]{:S(2)}, u32[]{:S(2)}) %collective-permute-start.6) | collective-permute-done | bytes 65568 | tf_op jit(solution)/shard_map/rows_out/ppermute | solution.py:570
  112.2 0.0 all-to-all-done.3.refs_0_
  112.3 5.8 %collective-permute-start.8 = (bf16[32,36,128]{2,1,0:T(8,128)(2,1)S(1)}, bf16[32,36,128]{2,1,0:T(8,128)(2,1)S(1)}, u32[]{:S(2)}, u32[]{:S(2)}) collective-permute-start(bf16[32,36,128]{2,1,0:T(8,128)(2,1)S(1)} %weights_back.2.refs_1_), channel_id=1, source_target_pairs={{0,16},{16,0},{1,17},{17,1},{2,18},{18,2},{3,19},{19,3},{4,20},{20... | collective-permute-start | bytes 884744 | tf_op jit(solution)/shard_map/weights_back/ppermute | solution.py:591
  118.1 0.9 bands_out.1
  118.9 0.4 collective-permute-done.8.refs_2_
  119.3 1.2 weights_back.3
  (3 shorter events, 0.0 us)
Async XLA Ops:
  0.6 9.8 %copy-start.9 = (f32[384]{0:T(512)S(1)}, f32[384]{0:T(512)}, u32[]{:S(2)}) copy-start(f32[384]{0:T(512)} %param.23) | copy-start | bytes 4612
  0.6 9.8 %copy-start.1 = (bf16[64,384]{1,0:T(8,128)(2,1)S(1)}, bf16[64,384]{1,0:T(8,128)(2,1)}, u32[]{:S(2)}) copy-start(bf16[64,384]{1,0:T(8,128)(2,1)} %refs_10_.1) | copy-start | bytes 147460
  0.7 9.9 %copy-start = (bf16[384,640]{1,0:T(8,128)(2,1)S(1)}, bf16[384,640]{1,0:T(8,128)(2,1)}, u32[]{:S(2)}) copy-start(bf16[384,640]{1,0:T(8,128)(2,1)} %refs_8_.3) | copy-start | bytes 1474564
  0.7 34.9 %copy-start.2 = (f32[32,64]{1,0:T(8,128)S(1)}, f32[32,64]{1,0:T(8,128)}, u32[]{:S(2)}) copy-start(f32[32,64]{1,0:T(8,128)} %refs_8_.2) | copy-start | bytes 24580
  0.7 34.9 %copy-start.3 = (f32[16,64]{1,0:T(8,128)S(1)}, f32[16,64]{1,0:T(8,128)}, u32[]{:S(2)}) copy-start(f32[16,64]{1,0:T(8,128)} %refs_7_.1) | copy-start | bytes 12292
  0.7 34.9 %copy-start.4 = (f32[2,64]{1,0:T(2,128)S(1)}, f32[2,64]{1,0:T(2,128)}, u32[]{:S(2)}) copy-start(f32[2,64]{1,0:T(2,128)} %refs_6_.1) | copy-start | bytes 1540
  0.7 34.9 %copy-start.5 = (s32[2]{0:T(128)S(1)}, s32[2]{0:T(128)}, u32[]{:S(2)}) copy-start(s32[2]{0:T(128)} %refs_1_.1) | copy-start | bytes 28
  0.7 34.9 %copy-start.6 = (bf16[384,512]{1,0:T(8,128)(2,1)S(1)}, bf16[384,512]{1,0:T(8,128)(2,1)}, u32[]{:S(2)}) copy-start(bf16[384,512]{1,0:T(8,128)(2,1)} %constant.70.clone.refs_5_.refs_4_) | copy-start | bytes 1179652
  0.7 34.9 %copy-start.7 = (bf16[384,512]{1,0:T(8,128)(2,1)S(1)}, bf16[384,512]{1,0:T(8,128)(2,1)}, u32[]{:S(2)}) copy-start(bf16[384,512]{1,0:T(8,128)(2,1)} %constant.69.clone.refs_4_.refs_3_) | copy-start | bytes 1179652
  0.7 34.9 %copy-start.8 = (f32[192,384]{1,0:T(8,128)S(1)}, f32[192,384]{1,0:T(8,128)}, u32[]{:S(2)}) copy-start(f32[192,384]{1,0:T(8,128)} %constant.71.clone.refs_3_.refs_2_) | copy-start | bytes 884740
  2.7 21.7 %all-to-all-start = ((f32[4,264,128]{2,1,0:T(8,128)}), f32[4,264,128]{2,1,0:T(8,128)S(1)}, u32[]{:S(2)}, u32[]{:S(2)}) async-start(f32[4,264,128]{2,1,0:T(8,128)} %rows_in.1), calls=%async_computation | async-start | bytes 1081344 | tf_op jit(solution)/shard_map/rows_in/all_to_all | solution.py:408
  24.5 13.4 %collective-permute-start.1 = (bf16[4,64,128]{2,1,0:T(8,128)(2,1)S(1)}, bf16[4,64,128]{2,1,0:T(8,128)(2,1)S(1)}, u32[]{:S(2)}, u32[]{:S(2)}) collective-permute-start(bf16[4,64,128]{2,1,0:T(8,128)(2,1)S(1)} %get-tuple-element.43), channel_id=1, source_target_pairs={{0,4},{4,0},{8,12},{12,8},{16,20},{20,16},{24,28},{28,24},{32,36},... | collective-permute-start | bytes 196616 | tf_op jit(solution)/shard_map/row_halo/ppermute | solution.py:475
  30.3 7.7 %collective-permute-start = (bf16[4,64,128]{2,1,0:T(8,128)(2,1)S(1)}, bf16[4,64,128]{2,1,0:T(8,128)(2,1)S(1)}, u32[]{:S(2)}, u32[]{:S(2)}) collective-permute-start(bf16[4,64,128]{2,1,0:T(8,128)(2,1)S(1)} %get-tuple-element.44), channel_id=1, source_target_pairs={{4,20},{12,28},{16,32},{20,4},{24,40},{28,12},{32,16},{36,52},{40,... | collective-permute-start | bytes 196616 | tf_op jit(solution)/shard_map/row_halo/ppermute | solution.py:476
  41.1 3.5 %collective-permute-start.7 = (bf16[32,36,128]{2,1,0:T(8,128)(2,1)S(1)}, bf16[32,36,128]{2,1,0:T(8,128)(2,1)S(1)}, u32[]{:S(2)}, u32[]{:S(2)}) collective-permute-start(bf16[32,36,128]{2,1,0:T(8,128)(2,1)S(1)} %get-tuple-element.39), channel_id=1, source_target_pairs={{0,16},{16,0},{1,17},{17,1},{2,18},{18,2},{3,19},{19,3},{4,20},{20... | collective-permute-start | bytes 884744 | tf_op jit(solution)/shard_map/weights_core/ppermute | solution.py:548
  45.5 25.7 %all-to-all-start.1 = ((bf16[32,36,128]{2,1,0:T(8,128)(2,1)}), bf16[32,36,128]{2,1,0:T(8,128)(2,1)S(1)}, u32[]{:S(2)}, u32[]{:S(2)}) async-start(bf16[32,36,128]{2,1,0:T(8,128)(2,1)} %add_convert_fusion), calls=%async_computation.1 | async-start | bytes 655360 | tf_op jit(solution)/shard_map/weights_plane/all_to_all | solution.py:408
  60.1 5.9 %collective-permute-start.2 = (bf16[4,64,128]{2,1,0:T(8,128)(2,1)S(1)}, bf16[4,64,128]{2,1,0:T(8,128)(2,1)S(1)}, u32[]{:S(2)}, u32[]{:S(2)}) collective-permute-start(bf16[4,64,128]{2,1,0:T(8,128)(2,1)S(1)} %get-tuple-element.30), channel_id=1, source_target_pairs={{4,20},{12,28},{16,32},{20,4},{24,40},{28,12},{32,16},{36,52},{40,... | collective-permute-start | bytes 196616 | tf_op jit(solution)/shard_map/fields/ppermute | solution.py:551
  71.9 15.4 %all-to-all-start.2 = ((bf16[12,36,128]{2,1,0:T(8,128)(2,1)}), bf16[12,36,128]{2,1,0:T(8,128)(2,1)S(1)}, u32[]{:S(2)}, u32[]{:S(2)}) async-start(bf16[12,36,128]{2,1,0:T(8,128)(2,1)} %weights_plane.1), calls=%async_computation.2 | async-start | bytes 245760 | tf_op jit(solution)/shard_map/weights_length/all_to_all | solution.py:408
  76.8 7.0 %collective-permute-start.3 = (bf16[4,64,128]{2,1,0:T(8,128)(2,1)S(1)}, bf16[4,64,128]{2,1,0:T(8,128)(2,1)S(1)}, u32[]{:S(2)}, u32[]{:S(2)}) collective-permute-start(bf16[4,64,128]{2,1,0:T(8,128)(2,1)S(1)} %get-tuple-element.31), channel_id=1, source_target_pairs={{0,4},{4,0},{8,12},{12,8},{16,20},{20,16},{24,28},{28,24},{32,36},... | collective-permute-start | bytes 196616 | tf_op jit(solution)/shard_map/fields/ppermute | solution.py:552
  88.0 24.2 %all-to-all-start.3 = ((bf16[32,36,128]{2,1,0:T(8,128)(2,1)}), bf16[32,36,128]{2,1,0:T(8,128)(2,1)S(1)}, u32[]{:S(2)}, u32[]{:S(2)}) async-start(bf16[32,36,128]{2,1,0:T(8,128)(2,1)} %weights_length.1), calls=%async_computation.3 | async-start | bytes 655360 | tf_op jit(solution)/shard_map/weights_back/all_to_all | solution.py:408
  94.6 11.4 %collective-permute-start.4 = (bf16[256,128]{1,0:T(8,128)(2,1)S(1)}, bf16[256,128]{1,0:T(8,128)(2,1)S(1)}, u32[]{:S(2)}, u32[]{:S(2)}) collective-permute-start(bf16[256,128]{1,0:T(8,128)(2,1)S(1)} %get-tuple-element.33), channel_id=1, source_target_pairs={{0,4},{4,0},{8,12},{12,8},{1,5},{5,1},{9,13},{13,9},{2,6},{6,2},{1... | collective-permute-start | bytes 196616 | tf_op jit(solution)/shard_map/rows_out/ppermute | solution.py:570
  98.7 10.4 %collective-permute-start.5 = (bf16[256,128]{1,0:T(8,128)(2,1)S(1)}, bf16[256,128]{1,0:T(8,128)(2,1)S(1)}, u32[]{:S(2)}, u32[]{:S(2)}) collective-permute-start(bf16[256,128]{1,0:T(8,128)(2,1)S(1)} %get-tuple-element.34), channel_id=1, source_target_pairs={{0,8},{4,12},{8,0},{12,4},{1,9},{5,13},{9,1},{13,5},{2,10},{6,14},... | collective-permute-start | bytes 196616 | tf_op jit(solution)/shard_map/rows_out/ppermute | solution.py:570
  103.9 8.3 %collective-permute-start.6 = (bf16[256,128]{1,0:T(8,128)(2,1)S(1)}, bf16[256,128]{1,0:T(8,128)(2,1)S(1)}, u32[]{:S(2)}, u32[]{:S(2)}) collective-permute-start(bf16[256,128]{1,0:T(8,128)(2,1)S(1)} %get-tuple-element.35), channel_id=1, source_target_pairs={{0,12},{4,8},{8,4},{12,0},{1,13},{5,9},{9,5},{13,1},{2,14},{6,10},... | collective-permute-start | bytes 196616 | tf_op jit(solution)/shard_map/rows_out/ppermute | solution.py:570
  112.3 7.0 %collective-permute-start.8 = (bf16[32,36,128]{2,1,0:T(8,128)(2,1)S(1)}, bf16[32,36,128]{2,1,0:T(8,128)(2,1)S(1)}, u32[]{:S(2)}, u32[]{:S(2)}) collective-permute-start(bf16[32,36,128]{2,1,0:T(8,128)(2,1)S(1)} %weights_back.2.refs_1_), channel_id=1, source_target_pairs={{0,16},{16,0},{1,17},{17,1},{2,18},{18,2},{3,19},{19,3},{4,20},{20... | collective-permute-start | bytes 884744 | tf_op jit(solution)/shard_map/weights_back/ppermute | solution.py:591

commit v12 on v11

--- a/solution.py
+++ b/solution.py
@@ -205,17 +205,13 @@
     preact_ref,
     hidden_grad_ref,
     w_hidden_ref,
-    w_stencil_ref,
     w_tendency_ref,
-    to_across_ref,
-    to_inside_ref,
+    preact_grad_ref,
     moist_ref,
-    grad_ref,
     own_ref,
     other_ref,
     features_ref,
     flat_ref,
-    stage_ref,
 ):
     taken, in_channels, lon_total = features_ref.shape
     channels, hidden_units = w_tendency_ref.shape
@@ -232,7 +228,6 @@
         (jnp.where(northern, across, inside), 0, 0),
         (jnp.where(northern, inside, across), 2, taken - 1),
     )
-    sums = []
     for k in range(taken):
         part = slice(k * channels, (k + 1) * channels)
         features_ref[k] = early_ref[k]
@@ -251,7 +246,50 @@
         grad_in += dot(preact_grad, features_ref[k], ((1,), (1,)))
         grad_bias += dot(ones, preact_grad, ((1,), (1,)))
         moist_ref[part, :] = state[part] + dot(w_tendency_ref[...], hidden)
-        stencil_grad = dot(w_stencil_ref[...], preact_grad)
+        preact_grad_ref[k] = preact_grad
+
+    bias_high = grad_bias[0:1].astype(BF).astype(F32)
+    bias_low = grad_bias[0:1] - bias_high
+    tiles = hidden_units // LANES
+    pieces = own_ref.shape[0]
+    base, rest = split_rows(flat_ref.shape[1], pieces)
+    for h in range(2):
+        start = 0
+        for value in (grad_in, grad_out):
+            count = value.shape[0] // 2
+            for t in range(value.shape[1] // LANES):
+                flat_ref[h, start : start + count, :] = value[
+                    h * count : (h + 1) * count, t * LANES : (t + 1) * LANES
+                ]
+                start += count
+    core = position(place_ref[0], row_ref.shape[0])[0] % 2
+    for p in range(pieces):
+        start = pieces * base + p * rest
+        ends = [jnp.zeros((tiles, LANES), F32)]
+        if p < 2:
+            half = (bias_high, bias_low)[p]
+            ends = [half[:, t * LANES : (t + 1) * LANES] for t in range(tiles)]
+        for ref, h in ((own_ref, core), (other_ref, 1 - core)):
+            last = [flat_ref[h, start : start + rest, :]] if rest else []
+            piece = [flat_ref[h, p * base : (p + 1) * base, :]] + last + ends
+            ref[p] = jnp.concatenate(piece, axis=0).astype(ref.dtype)
+
+
+def stencil_kernel(
+    place_ref,
+    preact_grad_ref,
+    moist_grad_ref,
+    w_stencil_ref,
+    to_across_ref,
+    to_inside_ref,
+    grad_ref,
+):
+    taken = preact_grad_ref.shape[0]
+    sectors, channels = to_across_ref.shape[:2]
+    northern = position(place_ref[0], sectors)[2] == 0
+    sums = []
+    for k in range(taken):
+        stencil_grad = dot(w_stencil_ref[...], preact_grad_ref[k])
         sums.append([])
         for a in range(3):
             total = None
@@ -270,33 +308,6 @@
         if k + 1 < taken:
             total = total + sums[k + 1][0]
         store_split(grad_ref, k * channels, total)
-
-    bias_high = grad_bias[0:1].astype(BF).astype(F32)
-    bias_low = grad_bias[0:1] - bias_high
-    tiles = hidden_units // LANES
-    pieces = own_ref.shape[0]
-    base, rest = split_rows(flat_ref.shape[1], pieces)
-    stage_ref[:, :, base + rest :, :] = jnp.zeros((2, pieces, tiles, LANES), F32)
-    for h in range(2):
-        start = 0
-        for value in (grad_in, grad_out):
-            count = value.shape[0] // 2
-            for t in range(value.shape[1] // LANES):
-                flat_ref[h, start : start + count, :] = value[
-                    h * count : (h + 1) * count, t * LANES : (t + 1) * LANES
-                ]
-                start += count
-        for p in range(pieces):
-            stage_ref[h, p, :base, :] = flat_ref[h, p * base : (p + 1) * base, :]
-            start = pieces * base + p * rest
-            stage_ref[h, p, base : base + rest, :] = flat_ref[h, start : start + rest, :]
-        for p, half in enumerate((bias_high, bias_low)):
-            for t in range(tiles):
-                row = base + rest + t
-                stage_ref[h, p, row : row + 1, :] = half[:, t * LANES : (t + 1) * LANES]
-    core = position(place_ref[0], row_ref.shape[0])[0] % 2
-    own_ref[...] = stage_ref[core]
-    other_ref[...] = stage_ref[1 - core].astype(BF)
 
 
 def fields_kernel(
@@ -510,25 +521,19 @@
     with jax.named_scope("weights"):
         block = (sectors, rows, LANES)
         edge = (sectors, channels, LANES)
-        to_across, to_inside, moist, grad_rows, own, other = call(
+        preact_grad, moist, own, other = call(
             weights_kernel,
             (
-                shape(edge, BF),
-                shape(edge, BF),
+                shape((taken, hidden_units, lon_total), BF),
                 shape((rows, lon_total), F32),
-                shape(block, F32),
                 shape(share, F32),
                 shape(share, BF),
             ),
-            11,
+            10,
             smem=1,
-            scratch=[
-                pltpu.VMEM(features_shape, BF),
-                flat_rows,
-                pltpu.VMEM((2,) + share, F32),
-            ],
+            scratch=[pltpu.VMEM(features_shape, BF), flat_rows],
             flops=3_000_000_000,
-            vmem=28,
+            vmem=24,
         )(
             place,
             across,
@@ -539,9 +544,17 @@
             preact,
             hidden_grad,
             w_hidden,
-            w_hidden[:, : 9 * channels].T,
             w_tendency,
         )
+
+    with jax.named_scope("stencil"):
+        to_across, to_inside, grad_rows = call(
+            stencil_kernel,
+            (shape(edge, BF), shape(edge, BF), shape(block, F32)),
+            4,
+            smem=1,
+            flops=1_000_000_000,
+        )(place, preact_grad, moist_grad, w_hidden[:, : 9 * channels].T)
 
     with jax.named_scope("weights_core"):
         swap = [(0, 1), (1, 0)]

time: 121 us -> 122 us (level)
  local copies, waits for them, and re-layouts: 0.44 us -> 4 us
  waiting for transfers between devices: 35.4 us -> 32.5 us
    all_to_all x4, waiting for transfers between devices: 21.6 us -> 17.1 us  [exchange(): return lax.all_to_all(x, axes, 0, 0, tiled=True)]
    unnamed x22 -> x34, local copies, waits for them, and re-layouts: 0.42 us -> 3.97 us
    ppermute x1, starting transfers between devices: 5.75 us -> 2.32 us  [on_device(): inside = lax.ppermute(edge_row(1 - pair), PLACE, inside_swaps)]
    all_to_all x4, starting transfers between devices: 33.8 us -> 37.2 us  [exchange(): return lax.all_to_all(x, axes, 0, 0, tiled=True)]
    ppermute x1, waiting for transfers between devices: 0.01 us -> 1.89 us  [on_device(): inside = lax.ppermute(edge_row(1 - pair), PLACE, inside_swaps)]
    pallas_call x1 -> x2, Pallas kernels: 3.17 us -> 3.15 us  [the longest x1 2.25 us: on_device(): call(weights_kernel, (shape((taken, hidden_units, lon_total), BF), shape(...]
  transfers between devices with their start and end apart: 13 -> 13, of which waited for: 9 -> 10; matrix products, arithmetic and copies ran while one was open for 0% -> 0% of each run, Pallas kernels for 3% -> 4%
where the time goes in v12:
time: 122 us
  starting transfers between devices  71.8 us (59%)
  waiting for transfers between devices  32.5 us (27%)
  Pallas kernels  11.6 us (10%)
  local copies, waits for them, and re-layouts  4 us (3%)
    all_to_all x4, starting transfers between devices, exchange(): return lax.all_to_all(x, axes, 0, 0, tiled=True)  37.2 us
    all_to_all x4, waiting for transfers between devices, exchange(): return lax.all_to_all(x, axes, 0, 0, tiled=True)  17.1 us
    ppermute x3, starting transfers between devices, on_device(): lax.ppermute(fields[t], 'lon', [(i, i ^ t) for i in range(sectors)])  11.4 us
    ppermute x1, starting transfers between devices, on_device(): across = lax.ppermute(edge_row(pair), PLACE, across_swaps)  6.3 us
    ppermute x3, waiting for transfers between devices, on_device(): lax.ppermute(fields[t], 'lon', [(i, i ^ t) for i in range(sectors)])  5.93 us
    ppermute x1, starting transfers between devices, on_device(): from_inside = lax.ppermute(to_inside, PLACE, inside_swaps)  5.43 us
    ppermute x1, starting transfers between devices, on_device(): other = lax.ppermute(own, 'core', swap)  5.32 us
    unnamed x34, local copies, waits for them, and re-layouts  3.97 us
  transfers between devices with their start and end apart: 13, of which 10 were waited for; matrix products, arithmetic and copies ran while one was open for 0% of the time, Pallas kernels for 4%

profile of v12, /device:TPU:1, one launch (start us, length us, event | category | flops | bytes accessed | tf_op | source)
XLA Modules:
  0.0 121.7 jit_solution(6224763320455768058)
XLA Ops:
  0.6 0.0 copy-start.6
  0.6 0.0 copy-start.7
  0.7 0.0 copy-start.8
  0.7 0.0 copy-start.1
  0.7 0.0 copy-start.15
  0.7 0.0 copy-start.5
  0.7 0.0 copy-start.4
  0.7 0.0 copy-start.3
  0.7 0.0 copy-start.2
  0.7 0.0 copy-start
  0.8 1.9 %rows_in.1 = f32[4,264,128]{2,1,0:T(8,128)} custom-call(s32[1]{0:T(128)} %bitcast.refs_0_, f32[2,256,128]{2,1,0:T(8,128)} %bitcast.11, f32[2,256,128]{2,1,0:T(8,128)} %bitcast.12, s32[4,128]{1,0:T(4,128)} %refs_3_.3, s32[4,128]{1,0:T(4,128)} %refs_4_.3), custom_call_target="tpu_custom_call" | custom-call | bytes 1000000 | tf_op jit(solution)/shard_map/rows_in/pallas_call | solution.py:453
  2.7 7.7 %all-to-all-start = ((f32[4,264,128]{2,1,0:T(8,128)}), f32[4,264,128]{2,1,0:T(8,128)S(1)}, u32[]{:S(2)}, u32[]{:S(2)}) async-start(f32[4,264,128]{2,1,0:T(8,128)} %rows_in.1), calls=%async_computation | async-start | bytes 1081344 | tf_op jit(solution)/shard_map/rows_in/all_to_all | solution.py:419
  10.4 0.0 copy-done.1
  10.4 0.1 copy.19
  10.5 0.0 copy-done.15
  10.5 13.9 %all-to-all-done.refs_2_.refs_3_ = f32[4,264,128]{2,1,0:T(8,128)S(1)} async-done(((f32[4,264,128]{2,1,0:T(8,128)}), f32[4,264,128]{2,1,0:T(8,128)S(1)}, u32[]{:S(2)}, u32[]{:S(2)}) %all-to-all-start) | async-done | bytes 540704 | tf_op jit(solution)/shard_map/rows_in/all_to_all | solution.py:419
  24.5 6.3 %collective-permute-start = (bf16[4,64,128]{2,1,0:T(8,128)(2,1)S(1)}, bf16[4,64,128]{2,1,0:T(8,128)(2,1)S(1)}, u32[]{:S(2)}, u32[]{:S(2)}) collective-permute-start(bf16[4,64,128]{2,1,0:T(8,128)(2,1)S(1)} %get-tuple-element.46), channel_id=1, source_target_pairs={{4,20},{12,28},{16,32},{20,4},{24,40},{28,12},{32,16},{36,52},{40,... | collective-permute-start | bytes 196616 | tf_op jit(solution)/shard_map/row_halo/ppermute | solution.py:487
  30.8 2.3 %collective-permute-start.1 = (bf16[4,64,128]{2,1,0:T(8,128)(2,1)S(1)}, bf16[4,64,128]{2,1,0:T(8,128)(2,1)S(1)}, u32[]{:S(2)}, u32[]{:S(2)}) collective-permute-start(bf16[4,64,128]{2,1,0:T(8,128)(2,1)S(1)} %get-tuple-element.45), channel_id=1, source_target_pairs={{0,4},{4,0},{8,12},{12,8},{16,20},{20,16},{24,28},{28,24},{32,36},... | collective-permute-start | bytes 196616 | tf_op jit(solution)/shard_map/row_halo/ppermute | solution.py:486
  33.1 0.0 copy-done.6
  33.1 0.0 copy-done.7
  33.1 0.0 copy-done.8
  33.1 0.0 copy-done.5
  33.1 0.0 copy-done.4
  33.2 2.3 %early.1 = (f32[128,512]{1,0:T(8,128)S(1)}, bf16[2,640,512]{2,1,0:T(8,128)(2,1)S(1)}, f32[2,384,512]{2,1,0:T(8,128)S(1)}, f32[2,384,512]{2,1,0:T(8,128)S(1)}) custom-call(s32[1]{0:T(128)} %bitcast.refs_0_, s32[2]{0:T(128)S(1)} %copy-done.5, f32[4,264,128]{2,1,0:T(8,128)S(1)} %all-to-all-done.refs_2_.refs_3_, f32[192,384]{1,0:T(8,128)S(1)} %copy-done.8, ...), custom_call_target="tpu_custom_call" | custom-call | flops 3000000000 | bytes 1000000 | tf_op jit(solution)/shard_map/early/pallas_call | solution.py:493
  35.5 0.0 copy-start.13
  35.5 0.0 collective-permute-done.refs_1_
  35.5 1.9 %collective-permute-done.1.refs_2_ = bf16[4,64,128]{2,1,0:T(8,128)(2,1)S(1)} collective-permute-done((bf16[4,64,128]{2,1,0:T(8,128)(2,1)S(1)}, bf16[4,64,128]{2,1,0:T(8,128)(2,1)S(1)}, u32[]{:S(2)}, u32[]{:S(2)}) %collective-permute-start.1) | collective-permute-done | bytes 65568 | tf_op jit(solution)/shard_map/row_halo/ppermute | solution.py:486
  37.4 2.3 %weights.1 = (bf16[2,384,512]{2,1,0:T(8,128)(2,1)S(1)}, f32[128,512]{1,0:T(8,128)S(1)}, f32[32,36,128]{2,1,0:T(8,128)S(1)}, bf16[32,36,128]{2,1,0:T(8,128)(2,1)S(1)}) custom-call(s32[1]{0:T(128)} %bitcast.refs_0_, bf16[4,64,128]{2,1,0:T(8,128)(2,1)S(1)} %collective-permute-done.refs_1_, bf16[4,64,128]{2,1,0:T(8,128)(2,1)S(1)} %collective-permute-done.1.refs_2_, ...), custom_call_target="tpu_custom_call" | custom-call | flops 3000000000 | bytes 1000000 | tf_op jit(solution)/shard_map/weights/pallas_call | solution.py:524
  39.7 0.0 copy-done.13
  39.7 0.0 copy-start.9
  39.7 1.9 %collective-permute-start.7 = (bf16[32,36,128]{2,1,0:T(8,128)(2,1)S(1)}, bf16[32,36,128]{2,1,0:T(8,128)(2,1)S(1)}, u32[]{:S(2)}, u32[]{:S(2)}) collective-permute-start(bf16[32,36,128]{2,1,0:T(8,128)(2,1)S(1)} %get-tuple-element.41), channel_id=1, source_target_pairs={{0,16},{16,0},{1,17},{17,1},{2,18},{18,2},{3,19},{19,3},{4,20},{20... | collective-permute-start | bytes 884744 | tf_op jit(solution)/shard_map/weights_core/ppermute | solution.py:561
  41.6 1.6 %collective-permute-done.7 = bf16[32,36,128]{2,1,0:T(8,128)(2,1)S(1)} collective-permute-done((bf16[32,36,128]{2,1,0:T(8,128)(2,1)S(1)}, bf16[32,36,128]{2,1,0:T(8,128)(2,1)S(1)}, u32[]{:S(2)}, u32[]{:S(2)}) %collective-permute-start.7) | collective-permute-done | bytes 294944 | tf_op jit(solution)/shard_map/weights_core/ppermute | solution.py:561
  43.2 0.8 add_convert_fusion
  44.0 16.8 %all-to-all-start.1 = ((bf16[32,36,128]{2,1,0:T(8,128)(2,1)}), bf16[32,36,128]{2,1,0:T(8,128)(2,1)S(1)}, u32[]{:S(2)}, u32[]{:S(2)}) async-start(bf16[32,36,128]{2,1,0:T(8,128)(2,1)} %add_convert_fusion), calls=%async_computation.1 | async-start | bytes 655360 | tf_op jit(solution)/shard_map/weights_plane/all_to_all | solution.py:419
  60.8 0.2 copy.21
  61.0 0.0 copy-start.14
  61.0 0.9 copy-done.14
  62.0 0.9 stencil.1
  62.9 0.0 copy-start.11
  62.9 0.7 copy-done.11
  63.6 1.9 %collective-permute-start.2 = (bf16[4,64,128]{2,1,0:T(8,128)(2,1)S(1)}, bf16[4,64,128]{2,1,0:T(8,128)(2,1)S(1)}, u32[]{:S(2)}, u32[]{:S(2)}) collective-permute-start(bf16[4,64,128]{2,1,0:T(8,128)(2,1)S(1)} %get-tuple-element.32), channel_id=1, source_target_pairs={{4,20},{12,28},{16,32},{20,4},{24,40},{28,12},{32,16},{36,52},{40,... | collective-permute-start | bytes 196616 | tf_op jit(solution)/shard_map/fields/ppermute | solution.py:564
  65.5 4.0 %collective-permute-done.2.refs_6_.refs_1_ = bf16[4,64,128]{2,1,0:T(8,128)(2,1)S(1)} collective-permute-done((bf16[4,64,128]{2,1,0:T(8,128)(2,1)S(1)}, bf16[4,64,128]{2,1,0:T(8,128)(2,1)S(1)}, u32[]{:S(2)}, u32[]{:S(2)}) %collective-permute-start.2) | collective-permute-done | bytes 65568 | tf_op jit(solution)/shard_map/fields/ppermute | solution.py:564
  69.5 2.4 %all-to-all-done.1.refs_0_ = bf16[32,36,128]{2,1,0:T(8,128)(2,1)S(1)} async-done(((bf16[32,36,128]{2,1,0:T(8,128)(2,1)}), bf16[32,36,128]{2,1,0:T(8,128)(2,1)S(1)}, u32[]{:S(2)}, u32[]{:S(2)}) %all-to-all-start.1) | async-done | bytes 294944 | tf_op jit(solution)/shard_map/weights_plane/all_to_all | solution.py:419
  71.9 0.7 weights_plane.1
  72.6 4.6 %all-to-all-start.2 = ((bf16[12,36,128]{2,1,0:T(8,128)(2,1)}), bf16[12,36,128]{2,1,0:T(8,128)(2,1)S(1)}, u32[]{:S(2)}, u32[]{:S(2)}) async-start(bf16[12,36,128]{2,1,0:T(8,128)(2,1)} %weights_plane.1), calls=%async_computation.2 | async-start | bytes 245760 | tf_op jit(solution)/shard_map/weights_length/all_to_all | solution.py:419
  77.2 5.4 %collective-permute-start.3 = (bf16[4,64,128]{2,1,0:T(8,128)(2,1)S(1)}, bf16[4,64,128]{2,1,0:T(8,128)(2,1)S(1)}, u32[]{:S(2)}, u32[]{:S(2)}) collective-permute-start(bf16[4,64,128]{2,1,0:T(8,128)(2,1)S(1)} %get-tuple-element.33), channel_id=1, source_target_pairs={{0,4},{4,0},{8,12},{12,8},{16,20},{20,16},{24,28},{28,24},{32,36},... | collective-permute-start | bytes 196616 | tf_op jit(solution)/shard_map/fields/ppermute | solution.py:565
  82.6 1.6 %collective-permute-done.3.refs_7_ = bf16[4,64,128]{2,1,0:T(8,128)(2,1)S(1)} collective-permute-done((bf16[4,64,128]{2,1,0:T(8,128)(2,1)S(1)}, bf16[4,64,128]{2,1,0:T(8,128)(2,1)S(1)}, u32[]{:S(2)}, u32[]{:S(2)}) %collective-permute-start.3) | collective-permute-done | bytes 65568 | tf_op jit(solution)/shard_map/fields/ppermute | solution.py:565
  84.2 0.9 copy-done.10
  85.2 0.9 copy-done.12
  86.1 0.7 fields.1
  86.8 0.8 all-to-all-done.2.refs_0_
  87.6 0.8 weights_length.1
  88.4 8.2 %all-to-all-start.3 = ((bf16[32,36,128]{2,1,0:T(8,128)(2,1)}), bf16[32,36,128]{2,1,0:T(8,128)(2,1)S(1)}, u32[]{:S(2)}, u32[]{:S(2)}) async-start(bf16[32,36,128]{2,1,0:T(8,128)(2,1)} %weights_length.1), calls=%async_computation.3 | async-start | bytes 655360 | tf_op jit(solution)/shard_map/weights_back/all_to_all | solution.py:419
  96.6 4.0 %collective-permute-start.4 = (bf16[256,128]{1,0:T(8,128)(2,1)S(1)}, bf16[256,128]{1,0:T(8,128)(2,1)S(1)}, u32[]{:S(2)}, u32[]{:S(2)}) collective-permute-start(bf16[256,128]{1,0:T(8,128)(2,1)S(1)} %get-tuple-element.35), channel_id=1, source_target_pairs={{0,4},{4,0},{8,12},{12,8},{1,5},{5,1},{9,13},{13,9},{2,6},{6,2},{1... | collective-permute-start | bytes 196616 | tf_op jit(solution)/shard_map/rows_out/ppermute | solution.py:583
  100.6 5.2 %collective-permute-start.5 = (bf16[256,128]{1,0:T(8,128)(2,1)S(1)}, bf16[256,128]{1,0:T(8,128)(2,1)S(1)}, u32[]{:S(2)}, u32[]{:S(2)}) collective-permute-start(bf16[256,128]{1,0:T(8,128)(2,1)S(1)} %get-tuple-element.36), channel_id=1, source_target_pairs={{0,8},{4,12},{8,0},{12,4},{1,9},{5,13},{9,1},{13,5},{2,10},{6,14},... | collective-permute-start | bytes 196616 | tf_op jit(solution)/shard_map/rows_out/ppermute | solution.py:583
  105.8 2.1 %collective-permute-start.6 = (bf16[256,128]{1,0:T(8,128)(2,1)S(1)}, bf16[256,128]{1,0:T(8,128)(2,1)S(1)}, u32[]{:S(2)}, u32[]{:S(2)}) collective-permute-start(bf16[256,128]{1,0:T(8,128)(2,1)S(1)} %get-tuple-element.37), channel_id=1, source_target_pairs={{0,12},{4,8},{8,4},{12,0},{1,13},{5,9},{9,5},{13,1},{2,14},{6,10},... | collective-permute-start | bytes 196616 | tf_op jit(solution)/shard_map/rows_out/ppermute | solution.py:583
  108.0 0.0 collective-permute-done.4.refs_2_.refs_1_
  108.0 3.2 %collective-permute-done.5.refs_3_.refs_2_ = bf16[256,128]{1,0:T(8,128)(2,1)S(1)} collective-permute-done((bf16[256,128]{1,0:T(8,128)(2,1)S(1)}, bf16[256,128]{1,0:T(8,128)(2,1)S(1)}, u32[]{:S(2)}, u32[]{:S(2)}) %collective-permute-start.5) | collective-permute-done | bytes 65568 | tf_op jit(solution)/shard_map/rows_out/ppermute | solution.py:583
  111.1 2.8 %collective-permute-done.6.refs_4_.refs_3_ = bf16[256,128]{1,0:T(8,128)(2,1)S(1)} collective-permute-done((bf16[256,128]{1,0:T(8,128)(2,1)S(1)}, bf16[256,128]{1,0:T(8,128)(2,1)S(1)}, u32[]{:S(2)}, u32[]{:S(2)}) %collective-permute-start.6) | collective-permute-done | bytes 65568 | tf_op jit(solution)/shard_map/rows_out/ppermute | solution.py:583
  113.9 0.0 all-to-all-done.3.refs_0_
  113.9 5.3 %collective-permute-start.8 = (bf16[32,36,128]{2,1,0:T(8,128)(2,1)S(1)}, bf16[32,36,128]{2,1,0:T(8,128)(2,1)S(1)}, u32[]{:S(2)}, u32[]{:S(2)}) collective-permute-start(bf16[32,36,128]{2,1,0:T(8,128)(2,1)S(1)} %weights_back.2.refs_1_), channel_id=1, source_target_pairs={{0,16},{16,0},{1,17},{17,1},{2,18},{18,2},{3,19},{19,3},{4,20},{20... | collective-permute-start | bytes 884744 | tf_op jit(solution)/shard_map/weights_back/ppermute | solution.py:604
  119.3 0.9 bands_out.1
  120.1 0.4 collective-permute-done.8.refs_2_
  120.5 1.2 weights_back.3
  (9 shorter events, 0.1 us)
Async XLA Ops:
  0.6 32.5 %copy-start.6 = (bf16[384,512]{1,0:T(8,128)(2,1)S(1)}, bf16[384,512]{1,0:T(8,128)(2,1)}, u32[]{:S(2)}) copy-start(bf16[384,512]{1,0:T(8,128)(2,1)} %constant.69.clone.refs_4_.refs_3_) | copy-start | bytes 1179652
  0.6 32.5 %copy-start.7 = (bf16[384,512]{1,0:T(8,128)(2,1)S(1)}, bf16[384,512]{1,0:T(8,128)(2,1)}, u32[]{:S(2)}) copy-start(bf16[384,512]{1,0:T(8,128)(2,1)} %constant.70.clone.refs_5_.refs_4_) | copy-start | bytes 1179652
  0.7 32.5 %copy-start.8 = (f32[192,384]{1,0:T(8,128)S(1)}, f32[192,384]{1,0:T(8,128)}, u32[]{:S(2)}) copy-start(f32[192,384]{1,0:T(8,128)} %constant.71.clone.refs_3_.refs_2_) | copy-start | bytes 884740
  0.7 9.7 %copy-start.1 = (bf16[64,384]{1,0:T(8,128)(2,1)S(1)}, bf16[64,384]{1,0:T(8,128)(2,1)}, u32[]{:S(2)}) copy-start(bf16[64,384]{1,0:T(8,128)(2,1)} %refs_9_.3) | copy-start | bytes 147460
  0.7 9.8 %copy-start.15 = (f32[384]{0:T(512)S(1)}, f32[384]{0:T(512)}, u32[]{:S(2)}) copy-start(f32[384]{0:T(512)} %param.23) | copy-start | bytes 4612
  0.7 32.4 %copy-start.5 = (s32[2]{0:T(128)S(1)}, s32[2]{0:T(128)}, u32[]{:S(2)}) copy-start(s32[2]{0:T(128)} %refs_1_.1) | copy-start | bytes 28
  0.7 32.4 %copy-start.4 = (f32[2,64]{1,0:T(2,128)S(1)}, f32[2,64]{1,0:T(2,128)}, u32[]{:S(2)}) copy-start(f32[2,64]{1,0:T(2,128)} %refs_6_.1) | copy-start | bytes 1540
  0.7 32.4 %copy-start.3 = (f32[16,64]{1,0:T(8,128)S(1)}, f32[16,64]{1,0:T(8,128)}, u32[]{:S(2)}) copy-start(f32[16,64]{1,0:T(8,128)} %refs_7_.1) | copy-start | bytes 12292
  0.7 32.4 %copy-start.2 = (f32[32,64]{1,0:T(8,128)S(1)}, f32[32,64]{1,0:T(8,128)}, u32[]{:S(2)}) copy-start(f32[32,64]{1,0:T(8,128)} %refs_8_.2) | copy-start | bytes 24580
  0.7 32.4 %copy-start = (bf16[384,640]{1,0:T(8,128)(2,1)S(1)}, bf16[384,640]{1,0:T(8,128)(2,1)}, u32[]{:S(2)}) copy-start(bf16[384,640]{1,0:T(8,128)(2,1)} %refs_8_.3) | copy-start | bytes 1474564
  2.7 21.7 %all-to-all-start = ((f32[4,264,128]{2,1,0:T(8,128)}), f32[4,264,128]{2,1,0:T(8,128)S(1)}, u32[]{:S(2)}, u32[]{:S(2)}) async-start(f32[4,264,128]{2,1,0:T(8,128)} %rows_in.1), calls=%async_computation | async-start | bytes 1081344 | tf_op jit(solution)/shard_map/rows_in/all_to_all | solution.py:419
  24.5 11.0 %collective-permute-start = (bf16[4,64,128]{2,1,0:T(8,128)(2,1)S(1)}, bf16[4,64,128]{2,1,0:T(8,128)(2,1)S(1)}, u32[]{:S(2)}, u32[]{:S(2)}) collective-permute-start(bf16[4,64,128]{2,1,0:T(8,128)(2,1)S(1)} %get-tuple-element.46), channel_id=1, source_target_pairs={{4,20},{12,28},{16,32},{20,4},{24,40},{28,12},{32,16},{36,52},{40,... | collective-permute-start | bytes 196616 | tf_op jit(solution)/shard_map/row_halo/ppermute | solution.py:487
  30.8 6.6 %collective-permute-start.1 = (bf16[4,64,128]{2,1,0:T(8,128)(2,1)S(1)}, bf16[4,64,128]{2,1,0:T(8,128)(2,1)S(1)}, u32[]{:S(2)}, u32[]{:S(2)}) collective-permute-start(bf16[4,64,128]{2,1,0:T(8,128)(2,1)S(1)} %get-tuple-element.45), channel_id=1, source_target_pairs={{0,4},{4,0},{8,12},{12,8},{16,20},{20,16},{24,28},{28,24},{32,36},... | collective-permute-start | bytes 196616 | tf_op jit(solution)/shard_map/row_halo/ppermute | solution.py:486
  35.5 4.2 %copy-start.13 = (f32[128,512]{1,0:T(8,128)}, f32[128,512]{1,0:T(8,128)S(1)}, u32[]{:S(2)}) copy-start(f32[128,512]{1,0:T(8,128)S(1)} %get-tuple-element.25.refs_4_.refs_2_) | copy-start | bytes 786436
  39.7 21.1 %copy-start.9 = (f32[128,512]{1,0:T(8,128)}, f32[128,512]{1,0:T(8,128)S(1)}, u32[]{:S(2)}) copy-start(f32[128,512]{1,0:T(8,128)S(1)} %get-tuple-element.29.refs_1_) | copy-start | bytes 786436
  39.7 3.5 %collective-permute-start.7 = (bf16[32,36,128]{2,1,0:T(8,128)(2,1)S(1)}, bf16[32,36,128]{2,1,0:T(8,128)(2,1)S(1)}, u32[]{:S(2)}, u32[]{:S(2)}) collective-permute-start(bf16[32,36,128]{2,1,0:T(8,128)(2,1)S(1)} %get-tuple-element.41), channel_id=1, source_target_pairs={{0,16},{16,0},{1,17},{17,1},{2,18},{18,2},{3,19},{19,3},{4,20},{20... | collective-permute-start | bytes 884744 | tf_op jit(solution)/shard_map/weights_core/ppermute | solution.py:561
  44.0 27.9 %all-to-all-start.1 = ((bf16[32,36,128]{2,1,0:T(8,128)(2,1)}), bf16[32,36,128]{2,1,0:T(8,128)(2,1)S(1)}, u32[]{:S(2)}, u32[]{:S(2)}) async-start(bf16[32,36,128]{2,1,0:T(8,128)(2,1)} %add_convert_fusion), calls=%async_computation.1 | async-start | bytes 655360 | tf_op jit(solution)/shard_map/weights_plane/all_to_all | solution.py:419
  61.0 1.0 copy-start.14
  62.9 0.7 copy-start.11
  63.6 5.9 %collective-permute-start.2 = (bf16[4,64,128]{2,1,0:T(8,128)(2,1)S(1)}, bf16[4,64,128]{2,1,0:T(8,128)(2,1)S(1)}, u32[]{:S(2)}, u32[]{:S(2)}) collective-permute-start(bf16[4,64,128]{2,1,0:T(8,128)(2,1)S(1)} %get-tuple-element.32), channel_id=1, source_target_pairs={{4,20},{12,28},{16,32},{20,4},{24,40},{28,12},{32,16},{36,52},{40,... | collective-permute-start | bytes 196616 | tf_op jit(solution)/shard_map/fields/ppermute | solution.py:564
  72.6 15.0 %all-to-all-start.2 = ((bf16[12,36,128]{2,1,0:T(8,128)(2,1)}), bf16[12,36,128]{2,1,0:T(8,128)(2,1)S(1)}, u32[]{:S(2)}, u32[]{:S(2)}) async-start(bf16[12,36,128]{2,1,0:T(8,128)(2,1)} %weights_plane.1), calls=%async_computation.2 | async-start | bytes 245760 | tf_op jit(solution)/shard_map/weights_length/all_to_all | solution.py:419
  77.2 7.1 %collective-permute-start.3 = (bf16[4,64,128]{2,1,0:T(8,128)(2,1)S(1)}, bf16[4,64,128]{2,1,0:T(8,128)(2,1)S(1)}, u32[]{:S(2)}, u32[]{:S(2)}) collective-permute-start(bf16[4,64,128]{2,1,0:T(8,128)(2,1)S(1)} %get-tuple-element.33), channel_id=1, source_target_pairs={{0,4},{4,0},{8,12},{12,8},{16,20},{20,16},{24,28},{28,24},{32,36},... | collective-permute-start | bytes 196616 | tf_op jit(solution)/shard_map/fields/ppermute | solution.py:565
  84.2 1.0 copy-start.10
  85.2 0.9 copy-start.12
  88.4 25.6 %all-to-all-start.3 = ((bf16[32,36,128]{2,1,0:T(8,128)(2,1)}), bf16[32,36,128]{2,1,0:T(8,128)(2,1)S(1)}, u32[]{:S(2)}, u32[]{:S(2)}) async-start(bf16[32,36,128]{2,1,0:T(8,128)(2,1)} %weights_length.1), calls=%async_computation.3 | async-start | bytes 655360 | tf_op jit(solution)/shard_map/weights_back/all_to_all | solution.py:419
  96.6 11.4 %collective-permute-start.4 = (bf16[256,128]{1,0:T(8,128)(2,1)S(1)}, bf16[256,128]{1,0:T(8,128)(2,1)S(1)}, u32[]{:S(2)}, u32[]{:S(2)}) collective-permute-start(bf16[256,128]{1,0:T(8,128)(2,1)S(1)} %get-tuple-element.35), channel_id=1, source_target_pairs={{0,4},{4,0},{8,12},{12,8},{1,5},{5,1},{9,13},{13,9},{2,6},{6,2},{1... | collective-permute-start | bytes 196616 | tf_op jit(solution)/shard_map/rows_out/ppermute | solution.py:583
  100.6 10.6 %collective-permute-start.5 = (bf16[256,128]{1,0:T(8,128)(2,1)S(1)}, bf16[256,128]{1,0:T(8,128)(2,1)S(1)}, u32[]{:S(2)}, u32[]{:S(2)}) collective-permute-start(bf16[256,128]{1,0:T(8,128)(2,1)S(1)} %get-tuple-element.36), channel_id=1, source_target_pairs={{0,8},{4,12},{8,0},{12,4},{1,9},{5,13},{9,1},{13,5},{2,10},{6,14},... | collective-permute-start | bytes 196616 | tf_op jit(solution)/shard_map/rows_out/ppermute | solution.py:583
  105.8 8.1 %collective-permute-start.6 = (bf16[256,128]{1,0:T(8,128)(2,1)S(1)}, bf16[256,128]{1,0:T(8,128)(2,1)S(1)}, u32[]{:S(2)}, u32[]{:S(2)}) collective-permute-start(bf16[256,128]{1,0:T(8,128)(2,1)S(1)} %get-tuple-element.37), channel_id=1, source_target_pairs={{0,12},{4,8},{8,4},{12,0},{1,13},{5,9},{9,5},{13,1},{2,14},{6,10},... | collective-permute-start | bytes 196616 | tf_op jit(solution)/shard_map/rows_out/ppermute | solution.py:583
  113.9 6.6 %collective-permute-start.8 = (bf16[32,36,128]{2,1,0:T(8,128)(2,1)S(1)}, bf16[32,36,128]{2,1,0:T(8,128)(2,1)S(1)}, u32[]{:S(2)}, u32[]{:S(2)}) collective-permute-start(bf16[32,36,128]{2,1,0:T(8,128)(2,1)S(1)} %weights_back.2.refs_1_), channel_id=1, source_target_pairs={{0,16},{16,0},{1,17},{17,1},{2,18},{18,2},{3,19},{19,3},{4,20},{20... | collective-permute-start | bytes 884744 | tf_op jit(solution)/shard_map/weights_back/ppermute | solution.py:604

commit v13 on v12

--- a/solution.py
+++ b/solution.py
@@ -197,8 +197,8 @@
 
 def weights_kernel(
     place_ref,
+    inside_ref,
     across_ref,
-    inside_ref,
     row_ref,
     moist_grad_ref,
     early_ref,
@@ -496,7 +496,7 @@
             12,
             smem=2,
             flops=3_000_000_000,
-            vmem=24,
+            vmem=16,
         )(
             place,
             member_seeds,
@@ -533,11 +533,11 @@
             smem=1,
             scratch=[pltpu.VMEM(features_shape, BF), flat_rows],
             flops=3_000_000_000,
-            vmem=24,
+            vmem=16,
         )(
             place,
+            inside,
             across,
-            inside,
             row,
             moist_grad,
             features,

time: 122 us -> 121 us (level)
  waiting for transfers between devices: 32.5 us -> 31 us
    ppermute x1, starting transfers between devices: 2.32 us -> 5.75 us  [on_device(): inside = lax.ppermute(edge_row(1 - pair), PLACE, inside_swaps)]
    all_to_all x4, starting transfers between devices: 37.2 us -> 34.8 us  [exchange(): return lax.all_to_all(x, axes, 0, 0, tiled=True)]
    ppermute x1, waiting for transfers between devices: 1.89 us -> 0.01 us  [on_device(): inside = lax.ppermute(edge_row(1 - pair), PLACE, inside_swaps)]
  transfers between devices with their start and end apart: 13 -> 13, of which waited for: 10 -> 9; matrix products, arithmetic and copies ran while one was open for 0% -> 0% of each run, Pallas kernels for 4% -> 4%
where the time goes in v13:
time: 121 us; the launch traced here: 120 us
  starting transfers between devices  71.9 us (59%)
  waiting for transfers between devices  31 us (26%)
  Pallas kernels  11.6 us (10%)
  local copies, waits for them, and re-layouts  4 us (3%)
    all_to_all x4, starting transfers between devices, exchange(): return lax.all_to_all(x, axes, 0, 0, tiled=True)  34.8 us
    all_to_all x4, waiting for transfers between devices, exchange(): return lax.all_to_all(x, axes, 0, 0, tiled=True)  17.3 us
    ppermute x3, starting transfers between devices, on_device(): lax.ppermute(fields[t], 'lon', [(i, i ^ t) for i in range(sectors)])  11.4 us
    ppermute x3, waiting for transfers between devices, on_device(): lax.ppermute(fields[t], 'lon', [(i, i ^ t) for i in range(sectors)])  6.1 us
    ppermute x1, starting transfers between devices, on_device(): inside = lax.ppermute(edge_row(1 - pair), PLACE, inside_swaps)  5.75 us
    ppermute x1, starting transfers between devices, on_device(): other = lax.ppermute(own, 'core', swap)  5.59 us
    ppermute x1, starting transfers between devices, on_device(): across = lax.ppermute(edge_row(pair), PLACE, across_swaps)  5.34 us
    ppermute x1, starting transfers between devices, on_device(): from_inside = lax.ppermute(to_inside, PLACE, inside_swaps)  5.17 us
  transfers between devices with their start and end apart: 13, of which 9 were waited for; matrix products, arithmetic and copies ran while one was open for 0% of the time, Pallas kernels for 4%

profile of v13, /device:TPU:1, one launch (start us, length us, event | category | flops | bytes accessed | tf_op | source)
XLA Modules:
  0.0 120.3 jit_solution(16320492313635607769)
XLA Ops:
  0.6 0.0 copy-start.6
  0.6 0.0 copy-start.7
  0.7 0.0 copy-start.8
  0.7 0.0 copy-start.1
  0.7 0.0 copy-start.15
  0.7 0.0 copy-start.5
  0.7 0.0 copy-start.4
  0.7 0.0 copy-start.3
  0.7 0.0 copy-start.2
  0.7 0.0 copy-start
  0.8 1.9 %rows_in.1 = f32[4,264,128]{2,1,0:T(8,128)} custom-call(s32[1]{0:T(128)} %bitcast.refs_0_, f32[2,256,128]{2,1,0:T(8,128)} %bitcast.11, f32[2,256,128]{2,1,0:T(8,128)} %bitcast.12, s32[4,128]{1,0:T(4,128)} %refs_3_.3, s32[4,128]{1,0:T(4,128)} %refs_4_.3), custom_call_target="tpu_custom_call" | custom-call | bytes 1000000 | tf_op jit(solution)/shard_map/rows_in/pallas_call | solution.py:453
  2.7 7.7 %all-to-all-start = ((f32[4,264,128]{2,1,0:T(8,128)}), f32[4,264,128]{2,1,0:T(8,128)S(1)}, u32[]{:S(2)}, u32[]{:S(2)}) async-start(f32[4,264,128]{2,1,0:T(8,128)} %rows_in.1), calls=%async_computation | async-start | bytes 1081344 | tf_op jit(solution)/shard_map/rows_in/all_to_all | solution.py:419
  10.4 0.1 copy.19
  10.5 13.9 %all-to-all-done.refs_2_.refs_3_ = f32[4,264,128]{2,1,0:T(8,128)S(1)} async-done(((f32[4,264,128]{2,1,0:T(8,128)}), f32[4,264,128]{2,1,0:T(8,128)S(1)}, u32[]{:S(2)}, u32[]{:S(2)}) %all-to-all-start) | async-done | bytes 540704 | tf_op jit(solution)/shard_map/rows_in/all_to_all | solution.py:419
  24.5 5.8 %collective-permute-start = (bf16[4,64,128]{2,1,0:T(8,128)(2,1)S(1)}, bf16[4,64,128]{2,1,0:T(8,128)(2,1)S(1)}, u32[]{:S(2)}, u32[]{:S(2)}) collective-permute-start(bf16[4,64,128]{2,1,0:T(8,128)(2,1)S(1)} %get-tuple-element.46), channel_id=1, source_target_pairs={{0,4},{4,0},{8,12},{12,8},{16,20},{20,16},{24,28},{28,24},{32,36},... | collective-permute-start | bytes 196616 | tf_op jit(solution)/shard_map/row_halo/ppermute | solution.py:486
  30.2 5.3 %collective-permute-start.1 = (bf16[4,64,128]{2,1,0:T(8,128)(2,1)S(1)}, bf16[4,64,128]{2,1,0:T(8,128)(2,1)S(1)}, u32[]{:S(2)}, u32[]{:S(2)}) collective-permute-start(bf16[4,64,128]{2,1,0:T(8,128)(2,1)S(1)} %get-tuple-element.45), channel_id=1, source_target_pairs={{4,20},{12,28},{16,32},{20,4},{24,40},{28,12},{32,16},{36,52},{40,... | collective-permute-start | bytes 196616 | tf_op jit(solution)/shard_map/row_halo/ppermute | solution.py:487
  35.6 0.0 copy-done.6
  35.6 0.0 copy-done.7
  35.6 0.0 copy-done.8
  35.6 0.0 copy-done.5
  35.6 0.0 copy-done.4
  35.6 0.0 copy-done.3
  35.6 0.0 copy-done.2
  35.6 0.0 copy-done
  35.7 2.3 %early.1 = (f32[128,512]{1,0:T(8,128)S(1)}, bf16[2,640,512]{2,1,0:T(8,128)(2,1)S(1)}, f32[2,384,512]{2,1,0:T(8,128)S(1)}, f32[2,384,512]{2,1,0:T(8,128)S(1)}) custom-call(s32[1]{0:T(128)} %bitcast.refs_0_, s32[2]{0:T(128)S(1)} %copy-done.5, f32[4,264,128]{2,1,0:T(8,128)S(1)} %all-to-all-done.refs_2_.refs_3_, f32[192,384]{1,0:T(8,128)S(1)} %copy-done.8, ...), custom_call_target="tpu_custom_call" | custom-call | flops 3000000000 | bytes 1000000 | tf_op jit(solution)/shard_map/early/pallas_call | solution.py:493
  37.9 0.0 copy-start.13
  37.9 0.0 collective-permute-done.refs_1_
  38.0 0.0 collective-permute-done.1.refs_2_
  38.0 2.3 %weights.1 = (bf16[2,384,512]{2,1,0:T(8,128)(2,1)S(1)}, f32[128,512]{1,0:T(8,128)S(1)}, f32[32,36,128]{2,1,0:T(8,128)S(1)}, bf16[32,36,128]{2,1,0:T(8,128)(2,1)S(1)}) custom-call(s32[1]{0:T(128)} %bitcast.refs_0_, bf16[4,64,128]{2,1,0:T(8,128)(2,1)S(1)} %collective-permute-done.refs_1_, bf16[4,64,128]{2,1,0:T(8,128)(2,1)S(1)} %collective-permute-done.1.refs_2_, ...), custom_call_target="tpu_custom_call" | custom-call | flops 3000000000 | bytes 1000000 | tf_op jit(solution)/shard_map/weights/pallas_call | solution.py:524
  40.2 0.0 copy-start.9
  40.3 1.9 %collective-permute-start.7 = (bf16[32,36,128]{2,1,0:T(8,128)(2,1)S(1)}, bf16[32,36,128]{2,1,0:T(8,128)(2,1)S(1)}, u32[]{:S(2)}, u32[]{:S(2)}) collective-permute-start(bf16[32,36,128]{2,1,0:T(8,128)(2,1)S(1)} %get-tuple-element.41), channel_id=1, source_target_pairs={{0,16},{16,0},{1,17},{17,1},{2,18},{18,2},{3,19},{19,3},{4,20},{20... | collective-permute-start | bytes 884744 | tf_op jit(solution)/shard_map/weights_core/ppermute | solution.py:561
  42.2 1.6 %collective-permute-done.7 = bf16[32,36,128]{2,1,0:T(8,128)(2,1)S(1)} collective-permute-done((bf16[32,36,128]{2,1,0:T(8,128)(2,1)S(1)}, bf16[32,36,128]{2,1,0:T(8,128)(2,1)S(1)}, u32[]{:S(2)}, u32[]{:S(2)}) %collective-permute-start.7) | collective-permute-done | bytes 294944 | tf_op jit(solution)/shard_map/weights_core/ppermute | solution.py:561
  43.8 0.8 add_convert_fusion
  44.6 14.6 %all-to-all-start.1 = ((bf16[32,36,128]{2,1,0:T(8,128)(2,1)}), bf16[32,36,128]{2,1,0:T(8,128)(2,1)S(1)}, u32[]{:S(2)}, u32[]{:S(2)}) async-start(bf16[32,36,128]{2,1,0:T(8,128)(2,1)} %add_convert_fusion), calls=%async_computation.1 | async-start | bytes 655360 | tf_op jit(solution)/shard_map/weights_plane/all_to_all | solution.py:419
  59.2 0.2 copy.21
  59.5 0.0 copy-start.14
  59.5 0.9 copy-done.14
  60.4 0.9 stencil.1
  61.3 0.0 copy-start.11
  61.3 0.7 copy-done.11
  62.0 1.9 %collective-permute-start.2 = (bf16[4,64,128]{2,1,0:T(8,128)(2,1)S(1)}, bf16[4,64,128]{2,1,0:T(8,128)(2,1)S(1)}, u32[]{:S(2)}, u32[]{:S(2)}) collective-permute-start(bf16[4,64,128]{2,1,0:T(8,128)(2,1)S(1)} %get-tuple-element.32), channel_id=1, source_target_pairs={{4,20},{12,28},{16,32},{20,4},{24,40},{28,12},{32,16},{36,52},{40,... | collective-permute-start | bytes 196616 | tf_op jit(solution)/shard_map/fields/ppermute | solution.py:564
  63.9 4.0 %collective-permute-done.2.refs_6_.refs_1_ = bf16[4,64,128]{2,1,0:T(8,128)(2,1)S(1)} collective-permute-done((bf16[4,64,128]{2,1,0:T(8,128)(2,1)S(1)}, bf16[4,64,128]{2,1,0:T(8,128)(2,1)S(1)}, u32[]{:S(2)}, u32[]{:S(2)}) %collective-permute-start.2) | collective-permute-done | bytes 65568 | tf_op jit(solution)/shard_map/fields/ppermute | solution.py:564
  67.9 2.4 %all-to-all-done.1.refs_0_ = bf16[32,36,128]{2,1,0:T(8,128)(2,1)S(1)} async-done(((bf16[32,36,128]{2,1,0:T(8,128)(2,1)}), bf16[32,36,128]{2,1,0:T(8,128)(2,1)S(1)}, u32[]{:S(2)}, u32[]{:S(2)}) %all-to-all-start.1) | async-done | bytes 294944 | tf_op jit(solution)/shard_map/weights_plane/all_to_all | solution.py:419
  70.3 0.7 weights_plane.1
  71.0 4.9 %all-to-all-start.2 = ((bf16[12,36,128]{2,1,0:T(8,128)(2,1)}), bf16[12,36,128]{2,1,0:T(8,128)(2,1)S(1)}, u32[]{:S(2)}, u32[]{:S(2)}) async-start(bf16[12,36,128]{2,1,0:T(8,128)(2,1)} %weights_plane.1), calls=%async_computation.2 | async-start | bytes 245760 | tf_op jit(solution)/shard_map/weights_length/all_to_all | solution.py:419
  76.0 5.2 %collective-permute-start.3 = (bf16[4,64,128]{2,1,0:T(8,128)(2,1)S(1)}, bf16[4,64,128]{2,1,0:T(8,128)(2,1)S(1)}, u32[]{:S(2)}, u32[]{:S(2)}) collective-permute-start(bf16[4,64,128]{2,1,0:T(8,128)(2,1)S(1)} %get-tuple-element.33), channel_id=1, source_target_pairs={{0,4},{4,0},{8,12},{12,8},{16,20},{20,16},{24,28},{28,24},{32,36},... | collective-permute-start | bytes 196616 | tf_op jit(solution)/shard_map/fields/ppermute | solution.py:565
  81.1 1.6 %collective-permute-done.3.refs_7_ = bf16[4,64,128]{2,1,0:T(8,128)(2,1)S(1)} collective-permute-done((bf16[4,64,128]{2,1,0:T(8,128)(2,1)S(1)}, bf16[4,64,128]{2,1,0:T(8,128)(2,1)S(1)}, u32[]{:S(2)}, u32[]{:S(2)}) %collective-permute-start.3) | collective-permute-done | bytes 65568 | tf_op jit(solution)/shard_map/fields/ppermute | solution.py:565
  82.8 0.9 copy-done.10
  83.7 0.9 copy-done.12
  84.7 0.7 fields.1
  85.4 1.0 all-to-all-done.2.refs_0_
  86.4 0.8 weights_length.1
  87.2 7.6 %all-to-all-start.3 = ((bf16[32,36,128]{2,1,0:T(8,128)(2,1)}), bf16[32,36,128]{2,1,0:T(8,128)(2,1)S(1)}, u32[]{:S(2)}, u32[]{:S(2)}) async-start(bf16[32,36,128]{2,1,0:T(8,128)(2,1)} %weights_length.1), calls=%async_computation.3 | async-start | bytes 655360 | tf_op jit(solution)/shard_map/weights_back/all_to_all | solution.py:419
  94.8 4.0 %collective-permute-start.4 = (bf16[256,128]{1,0:T(8,128)(2,1)S(1)}, bf16[256,128]{1,0:T(8,128)(2,1)S(1)}, u32[]{:S(2)}, u32[]{:S(2)}) collective-permute-start(bf16[256,128]{1,0:T(8,128)(2,1)S(1)} %get-tuple-element.35), channel_id=1, source_target_pairs={{0,4},{4,0},{8,12},{12,8},{1,5},{5,1},{9,13},{13,9},{2,6},{6,2},{1... | collective-permute-start | bytes 196616 | tf_op jit(solution)/shard_map/rows_out/ppermute | solution.py:583
  98.8 5.2 %collective-permute-start.5 = (bf16[256,128]{1,0:T(8,128)(2,1)S(1)}, bf16[256,128]{1,0:T(8,128)(2,1)S(1)}, u32[]{:S(2)}, u32[]{:S(2)}) collective-permute-start(bf16[256,128]{1,0:T(8,128)(2,1)S(1)} %get-tuple-element.36), channel_id=1, source_target_pairs={{0,8},{4,12},{8,0},{12,4},{1,9},{5,13},{9,1},{13,5},{2,10},{6,14},... | collective-permute-start | bytes 196616 | tf_op jit(solution)/shard_map/rows_out/ppermute | solution.py:583
  104.0 2.1 %collective-permute-start.6 = (bf16[256,128]{1,0:T(8,128)(2,1)S(1)}, bf16[256,128]{1,0:T(8,128)(2,1)S(1)}, u32[]{:S(2)}, u32[]{:S(2)}) collective-permute-start(bf16[256,128]{1,0:T(8,128)(2,1)S(1)} %get-tuple-element.37), channel_id=1, source_target_pairs={{0,12},{4,8},{8,4},{12,0},{1,13},{5,9},{9,5},{13,1},{2,14},{6,10},... | collective-permute-start | bytes 196616 | tf_op jit(solution)/shard_map/rows_out/ppermute | solution.py:583
  106.2 0.0 collective-permute-done.4.refs_2_.refs_1_
  106.2 3.1 %collective-permute-done.5.refs_3_.refs_2_ = bf16[256,128]{1,0:T(8,128)(2,1)S(1)} collective-permute-done((bf16[256,128]{1,0:T(8,128)(2,1)S(1)}, bf16[256,128]{1,0:T(8,128)(2,1)S(1)}, u32[]{:S(2)}, u32[]{:S(2)}) %collective-permute-start.5) | collective-permute-done | bytes 65568 | tf_op jit(solution)/shard_map/rows_out/ppermute | solution.py:583
  109.3 3.0 %collective-permute-done.6.refs_4_.refs_3_ = bf16[256,128]{1,0:T(8,128)(2,1)S(1)} collective-permute-done((bf16[256,128]{1,0:T(8,128)(2,1)S(1)}, bf16[256,128]{1,0:T(8,128)(2,1)S(1)}, u32[]{:S(2)}, u32[]{:S(2)}) %collective-permute-start.6) | collective-permute-done | bytes 65568 | tf_op jit(solution)/shard_map/rows_out/ppermute | solution.py:583
  112.3 0.0 all-to-all-done.3.refs_0_
  112.3 5.6 %collective-permute-start.8 = (bf16[32,36,128]{2,1,0:T(8,128)(2,1)S(1)}, bf16[32,36,128]{2,1,0:T(8,128)(2,1)S(1)}, u32[]{:S(2)}, u32[]{:S(2)}) collective-permute-start(bf16[32,36,128]{2,1,0:T(8,128)(2,1)S(1)} %weights_back.2.refs_1_), channel_id=1, source_target_pairs={{0,16},{16,0},{1,17},{17,1},{2,18},{18,2},{3,19},{19,3},{4,20},{20... | collective-permute-start | bytes 884744 | tf_op jit(solution)/shard_map/weights_back/ppermute | solution.py:604
  117.9 0.9 bands_out.1
  118.8 0.4 collective-permute-done.8.refs_2_
  119.2 1.2 weights_back.3
  (9 shorter events, 0.1 us)
Async XLA Ops:
  0.6 34.9 %copy-start.6 = (bf16[384,512]{1,0:T(8,128)(2,1)S(1)}, bf16[384,512]{1,0:T(8,128)(2,1)}, u32[]{:S(2)}) copy-start(bf16[384,512]{1,0:T(8,128)(2,1)} %constant.69.clone.refs_4_.refs_3_) | copy-start | bytes 1179652
  0.6 34.9 %copy-start.7 = (bf16[384,512]{1,0:T(8,128)(2,1)S(1)}, bf16[384,512]{1,0:T(8,128)(2,1)}, u32[]{:S(2)}) copy-start(bf16[384,512]{1,0:T(8,128)(2,1)} %constant.70.clone.refs_5_.refs_4_) | copy-start | bytes 1179652
  0.7 34.9 %copy-start.8 = (f32[192,384]{1,0:T(8,128)S(1)}, f32[192,384]{1,0:T(8,128)}, u32[]{:S(2)}) copy-start(f32[192,384]{1,0:T(8,128)} %constant.71.clone.refs_3_.refs_2_) | copy-start | bytes 884740
  0.7 9.7 %copy-start.1 = (bf16[64,384]{1,0:T(8,128)(2,1)S(1)}, bf16[64,384]{1,0:T(8,128)(2,1)}, u32[]{:S(2)}) copy-start(bf16[64,384]{1,0:T(8,128)(2,1)} %refs_9_.3) | copy-start | bytes 147460
  0.7 9.8 %copy-start.15 = (f32[384]{0:T(512)S(1)}, f32[384]{0:T(512)}, u32[]{:S(2)}) copy-start(f32[384]{0:T(512)} %param.23) | copy-start | bytes 4612
  0.7 34.9 %copy-start.5 = (s32[2]{0:T(128)S(1)}, s32[2]{0:T(128)}, u32[]{:S(2)}) copy-start(s32[2]{0:T(128)} %refs_1_.1) | copy-start | bytes 28
  0.7 34.9 %copy-start.4 = (f32[2,64]{1,0:T(2,128)S(1)}, f32[2,64]{1,0:T(2,128)}, u32[]{:S(2)}) copy-start(f32[2,64]{1,0:T(2,128)} %refs_6_.1) | copy-start | bytes 1540
  0.7 34.9 %copy-start.3 = (f32[16,64]{1,0:T(8,128)S(1)}, f32[16,64]{1,0:T(8,128)}, u32[]{:S(2)}) copy-start(f32[16,64]{1,0:T(8,128)} %refs_7_.1) | copy-start | bytes 12292
  0.7 34.9 %copy-start.2 = (f32[32,64]{1,0:T(8,128)S(1)}, f32[32,64]{1,0:T(8,128)}, u32[]{:S(2)}) copy-start(f32[32,64]{1,0:T(8,128)} %refs_8_.2) | copy-start | bytes 24580
  0.7 34.9 %copy-start = (bf16[384,640]{1,0:T(8,128)(2,1)S(1)}, bf16[384,640]{1,0:T(8,128)(2,1)}, u32[]{:S(2)}) copy-start(bf16[384,640]{1,0:T(8,128)(2,1)} %refs_8_.3) | copy-start | bytes 1474564
  2.7 21.7 %all-to-all-start = ((f32[4,264,128]{2,1,0:T(8,128)}), f32[4,264,128]{2,1,0:T(8,128)S(1)}, u32[]{:S(2)}, u32[]{:S(2)}) async-start(f32[4,264,128]{2,1,0:T(8,128)} %rows_in.1), calls=%async_computation | async-start | bytes 1081344 | tf_op jit(solution)/shard_map/rows_in/all_to_all | solution.py:419
  24.5 13.5 %collective-permute-start = (bf16[4,64,128]{2,1,0:T(8,128)(2,1)S(1)}, bf16[4,64,128]{2,1,0:T(8,128)(2,1)S(1)}, u32[]{:S(2)}, u32[]{:S(2)}) collective-permute-start(bf16[4,64,128]{2,1,0:T(8,128)(2,1)S(1)} %get-tuple-element.46), channel_id=1, source_target_pairs={{0,4},{4,0},{8,12},{12,8},{16,20},{20,16},{24,28},{28,24},{32,36},... | collective-permute-start | bytes 196616 | tf_op jit(solution)/shard_map/row_halo/ppermute | solution.py:486
  30.2 7.7 %collective-permute-start.1 = (bf16[4,64,128]{2,1,0:T(8,128)(2,1)S(1)}, bf16[4,64,128]{2,1,0:T(8,128)(2,1)S(1)}, u32[]{:S(2)}, u32[]{:S(2)}) collective-permute-start(bf16[4,64,128]{2,1,0:T(8,128)(2,1)S(1)} %get-tuple-element.45), channel_id=1, source_target_pairs={{4,20},{12,28},{16,32},{20,4},{24,40},{28,12},{32,16},{36,52},{40,... | collective-permute-start | bytes 196616 | tf_op jit(solution)/shard_map/row_halo/ppermute | solution.py:487
  37.9 2.3 %copy-start.13 = (f32[128,512]{1,0:T(8,128)}, f32[128,512]{1,0:T(8,128)S(1)}, u32[]{:S(2)}) copy-start(f32[128,512]{1,0:T(8,128)S(1)} %get-tuple-element.25.refs_4_.refs_2_) | copy-start | bytes 786436
  40.2 19.0 %copy-start.9 = (f32[128,512]{1,0:T(8,128)}, f32[128,512]{1,0:T(8,128)S(1)}, u32[]{:S(2)}) copy-start(f32[128,512]{1,0:T(8,128)S(1)} %get-tuple-element.29.refs_1_) | copy-start | bytes 786436
  40.3 3.5 %collective-permute-start.7 = (bf16[32,36,128]{2,1,0:T(8,128)(2,1)S(1)}, bf16[32,36,128]{2,1,0:T(8,128)(2,1)S(1)}, u32[]{:S(2)}, u32[]{:S(2)}) collective-permute-start(bf16[32,36,128]{2,1,0:T(8,128)(2,1)S(1)} %get-tuple-element.41), channel_id=1, source_target_pairs={{0,16},{16,0},{1,17},{17,1},{2,18},{18,2},{3,19},{19,3},{4,20},{20... | collective-permute-start | bytes 884744 | tf_op jit(solution)/shard_map/weights_core/ppermute | solution.py:561
  44.6 25.7 %all-to-all-start.1 = ((bf16[32,36,128]{2,1,0:T(8,128)(2,1)}), bf16[32,36,128]{2,1,0:T(8,128)(2,1)S(1)}, u32[]{:S(2)}, u32[]{:S(2)}) async-start(bf16[32,36,128]{2,1,0:T(8,128)(2,1)} %add_convert_fusion), calls=%async_computation.1 | async-start | bytes 655360 | tf_op jit(solution)/shard_map/weights_plane/all_to_all | solution.py:419
  59.5 1.0 copy-start.14
  61.3 0.7 copy-start.11
  62.0 5.9 %collective-permute-start.2 = (bf16[4,64,128]{2,1,0:T(8,128)(2,1)S(1)}, bf16[4,64,128]{2,1,0:T(8,128)(2,1)S(1)}, u32[]{:S(2)}, u32[]{:S(2)}) collective-permute-start(bf16[4,64,128]{2,1,0:T(8,128)(2,1)S(1)} %get-tuple-element.32), channel_id=1, source_target_pairs={{4,20},{12,28},{16,32},{20,4},{24,40},{28,12},{32,16},{36,52},{40,... | collective-permute-start | bytes 196616 | tf_op jit(solution)/shard_map/fields/ppermute | solution.py:564
  71.0 15.4 %all-to-all-start.2 = ((bf16[12,36,128]{2,1,0:T(8,128)(2,1)}), bf16[12,36,128]{2,1,0:T(8,128)(2,1)S(1)}, u32[]{:S(2)}, u32[]{:S(2)}) async-start(bf16[12,36,128]{2,1,0:T(8,128)(2,1)} %weights_plane.1), calls=%async_computation.2 | async-start | bytes 245760 | tf_op jit(solution)/shard_map/weights_length/all_to_all | solution.py:419
  76.0 6.8 %collective-permute-start.3 = (bf16[4,64,128]{2,1,0:T(8,128)(2,1)S(1)}, bf16[4,64,128]{2,1,0:T(8,128)(2,1)S(1)}, u32[]{:S(2)}, u32[]{:S(2)}) collective-permute-start(bf16[4,64,128]{2,1,0:T(8,128)(2,1)S(1)} %get-tuple-element.33), channel_id=1, source_target_pairs={{0,4},{4,0},{8,12},{12,8},{16,20},{20,16},{24,28},{28,24},{32,36},... | collective-permute-start | bytes 196616 | tf_op jit(solution)/shard_map/fields/ppermute | solution.py:565
  82.8 1.0 copy-start.10
  83.7 0.9 copy-start.12
  87.2 25.2 %all-to-all-start.3 = ((bf16[32,36,128]{2,1,0:T(8,128)(2,1)}), bf16[32,36,128]{2,1,0:T(8,128)(2,1)S(1)}, u32[]{:S(2)}, u32[]{:S(2)}) async-start(bf16[32,36,128]{2,1,0:T(8,128)(2,1)} %weights_length.1), calls=%async_computation.3 | async-start | bytes 655360 | tf_op jit(solution)/shard_map/weights_back/all_to_all | solution.py:419
  94.8 11.4 %collective-permute-start.4 = (bf16[256,128]{1,0:T(8,128)(2,1)S(1)}, bf16[256,128]{1,0:T(8,128)(2,1)S(1)}, u32[]{:S(2)}, u32[]{:S(2)}) collective-permute-start(bf16[256,128]{1,0:T(8,128)(2,1)S(1)} %get-tuple-element.35), channel_id=1, source_target_pairs={{0,4},{4,0},{8,12},{12,8},{1,5},{5,1},{9,13},{13,9},{2,6},{6,2},{1... | collective-permute-start | bytes 196616 | tf_op jit(solution)/shard_map/rows_out/ppermute | solution.py:583
  98.8 10.5 %collective-permute-start.5 = (bf16[256,128]{1,0:T(8,128)(2,1)S(1)}, bf16[256,128]{1,0:T(8,128)(2,1)S(1)}, u32[]{:S(2)}, u32[]{:S(2)}) collective-permute-start(bf16[256,128]{1,0:T(8,128)(2,1)S(1)} %get-tuple-element.36), channel_id=1, source_target_pairs={{0,8},{4,12},{8,0},{12,4},{1,9},{5,13},{9,1},{13,5},{2,10},{6,14},... | collective-permute-start | bytes 196616 | tf_op jit(solution)/shard_map/rows_out/ppermute | solution.py:583
  104.0 8.3 %collective-permute-start.6 = (bf16[256,128]{1,0:T(8,128)(2,1)S(1)}, bf16[256,128]{1,0:T(8,128)(2,1)S(1)}, u32[]{:S(2)}, u32[]{:S(2)}) collective-permute-start(bf16[256,128]{1,0:T(8,128)(2,1)S(1)} %get-tuple-element.37), channel_id=1, source_target_pairs={{0,12},{4,8},{8,4},{12,0},{1,13},{5,9},{9,5},{13,1},{2,14},{6,10},... | collective-permute-start | bytes 196616 | tf_op jit(solution)/shard_map/rows_out/ppermute | solution.py:583
  112.3 6.8 %collective-permute-start.8 = (bf16[32,36,128]{2,1,0:T(8,128)(2,1)S(1)}, bf16[32,36,128]{2,1,0:T(8,128)(2,1)S(1)}, u32[]{:S(2)}, u32[]{:S(2)}) collective-permute-start(bf16[32,36,128]{2,1,0:T(8,128)(2,1)S(1)} %weights_back.2.refs_1_), channel_id=1, source_target_pairs={{0,16},{16,0},{1,17},{17,1},{2,18},{18,2},{3,19},{19,3},{4,20},{20... | collective-permute-start | bytes 884744 | tf_op jit(solution)/shard_map/weights_back/ppermute | solution.py:604
